TPU v7x, 32 devices: a whole 2x2x4 slice. The times are simulated.
32 devices in a mesh: fsdp: 8 (over z, core), grp: 2 (over y), tp: 2 (over x).
Axes of the slice: x: 2, y: 2, z: 4, core: 2. Of those that a mesh axis runs over, the one named last changes fastest.
Arguments:
- hidden_states: bfloat16 [4, 128, 8192], P(None, ('fsdp', 'grp'), 'tp'), may hold values from -6 to 6
- queries: bfloat16 [4, 128, 64, 128], P(None, ('fsdp', 'grp'), 'tp'), as said below
- cache_keys: bfloat16 [128, 768, 8, 128], P(('fsdp', 'grp'), None, 'tp'), as said below
- cache_values: bfloat16 [128, 768, 8, 128], P(('fsdp', 'grp'), None, 'tp'), may hold values from -6 to 6
- cache_lengths: int32 [128], P(('fsdp', 'grp')), may hold values from 2 to 768, as said below
- projection_weight_matrices: bfloat16 [2, 8192, 1024], P(None, None, 'tp'), may hold values from -0.0625 to 0.0625
- factor_down: bfloat16 [2, 8192, 64], P(None, ('fsdp', 'grp')), may hold values from -0.0625 to 0.0625
- factor_up: bfloat16 [2, 64, 1024], P(None, None, ('fsdp', 'grp')), may hold values from -0.375 to 0.375
Outputs:
- merged: bfloat16 [2, 8192, 1024], P(None, None, 'tp')
- attended: bfloat16 [4, 128, 64, 128], P(None, ('fsdp', 'grp'), 'tp')
Inputs may be any that keep to these rules, and one draw needn't show every extreme that they name: `cache_lengths`: at least 2; some row has exactly 768. `queries`: real-valued. `cache_keys`: real-valued.
All inputs are finite; a program needn't handle non-finite values.
Results may differ from a plain program's by a relative error of at most 0.0066.
Values may be sent and summed in bfloat16 or wider, within the bound.
No kernel may reach another device: no remote copies, remote signals or barrier semaphores. Data moves between devices by JAX's collectives and lax.ppermute only.
A program may use at most 192 MiB of HBM per device.

v0:
```python
import math

import jax
import jax.numpy as jnp
from jax import lax
from jax.sharding import PartitionSpec as P

ADAPTER_SCALING = 2.0


def shards(
    hidden_states,
    queries,
    cache_keys,
    cache_values,
    cache_lengths,
    projection_weight_matrices,
    factor_down,
    factor_up,
):
    lane_index = lax.axis_index("tp")
    local_width = projection_weight_matrices.shape[2]
    pair_count = factor_down.shape[0]
    step_count, row_count, head_count, head_size = queries.shape
    kv_count = cache_keys.shape[2]
    inverse = 1.0 / math.sqrt(head_size)
    grouped = queries.reshape(step_count, row_count, kv_count, head_count // kv_count, head_size)
    old_scores = (
        jnp.einsum("srkgh,rckh->srkgc", grouped, cache_keys, preferred_element_type=jnp.float32)
        * inverse
    )
    places = jnp.arange(cache_keys.shape[1], dtype=jnp.int32)
    filled = places[None, :] < cache_lengths[:, None]
    old_scores = jnp.where(filled[None, :, None, None, :], old_scores, -jnp.inf)
    down_all, up_all = (
        lax.all_gather(factor_down, ("fsdp", "grp"), axis=1, tiled=True),
        lax.all_gather(factor_up, ("fsdp", "grp"), axis=2, tiled=True),
    )
    up_mine = lax.dynamic_slice_in_dim(up_all, lane_index * local_width, local_width, 2)
    weight_increment = jnp.einsum(
        "kdr,krw->kdw", down_all, up_mine, preferred_element_type=jnp.float32
    )
    merged = (
        projection_weight_matrices.astype(jnp.float32) + ADAPTER_SCALING * weight_increment
    ).astype(jnp.bfloat16)
    full_states = lax.all_gather(hidden_states, "tp", axis=2, tiled=True)
    fresh_rows = jnp.einsum(
        "srd,kdw->ksrw", full_states, merged, preferred_element_type=jnp.float32
    )
    fresh_rows = fresh_rows.astype(jnp.bfloat16).reshape(
        pair_count, step_count, row_count, kv_count, head_size
    )
    new_keys = fresh_rows[0]
    new_values = fresh_rows[1]
    new_scores = (
        jnp.einsum("srkgh,urkh->srkgu", grouped, new_keys, preferred_element_type=jnp.float32)
        * inverse
    )
    order = jnp.arange(step_count, dtype=jnp.int32)
    earlier = order[None, :] <= order[:, None]
    new_scores = jnp.where(earlier[:, None, None, None, :], new_scores, -jnp.inf)
    highest = jnp.maximum(jnp.max(old_scores, -1), jnp.max(new_scores, -1))[..., None]
    old_exp = jnp.exp(old_scores - highest)
    new_exp = jnp.exp(new_scores - highest)
    softmax_divisor = (jnp.sum(old_exp, -1) + jnp.sum(new_exp, -1))[..., None]
    old_weights = (old_exp / softmax_divisor).astype(jnp.bfloat16)
    new_weights = (new_exp / softmax_divisor).astype(jnp.bfloat16)
    result = jnp.einsum(
        "srkgc,rckh->srkgh", old_weights, cache_values, preferred_element_type=jnp.float32
    )
    result = result + jnp.einsum(
        "srkgu,urkh->srkgh", new_weights, new_values, preferred_element_type=jnp.float32
    )
    attended = result.reshape(step_count, row_count, head_count, head_size).astype(jnp.bfloat16)
    return (merged, attended)


def solution(mesh):
    return jax.shard_map(
        shards,
        mesh=mesh,
        in_specs=(
            P(None, ("fsdp", "grp"), "tp"),
            P(None, ("fsdp", "grp"), "tp", None),
            P(("fsdp", "grp"), None, "tp", None),
            P(("fsdp", "grp"), None, "tp", None),
            P(("fsdp", "grp")),
            P(None, None, "tp"),
            P(None, ("fsdp", "grp"), None),
            P(None, None, ("fsdp", "grp")),
        ),
        out_specs=(P(None, None, "tp"), P(None, ("fsdp", "grp"), "tp", None)),
        check_vma=False,
    )
```

profile of v0, /device:TPU:0, one launch (start us, length us, event | category | flops | bytes accessed | tf_op | source)
XLA Modules:
  0.0 140.1 jit_solution(12960723415668588160)
XLA Ops:
  7.2 0.0 copy-start
  7.2 0.0 all-gather.2.cloned.1.call-start
  7.2 0.7 all-gather.2.cloned.1.call-update
  7.9 0.8 copy.30
  8.8 0.0 copy-start.1
  8.8 0.0 copy-start.2
  8.8 21.3 %copy.29 = bf16[2,8192,512]{1,2,0:T(8,128)(2,1)} copy(bf16[2,8192,512]{2,1,0:T(8,128)(2,1)} %param.13) | data formatting | bytes 33554432 | tf_op args[5]
  30.1 38.1 %all_gather.9 = bf16[2,64,1024]{1,0,2:T(2,128)(2,1)S(1)} all-gather(bf16[2,64,64]{1,0,2:T(2,128)(2,1)S(1)} %copy.30), channel_id=1, replica_groups=mesh['fsdp'=8,'grp'=2,'tp'=2] {'fsdp','grp'}, dimensions={2}, use_global_device_ids=true | all-gather | bytes 278528 | tf_op jit(solution)/shard_map/all_gather | solution.py:37
  68.2 0.9 constant_dynamic-slice_fusion
  69.1 0.0 copy-done.1
  69.1 7.1 %all_gather.11 = bf16[4,8,8192]{2,1,0:T(8,128)(2,1)} all-gather(bf16[4,8,4096]{2,1,0:T(8,128)(2,1)S(1)} %copy-done.1), channel_id=1, replica_groups=mesh['fsdp'=8,'grp'=2,'tp'=2] {'tp'}, dimensions={2}, use_global_device_ids=true | all-gather | bytes 786432 | tf_op jit(solution)/shard_map/all_gather | solution.py:46
  76.3 0.0 copy-done.2
  76.3 0.1 iota_compare_fusion
  76.3 0.0 copy-done
  76.3 5.0 %bitcast_reduce_fusion = (f32[4,8,4,8]{3,0,2,1:T(4,128)S(1)}, f32[8,4,768,4,8]{2,4,3,1,0:T(8,128)S(1)}) fusion(pred[8,768]{1,0:T(8,128)(4,1)S(1)} %iota_compare_fusion, bf16[8,768,4,128,1]{3,2,1,0,4:T(4,128)(2,1)} %bitcast.64, bf16[4,8,32,128]{3,2,1,0:T(8,128)(2,1)S(1)} %copy-done), kind=kOutput, calls=%fused_computation.9 | convolution fusion | flops 203684864 | bytes 9709568 | tf_op jit(solution)/shard_map/srkgh,rckh->srkgc/dot_general | solution.py:29
  81.4 0.0 all-gather.2.cloned.1.call-done
  81.4 12.0 %fusion = bf16[2,8192,512]{1,2,0:T(8,128)(2,1)} fusion(bf16[2,8192,512]{1,2,0:T(8,128)(2,1)} %copy.29, bf16[2,8192,64]{1,2,0:T(8,128)(2,1)} %all-gather.2.cloned.1.call-done, bf16[2,64,512]{1,0,2:T(2,128)(2,1)} %constant_dynamic-slice_fusion), kind=kOutput, calls=%fused_computation.1 | convolution fusion | flops 1107296256 | bytes 35782656 | tf_op jit(solution)/shard_map/kdr,krw->kdw/dot_general | solution.py:40
  93.5 21.2 %copy.40 = bf16[2,8192,512]{2,1,0:T(8,128)(2,1)} copy(bf16[2,8192,512]{1,2,0:T(8,128)(2,1)} %fusion) | data formatting | bytes 33554432
  114.7 10.7 %fusion.24 = bf16[2,4,8,512]{3,2,1,0:T(8,128)(2,1)S(1)} fusion(bf16[2,8192,512]{1,2,0:T(8,128)(2,1)} %fusion, bf16[4,8,8192]{2,1,0:T(8,128)(2,1)} %all_gather.11), kind=kOutput, calls=%fused_computation.27 | convolution fusion | flops 536903680 | bytes 17367040 | tf_op jit(solution)/shard_map/srd,kdw->ksrw/dot_general | solution.py:47
  125.4 1.3 fusion.38
  126.7 0.2 fusion.31
  127.0 1.0 fusion.8
  128.0 4.1 %fusion.14 = f32[4,8,4,8,128]{4,3,0,2,1:T(8,128)S(1)} fusion(bf16[8,768,4,128,1]{3,2,1,0,4:T(4,128)(2,1)} %bitcast.65, f32[8,4,768,4,8]{2,4,3,1,0:T(8,128)S(1)} %get-tuple-element.11, f32[4,8,4,8]{3,0,2,1:T(4,128)S(1)} %add.18, f32[4,8,4,8]{3,0,2,1:T(4,128)S(1)} %max.7, pred[8,768]{1,0:T(8,128)(4,1)S(1)} %iota_compare_fusion), kind=kOutput, calls=%fused_computation.19 | convolution fusion | flops 205258752 | bytes 9975808 | tf_op jit(solution)/shard_map/srkgc,rckh->srkgh/dot_general | solution.py:68
  132.1 0.4 fusion.18
  132.5 0.8 copy.82
  (4 shorter events, 0.1 us)
Async XLA Ops:
  7.2 69.2 %copy-start = (bf16[4,8,32,128]{3,2,1,0:T(8,128)(2,1)S(1)}, bf16[4,8,32,128]{3,2,1,0:T(8,128)(2,1)}, u32[]{:S(2)}) copy-start(bf16[4,8,32,128]{3,2,1,0:T(8,128)(2,1)} %param.9) | copy-start | bytes 786436
  7.2 74.2 %all-gather.2.cloned.1.call-start = ((), (), s32[]{:S(2)}) async-start(), calls=%async_computation | async-start | bytes 2228224 | tf_op jit(solution)/shard_map/all_gather | solution.py:36
  8.8 60.3 %copy-start.1 = (bf16[4,8,4096]{2,1,0:T(8,128)(2,1)S(1)}, bf16[4,8,4096]{2,1,0:T(8,128)(2,1)}, u32[]{:S(2)}) copy-start(bf16[4,8,4096]{2,1,0:T(8,128)(2,1)} %param.8) | copy-start | bytes 786436
  8.8 67.5 %copy-start.2 = (s32[8]{0:T(128)S(1)}, s32[8]{0:T(128)}, u32[]{:S(2)}) copy-start(s32[8]{0:T(128)} %param.12) | copy-start | bytes 100
Sparse Core Ops, SparseCore 0:
  10.1 46.6 all-gather.1
where the time goes:
time: 141 us; the launch traced here: 140 us
  blocking collectives  45.3 us (32%)
  local copies, waits for them, and re-layouts  45 us (32%)
  matrix products  33.6 us (24%)
  between operations  14.1 us (10%)
    unnamed x9, local copies, waits for them, and re-layouts  43.4 us
    all_gather x1, blocking collectives, shards(): lax.all_gather(factor_up, ('fsdp', 'grp'), axis=2, tiled=True)  38.1 us
    dot_general x1, matrix products, shards(): jnp.einsum('kdr,krw->kdw', down_all, up_mine, preferred_element_type=jnp....  12 us
    dot_general x1, matrix products, shards(): jnp.einsum('srd,kdw->ksrw', full_states, merged, preferred_element_type=j...  10.7 us
    all_gather x1, blocking collectives, shards(): full_states = lax.all_gather(hidden_states, 'tp', axis=2, tiled=True)  7.14 us
    dot_general x1, matrix products, shards(): jnp.einsum('srkgh,rckh->srkgc', grouped, cache_keys, preferred_element_ty...  5.03 us
    dot_general x1, matrix products, shards(): jnp.einsum('srkgc,rckh->srkgh', old_weights, cache_values, preferred_elem...  4.14 us
  transfers between devices with their start and end apart: 1, of which 0 were waited for; matrix products, arithmetic and copies ran while one was open for 20% of the time, Pallas kernels for 0%

commit v1 on v0

v1 whole, which is shorter than its diff:
```python
import functools
import math

import jax
import jax.numpy as jnp
from jax import lax
from jax.experimental import pallas as pl
from jax.experimental.pallas import tpu as pltpu
from jax.sharding import PartitionSpec as P

AXES = ("fsdp", "grp", "tp")
ADAPTER_SCALING = 2.0
LOG2E = math.log2(math.e)
MIB = 1024 * 1024
ANY = pl.BlockSpec(memory_space=pl.ANY)
VMEM = pl.BlockSpec(memory_space=pltpu.VMEM)
SMEM = pl.BlockSpec(memory_space=pltpu.SMEM)


class Layout:
    def __init__(self, mesh):
        self.fsdp, self.grp, self.tp = (mesh.shape[a] for a in AXES)
        self.depth = self.fsdp // 2
        self.ring = self.depth * self.grp
        self.block = self.depth // self.tp

    def flat(self, z, core, g, t):
        return ((z * 2 + core) * self.grp + g) * self.tp + t

    def devices(self):
        for z in range(self.depth):
            for core in range(2):
                for g in range(self.grp):
                    for t in range(self.tp):
                        yield z, core, g, t

    def place(self, z, g):
        return g * self.depth + (z if g % 2 == 0 else self.depth - 1 - z)

    def at(self, position):
        g, z = divmod(position, self.depth)
        return (z if g % 2 == 0 else self.depth - 1 - z), g

    def ring_step(self, step):
        pairs = []
        for z, core, g, t in self.devices():
            to_z, to_g = self.at((self.place(z, g) + step) % self.ring)
            pairs.append((self.flat(z, core, g, t), self.flat(to_z, core, to_g, t)))
        return pairs

    def core_swap(self):
        return [
            (self.flat(z, c, g, t), self.flat(z, 1 - c, g, t)) for z, c, g, t in self.devices()
        ]

    def feature_step(self, step):
        return [
            (self.flat(z, c, g, (t + step) % self.tp), self.flat(z, c, g, t))
            for z, c, g, t in self.devices()
        ]

    def column_step(self, shift, turn):
        pairs = []
        for z, c, g, t in self.devices():
            source = t * self.block + (z % self.block + shift) % self.block
            pairs.append(
                (
                    self.flat(source, c, (g + turn) % self.grp, z // self.block),
                    self.flat(z, c, g, t),
                )
            )
        return pairs


def attend_cache(first, count, sizes, scale, *refs):
    lengths, q_ref, k_hbm, v_hbm = refs[:4]
    o_ref, lse_ref, k_buf, v_buf, bias, sems = refs[-6:]
    steps, _, heads, size = q_ref.shape
    kv = k_hbm.shape[1] // sizes[-1]
    lanes = steps * heads
    width = k_buf.shape[1]

    def by_length(row, act):
        length = lengths[first + row]
        below = 0
        for slots in sizes:

            @pl.when((length > below) & (length <= slots))
            def _():
                act(row, slots, length)

            below = slots

    def copies(row, slots):
        part = pl.ds(0, slots * kv)
        return (
            pltpu.make_async_copy(
                k_hbm.at[first + row, part], k_buf.at[row, part], sems.at[row, 0]
            ),
            pltpu.make_async_copy(
                v_hbm.at[first + row, part], v_buf.at[row, part], sems.at[row, 1]
            ),
        )

    def begin(row, slots, length):
        for copy in copies(row, slots):
            copy.start()

    def compute(row, slots, length):
        k_copy, v_copy = copies(row, slots)
        n = slots * kv
        q = q_ref[:, first + row].reshape(lanes, size)
        k_copy.wait()
        s = lax.dot_general(
            q, k_buf[row, :n], (((1,), (1,)), ((), ())), preferred_element_type=jnp.float32
        )
        column = lax.broadcasted_iota(jnp.int32, (1, n), 1)
        open_slots = jnp.where(column < length * kv, 0.0, -jnp.inf)
        s = s * scale + bias[:, :n] + open_slots
        highest = jnp.max(s, axis=1, keepdims=True)
        p = jnp.exp2(s - highest)
        total = jnp.sum(p, axis=1, keepdims=True)
        v_copy.wait()
        o = jnp.dot(p.astype(jnp.bfloat16), v_buf[row, :n], preferred_element_type=jnp.float32)
        o_ref[:, row] = (o / total).reshape(steps, heads, size)
        lse = highest + jnp.log(total) * LOG2E
        lse_ref[:, row] = jnp.broadcast_to(lse, (lanes, size)).reshape(steps, heads, size)

    for row in range(count):
        by_length(row, begin)
    head = (lax.broadcasted_iota(jnp.int32, (lanes, width), 0) % heads) // (heads // kv)
    slot_head = lax.broadcasted_iota(jnp.int32, (lanes, width), 1) % kv
    bias[...] = jnp.where(head == slot_head, 0.0, -jnp.inf)

    @pl.loop(0, count)
    def _(row):
        by_length(row, compute)


def cache_attention(first, count, lengths, queries, keys, values, slots, after):
    steps, rows, heads, size = queries.shape
    kv = keys.shape[1] // slots
    sizes = (slots // 24, slots // 6, slots // 2, slots)
    scale = LOG2E / math.sqrt(size)
    part = jax.ShapeDtypeStruct((steps, count, heads, size), jnp.float32)
    return pl.pallas_call(
        functools.partial(attend_cache, first, count, sizes, scale),
        out_shape=(part, part),
        in_specs=[SMEM, VMEM, ANY, ANY] + [ANY] * len(after),
        out_specs=(VMEM, VMEM),
        scratch_shapes=[
            pltpu.VMEM((count, slots * kv, size), jnp.bfloat16),
            pltpu.VMEM((count, slots * kv, size), jnp.bfloat16),
            pltpu.VMEM((steps * heads, slots * kv), jnp.float32),
            pltpu.SemaphoreType.DMA((count, 2)),
        ],
        compiler_params=pltpu.CompilerParams(vmem_limit_bytes=32 * MIB),
        cost_estimate=pl.CostEstimate(
            flops=4 * steps * heads * count * slots * kv * size,
            bytes_accessed=4 * count * slots * kv * size,
            transcendentals=steps * heads * count * slots * kv,
        ),
        name="cache_attention",
    )(lengths, queries, keys, values, *after)


def merge_blocks(lay, plan, n_hidden, n_up, has_prev, final, scale, *refs):
    refs = list(refs)

    def take(n):
        out = refs[:n]
        del refs[:n]
        return out

    (w_hbm,) = take(1)
    hidden = take(n_hidden)
    ups = take(n_up)
    downs = [take(len(entry[2])) for entry in plan]
    if has_prev:
        take(1)
        (fresh_in,) = take(1)
    if final:
        (q_ref,) = take(1)
        caches = take(2 * final)
    n_after = len(refs) - 2 - 10
    take(n_after)
    m_hbm, last_out = take(2)
    w_buf, d_buf, h_buf, u_parts, u_buf, fresh, index, w_sems, d_sems, x_sems = refs

    pairs, rank, depth, width = w_buf.shape[1], d_buf.shape[2], w_buf.shape[2], w_buf.shape[3]
    fsdp, grp, tp = (lax.axis_index(a) for a in AXES)
    z, core = fsdp // 2, fsdp % 2
    even = grp % 2 == 0
    place = grp * lay.depth + jnp.where(even, z, lay.depth - 1 - z)

    x_copies = [
        pltpu.make_async_copy(h, h_buf.at[i], x_sems.at[i]) for i, h in enumerate(hidden)
    ]
    for i, up in enumerate(ups):
        flip, rest = i // (n_up // 2), i % (n_up // 2)
        shift, turn = rest // lay.grp, rest % lay.grp
        zz = lax.rem(lax.rem(z, lay.block) + shift, lay.block)
        cc = core if flip == 0 else 1 - core
        slot = (zz * 2 + cc) * lay.grp + lax.rem(grp + turn, lay.grp)
        x_copies.append(pltpu.make_async_copy(up, u_parts.at[slot], x_sems.at[n_hidden + i]))

    w_copies, d_copies = [], []
    for j, (delta, flip, count) in enumerate(plan):
        spot = lax.rem(place + (delta + lay.ring), lay.ring)
        g = spot // lay.depth
        along = lax.rem(spot, lay.depth)
        zz = jnp.where(g % 2 == 0, along, lay.depth - 1 - along)
        cc = 1 - core if flip else core
        index[j] = (zz * 2 + cc) * lay.grp + g
        start = pl.multiple_of(index[j] * depth, depth)
        w_copies.append(
            pltpu.make_async_copy(
                w_hbm.at[:, pl.ds(start, depth), :], w_buf.at[j], w_sems.at[j]
            )
        )
        parts = downs[j]
        if len(parts) == 1:
            d_copies.append(pltpu.make_async_copy(parts[0], d_buf.at[j], d_sems.at[j, 0]))
        else:
            for k, part in enumerate(parts):
                d_copies.append(
                    pltpu.make_async_copy(part, d_buf.at[j, pl.ds(k, 1)], d_sems.at[j, k])
                )
    for copy in x_copies + d_copies + w_copies:
        copy.start()

    if has_prev:
        fresh[...] = fresh_in[...]
    else:
        fresh[...] = jnp.zeros_like(fresh)
    for copy in x_copies:
        copy.wait()
    columns = u_parts.shape[2] // pairs
    for k in range(pairs):
        u_buf[k] = ADAPTER_SCALING * jnp.concatenate(
            [u_parts[i, :, k * columns : (k + 1) * columns] for i in range(n_up)], axis=1
        )
    for copy in d_copies:
        copy.wait()

    def out_copy(j):
        start = pl.multiple_of(index[j] * depth, depth)
        return pltpu.make_async_copy(
            w_buf.at[j], m_hbm.at[:, pl.ds(start, depth), :], w_sems.at[j]
        )

    chunk = min(depth, 256)
    per_lane = lay.fsdp * lay.grp // lay.tp

    @pl.loop(0, len(plan))
    def _(j):
        start = pl.multiple_of(index[j] * depth, depth)
        pltpu.make_async_copy(
            w_hbm.at[:, pl.ds(start, depth), :], w_buf.at[j], w_sems.at[j]
        ).wait()
        block = lax.rem(index[j], per_lane)
        source = lax.rem(index[j] // per_lane - tp + lay.tp, lay.tp)
        for k in range(pairs):
            for low in range(0, depth, chunk):
                rows = slice(low, low + chunk)
                added = lax.dot_general(
                    d_buf[j, k, :, rows],
                    u_buf[k],
                    (((0,), (0,)), ((), ())),
                    preferred_element_type=jnp.float32,
                )
                merged = (w_buf[j, k, rows, :].astype(jnp.float32) + added).astype(jnp.bfloat16)
                w_buf[j, k, rows, :] = merged
                h = h_buf[source, :, pl.ds(pl.multiple_of(block * depth + low, chunk), chunk)]
                fresh[k] += jnp.dot(h, merged, preferred_element_type=jnp.float32)
        out_copy(j).start()

    if final:
        add_new_tokens(q_ref, caches, fresh, last_out, scale)
    else:
        last_out[...] = fresh[...]
    for j in range(len(plan)):
        out_copy(j).wait()


def add_new_tokens(q_ref, caches, fresh, out_ref, scale):
    steps, rows, heads, size = q_ref.shape
    kv = fresh.shape[2] // size
    new = []
    for k in range(2):
        whole = fresh[k].astype(jnp.bfloat16)
        new.append(
            jnp.concatenate([whole[:, g * size : (g + 1) * size] for g in range(kv)], axis=0)
        )
    n = kv * steps * rows
    done = 0
    for o_ref, lse_ref in zip(caches[0::2], caches[1::2]):
        count = o_ref.shape[1]
        total = steps * count * heads
        q = q_ref[:, done : done + count].reshape(total, size)
        s = lax.dot_general(
            q, new[0], (((1,), (1,)), ((), ())), preferred_element_type=jnp.float32
        )
        left = lax.broadcasted_iota(jnp.int32, (total, n), 0)
        right = lax.broadcasted_iota(jnp.int32, (total, n), 1)
        step, row = left // (heads * count), (left // heads) % count + done
        head = (left % heads) // (heads // kv)
        keep = (
            (head == right // (steps * rows))
            & (row == right % rows)
            & ((right // rows) % steps <= step)
        )
        s = jnp.where(keep, s * scale, -jnp.inf)
        lse = lse_ref[...].reshape(total, size)[:, :1]
        highest = jnp.maximum(jnp.max(s, axis=1, keepdims=True), lse)
        p = jnp.exp2(s - highest)
        old = jnp.exp2(lse - highest)
        divisor = jnp.sum(p, axis=1, keepdims=True) + old
        o = old * o_ref[...].reshape(total, size) + jnp.dot(
            p.astype(jnp.bfloat16), new[1], preferred_element_type=jnp.float32
        )
        out_ref[:, done : done + count] = (
            (o / divisor).reshape(steps, count, heads, size).astype(out_ref.dtype)
        )
        done += count


def merge(lay, plan, weights, hidden, ups, downs, prev, final, after):
    pairs, total, width = weights.shape
    rank, depth = downs[0][0].shape[1:]
    tokens = hidden[0].shape[0]
    n = len(plan)
    flat_downs = [d for entry in downs for d in entry]
    operands = [weights] + hidden + ups + flat_downs
    specs = [ANY] * len(operands)
    aliases = {}
    if prev is not None:
        aliases = {len(operands): 0}
        operands += list(prev)
        specs += [ANY, VMEM]
    scale = 0.0
    last = jax.ShapeDtypeStruct((pairs, tokens, width), jnp.float32)
    if final is not None:
        queries, caches = final
        operands += [queries] + caches
        specs += [VMEM] * (1 + len(caches))
        last = jax.ShapeDtypeStruct(queries.shape, jnp.bfloat16)
        scale = LOG2E / math.sqrt(queries.shape[3])
    operands += after
    specs += [ANY] * len(after)
    return pl.pallas_call(
        functools.partial(
            merge_blocks,
            lay,
            [(d, f, e) for (d, f), e in zip(plan, downs)],
            len(hidden),
            len(ups),
            prev is not None,
            0 if final is None else len(final[1]) // 2,
            scale,
        ),
        out_shape=(jax.ShapeDtypeStruct(weights.shape, weights.dtype), last),
        in_specs=specs,
        out_specs=(ANY, VMEM),
        input_output_aliases=aliases,
        scratch_shapes=[
            pltpu.VMEM((n, pairs, depth, width), jnp.bfloat16),
            pltpu.VMEM((n, pairs, rank, depth), jnp.bfloat16),
            pltpu.VMEM((len(hidden),) + hidden[0].shape, jnp.bfloat16),
            pltpu.VMEM((len(ups),) + ups[0].shape, jnp.bfloat16),
            pltpu.VMEM((pairs, rank, width), jnp.bfloat16),
            pltpu.VMEM((pairs, tokens, width), jnp.float32),
            pltpu.SMEM((n,), jnp.int32),
            pltpu.SemaphoreType.DMA((n,)),
            pltpu.SemaphoreType.DMA((n, 2)),
            pltpu.SemaphoreType.DMA((len(hidden) + len(ups),)),
        ],
        compiler_params=pltpu.CompilerParams(vmem_limit_bytes=32 * MIB),
        cost_estimate=pl.CostEstimate(
            flops=2 * n * pairs * depth * width * (rank + tokens),
            bytes_accessed=2 * n * pairs * depth * width * 2,
            transcendentals=0,
        ),
        name="merge_blocks",
    )(*operands)


def shards(
    lay,
    hidden_states,
    queries,
    cache_keys,
    cache_values,
    cache_lengths,
    projection_weight_matrices,
    factor_down,
    factor_up,
):
    send = functools.partial(lax.ppermute, axis_name=AXES)
    steps, rows, features = hidden_states.shape
    slots, kv, size = cache_keys.shape[1:]
    own = jnp.swapaxes(factor_down, 1, 2)
    own_up = jnp.concatenate([factor_up[k] for k in range(factor_up.shape[0])], axis=1)
    tokens = hidden_states.reshape(steps * rows, features)
    keys = cache_keys.reshape(rows, slots * kv, size)
    values = cache_values.reshape(rows, slots * kv, size)
    swap = lay.core_swap()
    ring = {1: lay.ring_step(1), -1: lay.ring_step(-1)}

    arrived = {1: send(own, perm=ring[1]), -1: send(own, perm=ring[-1])}
    partner = send(own, perm=swap)
    ups = [
        send(own_up, perm=lay.column_step(shift, turn))
        for shift in range(lay.block)
        for turn in range(lay.grp)
    ]
    hidden = [tokens] + [send(tokens, perm=lay.feature_step(i)) for i in range(1, lay.tp)]

    entries = [((0, False), [own]), ((0, True), [partner])]
    half = rows // 2
    caches = []
    state = None
    after = []
    last_step = lay.ring // 2
    for step in range(1, last_step + 1):
        if step <= 2:
            caches += cache_attention(
                (step - 1) * half, half, cache_lengths, queries, keys, values, slots, after
            )
            state_now = [caches[-1]]
        else:
            state = merge(
                lay,
                [e[0] for e in entries],
                projection_weight_matrices,
                hidden,
                ups,
                [e[1] for e in entries],
                state,
                None,
                after,
            )
            entries = []
            state_now = [state[1]]
        if step == 1:
            ups = ups + [send(u, perm=swap) for u in ups]
        if step < last_step:
            came = arrived
            if step + 1 < last_step:
                arrived = {d: send(came[d], perm=ring[d]) for d in ring}
            else:
                arrived = {
                    1: send(came[1][:1], perm=ring[1]),
                    -1: send(came[-1][1:], perm=ring[-1]),
                }
            for d in ring:
                entries.append(((-d * step, False), [came[d]]))
                entries.append(((-d * step, True), [send(came[d], perm=swap)]))
            after = [came[1], came[-1]] + state_now
        else:
            came = [arrived[1], arrived[-1]]
            entries.append(((step, False), came))
            entries.append(((step, True), [send(c, perm=swap) for c in came]))
    return tuple(
        merge(
            lay,
            [e[0] for e in entries],
            projection_weight_matrices,
            hidden,
            ups,
            [e[1] for e in entries],
            state,
            (queries, caches),
            [],
        )
    )


def solution(mesh):
    return jax.shard_map(
        functools.partial(shards, Layout(mesh)),
        mesh=mesh,
        in_specs=(
            P(None, ("fsdp", "grp"), "tp"),
            P(None, ("fsdp", "grp"), "tp", None),
            P(("fsdp", "grp"), None, "tp", None),
            P(("fsdp", "grp"), None, "tp", None),
            P(("fsdp", "grp")),
            P(None, None, "tp"),
            P(None, ("fsdp", "grp"), None),
            P(None, None, ("fsdp", "grp")),
        ),
        out_specs=(P(None, None, "tp"), P(None, ("fsdp", "grp"), "tp", None)),
        check_vma=False,
    )
```

time: 141 us -> 107 us (0.76)
  the two profiles are of different devices: /device:TPU:0 before, /device:TPU:29 now
where the time goes in v1:
time: 107 us; the launch traced here: 106 us
  Pallas kernels  33.3 us (31%)
  starting transfers between devices  28.6 us (27%)
  local copies, waits for them, and re-layouts  25.2 us (24%)
  waiting for transfers between devices  18.2 us (17%)
    pallas_call x3, Pallas kernels, merge(): pl.pallas_call(functools.partial(merge_blocks, lay, [(d, f, e) for (d, f)...  25.4 us
    unnamed x20, local copies, waits for them, and re-layouts  24.5 us
    ppermute x4, waiting for transfers between devices, shards(): send(own_up, perm=lay.column_step(shift, turn))  11.7 us
    ppermute x4, starting transfers between devices, shards(): send(own_up, perm=lay.column_step(shift, turn))  9.16 us
    pallas_call x2, Pallas kernels, cache_attention(): pl.pallas_call(functools.partial(attend_cache, first, count, sizes, scale...  7.87 us
    ppermute x4, starting transfers between devices, shards(): ups = ups + [send(u, perm=swap) for u in ups]  7.6 us
    ppermute x4, waiting for transfers between devices, shards(): ups = ups + [send(u, perm=swap) for u in ups]  3.36 us
    ppermute x2, waiting for transfers between devices, shards(): arrived = {1: send(own, perm=ring[1]), -1: send(own, perm=ring[-1])}  3.11 us
  transfers between devices with their start and end apart: 26, of which 9 were waited for; matrix products, arithmetic and copies ran while one was open for 1% of the time, Pallas kernels for 27%

profile of v1, /device:TPU:29, one launch (start us, length us, event | category | flops | bytes accessed | tf_op | source)
XLA Modules:
  0.0 106.2 jit_solution(8524555395101472499)
XLA Ops:
  0.6 0.2 collective-permute-start.9
  0.9 1.3 %collective-permute-start.13 = (bf16[2,64,512]{2,1,0:T(8,128)(2,1)}, bf16[2,64,512]{2,1,0:T(8,128)(2,1)S(1)}, u32[]{:S(2)}, u32[]{:S(2)}) collective-permute-start(bf16[2,64,512]{2,1,0:T(8,128)(2,1)} %bitcast.17), channel_id=1, source_target_pairs={{0,2},{1,3},{2,10},{3,11},{4,6},{5,7},{6,14},{7,15},{8,0},{9,1},{1... | collective-permute-start | bytes 393224 | tf_op jit(solution)/shard_map/ppermute | solution.py:410
  2.1 3.1 %collective-permute-done.9.refs_4_.refs_13_ = bf16[2,64,512]{2,1,0:T(8,128)(2,1)S(1)} collective-permute-done((bf16[2,64,512]{2,1,0:T(8,128)(2,1)}, bf16[2,64,512]{2,1,0:T(8,128)(2,1)S(1)}, u32[]{:S(2)}, u32[]{:S(2)}) %collective-permute-start.9) | collective-permute-done | bytes 131104 | tf_op jit(solution)/shard_map/ppermute | solution.py:410
  5.3 0.2 collective-permute-start.10
  5.4 0.7 slice_bitcast_fusion.1
  6.2 1.3 %collective-permute-start.14 = (bf16[2,64,512]{2,1,0:T(8,128)(2,1)S(1)}, bf16[2,64,512]{2,1,0:T(8,128)(2,1)S(1)}, u32[]{:S(2)}, u32[]{:S(2)}) collective-permute-start(bf16[2,64,512]{2,1,0:T(8,128)(2,1)S(1)} %collective-permute-done.13.refs_5_.refs_15_), channel_id=1, source_target_pairs={{0,2},{1,3},{2,10},{3,11},{4,6},{5,7},{6,14},{7,15},{8,0},{9,1},{1... | collective-permute-start | bytes 393224 | tf_op jit(solution)/shard_map/ppermute | solution.py:450
  7.5 0.1 pad_maximum_fusion
  7.5 2.9 %collective-permute-start.1 = (bf16[64,128]{1,0:T(8,128)(2,1)S(1)}, bf16[64,128]{1,0:T(8,128)(2,1)S(1)}, u32[]{:S(2)}, u32[]{:S(2)}) collective-permute-start(bf16[64,128]{1,0:T(8,128)(2,1)S(1)} %pad_maximum_fusion), channel_id=1, source_target_pairs={{0,0},{16,1},{2,2},{18,3},{4,4},{20,5},{6,6},{22,7},{8,8},{24,9},{... | collective-permute-start | bytes 49160 | tf_op jit(solution)/shard_map/ppermute | solution.py:413
  10.4 2.5 %collective-permute-start.21 = (bf16[2,64,512]{2,1,0:T(8,128)(2,1)}, bf16[2,64,512]{2,1,0:T(8,128)(2,1)S(1)}, u32[]{:S(2)}, u32[]{:S(2)}) collective-permute-start(bf16[2,64,512]{2,1,0:T(8,128)(2,1)} %bitcast.18), channel_id=1, source_target_pairs={{0,4},{1,5},{2,6},{3,7},{4,0},{5,1},{6,2},{7,3},{8,12},{9,13},{10,... | collective-permute-start | bytes 393224 | tf_op jit(solution)/shard_map/ppermute | solution.py:411
  12.9 0.2 collective-permute-start.11
  13.1 0.8 collective-permute-done.1.refs_3_
  13.9 1.5 %collective-permute-start.2 = (bf16[64,128]{1,0:T(8,128)(2,1)S(1)}, bf16[64,128]{1,0:T(8,128)(2,1)S(1)}, u32[]{:S(2)}, u32[]{:S(2)}) collective-permute-start(bf16[64,128]{1,0:T(8,128)(2,1)S(1)} %pad_maximum_fusion), channel_id=1, source_target_pairs={{2,0},{18,1},{0,2},{16,3},{6,4},{22,5},{4,6},{20,7},{10,8},{26,9},... | collective-permute-start | bytes 49160 | tf_op jit(solution)/shard_map/ppermute | solution.py:413
  15.4 4.1 %collective-permute-done.2.refs_4_ = bf16[64,128]{1,0:T(8,128)(2,1)S(1)} collective-permute-done((bf16[64,128]{1,0:T(8,128)(2,1)S(1)}, bf16[64,128]{1,0:T(8,128)(2,1)S(1)}, u32[]{:S(2)}, u32[]{:S(2)}) %collective-permute-start.2) | collective-permute-done | bytes 16416 | tf_op jit(solution)/shard_map/ppermute | solution.py:413
  19.5 1.2 %collective-permute-start.3 = (bf16[64,128]{1,0:T(8,128)(2,1)S(1)}, bf16[64,128]{1,0:T(8,128)(2,1)S(1)}, u32[]{:S(2)}, u32[]{:S(2)}) collective-permute-start(bf16[64,128]{1,0:T(8,128)(2,1)S(1)} %pad_maximum_fusion), channel_id=1, source_target_pairs={{8,0},{24,1},{10,2},{26,3},{12,4},{28,5},{14,6},{30,7},{0,8},{16,9... | collective-permute-start | bytes 49160 | tf_op jit(solution)/shard_map/ppermute | solution.py:413
  20.7 4.2 %collective-permute-done.3.refs_5_ = bf16[64,128]{1,0:T(8,128)(2,1)S(1)} collective-permute-done((bf16[64,128]{1,0:T(8,128)(2,1)S(1)}, bf16[64,128]{1,0:T(8,128)(2,1)S(1)}, u32[]{:S(2)}, u32[]{:S(2)}) %collective-permute-start.3) | collective-permute-done | bytes 16416 | tf_op jit(solution)/shard_map/ppermute | solution.py:413
  24.9 3.6 %collective-permute-start.4 = (bf16[64,128]{1,0:T(8,128)(2,1)S(1)}, bf16[64,128]{1,0:T(8,128)(2,1)S(1)}, u32[]{:S(2)}, u32[]{:S(2)}) collective-permute-start(bf16[64,128]{1,0:T(8,128)(2,1)S(1)} %pad_maximum_fusion), channel_id=1, source_target_pairs={{10,0},{26,1},{8,2},{24,3},{14,4},{30,5},{12,6},{28,7},{2,8},{18,9... | collective-permute-start | bytes 49160 | tf_op jit(solution)/shard_map/ppermute | solution.py:413
  28.4 2.6 %collective-permute-done.4.refs_6_ = bf16[64,128]{1,0:T(8,128)(2,1)S(1)} collective-permute-done((bf16[64,128]{1,0:T(8,128)(2,1)S(1)}, bf16[64,128]{1,0:T(8,128)(2,1)S(1)}, u32[]{:S(2)}, u32[]{:S(2)}) %collective-permute-start.4) | collective-permute-done | bytes 16416 | tf_op jit(solution)/shard_map/ppermute | solution.py:413
  31.1 6.6 %collective-permute-start.5 = (bf16[64,128]{1,0:T(8,128)(2,1)S(1)}, bf16[64,128]{1,0:T(8,128)(2,1)S(1)}, u32[]{:S(2)}, u32[]{:S(2)}) collective-permute-start(bf16[64,128]{1,0:T(8,128)(2,1)S(1)} %collective-permute-done.1.refs_3_), channel_id=1, source_target_pairs={{0,4},{1,5},{2,6},{3,7},{4,0},{5,1},{6,2},{7,3},{8,12},{9,13},{10,... | collective-permute-start | bytes 49160 | tf_op jit(solution)/shard_map/ppermute | solution.py:446
  37.6 0.8 collective-permute-done.5.refs_7_
  38.5 0.3 collective-permute-start.6
  38.8 0.8 collective-permute-done.6.refs_8_
  39.7 0.3 collective-permute-start.7
  40.0 0.8 collective-permute-done.7.refs_9_
  40.8 0.3 collective-permute-start.8
  41.2 0.8 collective-permute-done.8.refs_10_
  42.0 0.3 collective-permute-start.22
  42.4 0.2 collective-permute-start.23
  42.5 0.3 collective-permute-start.24
  42.9 0.2 collective-permute-start.25
  43.1 2.8 %copy-done.3 = bf16[8,768,4,128]{3,2,1,0:T(4,128)(2,1)S(1)} copy-done((bf16[8,768,4,128]{3,2,1,0:T(4,128)(2,1)S(1)}, bf16[8,768,4,128]{3,2,1,0:T(4,128)(2,1)}, u32[]{:S(2)}) %copy-start.3) | copy-done | bytes 6291480
  45.8 2.8 %copy-done.4 = bf16[8,768,4,128]{3,2,1,0:T(4,128)(2,1)S(1)} copy-done((bf16[8,768,4,128]{3,2,1,0:T(4,128)(2,1)S(1)}, bf16[8,768,4,128]{3,2,1,0:T(4,128)(2,1)}, u32[]{:S(2)}) %copy-start.4) | copy-done | bytes 6291480
  48.6 0.9 copy-done.6
  49.6 0.7 copy-done.9
  50.2 4.1 %cache_attention.2 = (f32[4,4,32,128]{3,2,1,0:T(8,128)S(1)}, f32[4,4,32,128]{3,2,1,0:T(8,128)S(1)}) custom-call(s32[8]{0:T(128)S(1)} %copy-done.9, bf16[4,8,32,128]{3,2,1,0:T(8,128)(2,1)S(1)} %copy-done.6, bf16[8,3072,128]{2,1,0:T(8,128)(2,1)S(1)} %bitcast.8, bf16[8,3072,128]{2,1,0:T(8,128)(2,1)S(1)} %bitcast.10), custom_call_target="tpu_custom_call" | custom-call | flops 805306368 | bytes 6291456 | tf_op jit(solution)/shard_map/cache_attention/pallas_call | solution.py:146
  54.4 0.1 collective-permute-start.12
  54.5 1.4 %collective-permute-start.16 = (bf16[1,64,512]{2,1,0:T(8,128)(2,1)S(1)}, bf16[1,64,512]{2,1,0:T(8,128)(2,1)S(1)}, u32[]{:S(2)}, u32[]{:S(2)}) collective-permute-start(bf16[1,64,512]{2,1,0:T(8,128)(2,1)S(1)} %slice.17), channel_id=1, source_target_pairs={{0,2},{1,3},{2,10},{3,11},{4,6},{5,7},{6,14},{7,15},{8,0},{9,1},{1... | collective-permute-start | bytes 196616 | tf_op jit(solution)/shard_map/ppermute | solution.py:454
  55.9 1.8 %collective-permute-start.19 = (bf16[2,64,512]{2,1,0:T(8,128)(2,1)S(1)}, bf16[2,64,512]{2,1,0:T(8,128)(2,1)S(1)}, u32[]{:S(2)}, u32[]{:S(2)}) collective-permute-start(bf16[2,64,512]{2,1,0:T(8,128)(2,1)S(1)} %collective-permute-done.11.refs_11_.refs_17_), channel_id=1, source_target_pairs={{0,4},{1,5},{2,6},{3,7},{4,0},{5,1},{6,2},{7,3},{8,12},{9,13},{10,... | collective-permute-start | bytes 393224 | tf_op jit(solution)/shard_map/ppermute | solution.py:458
  57.8 0.1 collective-permute-start.20
  57.8 3.8 %cache_attention.3 = (f32[4,4,32,128]{3,2,1,0:T(8,128)S(1)}, f32[4,4,32,128]{3,2,1,0:T(8,128)S(1)}) custom-call(s32[8]{0:T(128)S(1)} %copy-done.9, bf16[4,8,32,128]{3,2,1,0:T(8,128)(2,1)S(1)} %copy-done.6, bf16[8,3072,128]{2,1,0:T(8,128)(2,1)S(1)} %bitcast.9, bf16[8,3072,128]{2,1,0:T(8,128)(2,1)S(1)} %bitcast.11, ...), custom_call_target="tpu_custom_call" | custom-call | flops 805306368 | bytes 6291456 | tf_op jit(solution)/shard_map/cache_attention/pallas_call | solution.py:146
  61.6 1.7 %collective-permute-start.17 = (bf16[1,64,512]{2,1,0:T(8,128)(2,1)S(1)}, bf16[1,64,512]{2,1,0:T(8,128)(2,1)S(1)}, u32[]{:S(2)}, u32[]{:S(2)}) collective-permute-start(bf16[1,64,512]{2,1,0:T(8,128)(2,1)S(1)} %collective-permute-done.12.refs_11_), channel_id=1, source_target_pairs={{0,4},{1,5},{2,6},{3,7},{4,0},{5,1},{6,2},{7,3},{8,12},{9,13},{10,... | collective-permute-start | bytes 196616 | tf_op jit(solution)/shard_map/ppermute | solution.py:463
  63.3 0.1 collective-permute-start.18
  63.4 0.0 copy-start
  63.4 5.8 %copy-done = bf16[2,8192,512]{2,1,0:T(8,128)(2,1)S(1)} copy-done((bf16[2,8192,512]{2,1,0:T(8,128)(2,1)S(1)}, bf16[2,8192,512]{2,1,0:T(8,128)(2,1)}, u32[]{:S(2)}) %copy-start) | copy-done | bytes 16777240
  69.2 14.2 %merge_blocks.3 = (bf16[2,8192,512]{2,1,0:T(8,128)(2,1)}, f32[2,32,512]{2,1,0:T(8,128)S(1)}) custom-call(bf16[2,8192,512]{2,1,0:T(8,128)(2,1)S(1)} %copy-done, bf16[32,4096]{1,0:T(8,128)(2,1)S(1)} %bitcast.13, bf16[32,4096]{1,0:T(8,128)(2,1)S(1)} %collective-permute-done.refs_2_, bf16[64,128]{1,0:T(8,128)(2,1)S(1)} %collective-permute-done.1.refs_3_, ...), custom_call_target="tpu_custom_call" | custom-call | flops 1006632960 | bytes 20971520 | tf_op jit(solution)/shard_map/merge_blocks/pallas_call | solution.py:351
  83.4 5.8 %copy-done.1 = bf16[2,8192,512]{2,1,0:T(8,128)(2,1)S(1)} copy-done((bf16[2,8192,512]{2,1,0:T(8,128)(2,1)S(1)}, bf16[2,8192,512]{2,1,0:T(8,128)(2,1)}, u32[]{:S(2)}) %copy-start.1) | copy-done | bytes 16777240
  89.2 6.4 %merge_blocks.4 = (bf16[2,8192,512]{2,1,0:T(8,128)(2,1)}, f32[2,32,512]{2,1,0:T(8,128)S(1)}) custom-call(bf16[2,8192,512]{2,1,0:T(8,128)(2,1)S(1)} %copy-done.1, bf16[32,4096]{1,0:T(8,128)(2,1)S(1)} %bitcast.14, bf16[32,4096]{1,0:T(8,128)(2,1)S(1)} %collective-permute-done.refs_2_, ...), custom_call_target="tpu_custom_call", output_to_operand_aliasing={{0}: (15, {})} | custom-call | flops 402653184 | bytes 8388608 | tf_op jit(solution)/shard_map/merge_blocks/pallas_call | solution.py:351
  95.7 5.8 %copy-done.2 = bf16[2,8192,512]{2,1,0:T(8,128)(2,1)S(1)} copy-done((bf16[2,8192,512]{2,1,0:T(8,128)(2,1)S(1)}, bf16[2,8192,512]{2,1,0:T(8,128)(2,1)}, u32[]{:S(2)}) %copy-start.2) | copy-done | bytes 16777240
  101.5 4.8 %merge_blocks.5 = (bf16[2,8192,512]{2,1,0:T(8,128)(2,1)}, bf16[4,8,32,128]{3,2,1,0:T(8,128)(2,1)}) custom-call(bf16[2,8192,512]{2,1,0:T(8,128)(2,1)S(1)} %copy-done.2, bf16[32,4096]{1,0:T(8,128)(2,1)S(1)} %bitcast.15, bf16[32,4096]{1,0:T(8,128)(2,1)S(1)} %collective-permute-done.refs_2_, ...), custom_call_target="tpu_custom_call", output_to_operand_aliasing={{0}: (15, {})} | custom-call | flops 201326592 | bytes 4194304 | tf_op jit(solution)/shard_map/merge_blocks/pallas_call | solution.py:351
  (33 shorter events, 0.1 us)
Async XLA Ops:
  0.6 4.6 %collective-permute-start.9 = (bf16[2,64,512]{2,1,0:T(8,128)(2,1)}, bf16[2,64,512]{2,1,0:T(8,128)(2,1)S(1)}, u32[]{:S(2)}, u32[]{:S(2)}) collective-permute-start(bf16[2,64,512]{2,1,0:T(8,128)(2,1)} %bitcast.16), channel_id=1, source_target_pairs={{0,8},{1,9},{2,0},{3,1},{4,12},{5,13},{6,4},{7,5},{8,16},{9,17},{1... | collective-permute-start | bytes 393224 | tf_op jit(solution)/shard_map/ppermute | solution.py:410
  0.9 5.3 %collective-permute-start.13 = (bf16[2,64,512]{2,1,0:T(8,128)(2,1)}, bf16[2,64,512]{2,1,0:T(8,128)(2,1)S(1)}, u32[]{:S(2)}, u32[]{:S(2)}) collective-permute-start(bf16[2,64,512]{2,1,0:T(8,128)(2,1)} %bitcast.17), channel_id=1, source_target_pairs={{0,2},{1,3},{2,10},{3,11},{4,6},{5,7},{6,14},{7,15},{8,0},{9,1},{1... | collective-permute-start | bytes 393224 | tf_op jit(solution)/shard_map/ppermute | solution.py:410
  5.3 7.6 %collective-permute-start.10 = (bf16[2,64,512]{2,1,0:T(8,128)(2,1)S(1)}, bf16[2,64,512]{2,1,0:T(8,128)(2,1)S(1)}, u32[]{:S(2)}, u32[]{:S(2)}) collective-permute-start(bf16[2,64,512]{2,1,0:T(8,128)(2,1)S(1)} %collective-permute-done.9.refs_4_.refs_13_), channel_id=1, source_target_pairs={{0,8},{1,9},{2,0},{3,1},{4,12},{5,13},{6,4},{7,5},{8,16},{9,17},{1... | collective-permute-start | bytes 393224 | tf_op jit(solution)/shard_map/ppermute | solution.py:450
  6.2 22.3 %collective-permute-start.14 = (bf16[2,64,512]{2,1,0:T(8,128)(2,1)S(1)}, bf16[2,64,512]{2,1,0:T(8,128)(2,1)S(1)}, u32[]{:S(2)}, u32[]{:S(2)}) collective-permute-start(bf16[2,64,512]{2,1,0:T(8,128)(2,1)S(1)} %collective-permute-done.13.refs_5_.refs_15_), channel_id=1, source_target_pairs={{0,2},{1,3},{2,10},{3,11},{4,6},{5,7},{6,14},{7,15},{8,0},{9,1},{1... | collective-permute-start | bytes 393224 | tf_op jit(solution)/shard_map/ppermute | solution.py:450
  7.5 6.3 %collective-permute-start.1 = (bf16[64,128]{1,0:T(8,128)(2,1)S(1)}, bf16[64,128]{1,0:T(8,128)(2,1)S(1)}, u32[]{:S(2)}, u32[]{:S(2)}) collective-permute-start(bf16[64,128]{1,0:T(8,128)(2,1)S(1)} %pad_maximum_fusion), channel_id=1, source_target_pairs={{0,0},{16,1},{2,2},{18,3},{4,4},{20,5},{6,6},{22,7},{8,8},{24,9},{... | collective-permute-start | bytes 49160 | tf_op jit(solution)/shard_map/ppermute | solution.py:413
  10.4 31.9 %collective-permute-start.21 = (bf16[2,64,512]{2,1,0:T(8,128)(2,1)}, bf16[2,64,512]{2,1,0:T(8,128)(2,1)S(1)}, u32[]{:S(2)}, u32[]{:S(2)}) collective-permute-start(bf16[2,64,512]{2,1,0:T(8,128)(2,1)} %bitcast.18), channel_id=1, source_target_pairs={{0,4},{1,5},{2,6},{3,7},{4,0},{5,1},{6,2},{7,3},{8,12},{9,13},{10,... | collective-permute-start | bytes 393224 | tf_op jit(solution)/shard_map/ppermute | solution.py:411
  12.9 43.0 %collective-permute-start = (bf16[32,4096]{1,0:T(8,128)(2,1)}, bf16[32,4096]{1,0:T(8,128)(2,1)S(1)}, u32[]{:S(2)}, u32[]{:S(2)}) collective-permute-start(bf16[32,4096]{1,0:T(8,128)(2,1)} %bitcast.12), channel_id=1, source_target_pairs={{1,0},{0,1},{3,2},{2,3},{5,4},{4,5},{7,6},{6,7},{9,8},{8,9},{11,10... | collective-permute-start | bytes 786440 | tf_op jit(solution)/shard_map/ppermute | solution.py:417
  12.9 29.6 %collective-permute-start.11 = (bf16[2,64,512]{2,1,0:T(8,128)(2,1)S(1)}, bf16[2,64,512]{2,1,0:T(8,128)(2,1)S(1)}, u32[]{:S(2)}, u32[]{:S(2)}) collective-permute-start(bf16[2,64,512]{2,1,0:T(8,128)(2,1)S(1)} %collective-permute-done.10.refs_17_.refs_21_), channel_id=1, source_target_pairs={{0,8},{1,9},{2,0},{3,1},{4,12},{5,13},{6,4},{7,5},{8,16},{9,17},{1... | collective-permute-start | bytes 393224 | tf_op jit(solution)/shard_map/ppermute | solution.py:450
  13.9 5.6 %collective-permute-start.2 = (bf16[64,128]{1,0:T(8,128)(2,1)S(1)}, bf16[64,128]{1,0:T(8,128)(2,1)S(1)}, u32[]{:S(2)}, u32[]{:S(2)}) collective-permute-start(bf16[64,128]{1,0:T(8,128)(2,1)S(1)} %pad_maximum_fusion), channel_id=1, source_target_pairs={{2,0},{18,1},{0,2},{16,3},{6,4},{22,5},{4,6},{20,7},{10,8},{26,9},... | collective-permute-start | bytes 49160 | tf_op jit(solution)/shard_map/ppermute | solution.py:413
  19.5 5.4 %collective-permute-start.3 = (bf16[64,128]{1,0:T(8,128)(2,1)S(1)}, bf16[64,128]{1,0:T(8,128)(2,1)S(1)}, u32[]{:S(2)}, u32[]{:S(2)}) collective-permute-start(bf16[64,128]{1,0:T(8,128)(2,1)S(1)} %pad_maximum_fusion), channel_id=1, source_target_pairs={{8,0},{24,1},{10,2},{26,3},{12,4},{28,5},{14,6},{30,7},{0,8},{16,9... | collective-permute-start | bytes 49160 | tf_op jit(solution)/shard_map/ppermute | solution.py:413
  24.9 6.2 %collective-permute-start.4 = (bf16[64,128]{1,0:T(8,128)(2,1)S(1)}, bf16[64,128]{1,0:T(8,128)(2,1)S(1)}, u32[]{:S(2)}, u32[]{:S(2)}) collective-permute-start(bf16[64,128]{1,0:T(8,128)(2,1)S(1)} %pad_maximum_fusion), channel_id=1, source_target_pairs={{10,0},{26,1},{8,2},{24,3},{14,4},{30,5},{12,6},{28,7},{2,8},{18,9... | collective-permute-start | bytes 49160 | tf_op jit(solution)/shard_map/ppermute | solution.py:413
  28.4 14.4 %collective-permute-start.15 = (bf16[2,64,512]{2,1,0:T(8,128)(2,1)S(1)}, bf16[2,64,512]{2,1,0:T(8,128)(2,1)S(1)}, u32[]{:S(2)}, u32[]{:S(2)}) collective-permute-start(bf16[2,64,512]{2,1,0:T(8,128)(2,1)S(1)} %collective-permute-done.14.refs_19_.refs_22_), channel_id=1, source_target_pairs={{0,2},{1,3},{2,10},{3,11},{4,6},{5,7},{6,14},{7,15},{8,0},{9,1},{1... | collective-permute-start | bytes 393224 | tf_op jit(solution)/shard_map/ppermute | solution.py:450
  31.1 7.4 %collective-permute-start.5 = (bf16[64,128]{1,0:T(8,128)(2,1)S(1)}, bf16[64,128]{1,0:T(8,128)(2,1)S(1)}, u32[]{:S(2)}, u32[]{:S(2)}) collective-permute-start(bf16[64,128]{1,0:T(8,128)(2,1)S(1)} %collective-permute-done.1.refs_3_), channel_id=1, source_target_pairs={{0,4},{1,5},{2,6},{3,7},{4,0},{5,1},{6,2},{7,3},{8,12},{9,13},{10,... | collective-permute-start | bytes 49160 | tf_op jit(solution)/shard_map/ppermute | solution.py:446
  38.5 1.2 %collective-permute-start.6 = (bf16[64,128]{1,0:T(8,128)(2,1)S(1)}, bf16[64,128]{1,0:T(8,128)(2,1)S(1)}, u32[]{:S(2)}, u32[]{:S(2)}) collective-permute-start(bf16[64,128]{1,0:T(8,128)(2,1)S(1)} %collective-permute-done.2.refs_4_), channel_id=1, source_target_pairs={{0,4},{1,5},{2,6},{3,7},{4,0},{5,1},{6,2},{7,3},{8,12},{9,13},{10,... | collective-permute-start | bytes 49160 | tf_op jit(solution)/shard_map/ppermute | solution.py:446
  39.7 1.2 %collective-permute-start.7 = (bf16[64,128]{1,0:T(8,128)(2,1)S(1)}, bf16[64,128]{1,0:T(8,128)(2,1)S(1)}, u32[]{:S(2)}, u32[]{:S(2)}) collective-permute-start(bf16[64,128]{1,0:T(8,128)(2,1)S(1)} %collective-permute-done.3.refs_5_), channel_id=1, source_target_pairs={{0,4},{1,5},{2,6},{3,7},{4,0},{5,1},{6,2},{7,3},{8,12},{9,13},{10,... | collective-permute-start | bytes 49160 | tf_op jit(solution)/shard_map/ppermute | solution.py:446
  40.8 1.2 %collective-permute-start.8 = (bf16[64,128]{1,0:T(8,128)(2,1)S(1)}, bf16[64,128]{1,0:T(8,128)(2,1)S(1)}, u32[]{:S(2)}, u32[]{:S(2)}) collective-permute-start(bf16[64,128]{1,0:T(8,128)(2,1)S(1)} %collective-permute-done.4.refs_6_), channel_id=1, source_target_pairs={{0,4},{1,5},{2,6},{3,7},{4,0},{5,1},{6,2},{7,3},{8,12},{9,13},{10,... | collective-permute-start | bytes 49160 | tf_op jit(solution)/shard_map/ppermute | solution.py:446
  42.0 12.3 %collective-permute-start.22 = (bf16[2,64,512]{2,1,0:T(8,128)(2,1)S(1)}, bf16[2,64,512]{2,1,0:T(8,128)(2,1)S(1)}, u32[]{:S(2)}, u32[]{:S(2)}) collective-permute-start(bf16[2,64,512]{2,1,0:T(8,128)(2,1)S(1)} %collective-permute-done.9.refs_4_.refs_13_), channel_id=1, source_target_pairs={{0,4},{1,5},{2,6},{3,7},{4,0},{5,1},{6,2},{7,3},{8,12},{9,13},{10,... | collective-permute-start | bytes 393224 | tf_op jit(solution)/shard_map/ppermute | solution.py:458
  42.4 12.1 %collective-permute-start.23 = (bf16[2,64,512]{2,1,0:T(8,128)(2,1)S(1)}, bf16[2,64,512]{2,1,0:T(8,128)(2,1)S(1)}, u32[]{:S(2)}, u32[]{:S(2)}) collective-permute-start(bf16[2,64,512]{2,1,0:T(8,128)(2,1)S(1)} %collective-permute-done.13.refs_5_.refs_15_), channel_id=1, source_target_pairs={{0,4},{1,5},{2,6},{3,7},{4,0},{5,1},{6,2},{7,3},{8,12},{9,13},{10,... | collective-permute-start | bytes 393224 | tf_op jit(solution)/shard_map/ppermute | solution.py:458
  42.5 15.2 %collective-permute-start.24 = (bf16[2,64,512]{2,1,0:T(8,128)(2,1)S(1)}, bf16[2,64,512]{2,1,0:T(8,128)(2,1)S(1)}, u32[]{:S(2)}, u32[]{:S(2)}) collective-permute-start(bf16[2,64,512]{2,1,0:T(8,128)(2,1)S(1)} %collective-permute-done.10.refs_17_.refs_21_), channel_id=1, source_target_pairs={{0,4},{1,5},{2,6},{3,7},{4,0},{5,1},{6,2},{7,3},{8,12},{9,13},{10,... | collective-permute-start | bytes 393224 | tf_op jit(solution)/shard_map/ppermute | solution.py:458
  42.9 20.5 %collective-permute-start.25 = (bf16[2,64,512]{2,1,0:T(8,128)(2,1)S(1)}, bf16[2,64,512]{2,1,0:T(8,128)(2,1)S(1)}, u32[]{:S(2)}, u32[]{:S(2)}) collective-permute-start(bf16[2,64,512]{2,1,0:T(8,128)(2,1)S(1)} %collective-permute-done.14.refs_19_.refs_22_), channel_id=1, source_target_pairs={{0,4},{1,5},{2,6},{3,7},{4,0},{5,1},{6,2},{7,3},{8,12},{9,13},{10,... | collective-permute-start | bytes 393224 | tf_op jit(solution)/shard_map/ppermute | solution.py:458
  43.1 2.8 %copy-start.3 = (bf16[8,768,4,128]{3,2,1,0:T(4,128)(2,1)S(1)}, bf16[8,768,4,128]{3,2,1,0:T(4,128)(2,1)}, u32[]{:S(2)}) copy-start(bf16[8,768,4,128]{3,2,1,0:T(4,128)(2,1)} %param.10) | copy-start | bytes 18874372
  45.8 2.8 %copy-start.4 = (bf16[8,768,4,128]{3,2,1,0:T(4,128)(2,1)S(1)}, bf16[8,768,4,128]{3,2,1,0:T(4,128)(2,1)}, u32[]{:S(2)}) copy-start(bf16[8,768,4,128]{3,2,1,0:T(4,128)(2,1)} %param.11) | copy-start | bytes 18874372
  48.6 0.9 copy-start.6
  49.6 0.7 copy-start.9
  50.2 13.2 %copy-start.5 = (bf16[4,8,4096]{2,1,0:T(8,128)(2,1)S(1)}, bf16[4,8,4096]{2,1,0:T(8,128)(2,1)}, u32[]{:S(2)}) copy-start(bf16[4,8,4096]{2,1,0:T(8,128)(2,1)} %param.8) | copy-start | bytes 786436
  50.2 13.2 %copy-start.8 = (bf16[2,512,64]{1,2,0:T(8,128)(2,1)S(1)}, bf16[2,512,64]{1,2,0:T(8,128)(2,1)}, u32[]{:S(2)}) copy-start(bf16[2,512,64]{1,2,0:T(8,128)(2,1)} %param.14) | copy-start | bytes 393220
  54.4 7.2 %collective-permute-start.12 = (bf16[1,64,512]{2,1,0:T(8,128)(2,1)S(1)}, bf16[1,64,512]{2,1,0:T(8,128)(2,1)S(1)}, u32[]{:S(2)}, u32[]{:S(2)}) collective-permute-start(bf16[1,64,512]{2,1,0:T(8,128)(2,1)S(1)} %slice.16), channel_id=1, source_target_pairs={{0,8},{1,9},{2,0},{3,1},{4,12},{5,13},{6,4},{7,5},{8,16},{9,17},{1... | collective-permute-start | bytes 196616 | tf_op jit(solution)/shard_map/ppermute | solution.py:453
  54.5 8.9 %collective-permute-start.16 = (bf16[1,64,512]{2,1,0:T(8,128)(2,1)S(1)}, bf16[1,64,512]{2,1,0:T(8,128)(2,1)S(1)}, u32[]{:S(2)}, u32[]{:S(2)}) collective-permute-start(bf16[1,64,512]{2,1,0:T(8,128)(2,1)S(1)} %slice.17), channel_id=1, source_target_pairs={{0,2},{1,3},{2,10},{3,11},{4,6},{5,7},{6,14},{7,15},{8,0},{9,1},{1... | collective-permute-start | bytes 196616 | tf_op jit(solution)/shard_map/ppermute | solution.py:454
  55.9 27.5 %collective-permute-start.19 = (bf16[2,64,512]{2,1,0:T(8,128)(2,1)S(1)}, bf16[2,64,512]{2,1,0:T(8,128)(2,1)S(1)}, u32[]{:S(2)}, u32[]{:S(2)}) collective-permute-start(bf16[2,64,512]{2,1,0:T(8,128)(2,1)S(1)} %collective-permute-done.11.refs_11_.refs_17_), channel_id=1, source_target_pairs={{0,4},{1,5},{2,6},{3,7},{4,0},{5,1},{6,2},{7,3},{8,12},{9,13},{10,... | collective-permute-start | bytes 393224 | tf_op jit(solution)/shard_map/ppermute | solution.py:458
  57.8 25.7 %collective-permute-start.20 = (bf16[2,64,512]{2,1,0:T(8,128)(2,1)S(1)}, bf16[2,64,512]{2,1,0:T(8,128)(2,1)S(1)}, u32[]{:S(2)}, u32[]{:S(2)}) collective-permute-start(bf16[2,64,512]{2,1,0:T(8,128)(2,1)S(1)} %collective-permute-done.15.refs_13_.refs_18_), channel_id=1, source_target_pairs={{0,4},{1,5},{2,6},{3,7},{4,0},{5,1},{6,2},{7,3},{8,12},{9,13},{10,... | collective-permute-start | bytes 393224 | tf_op jit(solution)/shard_map/ppermute | solution.py:458
  61.6 34.0 %collective-permute-start.17 = (bf16[1,64,512]{2,1,0:T(8,128)(2,1)S(1)}, bf16[1,64,512]{2,1,0:T(8,128)(2,1)S(1)}, u32[]{:S(2)}, u32[]{:S(2)}) collective-permute-start(bf16[1,64,512]{2,1,0:T(8,128)(2,1)S(1)} %collective-permute-done.12.refs_11_), channel_id=1, source_target_pairs={{0,4},{1,5},{2,6},{3,7},{4,0},{5,1},{6,2},{7,3},{8,12},{9,13},{10,... | collective-permute-start | bytes 196616 | tf_op jit(solution)/shard_map/ppermute | solution.py:463
  63.3 32.3 %collective-permute-start.18 = (bf16[1,64,512]{2,1,0:T(8,128)(2,1)S(1)}, bf16[1,64,512]{2,1,0:T(8,128)(2,1)S(1)}, u32[]{:S(2)}, u32[]{:S(2)}) collective-permute-start(bf16[1,64,512]{2,1,0:T(8,128)(2,1)S(1)} %collective-permute-done.16.refs_12_), channel_id=1, source_target_pairs={{0,4},{1,5},{2,6},{3,7},{4,0},{5,1},{6,2},{7,3},{8,12},{9,13},{10,... | collective-permute-start | bytes 196616 | tf_op jit(solution)/shard_map/ppermute | solution.py:463
  63.4 5.8 %copy-start = (bf16[2,8192,512]{2,1,0:T(8,128)(2,1)S(1)}, bf16[2,8192,512]{2,1,0:T(8,128)(2,1)}, u32[]{:S(2)}) copy-start(bf16[2,8192,512]{2,1,0:T(8,128)(2,1)} %refs_0_.9) | copy-start | bytes 50331652
  83.4 5.8 %copy-start.1 = (bf16[2,8192,512]{2,1,0:T(8,128)(2,1)S(1)}, bf16[2,8192,512]{2,1,0:T(8,128)(2,1)}, u32[]{:S(2)}) copy-start(bf16[2,8192,512]{2,1,0:T(8,128)(2,1)} %refs_0_.9) | copy-start | bytes 50331652
  89.2 6.5 %copy-start.7 = (bf16[4,8,32,128]{3,2,1,0:T(8,128)(2,1)S(1)}, bf16[4,8,32,128]{3,2,1,0:T(8,128)(2,1)}, u32[]{:S(2)}) copy-start(bf16[4,8,32,128]{3,2,1,0:T(8,128)(2,1)} %refs_17_.1) | copy-start | bytes 786436
  95.7 5.8 %copy-start.2 = (bf16[2,8192,512]{2,1,0:T(8,128)(2,1)S(1)}, bf16[2,8192,512]{2,1,0:T(8,128)(2,1)}, u32[]{:S(2)}) copy-start(bf16[2,8192,512]{2,1,0:T(8,128)(2,1)} %refs_0_.9) | copy-start | bytes 50331652

commit v2 on v0

v2 whole, which is shorter than its diff:
```python
import functools
import math

import jax
import jax.numpy as jnp
from jax import lax
from jax.experimental import pallas as pl
from jax.experimental.pallas import tpu as pltpu
from jax.sharding import PartitionSpec as P

AXES = ("fsdp", "grp", "tp")
ADAPTER_SCALING = 2.0
LOG2E = math.log2(math.e)
MIB = 1024 * 1024
ANY = pl.BlockSpec(memory_space=pl.ANY)
HBM = pl.BlockSpec(memory_space=pltpu.HBM)
VMEM = pl.BlockSpec(memory_space=pltpu.VMEM)
SMEM = pl.BlockSpec(memory_space=pltpu.SMEM)


class Layout:
    def __init__(self, mesh):
        self.fsdp, self.grp, self.tp = (mesh.shape[a] for a in AXES)
        self.depth = self.fsdp // 2
        self.ring = self.depth * self.grp
        self.block = self.depth // self.tp

    def flat(self, z, core, g, t):
        return ((z * 2 + core) * self.grp + g) * self.tp + t

    def devices(self):
        for z in range(self.depth):
            for core in range(2):
                for g in range(self.grp):
                    for t in range(self.tp):
                        yield z, core, g, t

    def place(self, z, g):
        return g * self.depth + (z if g % 2 == 0 else self.depth - 1 - z)

    def at(self, position):
        g, z = divmod(position, self.depth)
        return (z if g % 2 == 0 else self.depth - 1 - z), g

    def ring_step(self, step):
        pairs = []
        for z, core, g, t in self.devices():
            to_z, to_g = self.at((self.place(z, g) + step) % self.ring)
            pairs.append((self.flat(z, core, g, t), self.flat(to_z, core, to_g, t)))
        return pairs

    def core_swap(self):
        return [
            (self.flat(z, c, g, t), self.flat(z, 1 - c, g, t)) for z, c, g, t in self.devices()
        ]

    def feature_step(self, step):
        return [
            (self.flat(z, c, g, (t + step) % self.tp), self.flat(z, c, g, t))
            for z, c, g, t in self.devices()
        ]

    def column_step(self, shift, turn):
        pairs = []
        for z, c, g, t in self.devices():
            source = t * self.block + (z % self.block + shift) % self.block
            pairs.append(
                (
                    self.flat(source, c, (g + turn) % self.grp, z // self.block),
                    self.flat(z, c, g, t),
                )
            )
        return pairs


def gate(arrays, token):
    return lax.optimization_barrier((arrays, token))


def pinned(x, space=pltpu.HBM):
    return pltpu.with_memory_space_constraint(x, space)


def sort_rows(lengths, order):
    rows = lengths.shape[0]
    held = [lengths[r] for r in range(rows)]
    for r in range(rows):
        rank = jnp.int32(0)
        for other in range(rows):
            if other != r:
                ahead = held[other] >= held[r] if other < r else held[other] > held[r]
                rank = rank + ahead.astype(jnp.int32)
        order[rank] = r


def attend_cache(part, pairs, sizes, scale, *refs):
    lengths, q_ref, k_hbm, v_hbm, w_hbm = refs[:5]
    o_ref, lse_ref, w_ref, k_buf, v_buf, order, sems, w_sem = refs[-8:]
    steps, _, heads, size = q_ref.shape
    kv = k_hbm.shape[1] // sizes[-1]
    lanes = steps * heads
    sort_rows(lengths, order)

    def by_length(pair, act):
        length = lengths[order[2 * (part * pairs + pair)]]
        below = 0
        for slots in sizes:

            @pl.when((length > below) & (length <= slots))
            def _():
                act(pair, slots)

            below = slots

    def copies(pair, slots):
        span = pl.ds(0, slots * kv)
        made = []
        for i in range(2):
            spot = 2 * pair + i
            row = order[2 * part * pairs + spot]
            made.append(
                [
                    pltpu.make_async_copy(
                        hbm.at[row, span], buf.at[spot, span], sems.at[spot, which]
                    )
                    for which, (hbm, buf) in enumerate(((k_hbm, k_buf), (v_hbm, v_buf)))
                ]
            )
        return made

    def begin(pair, slots):
        for row in copies(pair, slots):
            for copy in row:
                copy.start()

    def compute(pair, slots):
        made = copies(pair, slots)
        n = slots * kv
        lane = min(n, size)
        head = (lax.broadcasted_iota(jnp.int32, (lanes, lane), 0) % heads) // (heads // kv)
        slot_head = lax.broadcasted_iota(jnp.int32, (lanes, lane), 1) % kv
        bias = jnp.where(head == slot_head, 0.0, -jnp.inf)
        bias = jnp.concatenate([bias] * (n // lane), axis=1)
        column = lax.broadcasted_iota(jnp.int32, (1, n), 1)
        scores = []
        for i in range(2):
            spot = 2 * pair + i
            row = order[2 * part * pairs + spot]
            q = q_ref[:, row].reshape(lanes, size)
            made[i][0].wait()
            s = lax.dot_general(
                q, k_buf[spot, :n], (((1,), (1,)), ((), ())), preferred_element_type=jnp.float32
            )
            open_slots = jnp.where(column < lengths[row] * kv, 0.0, -jnp.inf)
            scores.append(s * scale + (bias + open_slots))
        highest = [jnp.max(s, axis=1, keepdims=True) for s in scores]
        weights = [jnp.exp2(s - h) for s, h in zip(scores, highest)]
        totals = [jnp.sum(p, axis=1, keepdims=True) for p in weights]
        for i in range(2):
            spot = 2 * pair + i
            made[i][1].wait()
            o = jnp.dot(
                weights[i].astype(jnp.bfloat16),
                v_buf[spot, :n],
                preferred_element_type=jnp.float32,
            )
            o_ref[spot] = o / totals[i]
            lse = highest[i] + jnp.log(totals[i]) * LOG2E
            lse_ref[spot] = jnp.broadcast_to(lse, (lanes, size))

    for pair in range(pairs):
        by_length(pair, begin)
    w_copy = pltpu.make_async_copy(w_hbm.at[part], w_ref, w_sem)
    w_copy.start()

    @pl.loop(0, pairs)
    def _(pair):
        by_length(pair, compute)

    w_copy.wait()


def cache_attention(part, pairs, lengths, queries, keys, values, weights, slots, after):
    steps, rows, heads, size = queries.shape
    kv = keys.shape[1] // slots
    sizes = (slots // 24, slots // 6, slots // 2, slots)
    scale = LOG2E / math.sqrt(size)
    piece = jax.ShapeDtypeStruct((2 * pairs, steps * heads, size), jnp.float32)
    return pl.pallas_call(
        functools.partial(attend_cache, part, pairs, sizes, scale),
        out_shape=(piece, piece, pltpu.VMEM(weights.shape[1:], weights.dtype)),
        in_specs=[SMEM, VMEM, HBM, HBM, HBM] + [ANY] * len(after),
        out_specs=(VMEM, VMEM, VMEM),
        scratch_shapes=[
            pltpu.VMEM((2 * pairs, slots * kv, size), jnp.bfloat16),
            pltpu.VMEM((2 * pairs, slots * kv, size), jnp.bfloat16),
            pltpu.SMEM((rows,), jnp.int32),
            pltpu.SemaphoreType.DMA((2 * pairs, 2)),
            pltpu.SemaphoreType.DMA,
        ],
        compiler_params=pltpu.CompilerParams(vmem_limit_bytes=24 * MIB),
        cost_estimate=pl.CostEstimate(
            flops=8 * steps * heads * pairs * slots * kv * size,
            bytes_accessed=8 * pairs * slots * kv * size + 2 * weights[0].size,
            transcendentals=2 * steps * heads * pairs * slots * kv,
        ),
        name="cache_attention",
    )(lengths, queries, pinned(keys), pinned(values), pinned(weights), *after)


def merge_blocks(lay, plan, counts, first, last, scale, *refs):
    refs = list(refs)

    def take(n):
        out = refs[:n]
        del refs[:n]
        return out

    weights = take(2)
    downs = [take(n) for _, _, n in plan]
    if first:
        hidden, ups = take(counts[0]), take(counts[1])
    else:
        u_in, h_in, _, fresh_in, low_in = take(5)
    if last:
        lengths, q_ref = take(2)
        caches = [take(2) for _ in range(2)]
    take(len(refs) - (2 if last else 3) - (3 if first else 0) - 2 - (3 if last else 0))
    (m_hbm,) = take(1)
    (out_ref,) = take(1) if last else (None,)
    if first:
        u_buf, h_buf = take(2)
    else:
        u_buf, h_buf = u_in, h_in
    if last:
        fresh, low, order = refs[-3:]
        del refs[-3:]
    else:
        fresh, low = take(2)
    if first:
        u_parts = refs.pop()
    m_buf, sems = refs

    pairs, depth = m_buf.shape[1], m_buf.shape[2]
    fsdp, grp, tp = (lax.axis_index(a) for a in AXES)
    z, core = fsdp // 2, lax.rem(fsdp, 2)
    place = grp * lay.depth + jnp.where(lax.rem(grp, 2) == 0, z, lay.depth - 1 - z)
    per_lane = lay.fsdp * lay.grp // lay.tp

    if first:
        for i, h in enumerate(hidden):
            h_buf[lax.rem(tp + i, lay.tp)] = h[...]
        for i, up in enumerate(ups):
            flip, rest = divmod(i, len(ups) // 2)
            shift, turn = divmod(rest, lay.grp)
            zz = lax.rem(lax.rem(z, lay.block) + shift, lay.block)
            cc = 1 - core if flip else core
            slot = (zz * 2 + cc) * lay.grp + lax.rem(grp + turn, lay.grp)
            u_parts[slot] = up[...]
        columns = u_parts.shape[2] // pairs
        for k in range(pairs):
            u_buf[k] = ADAPTER_SCALING * jnp.concatenate(
                [u_parts[i, :, k * columns : (k + 1) * columns] for i in range(len(ups))], axis=1
            )
        fresh[...] = jnp.zeros_like(fresh)
        low[...] = jnp.zeros_like(low)
    else:
        fresh[...] = fresh_in[...]
        low[...] = low_in[...]

    chunk = min(depth, 256)
    copies = []
    for j, (delta, flip, n_parts) in enumerate(plan):
        spot = lax.rem(place + (delta + lay.ring), lay.ring)
        g = spot // lay.depth
        along = lax.rem(spot, lay.depth)
        zz = jnp.where(lax.rem(g, 2) == 0, along, lay.depth - 1 - along)
        index = (zz * 2 + (1 - core if flip else core)) * lay.grp + g
        start = pl.multiple_of(index * depth, depth)
        column = pl.multiple_of(lax.rem(index, per_lane) * depth, depth)
        source = index // per_lane
        for k in range(pairs):
            d_ref = downs[j][0].at[k] if n_parts == 1 else downs[j][k].at[0]
            for begin in range(0, depth, chunk):
                rows = slice(begin, begin + chunk)
                d = d_ref[:, rows]
                w = weights[k][pl.ds(start + begin, chunk), :]
                h = h_buf[source, :, pl.ds(column + begin, chunk)]
                added = lax.dot_general(
                    d, u_buf[k], (((0,), (0,)), ((), ())), preferred_element_type=jnp.float32
                )
                m_buf[j, k, rows, :] = (w.astype(jnp.float32) + added).astype(jnp.bfloat16)
                fresh[k] += jnp.dot(h, w, preferred_element_type=jnp.float32)
                low[k] += lax.dot_general(
                    h, d, (((1,), (1,)), ((), ())), preferred_element_type=jnp.float32
                )
            copy = pltpu.make_async_copy(
                m_buf.at[j, k], m_hbm.at[k, pl.ds(start, depth), :], sems.at[j, k]
            )
            copy.start()
            copies.append(copy)

    if last:
        sort_rows(lengths, order)
        new = []
        for k in range(pairs):
            high = low[k].astype(jnp.bfloat16)
            rest = (low[k] - high.astype(jnp.float32)).astype(jnp.bfloat16)
            new.append(
                (
                    fresh[k]
                    + jnp.dot(high, u_buf[k], preferred_element_type=jnp.float32)
                    + jnp.dot(rest, u_buf[k], preferred_element_type=jnp.float32)
                ).astype(jnp.bfloat16)
            )
        add_new_tokens(q_ref, order, caches, new, out_ref, scale)
    for copy in copies:
        copy.wait()


def add_new_tokens(q_ref, order, caches, new, out_ref, scale):
    steps, rows, heads, size = q_ref.shape
    kv = new[0].shape[1] // size
    new = [
        jnp.concatenate([x[:, g * size : (g + 1) * size] for g in range(kv)], axis=0) for x in new
    ]
    n = kv * steps * rows
    lanes = steps * heads
    left = lax.broadcasted_iota(jnp.int32, (lanes, n), 0)
    right = lax.broadcasted_iota(jnp.int32, (lanes, n), 1)
    same_head = (left % heads) // (heads // kv) == right // (steps * rows)
    earlier = (right // rows) % steps <= left // heads
    right_row = jnp.where(same_head & earlier, right % rows, -1)
    spot = 0
    for o_ref, lse_ref in caches:
        for i in range(o_ref.shape[0]):
            row = order[spot]
            q = q_ref[:, row].reshape(lanes, size)
            s = lax.dot_general(
                q, new[0], (((1,), (1,)), ((), ())), preferred_element_type=jnp.float32
            )
            s = jnp.where(right_row == row, s * scale, -jnp.inf)
            lse = lse_ref[i][:, :1]
            highest = jnp.maximum(jnp.max(s, axis=1, keepdims=True), lse)
            p = jnp.exp2(s - highest)
            old = jnp.exp2(lse - highest)
            divisor = jnp.sum(p, axis=1, keepdims=True) + old
            o = old * o_ref[i] + jnp.dot(
                p.astype(jnp.bfloat16), new[1], preferred_element_type=jnp.float32
            )
            out_ref[:, row] = (o / divisor).reshape(steps, heads, size).astype(out_ref.dtype)
            spot += 1


def merge(lay, shape, entries, weights, inputs, state, final, after):
    pairs, total, width = shape
    rank, depth = entries[0][2][0].shape[1:]
    first, last = state is None, final is not None
    n = len(entries)
    operands = [pinned(w, pltpu.VMEM) for w in weights] + [d for e in entries for d in e[2]]
    specs = [VMEM] * len(operands)
    counts = (0, 0)
    aliases = {}
    if first:
        hidden, ups = inputs
        counts = (len(hidden), len(ups))
        operands += hidden + ups
        specs += [VMEM] * (len(hidden) + len(ups))
        tokens, features = hidden[0].shape
        up_shape = (pairs, rank, width)
        h_shape = (lay.tp, tokens, features)
    else:
        m_prev, u, h, fresh, low = state
        aliases = {len(operands) + 2: 0}
        operands += [u, h, pinned(m_prev), fresh, low]
        specs += [VMEM, VMEM, HBM, VMEM, VMEM]
        tokens = h.shape[1]
    out_shape = [pltpu.HBM(shape, jnp.bfloat16)]
    sums = [(pairs, tokens, width), (pairs, tokens, rank)]
    scratch = [
        pltpu.VMEM((n, pairs, depth, width), jnp.bfloat16),
        pltpu.SemaphoreType.DMA((n, 2)),
    ]
    scale = 0.0
    if first:
        out_shape += [jax.ShapeDtypeStruct(s, jnp.bfloat16) for s in (up_shape, h_shape)]
        scratch.append(pltpu.VMEM((len(ups),) + ups[0].shape, jnp.bfloat16))
    if last:
        lengths, queries, caches = final
        operands += [lengths, queries] + caches
        specs += [SMEM] + [VMEM] * (1 + len(caches))
        out_shape.append(jax.ShapeDtypeStruct(queries.shape, jnp.bfloat16))
        scale = LOG2E / math.sqrt(queries.shape[3])
        scratch += [pltpu.VMEM(s, jnp.float32) for s in sums]
        scratch.append(pltpu.SMEM((queries.shape[1],), jnp.int32))
    else:
        out_shape += [jax.ShapeDtypeStruct(s, jnp.float32) for s in sums]
    operands += after
    specs += [ANY] * len(after)
    out = pl.pallas_call(
        functools.partial(
            merge_blocks,
            lay,
            [(delta, flip, len(arrays)) for delta, flip, arrays in entries],
            counts,
            first,
            last,
            scale,
        ),
        out_shape=out_shape,
        in_specs=specs,
        out_specs=[HBM] + [VMEM] * (len(out_shape) - 1),
        input_output_aliases=aliases,
        scratch_shapes=scratch,
        compiler_params=pltpu.CompilerParams(vmem_limit_bytes=14 * MIB),
        cost_estimate=pl.CostEstimate(
            flops=2 * n * pairs * depth * width * (rank + tokens),
            bytes_accessed=2 * n * pairs * depth * width,
            transcendentals=0,
        ),
        name="merge_blocks",
    )(*operands)
    if last or first:
        return list(out)
    return [out[0], u, h, *out[1:]]


def shards(
    lay,
    hidden_states,
    queries,
    cache_keys,
    cache_values,
    cache_lengths,
    projection_weight_matrices,
    factor_down,
    factor_up,
):
    send = functools.partial(lax.ppermute, axis_name=AXES)
    steps, rows, features = hidden_states.shape
    slots, kv, size = cache_keys.shape[1:]
    shape = projection_weight_matrices.shape
    own = jnp.swapaxes(factor_down, 1, 2)
    own_up = jnp.concatenate([factor_up[k] for k in range(factor_up.shape[0])], axis=1)
    tokens = hidden_states.reshape(steps * rows, features)
    keys = cache_keys.reshape(rows, slots * kv, size)
    values = cache_values.reshape(rows, slots * kv, size)
    swap = lay.core_swap()
    ring = {1: lay.ring_step(1), -1: lay.ring_step(-1)}
    caches, weights = [], []

    def attention(part, after):
        o, lse, w = cache_attention(
            part,
            rows // 4,
            cache_lengths,
            queries,
            keys,
            values,
            projection_weight_matrices,
            slots,
            after,
        )
        caches.extend([o, lse])
        weights.append(w)
        return o

    ups = [
        send(own_up, perm=lay.column_step(shift, turn))
        for shift in range(lay.block)
        for turn in range(lay.grp)
    ]
    came = {d: send(own, perm=ring[d]) for d in ring}
    partner = send(own, perm=swap)
    hidden = [tokens] + [send(tokens, perm=lay.feature_step(i)) for i in range(1, lay.tp)]
    ups, token = gate(ups, attention(0, []))
    other_ups = [send(u, perm=swap) for u in ups]
    token = attention(1, [token])
    arrivals, token = gate([came[1], came[-1], partner] + hidden[1:] + other_ups, token)
    came = {1: arrivals[0], -1: arrivals[1]}
    partner = arrivals[2]
    hidden[1:] = list(arrivals[3 : 2 + lay.tp])
    other_ups = list(arrivals[2 + lay.tp :])

    entries = [(0, False, [own]), (0, True, [partner])]
    inputs = (hidden, list(ups) + other_ups)
    state = None
    last_step = lay.ring // 2
    for step in range(1, last_step):
        entries += [(-d * step, False, [came[d]]) for d in ring]
        if step + 1 < last_step:
            sent = {d: send(came[d], perm=ring[d]) for d in ring}
        else:
            sent = {1: send(came[1][:1], perm=ring[1]), -1: send(came[-1][1:], perm=ring[-1])}
        swapped = [send(came[d], perm=swap) for d in ring]
        state = merge(lay, shape, entries, weights, inputs, state, None, [token])
        arrivals, token = gate([sent[1], sent[-1]] + swapped, state[3])
        came = {1: arrivals[0], -1: arrivals[1]}
        entries = [(-d * step, True, [a]) for d, a in zip(ring, arrivals[2:])]
    halves = [came[1], came[-1]]
    swapped = [send(c, perm=swap) for c in halves]
    entries.append((last_step, False, halves))
    state = merge(lay, shape, entries, weights, inputs, state, None, [token])
    entries = [(last_step, True, swapped)]
    final = (cache_lengths, queries, caches)
    return tuple(merge(lay, shape, entries, weights, inputs, state, final, []))


def solution(mesh):
    return jax.shard_map(
        functools.partial(shards, Layout(mesh)),
        mesh=mesh,
        in_specs=(
            P(None, ("fsdp", "grp"), "tp"),
            P(None, ("fsdp", "grp"), "tp", None),
            P(("fsdp", "grp"), None, "tp", None),
            P(("fsdp", "grp"), None, "tp", None),
            P(("fsdp", "grp")),
            P(None, None, "tp"),
            P(None, ("fsdp", "grp"), None),
            P(None, None, ("fsdp", "grp")),
        ),
        out_specs=(P(None, None, "tp"), P(None, ("fsdp", "grp"), "tp", None)),
        check_vma=False,
    )
```

time: 141 us -> 63.9 us (0.45)
  blocking collectives: 45.3 us -> 0 us
  local copies, waits for them, and re-layouts: 45 us -> 2.36 us
  matrix products: 33.6 us -> 0 us
  Pallas kernels: 0 us -> 24.4 us
  starting transfers between devices: 0.04 us -> 20.5 us
  waiting for transfers between devices: 0.7 us -> 15.5 us
  between operations: 14.1 us -> 1.02 us
    all_gather x2 -> x0, blocking collectives: 45.3 us -> none  [the longest x1 38.1 us: shards(): lax.all_gather(factor_up, ('fsdp', 'grp'), axis=2, tiled=True)]
    unnamed x9 -> x8, local copies, waits for them, and re-layouts: 43.4 us -> 1.62 us
    dot_general x6 -> x0, matrix products: 33.6 us -> none  [the longest x1 12 us: shards(): jnp.einsum('kdr,krw->kdw', down_all, up_mine, preferred_element_type=jnp....]
    pallas_call x0 -> x7, Pallas kernels: none -> 24.4 us  [the longest x5 14.7 us: merge(): pl.pallas_call(functools.partial(merge_blocks, lay, [(delta, flip, len(ar...]
    ppermute x0 -> x26, starting transfers between devices: none -> 20.5 us  [the longest x4 6.98 us: shards(): sent = {d: send(came[d], perm=ring[d]) for d in ring}]
    ppermute x0 -> x26, waiting for transfers between devices: none -> 15.5 us  [the longest x4 10.2 us: shards(): sent = {d: send(came[d], perm=ring[d]) for d in ring}]
  transfers between devices with their start and end apart: 1 -> 26, of which waited for: 0 -> 9; matrix products, arithmetic and copies ran while one was open for 20% -> 1% of each run, Pallas kernels for 0% -> 31%
where the time goes in v2:
time: 63.9 us; the launch traced here: 64 us
  Pallas kernels  24.4 us (38%)
  starting transfers between devices  20.5 us (32%)
  waiting for transfers between devices  15.5 us (24%)
  local copies, waits for them, and re-layouts  2.36 us (4%)
  between operations  1.02 us (2%)
    pallas_call x5, Pallas kernels, merge(): pl.pallas_call(functools.partial(merge_blocks, lay, [(delta, flip, len(ar...  14.7 us
    ppermute x4, waiting for transfers between devices, shards(): sent = {d: send(came[d], perm=ring[d]) for d in ring}  10.2 us
    pallas_call x2, Pallas kernels, cache_attention(): pl.pallas_call(functools.partial(attend_cache, part, pairs, sizes, scale)...  9.76 us
    ppermute x4, starting transfers between devices, shards(): sent = {d: send(came[d], perm=ring[d]) for d in ring}  6.98 us
    ppermute x4, starting transfers between devices, shards(): send(own_up, perm=lay.column_step(shift, turn))  4.14 us
    ppermute x4, waiting for transfers between devices, shards(): other_ups = [send(u, perm=swap) for u in ups]  3.21 us
    ppermute x1, starting transfers between devices, shards(): send(tokens, perm=lay.feature_step(i))  3 us
    ppermute x4, waiting for transfers between devices, shards(): send(own_up, perm=lay.column_step(shift, turn))  2.13 us
  transfers between devices with their start and end apart: 26, of which 9 were waited for; matrix products, arithmetic and copies ran while one was open for 1% of the time, Pallas kernels for 31%

profile of v2, /device:TPU:0, one launch (start us, length us, event | category | flops | bytes accessed | tf_op | source)
XLA Modules:
  0.0 64.0 jit_solution(3192525776843513731)
XLA Ops:
  0.6 3.0 %collective-permute-start.7 = (bf16[32,4096]{1,0:T(8,128)(2,1)}, bf16[32,4096]{1,0:T(8,128)(2,1)S(1)}, u32[]{:S(2)}, u32[]{:S(2)}) collective-permute-start(bf16[32,4096]{1,0:T(8,128)(2,1)} %bitcast.8), channel_id=1, source_target_pairs={{1,0},{0,1},{3,2},{2,3},{5,4},{4,5},{7,6},{6,7},{9,8},{8,9},{11,10... | collective-permute-start | bytes 786440 | tf_op jit(solution)/shard_map/ppermute | solution.py:475
  3.6 0.7 %slice_bitcast_fusion.1 = (bf16[64,64]{1,0:T(8,128)(2,1)S(1)}, bf16[64,64]{1,0:T(8,128)(2,1)S(1)}) fusion(bf16[2,64,64]{2,1,0:T(8,128)(2,1)} %param.15), kind=kLoop, calls=%fused_computation.2 | loop fusion | bytes 32768 | tf_op jit(solution)/shard_map/squeeze | solution.py:444
  4.4 0.1 pad_maximum_fusion
  4.5 2.5 %collective-permute-start.3 = (bf16[64,128]{1,0:T(8,128)(2,1)S(1)}, bf16[64,128]{1,0:T(8,128)(2,1)S(1)}, u32[]{:S(2)}, u32[]{:S(2)}) collective-permute-start(bf16[64,128]{1,0:T(8,128)(2,1)S(1)} %pad_maximum_fusion), channel_id=1, source_target_pairs={{10,0},{26,1},{8,2},{24,3},{14,4},{30,5},{12,6},{28,7},{2,8},{18,9... | collective-permute-start | bytes 49160 | tf_op jit(solution)/shard_map/ppermute | solution.py:469
  7.0 0.4 collective-permute-start.2
  7.4 0.5 collective-permute-start.1
  7.9 0.7 %collective-permute-start = (bf16[64,128]{1,0:T(8,128)(2,1)S(1)}, bf16[64,128]{1,0:T(8,128)(2,1)S(1)}, u32[]{:S(2)}, u32[]{:S(2)}) collective-permute-start(bf16[64,128]{1,0:T(8,128)(2,1)S(1)} %pad_maximum_fusion), channel_id=1, source_target_pairs={{0,0},{16,1},{2,2},{18,3},{4,4},{20,5},{6,6},{22,7},{8,8},{24,9},{... | collective-permute-start | bytes 49160 | tf_op jit(solution)/shard_map/ppermute | solution.py:469
  8.6 0.7 %collective-permute-done.3.refs_11_ = bf16[64,128]{1,0:T(8,128)(2,1)S(1)} collective-permute-done((bf16[64,128]{1,0:T(8,128)(2,1)S(1)}, bf16[64,128]{1,0:T(8,128)(2,1)S(1)}, u32[]{:S(2)}, u32[]{:S(2)}) %collective-permute-start.3) | collective-permute-done | bytes 16416 | tf_op jit(solution)/shard_map/ppermute | solution.py:469
  9.3 0.0 collective-permute-start.6
  9.3 1.5 %collective-permute-done.2.refs_10_ = bf16[64,128]{1,0:T(8,128)(2,1)S(1)} collective-permute-done((bf16[64,128]{1,0:T(8,128)(2,1)S(1)}, bf16[64,128]{1,0:T(8,128)(2,1)S(1)}, u32[]{:S(2)}, u32[]{:S(2)}) %collective-permute-start.2) | collective-permute-done | bytes 16416 | tf_op jit(solution)/shard_map/ppermute | solution.py:469
  10.7 0.7 %collective-permute-start.5 = (bf16[2,64,512]{2,1,0:T(8,128)(2,1)}, bf16[2,64,512]{2,1,0:T(8,128)(2,1)S(1)}, u32[]{:S(2)}, u32[]{:S(2)}) collective-permute-start(bf16[2,64,512]{2,1,0:T(8,128)(2,1)} %bitcast.11), channel_id=1, source_target_pairs={{0,2},{1,3},{2,10},{3,11},{4,6},{5,7},{6,14},{7,15},{8,0},{9,1},{1... | collective-permute-start | bytes 393224 | tf_op jit(solution)/shard_map/ppermute | solution.py:473
  11.4 0.0 collective-permute-done.1.refs_9_
  11.4 1.3 %collective-permute-start.4 = (bf16[2,64,512]{2,1,0:T(8,128)(2,1)}, bf16[2,64,512]{2,1,0:T(8,128)(2,1)S(1)}, u32[]{:S(2)}, u32[]{:S(2)}) collective-permute-start(bf16[2,64,512]{2,1,0:T(8,128)(2,1)} %bitcast.12), channel_id=1, source_target_pairs={{0,8},{1,9},{2,0},{3,1},{4,12},{5,13},{6,4},{7,5},{8,16},{9,17},{1... | collective-permute-start | bytes 393224 | tf_op jit(solution)/shard_map/ppermute | solution.py:473
  12.8 0.9 %copy-done = bf16[4,8,32,128]{3,2,1,0:T(8,128)(2,1)S(1)} copy-done((bf16[4,8,32,128]{3,2,1,0:T(8,128)(2,1)S(1)}, bf16[4,8,32,128]{3,2,1,0:T(8,128)(2,1)}, u32[]{:S(2)}) %copy-start) | copy-done | bytes 262168
  13.7 0.7 %copy-done.3 = s32[8]{0:T(128)S(1)} copy-done((s32[8]{0:T(128)S(1)}, s32[8]{0:T(128)}, u32[]{:S(2)}) %copy-start.3) | copy-done | bytes 56
  14.4 5.5 %cache_attention.2 = (f32[4,128,128]{2,1,0:T(8,128)S(1)}, f32[4,128,128]{2,1,0:T(8,128)S(1)}, bf16[8192,512]{1,0:T(8,128)(2,1)S(1)}) custom-call(s32[8]{0:T(128)S(1)} %copy-done.3, bf16[4,8,32,128]{3,2,1,0:T(8,128)(2,1)S(1)} %copy-done, bf16[8,3072,128]{2,1,0:T(8,128)(2,1)} %bitcast.14, bf16[8,3072,128]{2,1,0:T(8,128)(2,1)} %bitcast.16, ...), custom_call_target="tpu_custom_call" | custom-call | flops 805306368 | bytes 14680064 | tf_op jit(solution)/shard_map/cache_attention/pallas_call | solution.py:189
  19.9 0.0 copy-start.1
  19.9 0.0 copy-start.2
  19.9 0.0 collective-permute-done.refs_8_
  19.9 0.1 collective-permute-start.8
  20.0 1.2 %collective-permute-done.8.refs_12_ = bf16[64,128]{1,0:T(8,128)(2,1)S(1)} collective-permute-done((bf16[64,128]{1,0:T(8,128)(2,1)S(1)}, bf16[64,128]{1,0:T(8,128)(2,1)S(1)}, u32[]{:S(2)}, u32[]{:S(2)}) %collective-permute-start.8) | collective-permute-done | bytes 16416 | tf_op jit(solution)/shard_map/ppermute | solution.py:477
  21.2 0.2 collective-permute-start.9
  21.4 1.0 %collective-permute-done.9.refs_13_ = bf16[64,128]{1,0:T(8,128)(2,1)S(1)} collective-permute-done((bf16[64,128]{1,0:T(8,128)(2,1)S(1)}, bf16[64,128]{1,0:T(8,128)(2,1)S(1)}, u32[]{:S(2)}, u32[]{:S(2)}) %collective-permute-start.9) | collective-permute-done | bytes 16416 | tf_op jit(solution)/shard_map/ppermute | solution.py:477
  22.4 0.2 collective-permute-start.10
  22.5 1.0 %collective-permute-done.10.refs_14_ = bf16[64,128]{1,0:T(8,128)(2,1)S(1)} collective-permute-done((bf16[64,128]{1,0:T(8,128)(2,1)S(1)}, bf16[64,128]{1,0:T(8,128)(2,1)S(1)}, u32[]{:S(2)}, u32[]{:S(2)}) %collective-permute-start.10) | collective-permute-done | bytes 16416 | tf_op jit(solution)/shard_map/ppermute | solution.py:477
  23.6 0.2 collective-permute-start.11
  23.7 4.2 %cache_attention.3 = (f32[4,128,128]{2,1,0:T(8,128)S(1)}, f32[4,128,128]{2,1,0:T(8,128)S(1)}, bf16[8192,512]{1,0:T(8,128)(2,1)S(1)}) custom-call(s32[8]{0:T(128)S(1)} %copy-done.3, bf16[4,8,32,128]{3,2,1,0:T(8,128)(2,1)S(1)} %copy-done, bf16[8,3072,128]{2,1,0:T(8,128)(2,1)} %bitcast.15, bf16[8,3072,128]{2,1,0:T(8,128)(2,1)} %bitcast.17, ...), custom_call_target="tpu_custom_call" | custom-call | flops 805306368 | bytes 14680064 | tf_op jit(solution)/shard_map/cache_attention/pallas_call | solution.py:189
  28.0 0.0 collective-permute-done.11.refs_15_
  28.0 0.0 collective-permute-done.5.refs_5_
  28.0 0.4 collective-permute-start.14
  28.4 5.0 %collective-permute-start.12 = (bf16[2,64,512]{2,1,0:T(8,128)(2,1)S(1)}, bf16[2,64,512]{2,1,0:T(8,128)(2,1)S(1)}, u32[]{:S(2)}, u32[]{:S(2)}) collective-permute-start(bf16[2,64,512]{2,1,0:T(8,128)(2,1)S(1)} %collective-permute-done.4.refs_4_), channel_id=1, source_target_pairs={{0,8},{1,9},{2,0},{3,1},{4,12},{5,13},{6,4},{7,5},{8,16},{9,17},{1... | collective-permute-start | bytes 393224 | tf_op jit(solution)/shard_map/ppermute | solution.py:492
  33.4 2.6 %merge_blocks.5 = (bf16[2,8192,512]{2,1,0:T(8,128)(2,1)}, bf16[2,64,512]{2,1,0:T(8,128)(2,1)S(1)}, bf16[2,32,4096]{2,1,0:T(8,128)(2,1)S(1)}, f32[2,32,512]{2,1,0:T(8,128)S(1)}, f32[2,32,64]{2,1,0:T(8,128)S(1)}) custom-call(bf16[8192,512]{1,0:T(8,128)(2,1)S(1)} %get-tuple-element.51.refs_0_, bf16[8192,512]{1,0:T(8,128)(2,1)S(1)} %get-tuple-element.54.refs_1_, ...), custom_call_target="tpu_custom_call" | custom-call | flops 402653184 | bytes 4194304 | tf_op jit(solution)/shard_map/merge_blocks/pallas_call | solution.py:400
  36.0 0.4 collective-permute-done.12.refs_4_
  36.5 6.8 %collective-permute-done.13.refs_5_ = bf16[2,64,512]{2,1,0:T(8,128)(2,1)S(1)} collective-permute-done((bf16[2,64,512]{2,1,0:T(8,128)(2,1)S(1)}, bf16[2,64,512]{2,1,0:T(8,128)(2,1)S(1)}, u32[]{:S(2)}, u32[]{:S(2)}) %collective-permute-start.13) | collective-permute-done | bytes 131104 | tf_op jit(solution)/shard_map/ppermute | solution.py:492
  43.3 1.7 %collective-permute-start.16 = (bf16[2,64,512]{2,1,0:T(8,128)(2,1)S(1)}, bf16[2,64,512]{2,1,0:T(8,128)(2,1)S(1)}, u32[]{:S(2)}, u32[]{:S(2)}) collective-permute-start(bf16[2,64,512]{2,1,0:T(8,128)(2,1)S(1)} %collective-permute-done.12.refs_4_), channel_id=1, source_target_pairs={{0,8},{1,9},{2,0},{3,1},{4,12},{5,13},{6,4},{7,5},{8,16},{9,17},{1... | collective-permute-start | bytes 393224 | tf_op jit(solution)/shard_map/ppermute | solution.py:492
  45.0 0.2 collective-permute-start.19
  45.3 0.3 collective-permute-start.17
  45.6 2.5 %merge_blocks.6 = (bf16[2,8192,512]{2,1,0:T(8,128)(2,1)}, f32[2,32,512]{2,1,0:T(8,128)S(1)}, f32[2,32,64]{2,1,0:T(8,128)S(1)}) custom-call(bf16[8192,512]{1,0:T(8,128)(2,1)S(1)} %get-tuple-element.51.refs_0_, bf16[8192,512]{1,0:T(8,128)(2,1)S(1)} %get-tuple-element.54.refs_1_, ...), custom_call_target="tpu_custom_call", output_to_operand_aliasing={{0}: (8, {})} | custom-call | flops 402653184 | bytes 4194304 | tf_op jit(solution)/shard_map/merge_blocks/pallas_call | solution.py:400
  48.1 1.1 %collective-permute-done.16.refs_4_ = bf16[2,64,512]{2,1,0:T(8,128)(2,1)S(1)} collective-permute-done((bf16[2,64,512]{2,1,0:T(8,128)(2,1)S(1)}, bf16[2,64,512]{2,1,0:T(8,128)(2,1)S(1)}, u32[]{:S(2)}, u32[]{:S(2)}) %collective-permute-start.16) | collective-permute-done | bytes 131104 | tf_op jit(solution)/shard_map/ppermute | solution.py:492
  49.2 1.7 %collective-permute-done.17.refs_5_ = bf16[2,64,512]{2,1,0:T(8,128)(2,1)S(1)} collective-permute-done((bf16[2,64,512]{2,1,0:T(8,128)(2,1)S(1)}, bf16[2,64,512]{2,1,0:T(8,128)(2,1)S(1)}, u32[]{:S(2)}, u32[]{:S(2)}) %collective-permute-start.17) | collective-permute-done | bytes 131104 | tf_op jit(solution)/shard_map/ppermute | solution.py:492
  51.0 0.5 collective-permute-start.23
  51.5 0.3 collective-permute-start.21
  51.8 1.7 %collective-permute-start.20 = (bf16[1,64,512]{2,1,0:T(8,128)(2,1)S(1)}, bf16[1,64,512]{2,1,0:T(8,128)(2,1)S(1)}, u32[]{:S(2)}, u32[]{:S(2)}) collective-permute-start(bf16[1,64,512]{2,1,0:T(8,128)(2,1)S(1)} %slice.14), channel_id=1, source_target_pairs={{0,8},{1,9},{2,0},{3,1},{4,12},{5,13},{6,4},{7,5},{8,16},{9,17},{1... | collective-permute-start | bytes 196616 | tf_op jit(solution)/shard_map/ppermute | solution.py:494
  53.6 2.5 %merge_blocks.7 = (bf16[2,8192,512]{2,1,0:T(8,128)(2,1)}, f32[2,32,512]{2,1,0:T(8,128)S(1)}, f32[2,32,64]{2,1,0:T(8,128)S(1)}) custom-call(bf16[8192,512]{1,0:T(8,128)(2,1)S(1)} %get-tuple-element.51.refs_0_, bf16[8192,512]{1,0:T(8,128)(2,1)S(1)} %get-tuple-element.54.refs_1_, ...), custom_call_target="tpu_custom_call", output_to_operand_aliasing={{0}: (8, {})} | custom-call | flops 402653184 | bytes 4194304 | tf_op jit(solution)/shard_map/merge_blocks/pallas_call | solution.py:400
  56.2 0.1 collective-permute-start.24
  56.2 0.5 collective-permute-start.25
  56.7 2.1 %merge_blocks.8 = (bf16[2,8192,512]{2,1,0:T(8,128)(2,1)}, f32[2,32,512]{2,1,0:T(8,128)S(1)}, f32[2,32,64]{2,1,0:T(8,128)S(1)}) custom-call(bf16[8192,512]{1,0:T(8,128)(2,1)S(1)} %get-tuple-element.51.refs_0_, bf16[8192,512]{1,0:T(8,128)(2,1)S(1)} %get-tuple-element.54.refs_1_, ...), custom_call_target="tpu_custom_call", output_to_operand_aliasing={{0}: (8, {})} | custom-call | flops 301989888 | bytes 3145728 | tf_op jit(solution)/shard_map/merge_blocks/pallas_call | solution.py:400
  58.9 4.9 %merge_blocks.9 = (bf16[2,8192,512]{2,1,0:T(8,128)(2,1)}, bf16[4,8,32,128]{3,2,1,0:T(8,128)(2,1)}) custom-call(bf16[8192,512]{1,0:T(8,128)(2,1)S(1)} %get-tuple-element.51.refs_0_, bf16[8192,512]{1,0:T(8,128)(2,1)S(1)} %get-tuple-element.54.refs_1_, bf16[1,64,512]{2,1,0:T(8,128)(2,1)S(1)} %collective-permute-done.24.refs_2_, ...), custom_call_target="tpu_custom_call", output_to_operand_aliasing={{0}: (6, {})} | custom-call | flops 100663296 | bytes 1048576 | tf_op jit(solution)/shard_map/merge_blocks/pallas_call | solution.py:400
  (23 shorter events, 0.1 us)
Async XLA Ops:
  0.6 27.4 %collective-permute-start.7 = (bf16[32,4096]{1,0:T(8,128)(2,1)}, bf16[32,4096]{1,0:T(8,128)(2,1)S(1)}, u32[]{:S(2)}, u32[]{:S(2)}) collective-permute-start(bf16[32,4096]{1,0:T(8,128)(2,1)} %bitcast.8), channel_id=1, source_target_pairs={{1,0},{0,1},{3,2},{2,3},{5,4},{4,5},{7,6},{6,7},{9,8},{8,9},{11,10... | collective-permute-start | bytes 786440 | tf_op jit(solution)/shard_map/ppermute | solution.py:475
  4.5 4.8 %collective-permute-start.3 = (bf16[64,128]{1,0:T(8,128)(2,1)S(1)}, bf16[64,128]{1,0:T(8,128)(2,1)S(1)}, u32[]{:S(2)}, u32[]{:S(2)}) collective-permute-start(bf16[64,128]{1,0:T(8,128)(2,1)S(1)} %pad_maximum_fusion), channel_id=1, source_target_pairs={{10,0},{26,1},{8,2},{24,3},{14,4},{30,5},{12,6},{28,7},{2,8},{18,9... | collective-permute-start | bytes 49160 | tf_op jit(solution)/shard_map/ppermute | solution.py:469
  7.0 3.7 %collective-permute-start.2 = (bf16[64,128]{1,0:T(8,128)(2,1)S(1)}, bf16[64,128]{1,0:T(8,128)(2,1)S(1)}, u32[]{:S(2)}, u32[]{:S(2)}) collective-permute-start(bf16[64,128]{1,0:T(8,128)(2,1)S(1)} %pad_maximum_fusion), channel_id=1, source_target_pairs={{8,0},{24,1},{10,2},{26,3},{12,4},{28,5},{14,6},{30,7},{0,8},{16,9... | collective-permute-start | bytes 49160 | tf_op jit(solution)/shard_map/ppermute | solution.py:469
  7.4 4.0 %collective-permute-start.1 = (bf16[64,128]{1,0:T(8,128)(2,1)S(1)}, bf16[64,128]{1,0:T(8,128)(2,1)S(1)}, u32[]{:S(2)}, u32[]{:S(2)}) collective-permute-start(bf16[64,128]{1,0:T(8,128)(2,1)S(1)} %pad_maximum_fusion), channel_id=1, source_target_pairs={{2,0},{18,1},{0,2},{16,3},{6,4},{22,5},{4,6},{20,7},{10,8},{26,9},... | collective-permute-start | bytes 49160 | tf_op jit(solution)/shard_map/ppermute | solution.py:469
  7.9 12.0 %collective-permute-start = (bf16[64,128]{1,0:T(8,128)(2,1)S(1)}, bf16[64,128]{1,0:T(8,128)(2,1)S(1)}, u32[]{:S(2)}, u32[]{:S(2)}) collective-permute-start(bf16[64,128]{1,0:T(8,128)(2,1)S(1)} %pad_maximum_fusion), channel_id=1, source_target_pairs={{0,0},{16,1},{2,2},{18,3},{4,4},{20,5},{6,6},{22,7},{8,8},{24,9},{... | collective-permute-start | bytes 49160 | tf_op jit(solution)/shard_map/ppermute | solution.py:469
  9.3 18.7 %collective-permute-start.6 = (bf16[2,64,512]{2,1,0:T(8,128)(2,1)}, bf16[2,64,512]{2,1,0:T(8,128)(2,1)S(1)}, u32[]{:S(2)}, u32[]{:S(2)}) collective-permute-start(bf16[2,64,512]{2,1,0:T(8,128)(2,1)} %bitcast.10), channel_id=1, source_target_pairs={{0,4},{1,5},{2,6},{3,7},{4,0},{5,1},{6,2},{7,3},{8,12},{9,13},{10,... | collective-permute-start | bytes 393224 | tf_op jit(solution)/shard_map/ppermute | solution.py:474
  10.7 17.3 %collective-permute-start.5 = (bf16[2,64,512]{2,1,0:T(8,128)(2,1)}, bf16[2,64,512]{2,1,0:T(8,128)(2,1)S(1)}, u32[]{:S(2)}, u32[]{:S(2)}) collective-permute-start(bf16[2,64,512]{2,1,0:T(8,128)(2,1)} %bitcast.11), channel_id=1, source_target_pairs={{0,2},{1,3},{2,10},{3,11},{4,6},{5,7},{6,14},{7,15},{8,0},{9,1},{1... | collective-permute-start | bytes 393224 | tf_op jit(solution)/shard_map/ppermute | solution.py:473
  11.4 16.6 %collective-permute-start.4 = (bf16[2,64,512]{2,1,0:T(8,128)(2,1)}, bf16[2,64,512]{2,1,0:T(8,128)(2,1)S(1)}, u32[]{:S(2)}, u32[]{:S(2)}) collective-permute-start(bf16[2,64,512]{2,1,0:T(8,128)(2,1)} %bitcast.12), channel_id=1, source_target_pairs={{0,8},{1,9},{2,0},{3,1},{4,12},{5,13},{6,4},{7,5},{8,16},{9,17},{1... | collective-permute-start | bytes 393224 | tf_op jit(solution)/shard_map/ppermute | solution.py:473
  12.8 0.9 %copy-start = (bf16[4,8,32,128]{3,2,1,0:T(8,128)(2,1)S(1)}, bf16[4,8,32,128]{3,2,1,0:T(8,128)(2,1)}, u32[]{:S(2)}) copy-start(bf16[4,8,32,128]{3,2,1,0:T(8,128)(2,1)} %refs_10_.1) | copy-start | bytes 786436
  13.7 0.7 %copy-start.3 = (s32[8]{0:T(128)S(1)}, s32[8]{0:T(128)}, u32[]{:S(2)}) copy-start(s32[8]{0:T(128)} %refs_9_.1) | copy-start | bytes 100
  19.9 13.5 %copy-start.1 = (bf16[4,8,4096]{2,1,0:T(8,128)(2,1)S(1)}, bf16[4,8,4096]{2,1,0:T(8,128)(2,1)}, u32[]{:S(2)}) copy-start(bf16[4,8,4096]{2,1,0:T(8,128)(2,1)} %param.8) | copy-start | bytes 786436
  19.9 13.5 %copy-start.2 = (bf16[2,512,64]{1,2,0:T(8,128)(2,1)S(1)}, bf16[2,512,64]{1,2,0:T(8,128)(2,1)}, u32[]{:S(2)}) copy-start(bf16[2,512,64]{1,2,0:T(8,128)(2,1)} %param.14) | copy-start | bytes 393220
  19.9 1.2 %collective-permute-start.8 = (bf16[64,128]{1,0:T(8,128)(2,1)S(1)}, bf16[64,128]{1,0:T(8,128)(2,1)S(1)}, u32[]{:S(2)}, u32[]{:S(2)}) collective-permute-start(bf16[64,128]{1,0:T(8,128)(2,1)S(1)} %collective-permute-done.refs_8_), channel_id=1, source_target_pairs={{0,4},{1,5},{2,6},{3,7},{4,0},{5,1},{6,2},{7,3},{8,12},{9,13},{10,... | collective-permute-start | bytes 49160 | tf_op jit(solution)/shard_map/ppermute | solution.py:477
  21.2 1.2 %collective-permute-start.9 = (bf16[64,128]{1,0:T(8,128)(2,1)S(1)}, bf16[64,128]{1,0:T(8,128)(2,1)S(1)}, u32[]{:S(2)}, u32[]{:S(2)}) collective-permute-start(bf16[64,128]{1,0:T(8,128)(2,1)S(1)} %collective-permute-done.1.refs_9_), channel_id=1, source_target_pairs={{0,4},{1,5},{2,6},{3,7},{4,0},{5,1},{6,2},{7,3},{8,12},{9,13},{10,... | collective-permute-start | bytes 49160 | tf_op jit(solution)/shard_map/ppermute | solution.py:477
  22.4 1.2 %collective-permute-start.10 = (bf16[64,128]{1,0:T(8,128)(2,1)S(1)}, bf16[64,128]{1,0:T(8,128)(2,1)S(1)}, u32[]{:S(2)}, u32[]{:S(2)}) collective-permute-start(bf16[64,128]{1,0:T(8,128)(2,1)S(1)} %collective-permute-done.2.refs_10_), channel_id=1, source_target_pairs={{0,4},{1,5},{2,6},{3,7},{4,0},{5,1},{6,2},{7,3},{8,12},{9,13},{10,... | collective-permute-start | bytes 49160 | tf_op jit(solution)/shard_map/ppermute | solution.py:477
  23.6 4.4 %collective-permute-start.11 = (bf16[64,128]{1,0:T(8,128)(2,1)S(1)}, bf16[64,128]{1,0:T(8,128)(2,1)S(1)}, u32[]{:S(2)}, u32[]{:S(2)}) collective-permute-start(bf16[64,128]{1,0:T(8,128)(2,1)S(1)} %collective-permute-done.3.refs_11_), channel_id=1, source_target_pairs={{0,4},{1,5},{2,6},{3,7},{4,0},{5,1},{6,2},{7,3},{8,12},{9,13},{10,... | collective-permute-start | bytes 49160 | tf_op jit(solution)/shard_map/ppermute | solution.py:477
  28.0 8.0 %collective-permute-start.14 = (bf16[2,64,512]{2,1,0:T(8,128)(2,1)S(1)}, bf16[2,64,512]{2,1,0:T(8,128)(2,1)S(1)}, u32[]{:S(2)}, u32[]{:S(2)}) collective-permute-start(bf16[2,64,512]{2,1,0:T(8,128)(2,1)S(1)} %collective-permute-done.4.refs_4_), channel_id=1, source_target_pairs={{0,4},{1,5},{2,6},{3,7},{4,0},{5,1},{6,2},{7,3},{8,12},{9,13},{10,... | collective-permute-start | bytes 393224 | tf_op jit(solution)/shard_map/ppermute | solution.py:495
  28.4 8.0 %collective-permute-start.12 = (bf16[2,64,512]{2,1,0:T(8,128)(2,1)S(1)}, bf16[2,64,512]{2,1,0:T(8,128)(2,1)S(1)}, u32[]{:S(2)}, u32[]{:S(2)}) collective-permute-start(bf16[2,64,512]{2,1,0:T(8,128)(2,1)S(1)} %collective-permute-done.4.refs_4_), channel_id=1, source_target_pairs={{0,8},{1,9},{2,0},{3,1},{4,12},{5,13},{6,4},{7,5},{8,16},{9,17},{1... | collective-permute-start | bytes 393224 | tf_op jit(solution)/shard_map/ppermute | solution.py:492
  33.4 3.1 %collective-permute-start.15 = (bf16[2,64,512]{2,1,0:T(8,128)(2,1)S(1)}, bf16[2,64,512]{2,1,0:T(8,128)(2,1)S(1)}, u32[]{:S(2)}, u32[]{:S(2)}) collective-permute-start(bf16[2,64,512]{2,1,0:T(8,128)(2,1)S(1)} %collective-permute-done.5.refs_5_), channel_id=1, source_target_pairs={{0,4},{1,5},{2,6},{3,7},{4,0},{5,1},{6,2},{7,3},{8,12},{9,13},{10,... | collective-permute-start | bytes 393224 | tf_op jit(solution)/shard_map/ppermute | solution.py:495
  33.4 9.9 %collective-permute-start.13 = (bf16[2,64,512]{2,1,0:T(8,128)(2,1)S(1)}, bf16[2,64,512]{2,1,0:T(8,128)(2,1)S(1)}, u32[]{:S(2)}, u32[]{:S(2)}) collective-permute-start(bf16[2,64,512]{2,1,0:T(8,128)(2,1)S(1)} %collective-permute-done.5.refs_5_), channel_id=1, source_target_pairs={{0,2},{1,3},{2,10},{3,11},{4,6},{5,7},{6,14},{7,15},{8,0},{9,1},{1... | collective-permute-start | bytes 393224 | tf_op jit(solution)/shard_map/ppermute | solution.py:492
  43.3 4.8 %collective-permute-start.18 = (bf16[2,64,512]{2,1,0:T(8,128)(2,1)S(1)}, bf16[2,64,512]{2,1,0:T(8,128)(2,1)S(1)}, u32[]{:S(2)}, u32[]{:S(2)}) collective-permute-start(bf16[2,64,512]{2,1,0:T(8,128)(2,1)S(1)} %collective-permute-done.12.refs_4_), channel_id=1, source_target_pairs={{0,4},{1,5},{2,6},{3,7},{4,0},{5,1},{6,2},{7,3},{8,12},{9,13},{10,... | collective-permute-start | bytes 393224 | tf_op jit(solution)/shard_map/ppermute | solution.py:495
  43.3 5.9 %collective-permute-start.16 = (bf16[2,64,512]{2,1,0:T(8,128)(2,1)S(1)}, bf16[2,64,512]{2,1,0:T(8,128)(2,1)S(1)}, u32[]{:S(2)}, u32[]{:S(2)}) collective-permute-start(bf16[2,64,512]{2,1,0:T(8,128)(2,1)S(1)} %collective-permute-done.12.refs_4_), channel_id=1, source_target_pairs={{0,8},{1,9},{2,0},{3,1},{4,12},{5,13},{6,4},{7,5},{8,16},{9,17},{1... | collective-permute-start | bytes 393224 | tf_op jit(solution)/shard_map/ppermute | solution.py:492
  45.0 4.2 %collective-permute-start.19 = (bf16[2,64,512]{2,1,0:T(8,128)(2,1)S(1)}, bf16[2,64,512]{2,1,0:T(8,128)(2,1)S(1)}, u32[]{:S(2)}, u32[]{:S(2)}) collective-permute-start(bf16[2,64,512]{2,1,0:T(8,128)(2,1)S(1)} %collective-permute-done.13.refs_5_), channel_id=1, source_target_pairs={{0,4},{1,5},{2,6},{3,7},{4,0},{5,1},{6,2},{7,3},{8,12},{9,13},{10,... | collective-permute-start | bytes 393224 | tf_op jit(solution)/shard_map/ppermute | solution.py:495
  45.3 5.7 %collective-permute-start.17 = (bf16[2,64,512]{2,1,0:T(8,128)(2,1)S(1)}, bf16[2,64,512]{2,1,0:T(8,128)(2,1)S(1)}, u32[]{:S(2)}, u32[]{:S(2)}) collective-permute-start(bf16[2,64,512]{2,1,0:T(8,128)(2,1)S(1)} %collective-permute-done.13.refs_5_), channel_id=1, source_target_pairs={{0,2},{1,3},{2,10},{3,11},{4,6},{5,7},{6,14},{7,15},{8,0},{9,1},{1... | collective-permute-start | bytes 393224 | tf_op jit(solution)/shard_map/ppermute | solution.py:492
  51.0 5.2 %collective-permute-start.22 = (bf16[2,64,512]{2,1,0:T(8,128)(2,1)S(1)}, bf16[2,64,512]{2,1,0:T(8,128)(2,1)S(1)}, u32[]{:S(2)}, u32[]{:S(2)}) collective-permute-start(bf16[2,64,512]{2,1,0:T(8,128)(2,1)S(1)} %collective-permute-done.16.refs_4_), channel_id=1, source_target_pairs={{0,4},{1,5},{2,6},{3,7},{4,0},{5,1},{6,2},{7,3},{8,12},{9,13},{10,... | collective-permute-start | bytes 393224 | tf_op jit(solution)/shard_map/ppermute | solution.py:495
  51.0 5.2 %collective-permute-start.23 = (bf16[2,64,512]{2,1,0:T(8,128)(2,1)S(1)}, bf16[2,64,512]{2,1,0:T(8,128)(2,1)S(1)}, u32[]{:S(2)}, u32[]{:S(2)}) collective-permute-start(bf16[2,64,512]{2,1,0:T(8,128)(2,1)S(1)} %collective-permute-done.17.refs_5_), channel_id=1, source_target_pairs={{0,4},{1,5},{2,6},{3,7},{4,0},{5,1},{6,2},{7,3},{8,12},{9,13},{10,... | collective-permute-start | bytes 393224 | tf_op jit(solution)/shard_map/ppermute | solution.py:495
  51.5 4.6 %collective-permute-start.21 = (bf16[1,64,512]{2,1,0:T(8,128)(2,1)S(1)}, bf16[1,64,512]{2,1,0:T(8,128)(2,1)S(1)}, u32[]{:S(2)}, u32[]{:S(2)}) collective-permute-start(bf16[1,64,512]{2,1,0:T(8,128)(2,1)S(1)} %slice.15), channel_id=1, source_target_pairs={{0,2},{1,3},{2,10},{3,11},{4,6},{5,7},{6,14},{7,15},{8,0},{9,1},{1... | collective-permute-start | bytes 196616 | tf_op jit(solution)/shard_map/ppermute | solution.py:494
  51.8 4.3 %collective-permute-start.20 = (bf16[1,64,512]{2,1,0:T(8,128)(2,1)S(1)}, bf16[1,64,512]{2,1,0:T(8,128)(2,1)S(1)}, u32[]{:S(2)}, u32[]{:S(2)}) collective-permute-start(bf16[1,64,512]{2,1,0:T(8,128)(2,1)S(1)} %slice.14), channel_id=1, source_target_pairs={{0,8},{1,9},{2,0},{3,1},{4,12},{5,13},{6,4},{7,5},{8,16},{9,17},{1... | collective-permute-start | bytes 196616 | tf_op jit(solution)/shard_map/ppermute | solution.py:494
  56.2 2.7 %collective-permute-start.24 = (bf16[1,64,512]{2,1,0:T(8,128)(2,1)S(1)}, bf16[1,64,512]{2,1,0:T(8,128)(2,1)S(1)}, u32[]{:S(2)}, u32[]{:S(2)}) collective-permute-start(bf16[1,64,512]{2,1,0:T(8,128)(2,1)S(1)} %collective-permute-done.20.refs_4_), channel_id=1, source_target_pairs={{0,4},{1,5},{2,6},{3,7},{4,0},{5,1},{6,2},{7,3},{8,12},{9,13},{10,... | collective-permute-start | bytes 196616 | tf_op jit(solution)/shard_map/ppermute | solution.py:501
  56.2 2.7 %collective-permute-start.25 = (bf16[1,64,512]{2,1,0:T(8,128)(2,1)S(1)}, bf16[1,64,512]{2,1,0:T(8,128)(2,1)S(1)}, u32[]{:S(2)}, u32[]{:S(2)}) collective-permute-start(bf16[1,64,512]{2,1,0:T(8,128)(2,1)S(1)} %collective-permute-done.21.refs_5_), channel_id=1, source_target_pairs={{0,4},{1,5},{2,6},{3,7},{4,0},{5,1},{6,2},{7,3},{8,12},{9,13},{10,... | collective-permute-start | bytes 196616 | tf_op jit(solution)/shard_map/ppermute | solution.py:501

commit v3 on v0

v3 whole, which is shorter than its diff:
```python
import functools
import math

import jax
import jax.numpy as jnp
from jax import lax
from jax.experimental import pallas as pl
from jax.experimental.pallas import tpu as pltpu
from jax.sharding import PartitionSpec as P

AXES = ("fsdp", "grp", "tp")
ADAPTER_SCALING = 2.0
LOG2E = math.log2(math.e)
MIB = 1024 * 1024
ANY = pl.BlockSpec(memory_space=pl.ANY)
HBM = pl.BlockSpec(memory_space=pltpu.HBM)
VMEM = pl.BlockSpec(memory_space=pltpu.VMEM)
SMEM = pl.BlockSpec(memory_space=pltpu.SMEM)


class Layout:
    def __init__(self, mesh):
        self.fsdp, self.grp, self.tp = (mesh.shape[a] for a in AXES)
        self.depth = self.fsdp // 2
        self.ring = self.depth * self.grp
        self.block = self.depth // self.tp

    def flat(self, z, core, g, t):
        return ((z * 2 + core) * self.grp + g) * self.tp + t

    def devices(self):
        for z in range(self.depth):
            for core in range(2):
                for g in range(self.grp):
                    for t in range(self.tp):
                        yield z, core, g, t

    def place(self, z, g):
        return g * self.depth + (z if g % 2 == 0 else self.depth - 1 - z)

    def at(self, position):
        g, z = divmod(position, self.depth)
        return (z if g % 2 == 0 else self.depth - 1 - z), g

    def ring_step(self):
        pairs = []
        for z, core, g, t in self.devices():
            to_z, to_g = self.at((self.place(z, g) + (1 - 2 * core)) % self.ring)
            pairs.append((self.flat(z, core, g, t), self.flat(to_z, core, to_g, t)))
        return pairs

    def core_swap(self):
        return [
            (self.flat(z, c, g, t), self.flat(z, 1 - c, g, t)) for z, c, g, t in self.devices()
        ]

    def feature_step(self, step):
        return [
            (self.flat(z, c, g, (t + step) % self.tp), self.flat(z, c, g, t))
            for z, c, g, t in self.devices()
        ]


def over(x, n):
    return x >> (n.bit_length() - 1) if n & (n - 1) == 0 else x // n


def within(x, n):
    return x & (n - 1) if n & (n - 1) == 0 else x % n


def after_all(arrays, token):
    return lax.optimization_barrier((arrays, token))


def pinned(x, space=pltpu.HBM):
    return pltpu.with_memory_space_constraint(x, space)


def sort_rows(lengths, order):
    rows = lengths.shape[0]
    held = [lengths[r] for r in range(rows)]
    for r in range(rows):
        rank = jnp.int32(0)
        for other in range(rows):
            if other != r:
                ahead = held[other] >= held[r] if other < r else held[other] > held[r]
                rank = rank + ahead.astype(jnp.int32)
        order[rank] = r


def by_length(length, sizes, act):
    below = 0
    for slots in sizes:

        @pl.when((length > below) & (length <= slots))
        def _():
            act(slots)

        below = slots


def cache_copies(first, spot, slots, kv, order, hbms, bufs, sems):
    span = pl.ds(0, slots * kv)
    return [
        [
            pltpu.make_async_copy(
                hbm.at[order[first + i], span], buf.at[spot + i, span], sems.at[i, which]
            )
            for which, (hbm, buf) in enumerate(zip(hbms, bufs))
        ]
        for i in range(2)
    ]


def pack_own(down, up, pair, up_buf, sems, up_sem):
    lanes = pair.shape[3]
    count, _, depth = down.shape
    tiles = depth // lanes
    copies = [
        pltpu.make_async_copy(
            down.at[k, :, pl.ds(i * lanes, lanes)], pair.at[0, k * tiles + i], sems.at[k, i]
        )
        for k in range(count)
        for i in range(tiles)
    ]
    up_copy = pltpu.make_async_copy(up, up_buf, up_sem)
    up_copy.start()
    for copy in copies:
        copy.start()
    up_copy.wait()
    columns = jnp.concatenate([up_buf[k] for k in range(count)], axis=1)
    pair[0, count * tiles, :, : columns.shape[1]] = columns
    for copy in copies:
        copy.wait()


def pack_other(down, up, _, pair):
    lanes = pair.shape[3]
    count, _, depth = down.shape
    tiles = depth // lanes
    for k in range(count):
        for i in range(tiles):
            pair[1, k * tiles + i] = down[k, :, i * lanes : (i + 1) * lanes]
    columns = jnp.concatenate([up[k] for k in range(count)], axis=1)
    pair[1, count * tiles, :, : columns.shape[1]] = columns


def pack(own, other, own_up, other_up):
    count, rank, depth = own.shape
    tiles = depth // 128
    pair = pltpu.VMEM((2, count * tiles + 1, rank, 128), own.dtype)
    params = pltpu.CompilerParams(vmem_limit_bytes=2 * MIB)
    half = pl.pallas_call(
        pack_own,
        out_shape=pair,
        in_specs=[HBM, HBM],
        out_specs=VMEM,
        scratch_shapes=[
            pltpu.VMEM(own_up.shape, own.dtype),
            pltpu.SemaphoreType.DMA((count, tiles)),
            pltpu.SemaphoreType.DMA,
        ],
        compiler_params=params,
        name="pack_own",
    )(pinned(own), pinned(own_up))
    return pl.pallas_call(
        pack_other,
        out_shape=pair,
        in_specs=[VMEM, VMEM, VMEM],
        out_specs=VMEM,
        input_output_aliases={2: 0},
        compiler_params=params,
        name="pack_other",
    )(other, other_up, pinned(half, pltpu.VMEM))


def attend_cache(pairs, done, ready, sizes, scale, has_w, n_kept, *refs):
    refs = list(refs)
    sems, w_sem = refs[-2:]
    first = done == 0
    if first:
        len_hbm, q_hbm, k_hbm, v_hbm, w_hbm = refs[:5]
        lengths, order, q_ref, k_buf, v_buf, *outs = refs[-2 - 7 - has_w : -2]
        len_copy = pltpu.make_async_copy(len_hbm, lengths, sems.at[0, 0, 0])
        q_copy = pltpu.make_async_copy(q_hbm, q_ref, w_sem)
        len_copy.start()
        q_copy.start()
        len_copy.wait()
        sort_rows(lengths, order)
    else:
        lengths, order, q_ref, k_hbm, v_hbm, w_hbm = refs[:6]
        k_buf, v_buf, *outs = refs[-2 - 4 - has_w - n_kept : -2 - n_kept]
    o_ref, lse_ref = outs[:2]
    steps, _, heads, size = q_ref.shape
    kv = k_hbm.shape[1] // sizes[-1]
    lanes = steps * heads

    def copies(pair, slots):
        span = pl.ds(0, slots * kv)
        return [
            [
                pltpu.make_async_copy(
                    hbm.at[order[2 * pair + i], span],
                    buf.at[2 * pair + i, span],
                    sems.at[pair, i, which],
                )
                for which, (hbm, buf) in enumerate(((k_hbm, k_buf), (v_hbm, v_buf)))
            ]
            for i in range(2)
        ]

    def start(pair, slots):
        for made in copies(pair, slots):
            for copy in made:
                copy.start()

    def finish(pair, slots):
        for made in copies(pair, slots):
            for copy in made:
                copy.wait()

    for pair in range(*ready):
        by_length(lengths[order[2 * pair]], sizes, functools.partial(start, pair))
    if has_w:
        w_copy = pltpu.make_async_copy(w_hbm.at[0], outs[2], w_sem)
        w_copy.start()
    if first:
        q_copy.wait()

    row_head = over(within(lax.broadcasted_iota(jnp.int32, (lanes, size), 0), heads), heads // kv)
    slot_head = within(lax.broadcasted_iota(jnp.int32, (lanes, size), 1), kv)
    head_bias = jnp.where(row_head == slot_head, 0.0, -jnp.inf)

    def attend(pair):
        def compute(slots):
            @pl.when(pair >= ready[0])
            def _():
                finish(pair, slots)

            n = slots * kv
            bias = jnp.concatenate([head_bias[:, : min(n, size)]] * max(n // size, 1), axis=1)
            column = lax.broadcasted_iota(jnp.int32, (1, n), 1)
            scores = []
            for i in range(2):
                row = order[2 * pair + i]
                q = q_ref[:, row].reshape(lanes, size)
                s = lax.dot_general(
                    q,
                    k_buf[2 * pair + i, :n],
                    (((1,), (1,)), ((), ())),
                    preferred_element_type=jnp.float32,
                )
                closed = jnp.where(column < lengths[row] * kv, 0.0, -jnp.inf)
                scores.append(s + (bias + closed))
            highest = [jnp.max(s, axis=1, keepdims=True) * scale for s in scores]
            weights = [jnp.exp2(s * scale - h) for s, h in zip(scores, highest)]
            totals = [jnp.sum(p, axis=1, keepdims=True) for p in weights]
            for i in range(2):
                o = jnp.dot(
                    weights[i].astype(jnp.bfloat16),
                    v_buf[2 * pair + i, :n],
                    preferred_element_type=jnp.float32,
                )
                spot = 2 * (pair - done) + i
                o_ref[spot] = o / totals[i]
                lse = highest[i] + jnp.log(totals[i]) * LOG2E
                lse_ref[spot] = jnp.broadcast_to(lse, (lanes, size))

        by_length(lengths[order[2 * pair]], sizes, compute)

    if pairs[1] - pairs[0] == 1:
        attend(pairs[0])
    else:
        pl.loop(*pairs)(attend)
    for pair in range(max(pairs[1], ready[0]), ready[1]):
        by_length(lengths[order[2 * pair]], sizes, functools.partial(finish, pair))
    if has_w:
        w_copy.wait()


def like(x):
    return pltpu.VMEM(x.shape, x.dtype)


def cache_attention(pairs, ready, lengths, order, queries, keys, values, weights, buffers, has_w, sizes, after):
    rows, steps, _, heads, size = (keys.shape[0], *queries.shape)
    slots = sizes[-1]
    scale = LOG2E / math.sqrt(size)
    count = 2 * (pairs[1] - pairs[0])
    piece = pltpu.VMEM((count, steps * heads, size), jnp.float32)
    outs = [piece, piece] + ([pltpu.VMEM(weights.shape[1:], weights.dtype)] if has_w else [])
    aliases = {}
    if not buffers:
        operands = [pinned(x) for x in (lengths, queries, keys, values, weights)]
        specs = [HBM] * 5
        scalars = pltpu.SMEM((rows,), jnp.int32)
        buffer = pltpu.VMEM(keys.shape, keys.dtype)
        out_shape = [scalars, scalars, like(queries), buffer, buffer]
        out_specs = [SMEM, SMEM, VMEM, VMEM, VMEM]
    else:
        operands = [pinned(x, pltpu.SMEM) for x in (lengths, order)]
        operands += [pinned(queries, pltpu.VMEM)]
        operands += [pinned(x) for x in (keys, values, weights)]
        aliases = {len(operands) + i: i for i in range(len(buffers))}
        operands += [pinned(b, pltpu.VMEM) for b in buffers]
        specs = [SMEM, SMEM, VMEM, HBM, HBM, HBM] + [VMEM] * len(buffers)
        out_shape = [like(b) for b in buffers]
        out_specs = [VMEM] * len(buffers)
    out_shape += outs
    out_specs += [VMEM] * len(outs)
    return pl.pallas_call(
        functools.partial(attend_cache, pairs, pairs[0], ready, sizes, scale, int(has_w), 0),
        out_shape=out_shape,
        in_specs=specs + [ANY] * len(after),
        out_specs=out_specs,
        input_output_aliases=aliases,
        scratch_shapes=[
            pltpu.SemaphoreType.DMA((rows // 2, 2, 2)),
            pltpu.SemaphoreType.DMA,
        ],
        compiler_params=pltpu.CompilerParams(vmem_limit_bytes=8 * MIB),
        cost_estimate=pl.CostEstimate(
            flops=4 * steps * heads * count * keys.shape[1] * size,
            bytes_accessed=4 * count * keys.shape[1] * size + 2 * has_w * weights[0].size,
            transcendentals=steps * heads * count * keys.shape[1],
        ),
        name="cache_attention",
    )(*operands, *after)


def project_old(part, lay, n_hidden, *refs):
    refs = list(refs)
    tp = lax.axis_index("tp")
    if part == 0:
        hidden = refs[1 : 1 + n_hidden]
        w_hbm = refs[1 + n_hidden]
        w_ref, next_ref, h_ref, out_ref, sem = refs[-5:]
        copy = pltpu.make_async_copy(w_hbm.at[1], next_ref, sem)
        copy.start()
        for i, h in enumerate(hidden):
            h_ref[lax.rem(tp + i, lay.tp)] = h[...]
    else:
        h_ref = refs[2]
        w_ref, out_ref = refs[-2:]
    features = h_ref.shape[2]
    chunk = min(features, 1024)
    total = jnp.zeros(out_ref.shape, jnp.float32)
    for t in range(lay.tp):
        for low in range(0, features, chunk):
            start = t * features + low
            total += jnp.dot(
                h_ref[t, :, low : low + chunk],
                w_ref[start : start + chunk, :],
                preferred_element_type=jnp.float32,
            )
    out_ref[...] = total
    if part == 0:
        copy.wait()


def project(part, lay, w, hidden, weights, after):
    tokens, features = hidden[0].shape[-2:]
    out = pltpu.VMEM((tokens, w.shape[1]), jnp.float32)
    operands = [pinned(w, pltpu.VMEM)] + hidden
    specs = [VMEM] * len(operands)
    if part == 0:
        states = pltpu.VMEM((lay.tp, tokens, features), jnp.bfloat16)
        operands.append(pinned(weights))
        specs.append(HBM)
        out_shape = [like(w), like(w), states, out]
        aliases = {0: 0}
        scratch = [pltpu.SemaphoreType.DMA]
    else:
        operands = [pinned(weights, pltpu.VMEM)] + operands
        specs.append(VMEM)
        operands[2] = pinned(operands[2], pltpu.VMEM)
        out_shape = [like(w), like(w), out]
        aliases = {0: 0, 1: 1}
        scratch = []
    return pl.pallas_call(
        functools.partial(project_old, part, lay, len(hidden)),
        out_shape=out_shape,
        in_specs=specs + [ANY] * len(after),
        out_specs=[VMEM] * len(out_shape),
        input_output_aliases=aliases,
        scratch_shapes=scratch,
        compiler_params=pltpu.CompilerParams(vmem_limit_bytes=8 * MIB),
        cost_estimate=pl.CostEstimate(
            flops=2 * tokens * w.size, bytes_accessed=2 * w.size, transcendentals=0
        ),
        name="project",
    )(*operands, *after)


def merge_all(lay, plan, n_caches, scale, *refs):
    refs = list(refs)

    def take(n):
        out = refs[:n]
        del refs[:n]
        return out

    weights, downs = take(2), take(len(plan))
    h_buf, *olds = take(3)
    order, q_ref = take(2)
    caches = [take(2) for _ in range(n_caches)]
    m_hbm, out_ref, m_buf, u_parts, u_buf, low, sems = refs

    pairs, depth, width = m_buf.shape[1:]
    cut = min(width, 256)
    lanes = downs[0].shape[3]
    tiles = depth // lanes
    fsdp, grp, tp = (lax.axis_index(a) for a in AXES)
    z, core = fsdp // 2, lax.rem(fsdp, 2)
    place = grp * lay.depth + jnp.where(lax.rem(grp, 2) == 0, z, lay.depth - 1 - z)
    per_lane = lay.fsdp * lay.grp // lay.tp

    shards = []
    for (step, flip), down in zip(plan, downs):
        towards = 2 * core - 1
        spot = lax.rem(place + lay.ring + step * (-towards if flip else towards), lay.ring)
        g = spot // lay.depth
        along = lax.rem(spot, lay.depth)
        zz = jnp.where(lax.rem(g, 2) == 0, along, lay.depth - 1 - along)
        for c in range(2):
            cc = lax.rem(core + c + (1 if flip else 0), 2)
            shards.append((down, c, (zz * 2 + cc) * lay.grp + g))

    columns = width // per_lane
    for down, c, index in shards:
        @pl.when(index // per_lane == tp)
        def _():
            u_parts[lax.rem(index, per_lane)] = down[c, pairs * tiles, :, : pairs * columns]

    for k in range(pairs):
        u_buf[k] = ADAPTER_SCALING * jnp.concatenate(
            [u_parts[i, :, k * columns : (k + 1) * columns] for i in range(per_lane)], axis=1
        )
    low[...] = jnp.zeros_like(low)

    chunk = min(depth, 256)
    copies = []
    for j, (down, c, index) in enumerate(shards):
        start = pl.multiple_of(index * depth, depth)
        column = pl.multiple_of(lax.rem(index, per_lane) * depth, depth)
        source = index // per_lane
        for k in range(pairs):
            for begin in range(0, depth, chunk):
                rows = slice(begin, begin + chunk)
                tile = k * tiles + begin // lanes
                d = jnp.concatenate([down[c, tile + i] for i in range(chunk // lanes)], axis=1)
                for side in range(width // cut):
                    cols = slice(side * cut, (side + 1) * cut)
                    added = lax.dot_general(
                        d,
                        u_buf[k, :, cols],
                        (((0,), (0,)), ((), ())),
                        preferred_element_type=jnp.float32,
                    )
                    w = weights[k][pl.ds(start + begin, chunk), cols]
                    m_buf[j, k, rows, cols] = (w.astype(jnp.float32) + added).astype(jnp.bfloat16)
                low[k] += lax.dot_general(
                    h_buf[source, :, pl.ds(column + begin, chunk)],
                    d,
                    (((1,), (1,)), ((), ())),
                    preferred_element_type=jnp.float32,
                )
            copy = pltpu.make_async_copy(
                m_buf.at[j, k], m_hbm.at[k, pl.ds(start, depth), :], sems.at[j, k]
            )
            copy.start()
            copies.append(copy)

    new = []
    for k in range(pairs):
        high = low[k].astype(jnp.bfloat16)
        rest = (low[k] - high.astype(jnp.float32)).astype(jnp.bfloat16)
        new.append(
            (
                olds[k][...]
                + jnp.dot(high, u_buf[k], preferred_element_type=jnp.float32)
                + jnp.dot(rest, u_buf[k], preferred_element_type=jnp.float32)
            ).astype(jnp.bfloat16)
        )
    add_new_tokens(q_ref, order, caches, new, out_ref, scale)
    for copy in copies:
        copy.wait()


def add_new_tokens(q_ref, order, caches, new, out_ref, scale):
    steps, rows, heads, size = q_ref.shape
    kv = new[0].shape[1] // size
    new = [
        jnp.concatenate([x[:, g * size : (g + 1) * size] for g in range(kv)], axis=0) for x in new
    ]
    n = kv * steps * rows
    lanes = steps * heads
    left = lax.broadcasted_iota(jnp.int32, (lanes, n), 0)
    right = lax.broadcasted_iota(jnp.int32, (lanes, n), 1)
    same_head = over(within(left, heads), heads // kv) == over(right, steps * rows)
    earlier = within(over(right, rows), steps) <= over(left, heads)
    right_row = jnp.where(same_head & earlier, within(right, rows), -1)
    spots = [(o, lse, i) for o, lse in caches for i in range(o.shape[0])]
    for spot, (o_ref, lse_ref, i) in enumerate(spots):
        row = order[spot]
        q = q_ref[:, row].reshape(lanes, size)
        s = lax.dot_general(
            q, new[0], (((1,), (1,)), ((), ())), preferred_element_type=jnp.float32
        )
        s = jnp.where(right_row == row, s * scale, -jnp.inf)
        lse = lse_ref[i]
        highest = jnp.maximum(jnp.max(s, axis=1, keepdims=True), lse)
        p = jnp.exp2(s - highest[:, :n])
        old = jnp.exp2(lse - highest)
        divisor = jnp.sum(p, axis=1, keepdims=True) + old
        o = old * o_ref[i] + jnp.dot(
            p.astype(jnp.bfloat16), new[1], preferred_element_type=jnp.float32
        )
        out_ref[:, row] = (o / divisor).reshape(steps, heads, size).astype(out_ref.dtype)


def merge(lay, shape, entries, weights, states, olds, order, queries, caches):
    pairs, total, width = shape
    rank = entries[0][2].shape[2]
    tokens = states.shape[1]
    depth = total // (lay.fsdp * lay.grp)
    per_lane = lay.fsdp * lay.grp // lay.tp
    n = 2 * len(entries)
    operands = [pinned(w, pltpu.VMEM) for w in weights] + [e[2] for e in entries]
    operands += [states, *olds, pinned(order, pltpu.SMEM), pinned(queries, pltpu.VMEM), *caches]
    specs = [VMEM] * len(operands)
    specs[-2 - len(caches)] = SMEM
    return pl.pallas_call(
        functools.partial(
            merge_all,
            lay,
            [e[:2] for e in entries],
            len(caches) // 2,
            LOG2E / math.sqrt(queries.shape[3]),
        ),
        out_shape=(pltpu.HBM(shape, jnp.bfloat16), jax.ShapeDtypeStruct(queries.shape, jnp.bfloat16)),
        in_specs=specs,
        out_specs=(HBM, VMEM),
        scratch_shapes=[
            pltpu.VMEM((n, pairs, depth, width), jnp.bfloat16),
            pltpu.VMEM((per_lane, rank, pairs * width // per_lane), jnp.bfloat16),
            pltpu.VMEM((pairs, rank, width), jnp.bfloat16),
            pltpu.VMEM((pairs, tokens, rank), jnp.float32),
            pltpu.SemaphoreType.DMA((n, pairs)),
        ],
        compiler_params=pltpu.CompilerParams(vmem_limit_bytes=24 * MIB),
        cost_estimate=pl.CostEstimate(
            flops=2 * pairs * total * width * rank,
            bytes_accessed=2 * pairs * total * width,
            transcendentals=0,
        ),
        name="merge",
    )(*operands)


def shards(
    lay,
    hidden_states,
    queries,
    cache_keys,
    cache_values,
    cache_lengths,
    projection_weight_matrices,
    factor_down,
    factor_up,
):
    send = functools.partial(lax.ppermute, axis_name=AXES)
    steps, rows, features = hidden_states.shape
    slots, kv, size = cache_keys.shape[1:]
    shape = projection_weight_matrices.shape
    sizes = tuple(slots * i // 24 for i in (1, 4, 8, 16, 24))
    own = jnp.swapaxes(factor_down, 1, 2)
    tokens = hidden_states.reshape(steps * rows, features)
    keys = cache_keys.reshape(rows, slots * kv, size)
    values = cache_values.reshape(rows, slots * kv, size)
    swap, ring = lay.core_swap(), lay.ring_step()

    other, other_up = send(own, perm=swap), send(factor_up, perm=swap)
    pair = pack(own, other, factor_up, other_up)
    entries = [(0, False, pair)]

    projections = projection_weight_matrices
    came = send(pair, perm=ring)
    hidden = [tokens] + [send(tokens, perm=lay.feature_step(i)) for i in range(1, lay.tp)]
    lengths, order, q, *buffers, o, lse = cache_attention(
        (0, 1), (0, 2), cache_lengths, None, queries, keys, values, projections, [], False, sizes, [pair]
    )
    caches = [o, lse]
    (came, hidden), token = after_all((came, hidden), o)

    sent, swapped = send(came, perm=ring), send(came, perm=swap)
    *_, o, lse, w_keys = cache_attention(
        (1, rows // 2), (2, rows // 2), lengths, order, q, keys, values, projections, buffers, True, sizes, [token]
    )
    caches += [o, lse]
    entries += [(1, False, came), (1, True, swapped)]
    (came, swapped), token = after_all((sent, swapped), o)
    entries[-1] = (1, True, swapped)

    last_step = lay.ring // 2
    for step in range(2, last_step):
        sent, swapped = send(came, perm=ring), send(came, perm=swap)
        if step == 2:
            w_keys, w_values, states, old_keys = project(0, lay, w_keys, hidden, projections, [token])
            token = old_keys
        elif step == 3:
            w_keys, w_values, old_values = project(1, lay, w_values, [states], w_keys, [token])
            token = old_values
        entries += [(step, False, came), (step, True, swapped)]
        (came, swapped), token = after_all((sent, swapped), token)
        entries[-1] = (step, True, swapped)
    entries.append((last_step, False, came))
    return tuple(
        merge(
            lay,
            shape,
            entries,
            [w_keys, w_values],
            states,
            [old_keys, old_values],
            order,
            q,
            caches,
        )
    )


def solution(mesh):
    return jax.shard_map(
        functools.partial(shards, Layout(mesh)),
        mesh=mesh,
        in_specs=(
            P(None, ("fsdp", "grp"), "tp"),
            P(None, ("fsdp", "grp"), "tp", None),
            P(("fsdp", "grp"), None, "tp", None),
            P(("fsdp", "grp"), None, "tp", None),
            P(("fsdp", "grp")),
            P(None, None, "tp"),
            P(None, ("fsdp", "grp"), None),
            P(None, None, ("fsdp", "grp")),
        ),
        out_specs=(P(None, None, "tp"), P(None, ("fsdp", "grp"), "tp", None)),
        check_vma=False,
    )
```

time: 141 us -> 42.7 us (0.30)
  blocking collectives: 45.3 us -> 0 us
  local copies, waits for them, and re-layouts: 45 us -> 0.01 us
  matrix products: 33.6 us -> 0 us
  Pallas kernels: 0 us -> 24 us
  between operations: 14.1 us -> 0.85 us
  waiting for transfers between devices: 0.7 us -> 11.5 us
  starting transfers between devices: 0.04 us -> 6.11 us
    all_gather x2 -> x0, blocking collectives: 45.3 us -> none  [the longest x1 38.1 us: shards(): lax.all_gather(factor_up, ('fsdp', 'grp'), axis=2, tiled=True)]
    unnamed x9 -> x2, local copies, waits for them, and re-layouts: 43.4 us -> 0.01 us
    dot_general x6 -> x0, matrix products: 33.6 us -> none  [the longest x1 12 us: shards(): jnp.einsum('kdr,krw->kdw', down_all, up_mine, preferred_element_type=jnp....]
    pallas_call x0 -> x7, Pallas kernels: none -> 24 us  [the longest x2 8.3 us: cache_attention(): pl.pallas_call(functools.partial(attend_cache, pairs, pairs[0], ready, si...]
    ppermute x0 -> x10, waiting for transfers between devices: none -> 11.5 us  [the longest x6 8.65 us: shards(): sent, swapped = (send(came, perm=ring), send(came, perm=swap))]
    ppermute x0 -> x10, starting transfers between devices: none -> 6.11 us  [the longest x1 2.77 us: shards(): came = send(pair, perm=ring)]
  transfers between devices with their start and end apart: 1 -> 10, of which waited for: 0 -> 5; matrix products, arithmetic and copies ran while one was open for 20% -> 0% of each run, Pallas kernels for 0% -> 37%
where the time goes in v3:
time: 42.7 us; the launch traced here: 42.5 us
  Pallas kernels  24 us (56%)
  waiting for transfers between devices  11.5 us (27%)
  starting transfers between devices  6.11 us (14%)
  between operations  0.85 us (2%)
    ppermute x6, waiting for transfers between devices, shards(): sent, swapped = (send(came, perm=ring), send(came, perm=swap))  8.65 us
    pallas_call x2, Pallas kernels, cache_attention(): pl.pallas_call(functools.partial(attend_cache, pairs, pairs[0], ready, si...  8.3 us
    pallas_call x1, Pallas kernels, merge(): pl.pallas_call(functools.partial(merge_all, lay, [e[:2] for e in entries]...  8.28 us
    pallas_call x2, Pallas kernels, project(): pl.pallas_call(functools.partial(project_old, part, lay, len(hidden)), ou...  6.29 us
    ppermute x1, starting transfers between devices, shards(): came = send(pair, perm=ring)  2.77 us
    ppermute x1, waiting for transfers between devices, shards(): send(tokens, perm=lay.feature_step(i))  2.55 us
    ppermute x1, starting transfers between devices, shards(): send(tokens, perm=lay.feature_step(i))  1.49 us
    ppermute x6, starting transfers between devices, shards(): sent, swapped = (send(came, perm=ring), send(came, perm=swap))  1.26 us
  transfers between devices with their start and end apart: 10, of which 5 were waited for; matrix products, arithmetic and copies ran while one was open for 0% of the time, Pallas kernels for 37%

profile of v3, /device:TPU:0, one launch (start us, length us, event | category | flops | bytes accessed | tf_op | source)
XLA Modules:
  0.0 42.5 jit_solution(5284053060210766339)
XLA Ops:
  0.6 0.5 %collective-permute-start = (bf16[2,64,512]{2,1,0:T(8,128)(2,1)}, bf16[2,64,512]{2,1,0:T(8,128)(2,1)S(1)}, u32[]{:S(2)}, u32[]{:S(2)}) collective-permute-start(bf16[2,64,512]{2,1,0:T(8,128)(2,1)} %bitcast.10), channel_id=1, source_target_pairs={{0,4},{1,5},{2,6},{3,7},{4,0},{5,1},{6,2},{7,3},{8,12},{9,13},{10,... | collective-permute-start | bytes 393224 | tf_op jit(solution)/shard_map/ppermute | solution.py:584
  1.1 0.1 collective-permute-start.1
  1.2 1.0 %pack_own.1._ = bf16[2,9,64,128]{3,2,1,0:T(8,128)(2,1)S(1)} custom-call(bf16[2,64,512]{2,1,0:T(8,128)(2,1)} %bitcast.11, bf16[2,64,64]{2,1,0:T(8,128)(2,1)} %up.1), custom_call_target="tpu_custom_call" | custom-call | tf_op jit(solution)/shard_map/pack_own/pallas_call | solution.py:154
  2.3 0.3 collective-permute-done.1.up
  2.6 0.0 collective-permute-done.down
  2.6 0.1 pack_other.1.refs_5_.refs_2_
  2.6 2.8 %collective-permute-start.2 = (bf16[2,9,64,128]{3,2,1,0:T(8,128)(2,1)S(1)}, bf16[2,9,64,128]{3,2,1,0:T(8,128)(2,1)S(1)}, u32[]{:S(2)}, u32[]{:S(2)}) collective-permute-start(bf16[2,9,64,128]{3,2,1,0:T(8,128)(2,1)S(1)} %pack_other.1.refs_5_.refs_2_), channel_id=1, source_target_pairs={{0,8},{1,9},{2,0},{3,1},{4,6},{5,7},{6,14},{7,15},{8,16},{9,17},{1... | collective-permute-start | bytes 884744 | tf_op jit(solution)/shard_map/ppermute | solution.py:589
  5.4 1.5 %collective-permute-start.3 = (bf16[32,4096]{1,0:T(8,128)(2,1)}, bf16[32,4096]{1,0:T(8,128)(2,1)S(1)}, u32[]{:S(2)}, u32[]{:S(2)}) collective-permute-start(bf16[32,4096]{1,0:T(8,128)(2,1)} %bitcast.4), channel_id=1, source_target_pairs={{1,0},{0,1},{3,2},{2,3},{5,4},{4,5},{7,6},{6,7},{9,8},{8,9},{11,10... | collective-permute-start | bytes 786440 | tf_op jit(solution)/shard_map/ppermute | solution.py:590
  6.9 4.4 %cache_attention.2 = (s32[8]{0:T(128)S(4)}, s32[8]{0:T(128)S(4)}, bf16[4,8,32,128]{3,2,1,0:T(8,128)(2,1)S(1)}, bf16[8,3072,128]{2,1,0:T(8,128)(2,1)S(1)}, bf16[8...) custom-call(s32[8]{0:T(128)} %refs_0_.1, bf16[4,8,32,128]{3,2,1,0:T(8,128)(2,1)} %refs_1_.1, ...), custom_call_target="tpu_custom_call" | custom-call | flops 402653184 | bytes 3145728 | tf_op jit(solution)/shard_map/cache_attention/pallas_call | solution.py:312
  11.3 2.6 %collective-permute-done.3.refs_2_ = bf16[32,4096]{1,0:T(8,128)(2,1)S(1)} collective-permute-done((bf16[32,4096]{1,0:T(8,128)(2,1)}, bf16[32,4096]{1,0:T(8,128)(2,1)S(1)}, u32[]{:S(2)}, u32[]{:S(2)}) %collective-permute-start.3) | collective-permute-done | bytes 262176 | tf_op jit(solution)/shard_map/ppermute | solution.py:590
  13.8 0.0 collective-permute-done.2.refs_3_
  13.8 0.0 collective-permute-start.5
  13.8 0.4 collective-permute-start.4
  14.2 0.0 copy-start
  14.2 3.9 %cache_attention.3 = (bf16[8,3072,128]{2,1,0:T(8,128)(2,1)S(1)}, bf16[8,3072,128]{2,1,0:T(8,128)(2,1)S(1)}, f32[6,128,128]{2,1,0:T(8,128)S(1)}, f32[6,128,128]{2,1,0:T(8,128)S(1)}, bf16[8192,512]{1,0:T(8,128)(2,1)S(1)}) custom-call(s32[8]{0:T(128)S(4)} %get-tuple-element.31.refs_0_, ...), custom_call_target="tpu_custom_call", output_to_operand_aliasing={{0}: (6, {}), {1}: (7, {})} | custom-call | flops 1207959552 | bytes 17825792 | tf_op jit(solution)/shard_map/cache_attention/pallas_call | solution.py:312
  18.2 0.0 collective-permute-done.5.refs_4_
  18.2 2.3 %collective-permute-done.4.refs_5_ = bf16[2,9,64,128]{3,2,1,0:T(8,128)(2,1)S(1)} collective-permute-done((bf16[2,9,64,128]{3,2,1,0:T(8,128)(2,1)S(1)}, bf16[2,9,64,128]{3,2,1,0:T(8,128)(2,1)S(1)}, u32[]{:S(2)}, u32[]{:S(2)}) %collective-permute-start.4) | collective-permute-done | bytes 294944 | tf_op jit(solution)/shard_map/ppermute | solution.py:597
  20.6 0.0 collective-permute-start.7
  20.6 0.4 collective-permute-start.6
  21.0 0.0 copy-done
  21.0 4.8 %project.2 = (bf16[8192,512]{1,0:T(8,128)(2,1)S(1)}, bf16[8192,512]{1,0:T(8,128)(2,1)S(1)}, bf16[2,32,4096]{2,1,0:T(8,128)(2,1)S(1)}, f32[32,512]{1,0:T(8,128)S(1)}) custom-call(bf16[8192,512]{1,0:T(8,128)(2,1)S(1)} %get-tuple-element.38.refs_0_, bf16[32,4096]{1,0:T(8,128)(2,1)S(1)} %bitcast.5, ...), custom_call_target="tpu_custom_call", output_to_operand_aliasing={{0}: (0, {})} | custom-call | flops 268435456 | bytes 8388608 | tf_op jit(solution)/shard_map/project/pallas_call | solution.py:381
  25.8 0.0 collective-permute-done.7.refs_6_
  25.8 1.5 %collective-permute-done.6.refs_7_ = bf16[2,9,64,128]{3,2,1,0:T(8,128)(2,1)S(1)} collective-permute-done((bf16[2,9,64,128]{3,2,1,0:T(8,128)(2,1)S(1)}, bf16[2,9,64,128]{3,2,1,0:T(8,128)(2,1)S(1)}, u32[]{:S(2)}, u32[]{:S(2)}) %collective-permute-start.6) | collective-permute-done | bytes 294944 | tf_op jit(solution)/shard_map/ppermute | solution.py:608
  27.3 0.0 collective-permute-start.9
  27.3 0.4 collective-permute-start.8
  27.7 1.5 %project.3 = (bf16[8192,512]{1,0:T(8,128)(2,1)S(1)}, bf16[8192,512]{1,0:T(8,128)(2,1)S(1)}, f32[32,512]{1,0:T(8,128)S(1)}) custom-call(bf16[8192,512]{1,0:T(8,128)(2,1)S(1)} %get-tuple-element.44.refs_0_, bf16[8192,512]{1,0:T(8,128)(2,1)S(1)} %get-tuple-element.45.refs_1_, ...), custom_call_target="tpu_custom_call", output_to_operand_aliasing={{0}: (0, {}), {1}: (1, {})} | custom-call | flops 268435456 | bytes 8388608 | tf_op jit(solution)/shard_map/project/pallas_call | solution.py:381
  29.2 0.0 collective-permute-done.9.refs_8_
  29.2 4.8 %collective-permute-done.8.refs_9_ = bf16[2,9,64,128]{3,2,1,0:T(8,128)(2,1)S(1)} collective-permute-done((bf16[2,9,64,128]{3,2,1,0:T(8,128)(2,1)S(1)}, bf16[2,9,64,128]{3,2,1,0:T(8,128)(2,1)S(1)}, u32[]{:S(2)}, u32[]{:S(2)}) %collective-permute-start.8) | collective-permute-done | bytes 294944 | tf_op jit(solution)/shard_map/ppermute | solution.py:608
  34.0 8.3 %merge.1 = (bf16[2,8192,512]{2,1,0:T(8,128)(2,1)}, bf16[4,8,32,128]{3,2,1,0:T(8,128)(2,1)}) custom-call(bf16[8192,512]{1,0:T(8,128)(2,1)S(1)} %get-tuple-element.50.refs_0_, bf16[8192,512]{1,0:T(8,128)(2,1)S(1)} %get-tuple-element.51.refs_1_, bf16[2,9,64,128]{3,2,1,0:T(8,128)(2,1)S(1)} %pack_other.1.refs_5_.refs_2_, ...), custom_call_target="tpu_custom_call" | custom-call | flops 1073741824 | bytes 16777216 | tf_op jit(solution)/shard_map/merge/pallas_call | solution.py:534
Async XLA Ops:
  0.6 1.9 %collective-permute-start = (bf16[2,64,512]{2,1,0:T(8,128)(2,1)}, bf16[2,64,512]{2,1,0:T(8,128)(2,1)S(1)}, u32[]{:S(2)}, u32[]{:S(2)}) collective-permute-start(bf16[2,64,512]{2,1,0:T(8,128)(2,1)} %bitcast.10), channel_id=1, source_target_pairs={{0,4},{1,5},{2,6},{3,7},{4,0},{5,1},{6,2},{7,3},{8,12},{9,13},{10,... | collective-permute-start | bytes 393224 | tf_op jit(solution)/shard_map/ppermute | solution.py:584
  1.1 1.4 %collective-permute-start.1 = (bf16[2,64,64]{2,1,0:T(8,128)(2,1)}, bf16[2,64,64]{2,1,0:T(8,128)(2,1)S(1)}, u32[]{:S(2)}, u32[]{:S(2)}) collective-permute-start(bf16[2,64,64]{2,1,0:T(8,128)(2,1)} %up.1), channel_id=1, source_target_pairs={{0,4},{1,5},{2,6},{3,7},{4,0},{5,1},{6,2},{7,3},{8,12},{9,13},{10,... | collective-permute-start | bytes 49160 | tf_op jit(solution)/shard_map/ppermute | solution.py:584
  2.6 11.2 %collective-permute-start.2 = (bf16[2,9,64,128]{3,2,1,0:T(8,128)(2,1)S(1)}, bf16[2,9,64,128]{3,2,1,0:T(8,128)(2,1)S(1)}, u32[]{:S(2)}, u32[]{:S(2)}) collective-permute-start(bf16[2,9,64,128]{3,2,1,0:T(8,128)(2,1)S(1)} %pack_other.1.refs_5_.refs_2_), channel_id=1, source_target_pairs={{0,8},{1,9},{2,0},{3,1},{4,6},{5,7},{6,14},{7,15},{8,16},{9,17},{1... | collective-permute-start | bytes 884744 | tf_op jit(solution)/shard_map/ppermute | solution.py:589
  5.4 8.4 %collective-permute-start.3 = (bf16[32,4096]{1,0:T(8,128)(2,1)}, bf16[32,4096]{1,0:T(8,128)(2,1)S(1)}, u32[]{:S(2)}, u32[]{:S(2)}) collective-permute-start(bf16[32,4096]{1,0:T(8,128)(2,1)} %bitcast.4), channel_id=1, source_target_pairs={{1,0},{0,1},{3,2},{2,3},{5,4},{4,5},{7,6},{6,7},{9,8},{8,9},{11,10... | collective-permute-start | bytes 786440 | tf_op jit(solution)/shard_map/ppermute | solution.py:590
  13.8 4.4 %collective-permute-start.5 = (bf16[2,9,64,128]{3,2,1,0:T(8,128)(2,1)S(1)}, bf16[2,9,64,128]{3,2,1,0:T(8,128)(2,1)S(1)}, u32[]{:S(2)}, u32[]{:S(2)}) collective-permute-start(bf16[2,9,64,128]{3,2,1,0:T(8,128)(2,1)S(1)} %collective-permute-done.2.refs_3_), channel_id=1, source_target_pairs={{0,4},{1,5},{2,6},{3,7},{4,0},{5,1},{6,2},{7,3},{8,12},{9,13},{10,... | collective-permute-start | bytes 884744 | tf_op jit(solution)/shard_map/ppermute | solution.py:597
  13.8 6.7 %collective-permute-start.4 = (bf16[2,9,64,128]{3,2,1,0:T(8,128)(2,1)S(1)}, bf16[2,9,64,128]{3,2,1,0:T(8,128)(2,1)S(1)}, u32[]{:S(2)}, u32[]{:S(2)}) collective-permute-start(bf16[2,9,64,128]{3,2,1,0:T(8,128)(2,1)S(1)} %collective-permute-done.2.refs_3_), channel_id=1, source_target_pairs={{0,8},{1,9},{2,0},{3,1},{4,6},{5,7},{6,14},{7,15},{8,16},{9,17},{1... | collective-permute-start | bytes 884744 | tf_op jit(solution)/shard_map/ppermute | solution.py:597
  14.2 6.7 %copy-start = (bf16[4,8,4096]{2,1,0:T(8,128)(2,1)S(1)}, bf16[4,8,4096]{2,1,0:T(8,128)(2,1)}, u32[]{:S(2)}) copy-start(bf16[4,8,4096]{2,1,0:T(8,128)(2,1)} %param.8) | copy-start | bytes 786436
  20.6 5.2 %collective-permute-start.7 = (bf16[2,9,64,128]{3,2,1,0:T(8,128)(2,1)S(1)}, bf16[2,9,64,128]{3,2,1,0:T(8,128)(2,1)S(1)}, u32[]{:S(2)}, u32[]{:S(2)}) collective-permute-start(bf16[2,9,64,128]{3,2,1,0:T(8,128)(2,1)S(1)} %collective-permute-done.4.refs_5_), channel_id=1, source_target_pairs={{0,4},{1,5},{2,6},{3,7},{4,0},{5,1},{6,2},{7,3},{8,12},{9,13},{10,... | collective-permute-start | bytes 884744 | tf_op jit(solution)/shard_map/ppermute | solution.py:608
  20.6 6.7 %collective-permute-start.6 = (bf16[2,9,64,128]{3,2,1,0:T(8,128)(2,1)S(1)}, bf16[2,9,64,128]{3,2,1,0:T(8,128)(2,1)S(1)}, u32[]{:S(2)}, u32[]{:S(2)}) collective-permute-start(bf16[2,9,64,128]{3,2,1,0:T(8,128)(2,1)S(1)} %collective-permute-done.4.refs_5_), channel_id=1, source_target_pairs={{0,8},{1,9},{2,0},{3,1},{4,6},{5,7},{6,14},{7,15},{8,16},{9,17},{1... | collective-permute-start | bytes 884744 | tf_op jit(solution)/shard_map/ppermute | solution.py:608
  27.3 1.9 %collective-permute-start.9 = (bf16[2,9,64,128]{3,2,1,0:T(8,128)(2,1)S(1)}, bf16[2,9,64,128]{3,2,1,0:T(8,128)(2,1)S(1)}, u32[]{:S(2)}, u32[]{:S(2)}) collective-permute-start(bf16[2,9,64,128]{3,2,1,0:T(8,128)(2,1)S(1)} %collective-permute-done.6.refs_7_), channel_id=1, source_target_pairs={{0,4},{1,5},{2,6},{3,7},{4,0},{5,1},{6,2},{7,3},{8,12},{9,13},{10,... | collective-permute-start | bytes 884744 | tf_op jit(solution)/shard_map/ppermute | solution.py:608
  27.3 6.7 %collective-permute-start.8 = (bf16[2,9,64,128]{3,2,1,0:T(8,128)(2,1)S(1)}, bf16[2,9,64,128]{3,2,1,0:T(8,128)(2,1)S(1)}, u32[]{:S(2)}, u32[]{:S(2)}) collective-permute-start(bf16[2,9,64,128]{3,2,1,0:T(8,128)(2,1)S(1)} %collective-permute-done.6.refs_7_), channel_id=1, source_target_pairs={{0,8},{1,9},{2,0},{3,1},{4,6},{5,7},{6,14},{7,15},{8,16},{9,17},{1... | collective-permute-start | bytes 884744 | tf_op jit(solution)/shard_map/ppermute | solution.py:608

commit v4 on v3

--- a/solution.py
+++ b/solution.py
@@ -42,11 +42,11 @@
         g, z = divmod(position, self.depth)
         return (z if g % 2 == 0 else self.depth - 1 - z), g
 
-    def ring_step(self):
+    def ring_step(self, step, flip=0):
         pairs = []
         for z, core, g, t in self.devices():
-            to_z, to_g = self.at((self.place(z, g) + (1 - 2 * core)) % self.ring)
-            pairs.append((self.flat(z, core, g, t), self.flat(to_z, core, to_g, t)))
+            to_z, to_g = self.at((self.place(z, g) + step) % self.ring)
+            pairs.append((self.flat(z, core, g, t), self.flat(to_z, core ^ flip, to_g, t)))
         return pairs
 
     def core_swap(self):
@@ -113,84 +113,70 @@
     ]
 
 
-def pack_own(down, up, pair, up_buf, sems, up_sem):
-    lanes = pair.shape[3]
+def copy_pieces(src, dst, sems):
+    rows = dst.shape[0] // sems.shape[0]
+    return [
+        pltpu.make_async_copy(
+            src.at[pl.ds(i * rows, rows)], dst.at[pl.ds(i * rows, rows)], sems.at[i]
+        )
+        for i in range(sems.shape[0])
+    ]
+
+
+def begin_all(down, up, len_hbm, q_hbm, shard, lengths, order, q_ref, up_buf, sems, more):
+    lanes = shard.shape[2]
     count, _, depth = down.shape
     tiles = depth // lanes
     copies = [
         pltpu.make_async_copy(
-            down.at[k, :, pl.ds(i * lanes, lanes)], pair.at[0, k * tiles + i], sems.at[k, i]
+            down.at[k, :, pl.ds(i * lanes, lanes)], shard.at[k * tiles + i], sems.at[k, i]
         )
         for k in range(count)
         for i in range(tiles)
     ]
-    up_copy = pltpu.make_async_copy(up, up_buf, up_sem)
-    up_copy.start()
-    for copy in copies:
+    up_copy = pltpu.make_async_copy(up, up_buf, more.at[0])
+    len_copy = pltpu.make_async_copy(len_hbm, lengths, more.at[1])
+    q_copy = pltpu.make_async_copy(q_hbm, q_ref, more.at[2])
+    for copy in [up_copy, len_copy] + copies + [q_copy]:
         copy.start()
     up_copy.wait()
     columns = jnp.concatenate([up_buf[k] for k in range(count)], axis=1)
-    pair[0, count * tiles, :, : columns.shape[1]] = columns
-    for copy in copies:
+    shard[count * tiles, :, : columns.shape[1]] = columns
+    len_copy.wait()
+    sort_rows(lengths, order)
+    for copy in copies + [q_copy]:
         copy.wait()
 
 
-def pack_other(down, up, _, pair):
-    lanes = pair.shape[3]
-    count, _, depth = down.shape
-    tiles = depth // lanes
-    for k in range(count):
-        for i in range(tiles):
-            pair[1, k * tiles + i] = down[k, :, i * lanes : (i + 1) * lanes]
-    columns = jnp.concatenate([up[k] for k in range(count)], axis=1)
-    pair[1, count * tiles, :, : columns.shape[1]] = columns
-
-
-def pack(own, other, own_up, other_up):
-    count, rank, depth = own.shape
+def begin(down, up, lengths, queries):
+    count, rank, depth = down.shape
     tiles = depth // 128
-    pair = pltpu.VMEM((2, count * tiles + 1, rank, 128), own.dtype)
-    params = pltpu.CompilerParams(vmem_limit_bytes=2 * MIB)
-    half = pl.pallas_call(
-        pack_own,
-        out_shape=pair,
-        in_specs=[HBM, HBM],
-        out_specs=VMEM,
+    scalars = pltpu.SMEM(lengths.shape, jnp.int32)
+    return pl.pallas_call(
+        begin_all,
+        out_shape=(
+            pltpu.VMEM((count * tiles + 1, rank, 128), down.dtype),
+            scalars,
+            scalars,
+            pltpu.VMEM(queries.shape, queries.dtype),
+        ),
+        in_specs=[HBM] * 4,
+        out_specs=(VMEM, SMEM, SMEM, VMEM),
         scratch_shapes=[
-            pltpu.VMEM(own_up.shape, own.dtype),
+            pltpu.VMEM(up.shape, up.dtype),
             pltpu.SemaphoreType.DMA((count, tiles)),
-            pltpu.SemaphoreType.DMA,
+            pltpu.SemaphoreType.DMA((3,)),
         ],
-        compiler_params=params,
-        name="pack_own",
-    )(pinned(own), pinned(own_up))
-    return pl.pallas_call(
-        pack_other,
-        out_shape=pair,
-        in_specs=[VMEM, VMEM, VMEM],
-        out_specs=VMEM,
-        input_output_aliases={2: 0},
-        compiler_params=params,
-        name="pack_other",
-    )(other, other_up, pinned(half, pltpu.VMEM))
-
-
-def attend_cache(pairs, done, ready, sizes, scale, has_w, n_kept, *refs):
-    refs = list(refs)
-    sems, w_sem = refs[-2:]
-    first = done == 0
-    if first:
-        len_hbm, q_hbm, k_hbm, v_hbm, w_hbm = refs[:5]
-        lengths, order, q_ref, k_buf, v_buf, *outs = refs[-2 - 7 - has_w : -2]
-        len_copy = pltpu.make_async_copy(len_hbm, lengths, sems.at[0, 0, 0])
-        q_copy = pltpu.make_async_copy(q_hbm, q_ref, w_sem)
-        len_copy.start()
-        q_copy.start()
-        len_copy.wait()
-        sort_rows(lengths, order)
-    else:
-        lengths, order, q_ref, k_hbm, v_hbm, w_hbm = refs[:6]
-        k_buf, v_buf, *outs = refs[-2 - 4 - has_w - n_kept : -2 - n_kept]
+        compiler_params=pltpu.CompilerParams(vmem_limit_bytes=2 * MIB),
+        name="begin",
+    )(pinned(down), pinned(up), pinned(lengths), pinned(queries))
+
+
+def attend_cache(pairs, ready, sizes, scale, has_w, *refs):
+    lengths, order, q_ref, k_hbm, v_hbm, w_hbm = refs[:6]
+    sems, w_sems = refs[-2:]
+    k_buf, v_buf, *outs = refs[-6 - has_w : -2]
+    done = pairs[0]
     o_ref, lse_ref = outs[:2]
     steps, _, heads, size = q_ref.shape
     kv = k_hbm.shape[1] // sizes[-1]
@@ -223,10 +209,9 @@
     for pair in range(*ready):
         by_length(lengths[order[2 * pair]], sizes, functools.partial(start, pair))
     if has_w:
-        w_copy = pltpu.make_async_copy(w_hbm.at[0], outs[2], w_sem)
-        w_copy.start()
-    if first:
-        q_copy.wait()
+        w_copies = copy_pieces(w_hbm.at[0], outs[2], w_sems)
+        for copy in w_copies:
+            copy.start()
 
     row_head = over(within(lax.broadcasted_iota(jnp.int32, (lanes, size), 0), heads), heads // kv)
     slot_head = within(lax.broadcasted_iota(jnp.int32, (lanes, size), 1), kv)
@@ -276,7 +261,8 @@
     for pair in range(max(pairs[1], ready[0]), ready[1]):
         by_length(lengths[order[2 * pair]], sizes, functools.partial(finish, pair))
     if has_w:
-        w_copy.wait()
+        for copy in w_copies:
+            copy.wait()
 
 
 def like(x):
@@ -290,34 +276,25 @@
     count = 2 * (pairs[1] - pairs[0])
     piece = pltpu.VMEM((count, steps * heads, size), jnp.float32)
     outs = [piece, piece] + ([pltpu.VMEM(weights.shape[1:], weights.dtype)] if has_w else [])
-    aliases = {}
-    if not buffers:
-        operands = [pinned(x) for x in (lengths, queries, keys, values, weights)]
-        specs = [HBM] * 5
-        scalars = pltpu.SMEM((rows,), jnp.int32)
-        buffer = pltpu.VMEM(keys.shape, keys.dtype)
-        out_shape = [scalars, scalars, like(queries), buffer, buffer]
-        out_specs = [SMEM, SMEM, VMEM, VMEM, VMEM]
-    else:
-        operands = [pinned(x, pltpu.SMEM) for x in (lengths, order)]
-        operands += [pinned(queries, pltpu.VMEM)]
-        operands += [pinned(x) for x in (keys, values, weights)]
-        aliases = {len(operands) + i: i for i in range(len(buffers))}
-        operands += [pinned(b, pltpu.VMEM) for b in buffers]
-        specs = [SMEM, SMEM, VMEM, HBM, HBM, HBM] + [VMEM] * len(buffers)
-        out_shape = [like(b) for b in buffers]
-        out_specs = [VMEM] * len(buffers)
+    operands = [pinned(x, pltpu.SMEM) for x in (lengths, order)]
+    operands += [pinned(queries, pltpu.VMEM)]
+    operands += [pinned(x) for x in (keys, values, weights)]
+    aliases = {len(operands) + i: i for i in range(len(buffers))}
+    operands += [pinned(b, pltpu.VMEM) for b in buffers]
+    specs = [SMEM, SMEM, VMEM, HBM, HBM, HBM] + [VMEM] * len(buffers)
+    out_shape = [pltpu.VMEM(keys.shape, keys.dtype)] * 2
+    out_specs = [VMEM] * 2
     out_shape += outs
     out_specs += [VMEM] * len(outs)
     return pl.pallas_call(
-        functools.partial(attend_cache, pairs, pairs[0], ready, sizes, scale, int(has_w), 0),
+        functools.partial(attend_cache, pairs, ready, sizes, scale, int(has_w)),
         out_shape=out_shape,
         in_specs=specs + [ANY] * len(after),
         out_specs=out_specs,
         input_output_aliases=aliases,
         scratch_shapes=[
             pltpu.SemaphoreType.DMA((rows // 2, 2, 2)),
-            pltpu.SemaphoreType.DMA,
+            pltpu.SemaphoreType.DMA((8,)),
         ],
         compiler_params=pltpu.CompilerParams(vmem_limit_bytes=8 * MIB),
         cost_estimate=pl.CostEstimate(
@@ -335,9 +312,10 @@
     if part == 0:
         hidden = refs[1 : 1 + n_hidden]
         w_hbm = refs[1 + n_hidden]
-        w_ref, next_ref, h_ref, out_ref, sem = refs[-5:]
-        copy = pltpu.make_async_copy(w_hbm.at[1], next_ref, sem)
-        copy.start()
+        w_ref, next_ref, h_ref, out_ref, sems = refs[-5:]
+        copies = copy_pieces(w_hbm.at[1], next_ref, sems)
+        for copy in copies:
+            copy.start()
         for i, h in enumerate(hidden):
             h_ref[lax.rem(tp + i, lay.tp)] = h[...]
     else:
@@ -356,7 +334,8 @@
             )
     out_ref[...] = total
     if part == 0:
-        copy.wait()
+        for copy in copies:
+            copy.wait()
 
 
 def project(part, lay, w, hidden, weights, after):
@@ -370,7 +349,7 @@
         specs.append(HBM)
         out_shape = [like(w), like(w), states, out]
         aliases = {0: 0}
-        scratch = [pltpu.SemaphoreType.DMA]
+        scratch = [pltpu.SemaphoreType.DMA((8,))]
     else:
         operands = [pinned(weights, pltpu.VMEM)] + operands
         specs.append(VMEM)
@@ -409,7 +388,7 @@
 
     pairs, depth, width = m_buf.shape[1:]
     cut = min(width, 256)
-    lanes = downs[0].shape[3]
+    lanes = downs[0].shape[2]
     tiles = depth // lanes
     fsdp, grp, tp = (lax.axis_index(a) for a in AXES)
     z, core = fsdp // 2, lax.rem(fsdp, 2)
@@ -418,20 +397,18 @@
 
     shards = []
     for (step, flip), down in zip(plan, downs):
-        towards = 2 * core - 1
-        spot = lax.rem(place + lay.ring + step * (-towards if flip else towards), lay.ring)
+        spot = lax.rem(place + (lay.ring + step), lay.ring)
         g = spot // lay.depth
         along = lax.rem(spot, lay.depth)
         zz = jnp.where(lax.rem(g, 2) == 0, along, lay.depth - 1 - along)
-        for c in range(2):
-            cc = lax.rem(core + c + (1 if flip else 0), 2)
-            shards.append((down, c, (zz * 2 + cc) * lay.grp + g))
+        shards.append((down, (zz * 2 + (1 - core if flip else core)) * lay.grp + g))
 
     columns = width // per_lane
-    for down, c, index in shards:
+    for down, index in shards:
+
         @pl.when(index // per_lane == tp)
         def _():
-            u_parts[lax.rem(index, per_lane)] = down[c, pairs * tiles, :, : pairs * columns]
+            u_parts[lax.rem(index, per_lane)] = down[pairs * tiles, :, : pairs * columns]
 
     for k in range(pairs):
         u_buf[k] = ADAPTER_SCALING * jnp.concatenate(
@@ -441,7 +418,7 @@
 
     chunk = min(depth, 256)
     copies = []
-    for j, (down, c, index) in enumerate(shards):
+    for j, (down, index) in enumerate(shards):
         start = pl.multiple_of(index * depth, depth)
         column = pl.multiple_of(lax.rem(index, per_lane) * depth, depth)
         source = index // per_lane
@@ -449,7 +426,7 @@
             for begin in range(0, depth, chunk):
                 rows = slice(begin, begin + chunk)
                 tile = k * tiles + begin // lanes
-                d = jnp.concatenate([down[c, tile + i] for i in range(chunk // lanes)], axis=1)
+                d = jnp.concatenate([down[tile + i] for i in range(chunk // lanes)], axis=1)
                 for side in range(width // cut):
                     cols = slice(side * cut, (side + 1) * cut)
                     added = lax.dot_general(
@@ -522,11 +499,11 @@
 
 def merge(lay, shape, entries, weights, states, olds, order, queries, caches):
     pairs, total, width = shape
-    rank = entries[0][2].shape[2]
+    rank = entries[0][2].shape[1]
     tokens = states.shape[1]
     depth = total // (lay.fsdp * lay.grp)
     per_lane = lay.fsdp * lay.grp // lay.tp
-    n = 2 * len(entries)
+    n = len(entries)
     operands = [pinned(w, pltpu.VMEM) for w in weights] + [e[2] for e in entries]
     operands += [states, *olds, pinned(order, pltpu.SMEM), pinned(queries, pltpu.VMEM), *caches]
     specs = [VMEM] * len(operands)
@@ -579,43 +556,59 @@
     tokens = hidden_states.reshape(steps * rows, features)
     keys = cache_keys.reshape(rows, slots * kv, size)
     values = cache_values.reshape(rows, slots * kv, size)
-    swap, ring = lay.core_swap(), lay.ring_step()
-
-    other, other_up = send(own, perm=swap), send(factor_up, perm=swap)
-    pair = pack(own, other, factor_up, other_up)
-    entries = [(0, False, pair)]
+    swap, ring = lay.core_swap(), {d: lay.ring_step(d) for d in (1, -1)}
+    shard, lengths, order, q = begin(own, factor_up, cache_lengths, queries)
+    entries = [(0, False, shard)]
 
     projections = projection_weight_matrices
-    came = send(pair, perm=ring)
+    came = {d: send(shard, perm=ring[d]) for d in ring}
+    partner = send(shard, perm=swap)
     hidden = [tokens] + [send(tokens, perm=lay.feature_step(i)) for i in range(1, lay.tp)]
-    lengths, order, q, *buffers, o, lse = cache_attention(
-        (0, 1), (0, 2), cache_lengths, None, queries, keys, values, projections, [], False, sizes, [pair]
+    *buffers, o, lse = cache_attention(
+        (0, 1), (0, 2), lengths, order, q, keys, values, projections, [], False, sizes, [shard]
     )
     caches = [o, lse]
-    (came, hidden), token = after_all((came, hidden), o)
-
-    sent, swapped = send(came, perm=ring), send(came, perm=swap)
-    *_, o, lse, w_keys = cache_attention(
-        (1, rows // 2), (2, rows // 2), lengths, order, q, keys, values, projections, buffers, True, sizes, [token]
-    )
-    caches += [o, lse]
-    entries += [(1, False, came), (1, True, swapped)]
-    (came, swapped), token = after_all((sent, swapped), o)
-    entries[-1] = (1, True, swapped)
+    (came, partner), token = after_all((came, partner), o)
+    entries.append((0, True, partner))
 
     last_step = lay.ring // 2
-    for step in range(2, last_step):
-        sent, swapped = send(came, perm=ring), send(came, perm=swap)
-        if step == 2:
+    for step in range(1, last_step):
+        last = step + 1 == last_step
+        sent = {
+            1: send(came[1], perm=ring[1]),
+            -1: send(came[-1], perm=lay.ring_step(-1, 1) if last else ring[-1]),
+        }
+        swapped = {d: send(came[d], perm=swap) for d in ring}
+        if step == 1:
+            *_, o, lse, w_keys = cache_attention(
+                (1, rows // 4 * 2),
+                (2, rows // 4 * 2),
+                lengths,
+                order,
+                q,
+                keys,
+                values,
+                projections,
+                buffers,
+                True,
+                sizes,
+                [token],
+            )
+            caches += [o, lse]
+            token = o
+        elif step == 2:
             w_keys, w_values, states, old_keys = project(0, lay, w_keys, hidden, projections, [token])
             token = old_keys
         elif step == 3:
             w_keys, w_values, old_values = project(1, lay, w_values, [states], w_keys, [token])
             token = old_values
-        entries += [(step, False, came), (step, True, swapped)]
-        (came, swapped), token = after_all((sent, swapped), token)
-        entries[-1] = (step, True, swapped)
-    entries.append((last_step, False, came))
+        entries += [(-d * step, False, came[d]) for d in ring]
+        if step == 1:
+            (came, swapped, hidden), token = after_all((sent, swapped, hidden), token)
+        else:
+            (came, swapped), token = after_all((sent, swapped), token)
+        entries += [(-d * step, True, swapped[d]) for d in ring]
+    entries += [(-last_step, False, came[1]), (last_step, True, came[-1])]
     return tuple(
         merge(
             lay,

time: 42.7 us -> 41.4 us (0.970)
  waiting for transfers between devices: 11.5 us -> 5.4 us
  starting transfers between devices: 6.11 us -> 11.8 us
  Pallas kernels: 24 us -> 23.2 us
    ppermute x9 -> x15, starting transfers between devices: 4.62 us -> 9.84 us  [the longest x3 4.42 us: shards(): send(came[-1], perm=lay.ring_step(-1, 1) if last else ring[-1])]
    ppermute x9 -> x15, waiting for transfers between devices: 8.96 us -> 5.4 us  [the longest x3 4.92 us: shards(): send(came[1], perm=ring[1])]
    ppermute x1, waiting for transfers between devices: 2.55 us -> 0.01 us  [shards(): send(tokens, perm=lay.feature_step(i))]
    pallas_call x4 -> x3, Pallas kernels: 9.41 us -> 8.86 us  [the longest x2 7.66 us: cache_attention(): pl.pallas_call(functools.partial(attend_cache, pairs, ready, sizes, scale...]
  transfers between devices with their start and end apart: 10 -> 16, of which waited for: 5 -> 5; matrix products, arithmetic and copies ran while one was open for 0% -> 0% of each run, Pallas kernels for 37% -> 33%
where the time goes in v4:
time: 41.4 us; the launch traced here: 41.3 us
  Pallas kernels  23.2 us (56%)
  starting transfers between devices  11.8 us (29%)
  waiting for transfers between devices  5.4 us (13%)
  between operations  0.91 us (2%)
    pallas_call x1, Pallas kernels, merge(): pl.pallas_call(functools.partial(merge_all, lay, [e[:2] for e in entries]...  8.29 us
    pallas_call x2, Pallas kernels, cache_attention(): pl.pallas_call(functools.partial(attend_cache, pairs, ready, sizes, scale...  7.66 us
    pallas_call x2, Pallas kernels, project(): pl.pallas_call(functools.partial(project_old, part, lay, len(hidden)), ou...  6.07 us
    ppermute x3, waiting for transfers between devices, shards(): send(came[1], perm=ring[1])  4.92 us
    ppermute x3, starting transfers between devices, shards(): send(came[-1], perm=lay.ring_step(-1, 1) if last else ring[-1])  4.42 us
    ppermute x2, starting transfers between devices, shards(): came = {d: send(shard, perm=ring[d]) for d in ring}  2.67 us
    ppermute x1, starting transfers between devices, shards(): send(tokens, perm=lay.feature_step(i))  1.91 us
    ppermute x3, starting transfers between devices, shards(): send(came[1], perm=ring[1])  1.61 us
  transfers between devices with their start and end apart: 16, of which 5 were waited for; matrix products, arithmetic and copies ran while one was open for 0% of the time, Pallas kernels for 33%

profile of v4, /device:TPU:0, one launch (start us, length us, event | category | flops | bytes accessed | tf_op | source)
XLA Modules:
  0.0 41.3 jit_solution(6117435969983323276)
XLA Ops:
  0.6 1.2 %begin.1 = (bf16[9,64,128]{2,1,0:T(8,128)(2,1)S(1)}, s32[8]{0:T(128)S(4)}, s32[8]{0:T(128)S(4)}, bf16[4,8,32,128]{3,2,1,0:T(8,128)(2,1)S(1)}) custom-call(bf16[2,64,512]{2,1,0:T(8,128)(2,1)} %bitcast.10, bf16[2,64,64]{2,1,0:T(8,128)(2,1)} %up.1, s32[8]{0:T(128)} %len_hbm.1, bf16[4,8,32,128]{3,2,1,0:T(8,128)(2,1)} %q_hbm.1), custom_call_target="tpu_custom_call" | custom-call | tf_op jit(solution)/shard_map/begin/pallas_call | solution.py:155
  1.8 0.5 %collective-permute-start.2 = (bf16[9,64,128]{2,1,0:T(8,128)(2,1)S(1)}, bf16[9,64,128]{2,1,0:T(8,128)(2,1)S(1)}, u32[]{:S(2)}, u32[]{:S(2)}) collective-permute-start(bf16[9,64,128]{2,1,0:T(8,128)(2,1)S(1)} %get-tuple-element.43.refs_6_.refs_2_), channel_id=1, source_target_pairs={{0,4},{1,5},{2,6},{3,7},{4,0},{5,1},{6,2},{7,3},{8,12},{9,13},{10,... | collective-permute-start | bytes 442376 | tf_op jit(solution)/shard_map/ppermute | solution.py:565
  2.4 2.6 %collective-permute-start.1 = (bf16[9,64,128]{2,1,0:T(8,128)(2,1)S(1)}, bf16[9,64,128]{2,1,0:T(8,128)(2,1)S(1)}, u32[]{:S(2)}, u32[]{:S(2)}) collective-permute-start(bf16[9,64,128]{2,1,0:T(8,128)(2,1)S(1)} %get-tuple-element.43.refs_6_.refs_2_), channel_id=1, source_target_pairs={{0,8},{1,9},{2,0},{3,1},{4,12},{5,13},{6,4},{7,5},{8,16},{9,17},{1... | collective-permute-start | bytes 442376 | tf_op jit(solution)/shard_map/ppermute | solution.py:564
  5.0 0.0 collective-permute-start
  5.0 1.9 %collective-permute-start.7 = (bf16[32,4096]{1,0:T(8,128)(2,1)}, bf16[32,4096]{1,0:T(8,128)(2,1)S(1)}, u32[]{:S(2)}, u32[]{:S(2)}) collective-permute-start(bf16[32,4096]{1,0:T(8,128)(2,1)} %bitcast.4), channel_id=1, source_target_pairs={{1,0},{0,1},{3,2},{2,3},{5,4},{4,5},{7,6},{6,7},{9,8},{8,9},{11,10... | collective-permute-start | bytes 786440 | tf_op jit(solution)/shard_map/ppermute | solution.py:566
  6.9 3.7 %cache_attention.2 = (bf16[8,3072,128]{2,1,0:T(8,128)(2,1)S(1)}, bf16[8,3072,128]{2,1,0:T(8,128)(2,1)S(1)}, f32[2,128,128]{2,1,0:T(8,128)S(1)}, f32[2,128,128]{2,1,0:T(8,128)S(1)}) custom-call(s32[8]{0:T(128)S(4)} %get-tuple-element.40.refs_0_, s32[8]{0:T(128)S(4)} %get-tuple-element.41.refs_1_.refs_21_, ...), custom_call_target="tpu_custom_call" | custom-call | flops 402653184 | bytes 3145728 | tf_op jit(solution)/shard_map/cache_attention/pallas_call | solution.py:289
  10.6 0.0 collective-permute-done.2.refs_3_
  10.6 0.0 collective-permute-done.1.refs_4_
  10.6 0.3 collective-permute-done.refs_5_
  10.9 0.0 collective-permute-start.5
  10.9 1.4 %collective-permute-start.3 = (bf16[9,64,128]{2,1,0:T(8,128)(2,1)S(1)}, bf16[9,64,128]{2,1,0:T(8,128)(2,1)S(1)}, u32[]{:S(2)}, u32[]{:S(2)}) collective-permute-start(bf16[9,64,128]{2,1,0:T(8,128)(2,1)S(1)} %collective-permute-done.refs_5_), channel_id=1, source_target_pairs={{0,2},{1,3},{2,10},{3,11},{4,6},{5,7},{6,14},{7,15},{8,0},{9,1},{1... | collective-permute-start | bytes 442376 | tf_op jit(solution)/shard_map/ppermute | solution.py:579
  12.3 0.2 collective-permute-start.6
  12.4 0.7 %collective-permute-start.4 = (bf16[9,64,128]{2,1,0:T(8,128)(2,1)S(1)}, bf16[9,64,128]{2,1,0:T(8,128)(2,1)S(1)}, u32[]{:S(2)}, u32[]{:S(2)}) collective-permute-start(bf16[9,64,128]{2,1,0:T(8,128)(2,1)S(1)} %collective-permute-done.1.refs_4_), channel_id=1, source_target_pairs={{0,8},{1,9},{2,0},{3,1},{4,12},{5,13},{6,4},{7,5},{8,16},{9,17},{1... | collective-permute-start | bytes 442376 | tf_op jit(solution)/shard_map/ppermute | solution.py:578
  13.2 0.0 copy-start
  13.2 4.0 %cache_attention.3 = (bf16[8,3072,128]{2,1,0:T(8,128)(2,1)S(1)}, bf16[8,3072,128]{2,1,0:T(8,128)(2,1)S(1)}, f32[6,128,128]{2,1,0:T(8,128)S(1)}, f32[6,128,128]{2,1,0:T(8,128)S(1)}, bf16[8192,512]{1,0:T(8,128)(2,1)S(1)}) custom-call(s32[8]{0:T(128)S(4)} %get-tuple-element.40.refs_0_, ...), custom_call_target="tpu_custom_call", output_to_operand_aliasing={{0}: (6, {}), {1}: (7, {})} | custom-call | flops 1207959552 | bytes 17825792 | tf_op jit(solution)/shard_map/cache_attention/pallas_call | solution.py:289
  17.2 0.0 collective-permute-done.7.refs_2_
  17.2 0.0 collective-permute-done.5.refs_7_
  17.2 0.0 collective-permute-done.3.refs_9_
  17.2 0.0 collective-permute-done.6.refs_6_
  17.2 1.3 %collective-permute-done.4.refs_8_ = bf16[9,64,128]{2,1,0:T(8,128)(2,1)S(1)} collective-permute-done((bf16[9,64,128]{2,1,0:T(8,128)(2,1)S(1)}, bf16[9,64,128]{2,1,0:T(8,128)(2,1)S(1)}, u32[]{:S(2)}, u32[]{:S(2)}) %collective-permute-start.4) | collective-permute-done | bytes 147488 | tf_op jit(solution)/shard_map/ppermute | solution.py:578
  18.5 0.0 collective-permute-start.10
  18.5 1.6 %collective-permute-start.8 = (bf16[9,64,128]{2,1,0:T(8,128)(2,1)S(1)}, bf16[9,64,128]{2,1,0:T(8,128)(2,1)S(1)}, u32[]{:S(2)}, u32[]{:S(2)}) collective-permute-start(bf16[9,64,128]{2,1,0:T(8,128)(2,1)S(1)} %collective-permute-done.3.refs_9_), channel_id=1, source_target_pairs={{0,2},{1,3},{2,10},{3,11},{4,6},{5,7},{6,14},{7,15},{8,0},{9,1},{1... | collective-permute-start | bytes 442376 | tf_op jit(solution)/shard_map/ppermute | solution.py:579
  20.1 0.2 collective-permute-start.11
  20.4 0.4 %collective-permute-start.9 = (bf16[9,64,128]{2,1,0:T(8,128)(2,1)S(1)}, bf16[9,64,128]{2,1,0:T(8,128)(2,1)S(1)}, u32[]{:S(2)}, u32[]{:S(2)}) collective-permute-start(bf16[9,64,128]{2,1,0:T(8,128)(2,1)S(1)} %collective-permute-done.4.refs_8_), channel_id=1, source_target_pairs={{0,8},{1,9},{2,0},{3,1},{4,12},{5,13},{6,4},{7,5},{8,16},{9,17},{1... | collective-permute-start | bytes 442376 | tf_op jit(solution)/shard_map/ppermute | solution.py:578
  20.8 0.0 copy-done
  20.8 4.6 %project.2 = (bf16[8192,512]{1,0:T(8,128)(2,1)S(1)}, bf16[8192,512]{1,0:T(8,128)(2,1)S(1)}, bf16[2,32,4096]{2,1,0:T(8,128)(2,1)S(1)}, f32[32,512]{1,0:T(8,128)S(1)}) custom-call(bf16[8192,512]{1,0:T(8,128)(2,1)S(1)} %get-tuple-element.48.refs_0_, bf16[32,4096]{1,0:T(8,128)(2,1)S(1)} %bitcast.5, ...), custom_call_target="tpu_custom_call", output_to_operand_aliasing={{0}: (0, {})} | custom-call | flops 268435456 | bytes 8388608 | tf_op jit(solution)/shard_map/project/pallas_call | solution.py:360
  25.4 0.0 collective-permute-done.10.refs_11_
  25.4 0.0 collective-permute-done.8.refs_13_
  25.4 0.0 collective-permute-done.11.refs_10_
  25.4 1.0 %collective-permute-done.9.refs_12_ = bf16[9,64,128]{2,1,0:T(8,128)(2,1)S(1)} collective-permute-done((bf16[9,64,128]{2,1,0:T(8,128)(2,1)S(1)}, bf16[9,64,128]{2,1,0:T(8,128)(2,1)S(1)}, u32[]{:S(2)}, u32[]{:S(2)}) %collective-permute-start.9) | collective-permute-done | bytes 147488 | tf_op jit(solution)/shard_map/ppermute | solution.py:578
  26.4 0.0 collective-permute-start.15
  26.4 0.4 %collective-permute-start.13 = (bf16[9,64,128]{2,1,0:T(8,128)(2,1)S(1)}, bf16[9,64,128]{2,1,0:T(8,128)(2,1)S(1)}, u32[]{:S(2)}, u32[]{:S(2)}) collective-permute-start(bf16[9,64,128]{2,1,0:T(8,128)(2,1)S(1)} %collective-permute-done.9.refs_12_), channel_id=1, source_target_pairs={{0,8},{1,9},{2,0},{3,1},{4,12},{5,13},{6,4},{7,5},{8,16},{9,17},{1... | collective-permute-start | bytes 442376 | tf_op jit(solution)/shard_map/ppermute | solution.py:578
  26.8 0.2 collective-permute-start.14
  27.1 1.5 %collective-permute-start.12 = (bf16[9,64,128]{2,1,0:T(8,128)(2,1)S(1)}, bf16[9,64,128]{2,1,0:T(8,128)(2,1)S(1)}, u32[]{:S(2)}, u32[]{:S(2)}) collective-permute-start(bf16[9,64,128]{2,1,0:T(8,128)(2,1)S(1)} %collective-permute-done.8.refs_13_), channel_id=1, source_target_pairs={{0,6},{1,7},{2,14},{3,15},{4,2},{5,3},{6,10},{7,11},{8,4},{9,5},{1... | collective-permute-start | bytes 442376 | tf_op jit(solution)/shard_map/ppermute | solution.py:579
  28.5 1.5 %project.3 = (bf16[8192,512]{1,0:T(8,128)(2,1)S(1)}, bf16[8192,512]{1,0:T(8,128)(2,1)S(1)}, f32[32,512]{1,0:T(8,128)S(1)}) custom-call(bf16[8192,512]{1,0:T(8,128)(2,1)S(1)} %get-tuple-element.55.refs_0_, bf16[8192,512]{1,0:T(8,128)(2,1)S(1)} %get-tuple-element.56.refs_1_, ...), custom_call_target="tpu_custom_call", output_to_operand_aliasing={{0}: (0, {}), {1}: (1, {})} | custom-call | flops 268435456 | bytes 8388608 | tf_op jit(solution)/shard_map/project/pallas_call | solution.py:360
  30.1 0.0 collective-permute-done.15.refs_14_
  30.1 2.6 %collective-permute-done.13.refs_16_ = bf16[9,64,128]{2,1,0:T(8,128)(2,1)S(1)} collective-permute-done((bf16[9,64,128]{2,1,0:T(8,128)(2,1)S(1)}, bf16[9,64,128]{2,1,0:T(8,128)(2,1)S(1)}, u32[]{:S(2)}, u32[]{:S(2)}) %collective-permute-start.13) | collective-permute-done | bytes 147488 | tf_op jit(solution)/shard_map/ppermute | solution.py:578
  32.7 0.0 collective-permute-done.14.refs_15_
  32.7 0.2 collective-permute-done.12.refs_17_
  32.8 8.3 %merge.1 = (bf16[2,8192,512]{2,1,0:T(8,128)(2,1)}, bf16[4,8,32,128]{3,2,1,0:T(8,128)(2,1)}) custom-call(bf16[8192,512]{1,0:T(8,128)(2,1)S(1)} %get-tuple-element.62.refs_0_, bf16[8192,512]{1,0:T(8,128)(2,1)S(1)} %get-tuple-element.63.refs_1_, bf16[9,64,128]{2,1,0:T(8,128)(2,1)S(1)} %get-tuple-element.43.refs_6_.refs_2_, ...), custom_call_target="tpu_custom_call" | custom-call | flops 1073741824 | bytes 16777216 | tf_op jit(solution)/shard_map/merge/pallas_call | solution.py:511
Async XLA Ops:
  1.8 8.8 %collective-permute-start.2 = (bf16[9,64,128]{2,1,0:T(8,128)(2,1)S(1)}, bf16[9,64,128]{2,1,0:T(8,128)(2,1)S(1)}, u32[]{:S(2)}, u32[]{:S(2)}) collective-permute-start(bf16[9,64,128]{2,1,0:T(8,128)(2,1)S(1)} %get-tuple-element.43.refs_6_.refs_2_), channel_id=1, source_target_pairs={{0,4},{1,5},{2,6},{3,7},{4,0},{5,1},{6,2},{7,3},{8,12},{9,13},{10,... | collective-permute-start | bytes 442376 | tf_op jit(solution)/shard_map/ppermute | solution.py:565
  2.4 8.3 %collective-permute-start.1 = (bf16[9,64,128]{2,1,0:T(8,128)(2,1)S(1)}, bf16[9,64,128]{2,1,0:T(8,128)(2,1)S(1)}, u32[]{:S(2)}, u32[]{:S(2)}) collective-permute-start(bf16[9,64,128]{2,1,0:T(8,128)(2,1)S(1)} %get-tuple-element.43.refs_6_.refs_2_), channel_id=1, source_target_pairs={{0,8},{1,9},{2,0},{3,1},{4,12},{5,13},{6,4},{7,5},{8,16},{9,17},{1... | collective-permute-start | bytes 442376 | tf_op jit(solution)/shard_map/ppermute | solution.py:564
  5.0 5.9 %collective-permute-start = (bf16[9,64,128]{2,1,0:T(8,128)(2,1)S(1)}, bf16[9,64,128]{2,1,0:T(8,128)(2,1)S(1)}, u32[]{:S(2)}, u32[]{:S(2)}) collective-permute-start(bf16[9,64,128]{2,1,0:T(8,128)(2,1)S(1)} %get-tuple-element.43.refs_6_.refs_2_), channel_id=1, source_target_pairs={{0,2},{1,3},{2,10},{3,11},{4,6},{5,7},{6,14},{7,15},{8,0},{9,1},{1... | collective-permute-start | bytes 442376 | tf_op jit(solution)/shard_map/ppermute | solution.py:564
  5.0 12.2 %collective-permute-start.7 = (bf16[32,4096]{1,0:T(8,128)(2,1)}, bf16[32,4096]{1,0:T(8,128)(2,1)S(1)}, u32[]{:S(2)}, u32[]{:S(2)}) collective-permute-start(bf16[32,4096]{1,0:T(8,128)(2,1)} %bitcast.4), channel_id=1, source_target_pairs={{1,0},{0,1},{3,2},{2,3},{5,4},{4,5},{7,6},{6,7},{9,8},{8,9},{11,10... | collective-permute-start | bytes 786440 | tf_op jit(solution)/shard_map/ppermute | solution.py:566
  10.9 6.3 %collective-permute-start.5 = (bf16[9,64,128]{2,1,0:T(8,128)(2,1)S(1)}, bf16[9,64,128]{2,1,0:T(8,128)(2,1)S(1)}, u32[]{:S(2)}, u32[]{:S(2)}) collective-permute-start(bf16[9,64,128]{2,1,0:T(8,128)(2,1)S(1)} %collective-permute-done.refs_5_), channel_id=1, source_target_pairs={{0,4},{1,5},{2,6},{3,7},{4,0},{5,1},{6,2},{7,3},{8,12},{9,13},{10,... | collective-permute-start | bytes 442376 | tf_op jit(solution)/shard_map/ppermute | solution.py:581
  10.9 6.3 %collective-permute-start.3 = (bf16[9,64,128]{2,1,0:T(8,128)(2,1)S(1)}, bf16[9,64,128]{2,1,0:T(8,128)(2,1)S(1)}, u32[]{:S(2)}, u32[]{:S(2)}) collective-permute-start(bf16[9,64,128]{2,1,0:T(8,128)(2,1)S(1)} %collective-permute-done.refs_5_), channel_id=1, source_target_pairs={{0,2},{1,3},{2,10},{3,11},{4,6},{5,7},{6,14},{7,15},{8,0},{9,1},{1... | collective-permute-start | bytes 442376 | tf_op jit(solution)/shard_map/ppermute | solution.py:579
  12.3 4.9 %collective-permute-start.6 = (bf16[9,64,128]{2,1,0:T(8,128)(2,1)S(1)}, bf16[9,64,128]{2,1,0:T(8,128)(2,1)S(1)}, u32[]{:S(2)}, u32[]{:S(2)}) collective-permute-start(bf16[9,64,128]{2,1,0:T(8,128)(2,1)S(1)} %collective-permute-done.1.refs_4_), channel_id=1, source_target_pairs={{0,4},{1,5},{2,6},{3,7},{4,0},{5,1},{6,2},{7,3},{8,12},{9,13},{10,... | collective-permute-start | bytes 442376 | tf_op jit(solution)/shard_map/ppermute | solution.py:581
  12.4 6.1 %collective-permute-start.4 = (bf16[9,64,128]{2,1,0:T(8,128)(2,1)S(1)}, bf16[9,64,128]{2,1,0:T(8,128)(2,1)S(1)}, u32[]{:S(2)}, u32[]{:S(2)}) collective-permute-start(bf16[9,64,128]{2,1,0:T(8,128)(2,1)S(1)} %collective-permute-done.1.refs_4_), channel_id=1, source_target_pairs={{0,8},{1,9},{2,0},{3,1},{4,12},{5,13},{6,4},{7,5},{8,16},{9,17},{1... | collective-permute-start | bytes 442376 | tf_op jit(solution)/shard_map/ppermute | solution.py:578
  13.2 7.6 %copy-start = (bf16[4,8,4096]{2,1,0:T(8,128)(2,1)S(1)}, bf16[4,8,4096]{2,1,0:T(8,128)(2,1)}, u32[]{:S(2)}) copy-start(bf16[4,8,4096]{2,1,0:T(8,128)(2,1)} %param.8) | copy-start | bytes 786436
  18.5 6.8 %collective-permute-start.10 = (bf16[9,64,128]{2,1,0:T(8,128)(2,1)S(1)}, bf16[9,64,128]{2,1,0:T(8,128)(2,1)S(1)}, u32[]{:S(2)}, u32[]{:S(2)}) collective-permute-start(bf16[9,64,128]{2,1,0:T(8,128)(2,1)S(1)} %collective-permute-done.3.refs_9_), channel_id=1, source_target_pairs={{0,4},{1,5},{2,6},{3,7},{4,0},{5,1},{6,2},{7,3},{8,12},{9,13},{10,... | collective-permute-start | bytes 442376 | tf_op jit(solution)/shard_map/ppermute | solution.py:581
  18.5 6.8 %collective-permute-start.8 = (bf16[9,64,128]{2,1,0:T(8,128)(2,1)S(1)}, bf16[9,64,128]{2,1,0:T(8,128)(2,1)S(1)}, u32[]{:S(2)}, u32[]{:S(2)}) collective-permute-start(bf16[9,64,128]{2,1,0:T(8,128)(2,1)S(1)} %collective-permute-done.3.refs_9_), channel_id=1, source_target_pairs={{0,2},{1,3},{2,10},{3,11},{4,6},{5,7},{6,14},{7,15},{8,0},{9,1},{1... | collective-permute-start | bytes 442376 | tf_op jit(solution)/shard_map/ppermute | solution.py:579
  20.1 5.3 %collective-permute-start.11 = (bf16[9,64,128]{2,1,0:T(8,128)(2,1)S(1)}, bf16[9,64,128]{2,1,0:T(8,128)(2,1)S(1)}, u32[]{:S(2)}, u32[]{:S(2)}) collective-permute-start(bf16[9,64,128]{2,1,0:T(8,128)(2,1)S(1)} %collective-permute-done.4.refs_8_), channel_id=1, source_target_pairs={{0,4},{1,5},{2,6},{3,7},{4,0},{5,1},{6,2},{7,3},{8,12},{9,13},{10,... | collective-permute-start | bytes 442376 | tf_op jit(solution)/shard_map/ppermute | solution.py:581
  20.4 6.0 %collective-permute-start.9 = (bf16[9,64,128]{2,1,0:T(8,128)(2,1)S(1)}, bf16[9,64,128]{2,1,0:T(8,128)(2,1)S(1)}, u32[]{:S(2)}, u32[]{:S(2)}) collective-permute-start(bf16[9,64,128]{2,1,0:T(8,128)(2,1)S(1)} %collective-permute-done.4.refs_8_), channel_id=1, source_target_pairs={{0,8},{1,9},{2,0},{3,1},{4,12},{5,13},{6,4},{7,5},{8,16},{9,17},{1... | collective-permute-start | bytes 442376 | tf_op jit(solution)/shard_map/ppermute | solution.py:578
  26.4 3.7 %collective-permute-start.15 = (bf16[9,64,128]{2,1,0:T(8,128)(2,1)S(1)}, bf16[9,64,128]{2,1,0:T(8,128)(2,1)S(1)}, u32[]{:S(2)}, u32[]{:S(2)}) collective-permute-start(bf16[9,64,128]{2,1,0:T(8,128)(2,1)S(1)} %collective-permute-done.9.refs_12_), channel_id=1, source_target_pairs={{0,4},{1,5},{2,6},{3,7},{4,0},{5,1},{6,2},{7,3},{8,12},{9,13},{10,... | collective-permute-start | bytes 442376 | tf_op jit(solution)/shard_map/ppermute | solution.py:581
  26.4 6.3 %collective-permute-start.13 = (bf16[9,64,128]{2,1,0:T(8,128)(2,1)S(1)}, bf16[9,64,128]{2,1,0:T(8,128)(2,1)S(1)}, u32[]{:S(2)}, u32[]{:S(2)}) collective-permute-start(bf16[9,64,128]{2,1,0:T(8,128)(2,1)S(1)} %collective-permute-done.9.refs_12_), channel_id=1, source_target_pairs={{0,8},{1,9},{2,0},{3,1},{4,12},{5,13},{6,4},{7,5},{8,16},{9,17},{1... | collective-permute-start | bytes 442376 | tf_op jit(solution)/shard_map/ppermute | solution.py:578
  26.8 5.8 %collective-permute-start.14 = (bf16[9,64,128]{2,1,0:T(8,128)(2,1)S(1)}, bf16[9,64,128]{2,1,0:T(8,128)(2,1)S(1)}, u32[]{:S(2)}, u32[]{:S(2)}) collective-permute-start(bf16[9,64,128]{2,1,0:T(8,128)(2,1)S(1)} %collective-permute-done.8.refs_13_), channel_id=1, source_target_pairs={{0,4},{1,5},{2,6},{3,7},{4,0},{5,1},{6,2},{7,3},{8,12},{9,13},{10,... | collective-permute-start | bytes 442376 | tf_op jit(solution)/shard_map/ppermute | solution.py:581
  27.1 5.8 %collective-permute-start.12 = (bf16[9,64,128]{2,1,0:T(8,128)(2,1)S(1)}, bf16[9,64,128]{2,1,0:T(8,128)(2,1)S(1)}, u32[]{:S(2)}, u32[]{:S(2)}) collective-permute-start(bf16[9,64,128]{2,1,0:T(8,128)(2,1)S(1)} %collective-permute-done.8.refs_13_), channel_id=1, source_target_pairs={{0,6},{1,7},{2,14},{3,15},{4,2},{5,3},{6,10},{7,11},{8,4},{9,5},{1... | collective-permute-start | bytes 442376 | tf_op jit(solution)/shard_map/ppermute | solution.py:579

commit v5 on v4

--- a/solution.py
+++ b/solution.py
@@ -113,13 +113,15 @@
     ]
 
 
-def copy_pieces(src, dst, sems):
-    rows = dst.shape[0] // sems.shape[0]
+def quarter_copies(quarter, src, dst, sems):
+    k, half = divmod(quarter, 2)
+    rows = dst.shape[1] // (2 * sems.shape[0])
+    spans = [
+        pl.ds((half * sems.shape[0] + i) * rows, rows) for i in range(sems.shape[0])
+    ]
     return [
-        pltpu.make_async_copy(
-            src.at[pl.ds(i * rows, rows)], dst.at[pl.ds(i * rows, rows)], sems.at[i]
-        )
-        for i in range(sems.shape[0])
+        pltpu.make_async_copy(src.at[k, span], dst.at[k, span], sems.at[i])
+        for i, span in enumerate(spans)
     ]
 
 
@@ -172,46 +174,47 @@
     )(pinned(down), pinned(up), pinned(lengths), pinned(queries))
 
 
-def attend_cache(pairs, ready, sizes, scale, has_w, *refs):
+def attend_cache(pairs, ready, sizes, scale, quarter, n_packed, *refs):
     lengths, order, q_ref, k_hbm, v_hbm, w_hbm = refs[:6]
     sems, w_sems = refs[-2:]
-    k_buf, v_buf, *outs = refs[-6 - has_w : -2]
+    n_out = 6 if n_packed else 5
+    k_buf, v_buf, w_buf, *outs = refs[-2 - n_out : -2]
     done = pairs[0]
     o_ref, lse_ref = outs[:2]
     steps, _, heads, size = q_ref.shape
     kv = k_hbm.shape[1] // sizes[-1]
     lanes = steps * heads
 
-    def copies(pair, slots):
+    def copies(which, pair, slots):
         span = pl.ds(0, slots * kv)
+        hbm, buf = ((k_hbm, k_buf), (v_hbm, v_buf))[which]
         return [
-            [
-                pltpu.make_async_copy(
-                    hbm.at[order[2 * pair + i], span],
-                    buf.at[2 * pair + i, span],
-                    sems.at[pair, i, which],
-                )
-                for which, (hbm, buf) in enumerate(((k_hbm, k_buf), (v_hbm, v_buf)))
-            ]
+            pltpu.make_async_copy(
+                hbm.at[order[2 * pair + i], span],
+                buf.at[2 * pair + i, span],
+                sems.at[pair, i, which],
+            )
             for i in range(2)
         ]
 
     def start(pair, slots):
-        for made in copies(pair, slots):
-            for copy in made:
-                copy.start()
-
-    def finish(pair, slots):
-        for made in copies(pair, slots):
-            for copy in made:
+        for copy in copies(0, pair, slots) + copies(1, pair, slots):
+            copy.start()
+
+    def finish(which, pair, slots):
+        for i in which:
+            for copy in copies(i, pair, slots):
                 copy.wait()
 
     for pair in range(*ready):
         by_length(lengths[order[2 * pair]], sizes, functools.partial(start, pair))
-    if has_w:
-        w_copies = copy_pieces(w_hbm.at[0], outs[2], w_sems)
-        for copy in w_copies:
-            copy.start()
+    w_copies = quarter_copies(quarter, w_hbm, w_buf, w_sems)
+    for copy in w_copies:
+        copy.start()
+    if n_packed:
+        packed = refs[-2 - n_out - n_packed : -2 - n_out]
+        for i, ref in enumerate(packed):
+            outs[2][i] = ref[...]
 
     row_head = over(within(lax.broadcasted_iota(jnp.int32, (lanes, size), 0), heads), heads // kv)
     slot_head = within(lax.broadcasted_iota(jnp.int32, (lanes, size), 1), kv)
@@ -219,13 +222,15 @@
 
     def attend(pair):
         def compute(slots):
-            @pl.when(pair >= ready[0])
-            def _():
-                finish(pair, slots)
+            def wait(which):
+                @pl.when(pair >= ready[0])
+                def _():
+                    finish((which,), pair, slots)
 
             n = slots * kv
             bias = jnp.concatenate([head_bias[:, : min(n, size)]] * max(n // size, 1), axis=1)
             column = lax.broadcasted_iota(jnp.int32, (1, n), 1)
+            wait(0)
             scores = []
             for i in range(2):
                 row = order[2 * pair + i]
@@ -241,6 +246,7 @@
             highest = [jnp.max(s, axis=1, keepdims=True) * scale for s in scores]
             weights = [jnp.exp2(s * scale - h) for s, h in zip(scores, highest)]
             totals = [jnp.sum(p, axis=1, keepdims=True) for p in weights]
+            wait(1)
             for i in range(2):
                 o = jnp.dot(
                     weights[i].astype(jnp.bfloat16),
@@ -259,77 +265,85 @@
     else:
         pl.loop(*pairs)(attend)
     for pair in range(max(pairs[1], ready[0]), ready[1]):
-        by_length(lengths[order[2 * pair]], sizes, functools.partial(finish, pair))
-    if has_w:
-        for copy in w_copies:
-            copy.wait()
+        by_length(lengths[order[2 * pair]], sizes, functools.partial(finish, (0, 1), pair))
+    for copy in w_copies:
+        copy.wait()
 
 
 def like(x):
     return pltpu.VMEM(x.shape, x.dtype)
 
 
-def cache_attention(pairs, ready, lengths, order, queries, keys, values, weights, buffers, has_w, sizes, after):
+def cache_attention(pairs, ready, rows_args, caches, weights, quarter, buffers, packed, sizes, after):
+    lengths, order, queries = rows_args
+    keys, values = caches
     rows, steps, _, heads, size = (keys.shape[0], *queries.shape)
     slots = sizes[-1]
     scale = LOG2E / math.sqrt(size)
     count = 2 * (pairs[1] - pairs[0])
     piece = pltpu.VMEM((count, steps * heads, size), jnp.float32)
-    outs = [piece, piece] + ([pltpu.VMEM(weights.shape[1:], weights.dtype)] if has_w else [])
     operands = [pinned(x, pltpu.SMEM) for x in (lengths, order)]
     operands += [pinned(queries, pltpu.VMEM)]
     operands += [pinned(x) for x in (keys, values, weights)]
     aliases = {len(operands) + i: i for i in range(len(buffers))}
-    operands += [pinned(b, pltpu.VMEM) for b in buffers]
-    specs = [SMEM, SMEM, VMEM, HBM, HBM, HBM] + [VMEM] * len(buffers)
-    out_shape = [pltpu.VMEM(keys.shape, keys.dtype)] * 2
-    out_specs = [VMEM] * 2
-    out_shape += outs
-    out_specs += [VMEM] * len(outs)
+    specs = [SMEM, SMEM, VMEM, HBM, HBM, HBM] + [VMEM] * len(buffers) + [ANY] * len(after)
+    specs += [VMEM] * len(packed)
+    operands += [pinned(b, pltpu.VMEM) for b in buffers] + after + packed
+    out_shape = [pltpu.VMEM(x.shape, x.dtype) for x in (keys, values, weights)] + [piece] * 2
+    if packed:
+        out_shape.append(pltpu.VMEM((len(packed),) + packed[0].shape, packed[0].dtype))
     return pl.pallas_call(
-        functools.partial(attend_cache, pairs, ready, sizes, scale, int(has_w)),
+        functools.partial(attend_cache, pairs, ready, sizes, scale, quarter, len(packed)),
         out_shape=out_shape,
-        in_specs=specs + [ANY] * len(after),
-        out_specs=out_specs,
+        in_specs=specs,
+        out_specs=[VMEM] * len(out_shape),
         input_output_aliases=aliases,
         scratch_shapes=[
             pltpu.SemaphoreType.DMA((rows // 2, 2, 2)),
-            pltpu.SemaphoreType.DMA((8,)),
+            pltpu.SemaphoreType.DMA((4,)),
         ],
         compiler_params=pltpu.CompilerParams(vmem_limit_bytes=8 * MIB),
         cost_estimate=pl.CostEstimate(
             flops=4 * steps * heads * count * keys.shape[1] * size,
-            bytes_accessed=4 * count * keys.shape[1] * size + 2 * has_w * weights[0].size,
+            bytes_accessed=4 * count * keys.shape[1] * size + weights[0].size,
             transcendentals=steps * heads * count * keys.shape[1],
         ),
         name="cache_attention",
-    )(*operands, *after)
-
-
-def project_old(part, lay, n_hidden, *refs):
+    )(*operands)
+
+
+def project_old(part, lay, n_hidden, n_packed, *refs):
     refs = list(refs)
     tp = lax.axis_index("tp")
+    w_hbm = refs[1]
+    sems = refs.pop()
     if part == 0:
-        hidden = refs[1 : 1 + n_hidden]
-        w_hbm = refs[1 + n_hidden]
-        w_ref, next_ref, h_ref, out_ref, sems = refs[-5:]
-        copies = copy_pieces(w_hbm.at[1], next_ref, sems)
-        for copy in copies:
-            copy.start()
+        hidden = refs[2 : 2 + n_hidden]
+        packed = refs[2 + n_hidden : 2 + n_hidden + n_packed]
+        w_buf, out_ref, h_ref, pack_ref = refs[-4:]
+    else:
+        h_ref = refs[2]
+        w_buf, out_ref = refs[-2:]
+    copies = quarter_copies(2 + part, w_hbm, w_buf, sems)
+    for copy in copies:
+        copy.start()
+    if part == 0:
         for i, h in enumerate(hidden):
             h_ref[lax.rem(tp + i, lay.tp)] = h[...]
-    else:
-        h_ref = refs[2]
-        w_ref, out_ref = refs[-2:]
+        for i, ref in enumerate(packed):
+            pack_ref[i] = ref[...]
     features = h_ref.shape[2]
     chunk = min(features, 1024)
     total = jnp.zeros(out_ref.shape, jnp.float32)
     for t in range(lay.tp):
+        if part == 1 and 2 * t == lay.tp:
+            for copy in copies:
+                copy.wait()
         for low in range(0, features, chunk):
             start = t * features + low
             total += jnp.dot(
                 h_ref[t, :, low : low + chunk],
-                w_ref[start : start + chunk, :],
+                w_buf[part, start : start + chunk, :],
                 preferred_element_type=jnp.float32,
             )
     out_ref[...] = total
@@ -338,38 +352,30 @@
             copy.wait()
 
 
-def project(part, lay, w, hidden, weights, after):
+def project(part, lay, w_buf, weights, hidden, packed, after):
     tokens, features = hidden[0].shape[-2:]
-    out = pltpu.VMEM((tokens, w.shape[1]), jnp.float32)
-    operands = [pinned(w, pltpu.VMEM)] + hidden
-    specs = [VMEM] * len(operands)
+    operands = [pinned(w_buf, pltpu.VMEM), pinned(weights)]
+    specs = [VMEM, HBM] + [VMEM] * (len(hidden) + len(packed)) + [ANY] * len(after)
+    out_shape = [like(w_buf), pltpu.VMEM((tokens, weights.shape[2]), jnp.float32)]
     if part == 0:
-        states = pltpu.VMEM((lay.tp, tokens, features), jnp.bfloat16)
-        operands.append(pinned(weights))
-        specs.append(HBM)
-        out_shape = [like(w), like(w), states, out]
-        aliases = {0: 0}
-        scratch = [pltpu.SemaphoreType.DMA((8,))]
+        operands += hidden + packed + after
+        out_shape.append(pltpu.VMEM((lay.tp, tokens, features), jnp.bfloat16))
+        out_shape.append(pltpu.VMEM((len(packed),) + packed[0].shape, packed[0].dtype))
     else:
-        operands = [pinned(weights, pltpu.VMEM)] + operands
-        specs.append(VMEM)
-        operands[2] = pinned(operands[2], pltpu.VMEM)
-        out_shape = [like(w), like(w), out]
-        aliases = {0: 0, 1: 1}
-        scratch = []
+        operands += [pinned(h, pltpu.VMEM) for h in hidden] + after
     return pl.pallas_call(
-        functools.partial(project_old, part, lay, len(hidden)),
+        functools.partial(project_old, part, lay, len(hidden), len(packed)),
         out_shape=out_shape,
-        in_specs=specs + [ANY] * len(after),
+        in_specs=specs,
         out_specs=[VMEM] * len(out_shape),
-        input_output_aliases=aliases,
-        scratch_shapes=scratch,
+        input_output_aliases={0: 0},
+        scratch_shapes=[pltpu.SemaphoreType.DMA((4,))],
         compiler_params=pltpu.CompilerParams(vmem_limit_bytes=8 * MIB),
         cost_estimate=pl.CostEstimate(
-            flops=2 * tokens * w.size, bytes_accessed=2 * w.size, transcendentals=0
+            flops=2 * tokens * weights[0].size, bytes_accessed=weights.size, transcendentals=0
         ),
         name="project",
-    )(*operands, *after)
+    )(*operands)
 
 
 def merge_all(lay, plan, n_caches, scale, *refs):
@@ -380,15 +386,16 @@
         del refs[:n]
         return out
 
-    weights, downs = take(2), take(len(plan))
+    (weights,) = take(1)
+    downs = take(len(plan))
     h_buf, *olds = take(3)
     order, q_ref = take(2)
     caches = [take(2) for _ in range(n_caches)]
-    m_hbm, out_ref, m_buf, u_parts, u_buf, low, sems = refs
+    m_hbm, out_hbm, m_buf, u_parts, u_buf, out_buf, sems, out_sems = refs
 
     pairs, depth, width = m_buf.shape[1:]
     cut = min(width, 256)
-    lanes = downs[0].shape[2]
+    lanes = downs[0].shape[-1]
     tiles = depth // lanes
     fsdp, grp, tp = (lax.axis_index(a) for a in AXES)
     z, core = fsdp // 2, lax.rem(fsdp, 2)
@@ -396,12 +403,18 @@
     per_lane = lay.fsdp * lay.grp // lay.tp
 
     shards = []
-    for (step, flip), down in zip(plan, downs):
-        spot = lax.rem(place + (lay.ring + step), lay.ring)
-        g = spot // lay.depth
-        along = lax.rem(spot, lay.depth)
-        zz = jnp.where(lax.rem(g, 2) == 0, along, lay.depth - 1 - along)
-        shards.append((down, (zz * 2 + (1 - core if flip else core)) * lay.grp + g))
+    for (steps, flip), down in zip(plan, downs):
+        for i, step in enumerate(steps):
+            spot = lax.rem(place + (lay.ring + step), lay.ring)
+            g = spot // lay.depth
+            along = lax.rem(spot, lay.depth)
+            zz = jnp.where(lax.rem(g, 2) == 0, along, lay.depth - 1 - along)
+            shards.append(
+                (
+                    down.at[i] if len(steps) > 1 else down,
+                    (zz * 2 + (1 - core if flip else core)) * lay.grp + g,
+                )
+            )
 
     columns = width // per_lane
     for down, index in shards:
@@ -414,14 +427,40 @@
         u_buf[k] = ADAPTER_SCALING * jnp.concatenate(
             [u_parts[i, :, k * columns : (k + 1) * columns] for i in range(per_lane)], axis=1
         )
-    low[...] = jnp.zeros_like(low)
+
+    new = []
+    for k in range(pairs):
+        low = jnp.zeros((h_buf.shape[1], u_buf.shape[1]), jnp.float32)
+        for down, index in shards:
+            column = pl.multiple_of(lax.rem(index, per_lane) * depth, depth)
+            low += lax.dot_general(
+                h_buf[index // per_lane, :, pl.ds(column, depth)],
+                jnp.concatenate([down[k * tiles + i] for i in range(tiles)], axis=1),
+                (((1,), (1,)), ((), ())),
+                preferred_element_type=jnp.float32,
+            )
+        high = low.astype(jnp.bfloat16)
+        rest = (low - high.astype(jnp.float32)).astype(jnp.bfloat16)
+        new.append(
+            (
+                olds[k][...]
+                + jnp.dot(high, u_buf[k], preferred_element_type=jnp.float32)
+                + jnp.dot(rest, u_buf[k], preferred_element_type=jnp.float32)
+            ).astype(jnp.bfloat16)
+        )
+    finish_row = new_token_attention(q_ref, order, caches, new, out_buf, scale)
+    spots = q_ref.shape[1]
+
+    def out_copy(spot):
+        return pltpu.make_async_copy(
+            out_buf.at[:, spot], out_hbm.at[:, order[spot]], out_sems.at[spot]
+        )
 
     chunk = min(depth, 256)
     copies = []
+    rows_done = 0
     for j, (down, index) in enumerate(shards):
         start = pl.multiple_of(index * depth, depth)
-        column = pl.multiple_of(lax.rem(index, per_lane) * depth, depth)
-        source = index // per_lane
         for k in range(pairs):
             for begin in range(0, depth, chunk):
                 rows = slice(begin, begin + chunk)
@@ -435,37 +474,22 @@
                         (((0,), (0,)), ((), ())),
                         preferred_element_type=jnp.float32,
                     )
-                    w = weights[k][pl.ds(start + begin, chunk), cols]
+                    w = weights[k, pl.ds(start + begin, chunk), cols]
                     m_buf[j, k, rows, cols] = (w.astype(jnp.float32) + added).astype(jnp.bfloat16)
-                low[k] += lax.dot_general(
-                    h_buf[source, :, pl.ds(column + begin, chunk)],
-                    d,
-                    (((1,), (1,)), ((), ())),
-                    preferred_element_type=jnp.float32,
-                )
             copy = pltpu.make_async_copy(
                 m_buf.at[j, k], m_hbm.at[k, pl.ds(start, depth), :], sems.at[j, k]
             )
             copy.start()
             copies.append(copy)
-
-    new = []
-    for k in range(pairs):
-        high = low[k].astype(jnp.bfloat16)
-        rest = (low[k] - high.astype(jnp.float32)).astype(jnp.bfloat16)
-        new.append(
-            (
-                olds[k][...]
-                + jnp.dot(high, u_buf[k], preferred_element_type=jnp.float32)
-                + jnp.dot(rest, u_buf[k], preferred_element_type=jnp.float32)
-            ).astype(jnp.bfloat16)
-        )
-    add_new_tokens(q_ref, order, caches, new, out_ref, scale)
-    for copy in copies:
+        while rows_done < min(spots, (j + 1) * spots // (len(shards) - 2)):
+            finish_row(rows_done)
+            out_copy(rows_done).start()
+            rows_done += 1
+    for copy in copies + [out_copy(spot) for spot in range(spots)]:
         copy.wait()
 
 
-def add_new_tokens(q_ref, order, caches, new, out_ref, scale):
+def new_token_attention(q_ref, order, caches, new, out_buf, scale):
     steps, rows, heads, size = q_ref.shape
     kv = new[0].shape[1] // size
     new = [
@@ -479,7 +503,9 @@
     earlier = within(over(right, rows), steps) <= over(left, heads)
     right_row = jnp.where(same_head & earlier, within(right, rows), -1)
     spots = [(o, lse, i) for o, lse in caches for i in range(o.shape[0])]
-    for spot, (o_ref, lse_ref, i) in enumerate(spots):
+
+    def finish_row(spot):
+        o_ref, lse_ref, i = spots[spot]
         row = order[spot]
         q = q_ref[:, row].reshape(lanes, size)
         s = lax.dot_general(
@@ -494,17 +520,18 @@
         o = old * o_ref[i] + jnp.dot(
             p.astype(jnp.bfloat16), new[1], preferred_element_type=jnp.float32
         )
-        out_ref[:, row] = (o / divisor).reshape(steps, heads, size).astype(out_ref.dtype)
+        out_buf[:, spot] = (o / divisor).reshape(steps, heads, size).astype(out_buf.dtype)
+
+    return finish_row
 
 
 def merge(lay, shape, entries, weights, states, olds, order, queries, caches):
     pairs, total, width = shape
-    rank = entries[0][2].shape[1]
-    tokens = states.shape[1]
+    rank = entries[0][2].shape[-2]
     depth = total // (lay.fsdp * lay.grp)
     per_lane = lay.fsdp * lay.grp // lay.tp
-    n = len(entries)
-    operands = [pinned(w, pltpu.VMEM) for w in weights] + [e[2] for e in entries]
+    n = sum(len(e[0]) for e in entries)
+    operands = [pinned(weights, pltpu.VMEM)] + [e[2] for e in entries]
     operands += [states, *olds, pinned(order, pltpu.SMEM), pinned(queries, pltpu.VMEM), *caches]
     specs = [VMEM] * len(operands)
     specs[-2 - len(caches)] = SMEM
@@ -516,15 +543,16 @@
             len(caches) // 2,
             LOG2E / math.sqrt(queries.shape[3]),
         ),
-        out_shape=(pltpu.HBM(shape, jnp.bfloat16), jax.ShapeDtypeStruct(queries.shape, jnp.bfloat16)),
+        out_shape=(pltpu.HBM(shape, jnp.bfloat16), pltpu.HBM(queries.shape, jnp.bfloat16)),
         in_specs=specs,
-        out_specs=(HBM, VMEM),
+        out_specs=(HBM, HBM),
         scratch_shapes=[
             pltpu.VMEM((n, pairs, depth, width), jnp.bfloat16),
             pltpu.VMEM((per_lane, rank, pairs * width // per_lane), jnp.bfloat16),
             pltpu.VMEM((pairs, rank, width), jnp.bfloat16),
-            pltpu.VMEM((pairs, tokens, rank), jnp.float32),
+            pltpu.VMEM(queries.shape, jnp.bfloat16),
             pltpu.SemaphoreType.DMA((n, pairs)),
+            pltpu.SemaphoreType.DMA((queries.shape[1],)),
         ],
         compiler_params=pltpu.CompilerParams(vmem_limit_bytes=24 * MIB),
         cost_estimate=pl.CostEstimate(
@@ -557,71 +585,66 @@
     keys = cache_keys.reshape(rows, slots * kv, size)
     values = cache_values.reshape(rows, slots * kv, size)
     swap, ring = lay.core_swap(), {d: lay.ring_step(d) for d in (1, -1)}
-    shard, lengths, order, q = begin(own, factor_up, cache_lengths, queries)
-    entries = [(0, False, shard)]
-
+    shard, *rows_args = begin(own, factor_up, cache_lengths, queries)
+    lengths, order, q = rows_args
     projections = projection_weight_matrices
-    came = {d: send(shard, perm=ring[d]) for d in ring}
-    partner = send(shard, perm=swap)
+    entries = [((0,), False, shard)]
+    caches, olds = [], []
+    last_step = lay.ring // 2
+
+    def ring_sends(came, step):
+        back = lay.ring_step(-1, 1) if step == last_step else ring[-1]
+        return {-1: send(came[-1], perm=back), 1: send(came[1], perm=ring[1])}
+
     hidden = [tokens] + [send(tokens, perm=lay.feature_step(i)) for i in range(1, lay.tp)]
+    came = ring_sends({1: shard, -1: shard}, 1)
     *buffers, o, lse = cache_attention(
-        (0, 1), (0, 2), lengths, order, q, keys, values, projections, [], False, sizes, [shard]
+        (0, 1), (0, 2), rows_args, (keys, values), projections, 0, [], [], sizes, [shard]
     )
-    caches = [o, lse]
-    (came, partner), token = after_all((came, partner), o)
-    entries.append((0, True, partner))
-
-    last_step = lay.ring // 2
-    for step in range(1, last_step):
-        last = step + 1 == last_step
-        sent = {
-            1: send(came[1], perm=ring[1]),
-            -1: send(came[-1], perm=lay.ring_step(-1, 1) if last else ring[-1]),
-        }
-        swapped = {d: send(came[d], perm=swap) for d in ring}
-        if step == 1:
-            *_, o, lse, w_keys = cache_attention(
-                (1, rows // 4 * 2),
-                (2, rows // 4 * 2),
-                lengths,
-                order,
-                q,
-                keys,
-                values,
-                projections,
-                buffers,
-                True,
-                sizes,
-                [token],
+    caches += [o, lse]
+    came, token = after_all(came, o)
+
+    packed = [shard, came[1], came[-1]]
+    entries += [((-d,), False, came[d]) for d in ring]
+    came = ring_sends(came, 2)
+    *buffers, o, lse, packed = cache_attention(
+        (1, rows // 4 * 2),
+        (2, rows // 4 * 2),
+        rows_args,
+        (keys, values),
+        projections,
+        1,
+        buffers,
+        packed,
+        sizes,
+        [token],
+    )
+    caches += [o, lse]
+    (came, hidden, packed), token = after_all((came, hidden, packed), o)
+
+    w_buf, packed = buffers[2], [packed]
+    for step in range(3, last_step + 1):
+        entries += [((-d * (step - 1),), False, came[d]) for d in ring]
+        arrived, came = came, ring_sends(came, step)
+        swapped = [send(x, perm=swap) for x in packed]
+        if step == 3:
+            w_buf, old, states, packed = project(
+                0, lay, w_buf, projections, hidden, [arrived[1], arrived[-1]], [token]
             )
-            caches += [o, lse]
-            token = o
-        elif step == 2:
-            w_keys, w_values, states, old_keys = project(0, lay, w_keys, hidden, projections, [token])
-            token = old_keys
-        elif step == 3:
-            w_keys, w_values, old_values = project(1, lay, w_values, [states], w_keys, [token])
-            token = old_values
-        entries += [(-d * step, False, came[d]) for d in ring]
-        if step == 1:
-            (came, swapped, hidden), token = after_all((sent, swapped, hidden), token)
+            places, packed = [(0, -1, 1)], [packed]
+        elif step == 4:
+            w_buf, old = project(1, lay, w_buf, projections, [states], [], [token])
+            places, packed = [(-2, 2), (-3,), (3,)], []
         else:
-            (came, swapped), token = after_all((sent, swapped), token)
-        entries += [(-d * step, True, swapped[d]) for d in ring]
-    entries += [(-last_step, False, came[1]), (last_step, True, came[-1])]
-    return tuple(
-        merge(
-            lay,
-            shape,
-            entries,
-            [w_keys, w_values],
-            states,
-            [old_keys, old_values],
-            order,
-            q,
-            caches,
-        )
-    )
+            places, packed = [(1 - step,), (step - 1,)], []
+        if step < 5:
+            olds.append(old)
+            token = old
+        (came, swapped, packed), token = after_all((came, swapped, packed), token)
+        entries += [(p, True, x) for p, x in zip(places, swapped)]
+        packed += [came[1], came[-1]]
+    entries += [((-last_step,), False, came[1]), ((last_step,), True, came[-1])]
+    return tuple(merge(lay, shape, entries, w_buf, states, olds, order, q, caches))
 
 
 def solution(mesh):

time: 41.4 us -> 42.2 us (1.019)
    pallas_call x2, Pallas kernels: 6.07 us -> 5.23 us  [project(): pl.pallas_call(functools.partial(project_old, part, lay, len(hidden), len...]
    pallas_call x1, Pallas kernels: 8.29 us -> 9.02 us  [merge(): pl.pallas_call(functools.partial(merge_all, lay, [e[:2] for e in entries]...]
    pallas_call x2, Pallas kernels: 7.66 us -> 8.17 us  [cache_attention(): pl.pallas_call(functools.partial(attend_cache, pairs, ready, sizes, scale...]
    ppermute x15 -> x12, starting transfers between devices: 9.84 us -> 9.96 us  [the longest x8 9.43 us: ring_sends(): return {-1: send(came[-1], perm=back), 1: send(came[1], perm=ring[1])}]
    ppermute x15 -> x12, waiting for transfers between devices: 5.4 us -> 5.43 us  [the longest x8 5.42 us: ring_sends(): return {-1: send(came[-1], perm=back), 1: send(came[1], perm=ring[1])}]
  transfers between devices with their start and end apart: 16 -> 13, of which waited for: 5 -> 5; matrix products, arithmetic and copies ran while one was open for 0% -> 0% of each run, Pallas kernels for 33% -> 32%
where the time goes in v5:
time: 42.2 us; the launch traced here: 41.8 us
  Pallas kernels  23.6 us (56%)
  starting transfers between devices  11.8 us (28%)
  waiting for transfers between devices  5.44 us (13%)
  between operations  0.9 us (2%)
    ppermute x8, starting transfers between devices, ring_sends(): return {-1: send(came[-1], perm=back), 1: send(came[1], perm=ring[1])}  9.43 us
    pallas_call x1, Pallas kernels, merge(): pl.pallas_call(functools.partial(merge_all, lay, [e[:2] for e in entries]...  9.02 us
    pallas_call x2, Pallas kernels, cache_attention(): pl.pallas_call(functools.partial(attend_cache, pairs, ready, sizes, scale...  8.17 us
    ppermute x8, waiting for transfers between devices, ring_sends(): return {-1: send(came[-1], perm=back), 1: send(came[1], perm=ring[1])}  5.42 us
    pallas_call x2, Pallas kernels, project(): pl.pallas_call(functools.partial(project_old, part, lay, len(hidden), len...  5.23 us
    ppermute x1, starting transfers between devices, shards(): send(tokens, perm=lay.feature_step(i))  1.88 us
    pallas_call x1, Pallas kernels, begin(): pl.pallas_call(begin_all, out_shape=(pltpu.VMEM((count * tiles + 1, rank,...  1.19 us
  transfers between devices with their start and end apart: 13, of which 5 were waited for; matrix products, arithmetic and copies ran while one was open for 0% of the time, Pallas kernels for 32%

profile of v5, /device:TPU:0, one launch (start us, length us, event | category | flops | bytes accessed | tf_op | source)
XLA Modules:
  0.0 41.8 jit_solution(13882584118341960756)
XLA Ops:
  0.6 1.2 %begin.1 = (bf16[9,64,128]{2,1,0:T(8,128)(2,1)S(1)}, s32[8]{0:T(128)S(4)}, s32[8]{0:T(128)S(4)}, bf16[4,8,32,128]{3,2,1,0:T(8,128)(2,1)S(1)}) custom-call(bf16[2,64,512]{2,1,0:T(8,128)(2,1)} %bitcast.10, bf16[2,64,64]{2,1,0:T(8,128)(2,1)} %up.1, s32[8]{0:T(128)} %len_hbm.1, bf16[4,8,32,128]{3,2,1,0:T(8,128)(2,1)} %q_hbm.1), custom_call_target="tpu_custom_call" | custom-call | tf_op jit(solution)/shard_map/begin/pallas_call | solution.py:157
  1.8 3.0 %collective-permute-start = (bf16[9,64,128]{2,1,0:T(8,128)(2,1)S(1)}, bf16[9,64,128]{2,1,0:T(8,128)(2,1)S(1)}, u32[]{:S(2)}, u32[]{:S(2)}) collective-permute-start(bf16[9,64,128]{2,1,0:T(8,128)(2,1)S(1)} %get-tuple-element.43.refs_6_.refs_10_.refs_1_), channel_id=1, source_target_pairs={{0,2},{1,3},{2,10},{3,11},{4,6},{5,7},{6,14},{7,15},{8,0},{9,1},{1... | collective-permute-start | bytes 442376 | tf_op jit(solution)/shard_map/ppermute | solution.py:597
  4.9 0.1 collective-permute-start.1
  5.0 1.9 %collective-permute-start.4 = (bf16[32,4096]{1,0:T(8,128)(2,1)}, bf16[32,4096]{1,0:T(8,128)(2,1)S(1)}, u32[]{:S(2)}, u32[]{:S(2)}) collective-permute-start(bf16[32,4096]{1,0:T(8,128)(2,1)} %bitcast.4), channel_id=1, source_target_pairs={{1,0},{0,1},{3,2},{2,3},{5,4},{4,5},{7,6},{6,7},{9,8},{8,9},{11,10... | collective-permute-start | bytes 786440 | tf_op jit(solution)/shard_map/ppermute | solution.py:599
  6.9 4.2 %cache_attention.2 = (bf16[8,3072,128]{2,1,0:T(8,128)(2,1)S(1)}, bf16[8,3072,128]{2,1,0:T(8,128)(2,1)S(1)}, bf16[2,8192,512]{2,1,0:T(8,128)(2,1)S(1)}, f32[2,128,128]{2,1,0:T(8,128)S(1)}, f32[2,128,128]{2,1,0:T(8,128)S(1)}) custom-call(s32[8]{0:T(128)S(4)} %get-tuple-element.40.refs_0_, s32[8]{0:T(128)S(4)} %get-tuple-element.41.refs_1_.refs_17_, ...), custom_call_target="tpu_custom_call" | custom-call | flops 402653184 | bytes 7340032 | tf_op jit(solution)/shard_map/cache_attention/pallas_call | solution.py:295
  11.1 0.0 collective-permute-done.refs_12_.refs_3_
  11.1 0.0 collective-permute-done.1.refs_11_.refs_2_
  11.1 1.0 %collective-permute-start.2 = (bf16[9,64,128]{2,1,0:T(8,128)(2,1)S(1)}, bf16[9,64,128]{2,1,0:T(8,128)(2,1)S(1)}, u32[]{:S(2)}, u32[]{:S(2)}) collective-permute-start(bf16[9,64,128]{2,1,0:T(8,128)(2,1)S(1)} %collective-permute-done.refs_12_.refs_3_), channel_id=1, source_target_pairs={{0,2},{1,3},{2,10},{3,11},{4,6},{5,7},{6,14},{7,15},{8,0},{9,1},{1... | collective-permute-start | bytes 442376 | tf_op jit(solution)/shard_map/ppermute | solution.py:597
  12.1 1.1 %collective-permute-start.3 = (bf16[9,64,128]{2,1,0:T(8,128)(2,1)S(1)}, bf16[9,64,128]{2,1,0:T(8,128)(2,1)S(1)}, u32[]{:S(2)}, u32[]{:S(2)}) collective-permute-start(bf16[9,64,128]{2,1,0:T(8,128)(2,1)S(1)} %collective-permute-done.1.refs_11_.refs_2_), channel_id=1, source_target_pairs={{0,8},{1,9},{2,0},{3,1},{4,12},{5,13},{6,4},{7,5},{8,16},{9,17},{1... | collective-permute-start | bytes 442376 | tf_op jit(solution)/shard_map/ppermute | solution.py:597
  13.2 0.0 copy-start
  13.2 3.9 %cache_attention.3 = (bf16[8,3072,128]{2,1,0:T(8,128)(2,1)S(1)}, bf16[8,3072,128]{2,1,0:T(8,128)(2,1)S(1)}, bf16[2,8192,512]{2,1,0:T(8,128)(2,1)S(1)}, f32[6,128...) custom-call(s32[8]{0:T(128)S(4)} %get-tuple-element.40.refs_0_, ...), custom_call_target="tpu_custom_call", output_to_operand_aliasing={{0}: (6, {}), {1}: (7, {}), {2}: (8, {})} | custom-call | flops 1207959552 | bytes 13631488 | tf_op jit(solution)/shard_map/cache_attention/pallas_call | solution.py:295
  17.1 0.0 collective-permute-done.4.refs_3_
  17.1 0.0 collective-permute-done.2.refs_5_
  17.2 0.1 collective-permute-done.3.refs_4_
  17.2 0.0 collective-permute-start.7
  17.2 1.3 %collective-permute-start.5 = (bf16[9,64,128]{2,1,0:T(8,128)(2,1)S(1)}, bf16[9,64,128]{2,1,0:T(8,128)(2,1)S(1)}, u32[]{:S(2)}, u32[]{:S(2)}) collective-permute-start(bf16[9,64,128]{2,1,0:T(8,128)(2,1)S(1)} %collective-permute-done.2.refs_5_), channel_id=1, source_target_pairs={{0,2},{1,3},{2,10},{3,11},{4,6},{5,7},{6,14},{7,15},{8,0},{9,1},{1... | collective-permute-start | bytes 442376 | tf_op jit(solution)/shard_map/ppermute | solution.py:597
  18.6 0.8 %collective-permute-start.6 = (bf16[9,64,128]{2,1,0:T(8,128)(2,1)S(1)}, bf16[9,64,128]{2,1,0:T(8,128)(2,1)S(1)}, u32[]{:S(2)}, u32[]{:S(2)}) collective-permute-start(bf16[9,64,128]{2,1,0:T(8,128)(2,1)S(1)} %collective-permute-done.3.refs_4_), channel_id=1, source_target_pairs={{0,8},{1,9},{2,0},{3,1},{4,12},{5,13},{6,4},{7,5},{8,16},{9,17},{1... | collective-permute-start | bytes 442376 | tf_op jit(solution)/shard_map/ppermute | solution.py:597
  19.3 0.0 copy-done
  19.3 2.2 %project.2 = (bf16[2,8192,512]{2,1,0:T(8,128)(2,1)S(1)}, f32[32,512]{1,0:T(8,128)S(1)}, bf16[2,32,4096]{2,1,0:T(8,128)(2,1)S(1)}, bf16[2,9,64,128]{3,2,1,0:T(8,128)(2,1)S(1)}) custom-call(bf16[2,8192,512]{2,1,0:T(8,128)(2,1)S(1)} %get-tuple-element.51.refs_0_, bf16[2,8192,512]{2,1,0:T(8,128)(2,1)} %refs_1_.3, ...), custom_call_target="tpu_custom_call", output_to_operand_aliasing={{0}: (0, {})} | custom-call | flops 268435456 | bytes 8388608 | tf_op jit(solution)/shard_map/project/pallas_call | solution.py:366
  21.5 2.0 %collective-permute-done.5.refs_8_ = bf16[9,64,128]{2,1,0:T(8,128)(2,1)S(1)} collective-permute-done((bf16[9,64,128]{2,1,0:T(8,128)(2,1)S(1)}, bf16[9,64,128]{2,1,0:T(8,128)(2,1)S(1)}, u32[]{:S(2)}, u32[]{:S(2)}) %collective-permute-start.5) | collective-permute-done | bytes 147488 | tf_op jit(solution)/shard_map/ppermute | solution.py:597
  23.5 1.1 %collective-permute-done.6.refs_7_ = bf16[9,64,128]{2,1,0:T(8,128)(2,1)S(1)} collective-permute-done((bf16[9,64,128]{2,1,0:T(8,128)(2,1)S(1)}, bf16[9,64,128]{2,1,0:T(8,128)(2,1)S(1)}, u32[]{:S(2)}, u32[]{:S(2)}) %collective-permute-start.6) | collective-permute-done | bytes 147488 | tf_op jit(solution)/shard_map/ppermute | solution.py:597
  24.6 0.0 collective-permute-done.7.refs_6_
  24.6 0.0 collective-permute-start.10
  24.6 0.5 %collective-permute-start.11 = (bf16[9,64,128]{2,1,0:T(8,128)(2,1)S(1)}, bf16[9,64,128]{2,1,0:T(8,128)(2,1)S(1)}, u32[]{:S(2)}, u32[]{:S(2)}) collective-permute-start(bf16[9,64,128]{2,1,0:T(8,128)(2,1)S(1)} %collective-permute-done.6.refs_7_), channel_id=1, source_target_pairs={{0,4},{1,5},{2,6},{3,7},{4,0},{5,1},{6,2},{7,3},{8,12},{9,13},{10,... | collective-permute-start | bytes 442376 | tf_op jit(solution)/shard_map/ppermute | solution.py:629
  25.1 0.0 collective-permute-start.12
  25.1 1.8 %collective-permute-start.8 = (bf16[9,64,128]{2,1,0:T(8,128)(2,1)S(1)}, bf16[9,64,128]{2,1,0:T(8,128)(2,1)S(1)}, u32[]{:S(2)}, u32[]{:S(2)}) collective-permute-start(bf16[9,64,128]{2,1,0:T(8,128)(2,1)S(1)} %collective-permute-done.5.refs_8_), channel_id=1, source_target_pairs={{0,6},{1,7},{2,14},{3,15},{4,2},{5,3},{6,10},{7,11},{8,4},{9,5},{1... | collective-permute-start | bytes 442376 | tf_op jit(solution)/shard_map/ppermute | solution.py:597
  26.8 0.4 collective-permute-start.9
  27.2 3.0 %project.3 = (bf16[2,8192,512]{2,1,0:T(8,128)(2,1)S(1)}, f32[32,512]{1,0:T(8,128)S(1)}) custom-call(bf16[2,8192,512]{2,1,0:T(8,128)(2,1)S(1)} %get-tuple-element.59.refs_0_, bf16[2,8192,512]{2,1,0:T(8,128)(2,1)} %refs_1_.3, bf16[2,32,4096]{2,1,0:T(8,128)(2,1)S(1)} %get-tuple-element.60.refs_2_.refs_14_, ...), custom_call_target="tpu_custom_call", output_to_operand_aliasing={{0}: (0, {})} | custom-call | flops 268435456 | bytes 8388608 | tf_op jit(solution)/shard_map/project/pallas_call | solution.py:366
  30.2 0.0 collective-permute-done.11.refs_10_
  30.3 0.0 collective-permute-done.12.refs_11_
  30.3 0.3 collective-permute-done.8.refs_13_
  30.6 2.0 %collective-permute-done.9.refs_12_ = bf16[9,64,128]{2,1,0:T(8,128)(2,1)S(1)} collective-permute-done((bf16[9,64,128]{2,1,0:T(8,128)(2,1)S(1)}, bf16[9,64,128]{2,1,0:T(8,128)(2,1)S(1)}, u32[]{:S(2)}, u32[]{:S(2)}) %collective-permute-start.9) | collective-permute-done | bytes 147488 | tf_op jit(solution)/shard_map/ppermute | solution.py:597
  32.6 0.0 collective-permute-done.10.refs_9_
  32.6 9.0 %merge.1 = (bf16[2,8192,512]{2,1,0:T(8,128)(2,1)}, bf16[4,8,32,128]{3,2,1,0:T(8,128)(2,1)}) custom-call(bf16[2,8192,512]{2,1,0:T(8,128)(2,1)S(1)} %get-tuple-element.65.refs_0_, bf16[9,64,128]{2,1,0:T(8,128)(2,1)S(1)} %get-tuple-element.43.refs_6_.refs_10_.refs_1_, bf16[9,64,128]{2,1,0:T(8,128)(2,1)S(1)} %collective-permute-done.1.refs_11_.refs_2_, ...), custom_call_target="tpu_custom_call" | custom-call | flops 1073741824 | bytes 16777216 | tf_op jit(solution)/shard_map/merge/pallas_call | solution.py:538
Async XLA Ops:
  1.8 9.3 %collective-permute-start = (bf16[9,64,128]{2,1,0:T(8,128)(2,1)S(1)}, bf16[9,64,128]{2,1,0:T(8,128)(2,1)S(1)}, u32[]{:S(2)}, u32[]{:S(2)}) collective-permute-start(bf16[9,64,128]{2,1,0:T(8,128)(2,1)S(1)} %get-tuple-element.43.refs_6_.refs_10_.refs_1_), channel_id=1, source_target_pairs={{0,2},{1,3},{2,10},{3,11},{4,6},{5,7},{6,14},{7,15},{8,0},{9,1},{1... | collective-permute-start | bytes 442376 | tf_op jit(solution)/shard_map/ppermute | solution.py:597
  4.9 6.2 %collective-permute-start.1 = (bf16[9,64,128]{2,1,0:T(8,128)(2,1)S(1)}, bf16[9,64,128]{2,1,0:T(8,128)(2,1)S(1)}, u32[]{:S(2)}, u32[]{:S(2)}) collective-permute-start(bf16[9,64,128]{2,1,0:T(8,128)(2,1)S(1)} %get-tuple-element.43.refs_6_.refs_10_.refs_1_), channel_id=1, source_target_pairs={{0,8},{1,9},{2,0},{3,1},{4,12},{5,13},{6,4},{7,5},{8,16},{9,17},{1... | collective-permute-start | bytes 442376 | tf_op jit(solution)/shard_map/ppermute | solution.py:597
  5.0 12.2 %collective-permute-start.4 = (bf16[32,4096]{1,0:T(8,128)(2,1)}, bf16[32,4096]{1,0:T(8,128)(2,1)S(1)}, u32[]{:S(2)}, u32[]{:S(2)}) collective-permute-start(bf16[32,4096]{1,0:T(8,128)(2,1)} %bitcast.4), channel_id=1, source_target_pairs={{1,0},{0,1},{3,2},{2,3},{5,4},{4,5},{7,6},{6,7},{9,8},{8,9},{11,10... | collective-permute-start | bytes 786440 | tf_op jit(solution)/shard_map/ppermute | solution.py:599
  11.1 6.0 %collective-permute-start.2 = (bf16[9,64,128]{2,1,0:T(8,128)(2,1)S(1)}, bf16[9,64,128]{2,1,0:T(8,128)(2,1)S(1)}, u32[]{:S(2)}, u32[]{:S(2)}) collective-permute-start(bf16[9,64,128]{2,1,0:T(8,128)(2,1)S(1)} %collective-permute-done.refs_12_.refs_3_), channel_id=1, source_target_pairs={{0,2},{1,3},{2,10},{3,11},{4,6},{5,7},{6,14},{7,15},{8,0},{9,1},{1... | collective-permute-start | bytes 442376 | tf_op jit(solution)/shard_map/ppermute | solution.py:597
  12.1 5.1 %collective-permute-start.3 = (bf16[9,64,128]{2,1,0:T(8,128)(2,1)S(1)}, bf16[9,64,128]{2,1,0:T(8,128)(2,1)S(1)}, u32[]{:S(2)}, u32[]{:S(2)}) collective-permute-start(bf16[9,64,128]{2,1,0:T(8,128)(2,1)S(1)} %collective-permute-done.1.refs_11_.refs_2_), channel_id=1, source_target_pairs={{0,8},{1,9},{2,0},{3,1},{4,12},{5,13},{6,4},{7,5},{8,16},{9,17},{1... | collective-permute-start | bytes 442376 | tf_op jit(solution)/shard_map/ppermute | solution.py:597
  13.2 6.1 %copy-start = (bf16[4,8,4096]{2,1,0:T(8,128)(2,1)S(1)}, bf16[4,8,4096]{2,1,0:T(8,128)(2,1)}, u32[]{:S(2)}) copy-start(bf16[4,8,4096]{2,1,0:T(8,128)(2,1)} %param.8) | copy-start | bytes 786436
  17.2 7.3 %collective-permute-start.7 = (bf16[3,9,64,128]{3,2,1,0:T(8,128)(2,1)S(1)}, bf16[3,9,64,128]{3,2,1,0:T(8,128)(2,1)S(1)}, u32[]{:S(2)}, u32[]{:S(2)}) collective-permute-start(bf16[3,9,64,128]{3,2,1,0:T(8,128)(2,1)S(1)} %get-tuple-element.61), channel_id=1, source_target_pairs={{0,4},{1,5},{2,6},{3,7},{4,0},{5,1},{6,2},{7,3},{8,12},{9,13},{10,... | collective-permute-start | bytes 1327112 | tf_op jit(solution)/shard_map/ppermute | solution.py:629
  17.2 6.2 %collective-permute-start.5 = (bf16[9,64,128]{2,1,0:T(8,128)(2,1)S(1)}, bf16[9,64,128]{2,1,0:T(8,128)(2,1)S(1)}, u32[]{:S(2)}, u32[]{:S(2)}) collective-permute-start(bf16[9,64,128]{2,1,0:T(8,128)(2,1)S(1)} %collective-permute-done.2.refs_5_), channel_id=1, source_target_pairs={{0,2},{1,3},{2,10},{3,11},{4,6},{5,7},{6,14},{7,15},{8,0},{9,1},{1... | collective-permute-start | bytes 442376 | tf_op jit(solution)/shard_map/ppermute | solution.py:597
  18.6 6.0 %collective-permute-start.6 = (bf16[9,64,128]{2,1,0:T(8,128)(2,1)S(1)}, bf16[9,64,128]{2,1,0:T(8,128)(2,1)S(1)}, u32[]{:S(2)}, u32[]{:S(2)}) collective-permute-start(bf16[9,64,128]{2,1,0:T(8,128)(2,1)S(1)} %collective-permute-done.3.refs_4_), channel_id=1, source_target_pairs={{0,8},{1,9},{2,0},{3,1},{4,12},{5,13},{6,4},{7,5},{8,16},{9,17},{1... | collective-permute-start | bytes 442376 | tf_op jit(solution)/shard_map/ppermute | solution.py:597
  24.6 8.1 %collective-permute-start.10 = (bf16[2,9,64,128]{3,2,1,0:T(8,128)(2,1)S(1)}, bf16[2,9,64,128]{3,2,1,0:T(8,128)(2,1)S(1)}, u32[]{:S(2)}, u32[]{:S(2)}) collective-permute-start(bf16[2,9,64,128]{3,2,1,0:T(8,128)(2,1)S(1)} %get-tuple-element.69), channel_id=1, source_target_pairs={{0,4},{1,5},{2,6},{3,7},{4,0},{5,1},{6,2},{7,3},{8,12},{9,13},{10,... | collective-permute-start | bytes 884744 | tf_op jit(solution)/shard_map/ppermute | solution.py:629
  24.6 5.7 %collective-permute-start.11 = (bf16[9,64,128]{2,1,0:T(8,128)(2,1)S(1)}, bf16[9,64,128]{2,1,0:T(8,128)(2,1)S(1)}, u32[]{:S(2)}, u32[]{:S(2)}) collective-permute-start(bf16[9,64,128]{2,1,0:T(8,128)(2,1)S(1)} %collective-permute-done.6.refs_7_), channel_id=1, source_target_pairs={{0,4},{1,5},{2,6},{3,7},{4,0},{5,1},{6,2},{7,3},{8,12},{9,13},{10,... | collective-permute-start | bytes 442376 | tf_op jit(solution)/shard_map/ppermute | solution.py:629
  25.1 5.2 %collective-permute-start.12 = (bf16[9,64,128]{2,1,0:T(8,128)(2,1)S(1)}, bf16[9,64,128]{2,1,0:T(8,128)(2,1)S(1)}, u32[]{:S(2)}, u32[]{:S(2)}) collective-permute-start(bf16[9,64,128]{2,1,0:T(8,128)(2,1)S(1)} %collective-permute-done.5.refs_8_), channel_id=1, source_target_pairs={{0,4},{1,5},{2,6},{3,7},{4,0},{5,1},{6,2},{7,3},{8,12},{9,13},{10,... | collective-permute-start | bytes 442376 | tf_op jit(solution)/shard_map/ppermute | solution.py:629
  25.1 5.5 %collective-permute-start.8 = (bf16[9,64,128]{2,1,0:T(8,128)(2,1)S(1)}, bf16[9,64,128]{2,1,0:T(8,128)(2,1)S(1)}, u32[]{:S(2)}, u32[]{:S(2)}) collective-permute-start(bf16[9,64,128]{2,1,0:T(8,128)(2,1)S(1)} %collective-permute-done.5.refs_8_), channel_id=1, source_target_pairs={{0,6},{1,7},{2,14},{3,15},{4,2},{5,3},{6,10},{7,11},{8,4},{9,5},{1... | collective-permute-start | bytes 442376 | tf_op jit(solution)/shard_map/ppermute | solution.py:597
  26.8 5.8 %collective-permute-start.9 = (bf16[9,64,128]{2,1,0:T(8,128)(2,1)S(1)}, bf16[9,64,128]{2,1,0:T(8,128)(2,1)S(1)}, u32[]{:S(2)}, u32[]{:S(2)}) collective-permute-start(bf16[9,64,128]{2,1,0:T(8,128)(2,1)S(1)} %collective-permute-done.6.refs_7_), channel_id=1, source_target_pairs={{0,8},{1,9},{2,0},{3,1},{4,12},{5,13},{6,4},{7,5},{8,16},{9,17},{1... | collective-permute-start | bytes 442376 | tf_op jit(solution)/shard_map/ppermute | solution.py:597

commit v6 on v5

--- a/solution.py
+++ b/solution.py
@@ -59,6 +59,9 @@
             (self.flat(z, c, g, (t + step) % self.tp), self.flat(z, c, g, t))
             for z, c, g, t in self.devices()
         ]
+
+
+BRIEF = pl.CostEstimate(flops=1000, bytes_accessed=1000, transcendentals=0)
 
 
 def over(x, n):
@@ -98,19 +101,6 @@
             act(slots)
 
         below = slots
-
-
-def cache_copies(first, spot, slots, kv, order, hbms, bufs, sems):
-    span = pl.ds(0, slots * kv)
-    return [
-        [
-            pltpu.make_async_copy(
-                hbm.at[order[first + i], span], buf.at[spot + i, span], sems.at[i, which]
-            )
-            for which, (hbm, buf) in enumerate(zip(hbms, bufs))
-        ]
-        for i in range(2)
-    ]
 
 
 def quarter_copies(quarter, src, dst, sems):
@@ -170,15 +160,15 @@
             pltpu.SemaphoreType.DMA((3,)),
         ],
         compiler_params=pltpu.CompilerParams(vmem_limit_bytes=2 * MIB),
+        cost_estimate=BRIEF,
         name="begin",
     )(pinned(down), pinned(up), pinned(lengths), pinned(queries))
 
 
-def attend_cache(pairs, ready, sizes, scale, quarter, n_packed, *refs):
+def attend_cache(pairs, ready, sizes, scale, quarter, *refs):
     lengths, order, q_ref, k_hbm, v_hbm, w_hbm = refs[:6]
     sems, w_sems = refs[-2:]
-    n_out = 6 if n_packed else 5
-    k_buf, v_buf, w_buf, *outs = refs[-2 - n_out : -2]
+    k_buf, v_buf, w_buf, *outs = refs[-7:-2]
     done = pairs[0]
     o_ref, lse_ref = outs[:2]
     steps, _, heads, size = q_ref.shape
@@ -211,10 +201,6 @@
     w_copies = quarter_copies(quarter, w_hbm, w_buf, w_sems)
     for copy in w_copies:
         copy.start()
-    if n_packed:
-        packed = refs[-2 - n_out - n_packed : -2 - n_out]
-        for i, ref in enumerate(packed):
-            outs[2][i] = ref[...]
 
     row_head = over(within(lax.broadcasted_iota(jnp.int32, (lanes, size), 0), heads), heads // kv)
     slot_head = within(lax.broadcasted_iota(jnp.int32, (lanes, size), 1), kv)
@@ -274,7 +260,7 @@
     return pltpu.VMEM(x.shape, x.dtype)
 
 
-def cache_attention(pairs, ready, rows_args, caches, weights, quarter, buffers, packed, sizes, after):
+def cache_attention(pairs, ready, rows_args, caches, weights, quarter, buffers, sizes, after):
     lengths, order, queries = rows_args
     keys, values = caches
     rows, steps, _, heads, size = (keys.shape[0], *queries.shape)
@@ -287,13 +273,10 @@
     operands += [pinned(x) for x in (keys, values, weights)]
     aliases = {len(operands) + i: i for i in range(len(buffers))}
     specs = [SMEM, SMEM, VMEM, HBM, HBM, HBM] + [VMEM] * len(buffers) + [ANY] * len(after)
-    specs += [VMEM] * len(packed)
-    operands += [pinned(b, pltpu.VMEM) for b in buffers] + after + packed
+    operands += [pinned(b, pltpu.VMEM) for b in buffers] + after
     out_shape = [pltpu.VMEM(x.shape, x.dtype) for x in (keys, values, weights)] + [piece] * 2
-    if packed:
-        out_shape.append(pltpu.VMEM((len(packed),) + packed[0].shape, packed[0].dtype))
     return pl.pallas_call(
-        functools.partial(attend_cache, pairs, ready, sizes, scale, quarter, len(packed)),
+        functools.partial(attend_cache, pairs, ready, sizes, scale, quarter),
         out_shape=out_shape,
         in_specs=specs,
         out_specs=[VMEM] * len(out_shape),
@@ -303,42 +286,30 @@
             pltpu.SemaphoreType.DMA((4,)),
         ],
         compiler_params=pltpu.CompilerParams(vmem_limit_bytes=8 * MIB),
-        cost_estimate=pl.CostEstimate(
-            flops=4 * steps * heads * count * keys.shape[1] * size,
-            bytes_accessed=4 * count * keys.shape[1] * size + weights[0].size,
-            transcendentals=steps * heads * count * keys.shape[1],
-        ),
+        cost_estimate=BRIEF,
         name="cache_attention",
     )(*operands)
 
 
-def project_old(part, lay, n_hidden, n_packed, *refs):
+def project_old(part, lay, n_hidden, *refs):
     refs = list(refs)
     tp = lax.axis_index("tp")
-    w_hbm = refs[1]
-    sems = refs.pop()
     if part == 0:
-        hidden = refs[2 : 2 + n_hidden]
-        packed = refs[2 + n_hidden : 2 + n_hidden + n_packed]
-        w_buf, out_ref, h_ref, pack_ref = refs[-4:]
-    else:
-        h_ref = refs[2]
-        w_buf, out_ref = refs[-2:]
-    copies = quarter_copies(2 + part, w_hbm, w_buf, sems)
-    for copy in copies:
-        copy.start()
-    if part == 0:
+        sems = refs.pop()
+        w_hbm, *hidden = refs[1 : 2 + n_hidden]
+        w_buf, out_ref, h_ref = refs[-3:]
+        copies = quarter_copies(3, w_hbm, w_buf, sems)
+        for copy in copies:
+            copy.start()
         for i, h in enumerate(hidden):
             h_ref[lax.rem(tp + i, lay.tp)] = h[...]
-        for i, ref in enumerate(packed):
-            pack_ref[i] = ref[...]
+    else:
+        h_ref = refs[1]
+        w_buf, out_ref = refs[-2:]
     features = h_ref.shape[2]
     chunk = min(features, 1024)
     total = jnp.zeros(out_ref.shape, jnp.float32)
     for t in range(lay.tp):
-        if part == 1 and 2 * t == lay.tp:
-            for copy in copies:
-                copy.wait()
         for low in range(0, features, chunk):
             start = t * features + low
             total += jnp.dot(
@@ -352,33 +323,102 @@
             copy.wait()
 
 
-def project(part, lay, w_buf, weights, hidden, packed, after):
+def project(part, lay, w_buf, weights, hidden, after):
     tokens, features = hidden[0].shape[-2:]
-    operands = [pinned(w_buf, pltpu.VMEM), pinned(weights)]
-    specs = [VMEM, HBM] + [VMEM] * (len(hidden) + len(packed)) + [ANY] * len(after)
     out_shape = [like(w_buf), pltpu.VMEM((tokens, weights.shape[2]), jnp.float32)]
+    scratch = []
     if part == 0:
-        operands += hidden + packed + after
+        operands = [pinned(weights)] + hidden
+        specs = [HBM] + [VMEM] * len(hidden)
         out_shape.append(pltpu.VMEM((lay.tp, tokens, features), jnp.bfloat16))
-        out_shape.append(pltpu.VMEM((len(packed),) + packed[0].shape, packed[0].dtype))
+        scratch = [pltpu.SemaphoreType.DMA((4,))]
     else:
-        operands += [pinned(h, pltpu.VMEM) for h in hidden] + after
+        operands = [pinned(hidden[0], pltpu.VMEM)]
+        specs = [VMEM]
     return pl.pallas_call(
-        functools.partial(project_old, part, lay, len(hidden), len(packed)),
+        functools.partial(project_old, part, lay, len(hidden)),
         out_shape=out_shape,
-        in_specs=specs,
+        in_specs=[VMEM] + specs + [ANY] * len(after),
         out_specs=[VMEM] * len(out_shape),
         input_output_aliases={0: 0},
-        scratch_shapes=[pltpu.SemaphoreType.DMA((4,))],
+        scratch_shapes=scratch,
         compiler_params=pltpu.CompilerParams(vmem_limit_bytes=8 * MIB),
-        cost_estimate=pl.CostEstimate(
-            flops=2 * tokens * weights[0].size, bytes_accessed=weights.size, transcendentals=0
-        ),
+        cost_estimate=BRIEF,
         name="project",
-    )(*operands)
-
-
-def merge_all(lay, plan, n_caches, scale, *refs):
+    )(pinned(w_buf, pltpu.VMEM), *operands, *after)
+
+
+class Place:
+    def __init__(self, lay):
+        fsdp, grp, self.tp = (lax.axis_index(a) for a in AXES)
+        z, self.core = fsdp // 2, lax.rem(fsdp, 2)
+        self.lay = lay
+        self.own = grp * lay.depth + jnp.where(lax.rem(grp, 2) == 0, z, lay.depth - 1 - z)
+        self.per_lane = lay.fsdp * lay.grp // lay.tp
+
+    def find(self, plan, downs):
+        lay, found = self.lay, []
+        for (steps, flip), down in zip(plan, downs):
+            for i, step in enumerate(steps):
+                spot = lax.rem(self.own + (lay.ring + step), lay.ring)
+                g = spot // lay.depth
+                along = lax.rem(spot, lay.depth)
+                zz = jnp.where(lax.rem(g, 2) == 0, along, lay.depth - 1 - along)
+                core = 1 - self.core if flip else self.core
+                found.append(
+                    (down.at[i] if len(steps) > 1 else down, (zz * 2 + core) * lay.grp + g)
+                )
+        return found
+
+    def add_low(self, total, k, shards, h_ref, depth):
+        for down, index in shards:
+            tiles = depth // down.shape[-1]
+            column = pl.multiple_of(lax.rem(index, self.per_lane) * depth, depth)
+            total += lax.dot_general(
+                h_ref[index // self.per_lane, :, pl.ds(column, depth)],
+                jnp.concatenate([down[k * tiles + i] for i in range(tiles)], axis=1),
+                (((1,), (1,)), ((), ())),
+                preferred_element_type=jnp.float32,
+            )
+        return total
+
+
+def low_part(lay, plan, depth, *refs):
+    downs, h_ref, out_ref = refs[: len(plan)], refs[len(plan)], refs[-1]
+    place = Place(lay)
+    shards = place.find(plan, downs)
+    for k in range(out_ref.shape[0]):
+        old = refs[len(plan) + 1][k]
+        out_ref[k] = place.add_low(old, k, shards, h_ref, depth)
+
+
+def low_start(lay, plan, depth, *refs):
+    downs, h_ref, out_ref = refs[: len(plan)], refs[len(plan)], refs[-1]
+    place = Place(lay)
+    shards = place.find(plan, downs)
+    for k in range(out_ref.shape[0]):
+        out_ref[k] = place.add_low(jnp.zeros(out_ref.shape[1:], jnp.float32), k, shards, h_ref, depth)
+
+
+def project_low(lay, entries, states, pairs, depth, old, after):
+    operands = [e[2] for e in entries] + [pinned(states, pltpu.VMEM)]
+    body = low_start
+    if old is not None:
+        body = low_part
+        operands.append(pinned(old, pltpu.VMEM))
+    rank = entries[0][2].shape[-2]
+    return pl.pallas_call(
+        functools.partial(body, lay, [e[:2] for e in entries], depth),
+        out_shape=pltpu.VMEM((pairs, states.shape[1], rank), jnp.float32),
+        in_specs=[VMEM] * len(operands) + [ANY] * len(after),
+        out_specs=VMEM,
+        compiler_params=pltpu.CompilerParams(vmem_limit_bytes=2 * MIB),
+        cost_estimate=BRIEF,
+        name="project_low",
+    )(*operands, *after)
+
+
+def merge_all(lay, plan, n_low, n_caches, scale, *refs):
     refs = list(refs)
 
     def take(n):
@@ -388,38 +428,23 @@
 
     (weights,) = take(1)
     downs = take(len(plan))
-    h_buf, *olds = take(3)
+    h_buf, low_ref, *olds = take(4)
     order, q_ref = take(2)
     caches = [take(2) for _ in range(n_caches)]
-    m_hbm, out_hbm, m_buf, u_parts, u_buf, out_buf, sems, out_sems = refs
+    m_hbm, out_ref, m_buf, u_parts, u_buf, sems = refs
 
     pairs, depth, width = m_buf.shape[1:]
     cut = min(width, 256)
     lanes = downs[0].shape[-1]
     tiles = depth // lanes
-    fsdp, grp, tp = (lax.axis_index(a) for a in AXES)
-    z, core = fsdp // 2, lax.rem(fsdp, 2)
-    place = grp * lay.depth + jnp.where(lax.rem(grp, 2) == 0, z, lay.depth - 1 - z)
-    per_lane = lay.fsdp * lay.grp // lay.tp
-
-    shards = []
-    for (steps, flip), down in zip(plan, downs):
-        for i, step in enumerate(steps):
-            spot = lax.rem(place + (lay.ring + step), lay.ring)
-            g = spot // lay.depth
-            along = lax.rem(spot, lay.depth)
-            zz = jnp.where(lax.rem(g, 2) == 0, along, lay.depth - 1 - along)
-            shards.append(
-                (
-                    down.at[i] if len(steps) > 1 else down,
-                    (zz * 2 + (1 - core if flip else core)) * lay.grp + g,
-                )
-            )
+    place = Place(lay)
+    per_lane = place.per_lane
+    shards = place.find(plan, downs)
 
     columns = width // per_lane
     for down, index in shards:
 
-        @pl.when(index // per_lane == tp)
+        @pl.when(index // per_lane == place.tp)
         def _():
             u_parts[lax.rem(index, per_lane)] = down[pairs * tiles, :, : pairs * columns]
 
@@ -428,37 +453,8 @@
             [u_parts[i, :, k * columns : (k + 1) * columns] for i in range(per_lane)], axis=1
         )
 
-    new = []
-    for k in range(pairs):
-        low = jnp.zeros((h_buf.shape[1], u_buf.shape[1]), jnp.float32)
-        for down, index in shards:
-            column = pl.multiple_of(lax.rem(index, per_lane) * depth, depth)
-            low += lax.dot_general(
-                h_buf[index // per_lane, :, pl.ds(column, depth)],
-                jnp.concatenate([down[k * tiles + i] for i in range(tiles)], axis=1),
-                (((1,), (1,)), ((), ())),
-                preferred_element_type=jnp.float32,
-            )
-        high = low.astype(jnp.bfloat16)
-        rest = (low - high.astype(jnp.float32)).astype(jnp.bfloat16)
-        new.append(
-            (
-                olds[k][...]
-                + jnp.dot(high, u_buf[k], preferred_element_type=jnp.float32)
-                + jnp.dot(rest, u_buf[k], preferred_element_type=jnp.float32)
-            ).astype(jnp.bfloat16)
-        )
-    finish_row = new_token_attention(q_ref, order, caches, new, out_buf, scale)
-    spots = q_ref.shape[1]
-
-    def out_copy(spot):
-        return pltpu.make_async_copy(
-            out_buf.at[:, spot], out_hbm.at[:, order[spot]], out_sems.at[spot]
-        )
-
     chunk = min(depth, 256)
     copies = []
-    rows_done = 0
     for j, (down, index) in enumerate(shards):
         start = pl.multiple_of(index * depth, depth)
         for k in range(pairs):
@@ -481,15 +477,25 @@
             )
             copy.start()
             copies.append(copy)
-        while rows_done < min(spots, (j + 1) * spots // (len(shards) - 2)):
-            finish_row(rows_done)
-            out_copy(rows_done).start()
-            rows_done += 1
-    for copy in copies + [out_copy(spot) for spot in range(spots)]:
+
+    new = []
+    for k in range(pairs):
+        low = place.add_low(low_ref[k], k, shards[n_low:], h_buf, depth)
+        high = low.astype(jnp.bfloat16)
+        rest = (low - high.astype(jnp.float32)).astype(jnp.bfloat16)
+        new.append(
+            (
+                olds[k][...]
+                + jnp.dot(high, u_buf[k], preferred_element_type=jnp.float32)
+                + jnp.dot(rest, u_buf[k], preferred_element_type=jnp.float32)
+            ).astype(jnp.bfloat16)
+        )
+    add_new_tokens(q_ref, order, caches, new, out_ref, scale)
+    for copy in copies:
         copy.wait()
 
 
-def new_token_attention(q_ref, order, caches, new, out_buf, scale):
+def add_new_tokens(q_ref, order, caches, new, out_ref, scale):
     steps, rows, heads, size = q_ref.shape
     kv = new[0].shape[1] // size
     new = [
@@ -503,9 +509,7 @@
     earlier = within(over(right, rows), steps) <= over(left, heads)
     right_row = jnp.where(same_head & earlier, within(right, rows), -1)
     spots = [(o, lse, i) for o, lse in caches for i in range(o.shape[0])]
-
-    def finish_row(spot):
-        o_ref, lse_ref, i = spots[spot]
+    for spot, (o_ref, lse_ref, i) in enumerate(spots):
         row = order[spot]
         q = q_ref[:, row].reshape(lanes, size)
         s = lax.dot_general(
@@ -520,19 +524,18 @@
         o = old * o_ref[i] + jnp.dot(
             p.astype(jnp.bfloat16), new[1], preferred_element_type=jnp.float32
         )
-        out_buf[:, spot] = (o / divisor).reshape(steps, heads, size).astype(out_buf.dtype)
-
-    return finish_row
-
-
-def merge(lay, shape, entries, weights, states, olds, order, queries, caches):
+        out_ref[:, row] = (o / divisor).reshape(steps, heads, size).astype(out_ref.dtype)
+
+
+def merge(lay, shape, entries, n_low, weights, states, low, olds, order, queries, caches):
     pairs, total, width = shape
     rank = entries[0][2].shape[-2]
     depth = total // (lay.fsdp * lay.grp)
     per_lane = lay.fsdp * lay.grp // lay.tp
     n = sum(len(e[0]) for e in entries)
     operands = [pinned(weights, pltpu.VMEM)] + [e[2] for e in entries]
-    operands += [states, *olds, pinned(order, pltpu.SMEM), pinned(queries, pltpu.VMEM), *caches]
+    operands += [states, low, *olds, pinned(order, pltpu.SMEM), pinned(queries, pltpu.VMEM)]
+    operands += caches
     specs = [VMEM] * len(operands)
     specs[-2 - len(caches)] = SMEM
     return pl.pallas_call(
@@ -540,26 +543,24 @@
             merge_all,
             lay,
             [e[:2] for e in entries],
+            sum(len(e[0]) for e in entries[:n_low]),
             len(caches) // 2,
             LOG2E / math.sqrt(queries.shape[3]),
         ),
-        out_shape=(pltpu.HBM(shape, jnp.bfloat16), pltpu.HBM(queries.shape, jnp.bfloat16)),
+        out_shape=(
+            pltpu.HBM(shape, jnp.bfloat16),
+            jax.ShapeDtypeStruct(queries.shape, jnp.bfloat16),
+        ),
         in_specs=specs,
-        out_specs=(HBM, HBM),
+        out_specs=(HBM, VMEM),
         scratch_shapes=[
             pltpu.VMEM((n, pairs, depth, width), jnp.bfloat16),
             pltpu.VMEM((per_lane, rank, pairs * width // per_lane), jnp.bfloat16),
             pltpu.VMEM((pairs, rank, width), jnp.bfloat16),
-            pltpu.VMEM(queries.shape, jnp.bfloat16),
             pltpu.SemaphoreType.DMA((n, pairs)),
-            pltpu.SemaphoreType.DMA((queries.shape[1],)),
         ],
         compiler_params=pltpu.CompilerParams(vmem_limit_bytes=24 * MIB),
-        cost_estimate=pl.CostEstimate(
-            flops=2 * pairs * total * width * rank,
-            bytes_accessed=2 * pairs * total * width,
-            transcendentals=0,
-        ),
+        cost_estimate=BRIEF,
         name="merge",
     )(*operands)
 
@@ -588,63 +589,69 @@
     shard, *rows_args = begin(own, factor_up, cache_lengths, queries)
     lengths, order, q = rows_args
     projections = projection_weight_matrices
+    pair_count = rows // 2
+    depth = own.shape[2]
+    last_step = lay.ring // 2
+    back = lay.ring_step(-1, 1)
+    caches, olds = [], []
+    buffers = []
+
+    def attention(pairs, ready, quarter, after):
+        nonlocal buffers
+        out = cache_attention(
+            pairs, ready, rows_args, (keys, values), projections, quarter, buffers, sizes, after
+        )
+        buffers = list(out[:3])
+        caches.extend(out[3:])
+        return out[3]
+
+    def project_one(part, arrays, after):
+        out = project(part, lay, buffers[2], projections, arrays, after)
+        buffers[2] = out[0]
+        olds.append(out[1])
+        return out[1], out[2:]
+
+    sent = {d: send(shard, perm=ring[d]) for d in ring}
+    hidden = [tokens] + [send(tokens, perm=lay.feature_step(i)) for i in range(1, lay.tp)]
+    token = attention((0, 1), (0, 2), 0, [shard])
     entries = [((0,), False, shard)]
-    caches, olds = [], []
-    last_step = lay.ring // 2
-
-    def ring_sends(came, step):
-        back = lay.ring_step(-1, 1) if step == last_step else ring[-1]
-        return {-1: send(came[-1], perm=back), 1: send(came[1], perm=ring[1])}
-
-    hidden = [tokens] + [send(tokens, perm=lay.feature_step(i)) for i in range(1, lay.tp)]
-    came = ring_sends({1: shard, -1: shard}, 1)
-    *buffers, o, lse = cache_attention(
-        (0, 1), (0, 2), rows_args, (keys, values), projections, 0, [], [], sizes, [shard]
+    came, swapped = {}, []
+    states = low = None
+    slot = n_low = 0
+    for step in range(1, last_step):
+        for d in ring:
+            slot += 1
+            held = [x for _, x in swapped] + (hidden if slot == 2 else [])
+            (came[d], held), token = after_all((sent[d], held), token)
+            entries.append(((-d * step,), False, came[d]))
+            entries += [(places, True, x) for (places, _), x in zip(swapped, held)]
+            sent[d] = send(came[d], perm=back if d < 0 and step + 1 == last_step else ring[d])
+            swapped = [((-d * step,), send(came[d], perm=swap))]
+            if slot == 1:
+                token = attention((1, 2), (2, pair_count), 1, [token])
+            elif slot == 2:
+                hidden = held[-lay.tp :]
+                token = attention((2, pair_count), (pair_count, pair_count), 2, [token])
+            elif slot == 3:
+                token, (states,) = project_one(0, hidden, [token])
+            elif slot == 4:
+                swapped.append(((0,), send(shard, perm=swap)))
+                token, _ = project_one(1, [states], [token])
+            elif slot == 5:
+                n_low = len(entries)
+                low = project_low(lay, entries, states, shape[0], depth, None, [token])
+                token = low
+    low = project_low(lay, entries[n_low:], states, shape[0], depth, low, [token])
+    forward, low = after_all(sent[1], low)
+    entries.append(((-last_step,), False, forward))
+    low = project_low(lay, entries[-1:], states, shape[0], depth, low, [])
+    n_low = len(entries)
+    (last, held), low = after_all((sent[-1], [x for _, x in swapped]), low)
+    entries += [(places, True, x) for (places, _), x in zip(swapped, held)]
+    entries.append(((last_step,), True, last))
+    return tuple(
+        merge(lay, shape, entries, n_low, buffers[2], states, low, olds, order, q, caches)
     )
-    caches += [o, lse]
-    came, token = after_all(came, o)
-
-    packed = [shard, came[1], came[-1]]
-    entries += [((-d,), False, came[d]) for d in ring]
-    came = ring_sends(came, 2)
-    *buffers, o, lse, packed = cache_attention(
-        (1, rows // 4 * 2),
-        (2, rows // 4 * 2),
-        rows_args,
-        (keys, values),
-        projections,
-        1,
-        buffers,
-        packed,
-        sizes,
-        [token],
-    )
-    caches += [o, lse]
-    (came, hidden, packed), token = after_all((came, hidden, packed), o)
-
-    w_buf, packed = buffers[2], [packed]
-    for step in range(3, last_step + 1):
-        entries += [((-d * (step - 1),), False, came[d]) for d in ring]
-        arrived, came = came, ring_sends(came, step)
-        swapped = [send(x, perm=swap) for x in packed]
-        if step == 3:
-            w_buf, old, states, packed = project(
-                0, lay, w_buf, projections, hidden, [arrived[1], arrived[-1]], [token]
-            )
-            places, packed = [(0, -1, 1)], [packed]
-        elif step == 4:
-            w_buf, old = project(1, lay, w_buf, projections, [states], [], [token])
-            places, packed = [(-2, 2), (-3,), (3,)], []
-        else:
-            places, packed = [(1 - step,), (step - 1,)], []
-        if step < 5:
-            olds.append(old)
-            token = old
-        (came, swapped, packed), token = after_all((came, swapped, packed), token)
-        entries += [(p, True, x) for p, x in zip(places, swapped)]
-        packed += [came[1], came[-1]]
-    entries += [((-last_step,), False, came[1]), ((last_step,), True, came[-1])]
-    return tuple(merge(lay, shape, entries, w_buf, states, olds, order, q, caches))
 
 
 def solution(mesh):

time: 42.2 us -> 43.8 us (1.038); the launches traced: 41.8 us -> 43.9 us
  waiting for transfers between devices: 5.44 us -> 7.16 us
  starting transfers between devices: 11.8 us -> 12.4 us
    ppermute x12 -> x15, waiting for transfers between devices: 5.43 us -> 7.15 us  [the longest x6 7.13 us: shards(): send(came[d], perm=back if d < 0 and step + 1 == last_step else ring[d])]
    ppermute x12 -> x15, starting transfers between devices: 9.96 us -> 10.9 us  [the longest x6 5.88 us: shards(): send(came[d], perm=back if d < 0 and step + 1 == last_step else ring[d])]
    pallas_call x2 -> x3, Pallas kernels: 8.17 us -> 9.11 us  [cache_attention(): pl.pallas_call(functools.partial(attend_cache, pairs, ready, sizes, scale...]
    pallas_call x2 -> x5, Pallas kernels: 5.23 us -> 4.58 us  [the longest x2 3.72 us: project(): pl.pallas_call(functools.partial(project_old, part, lay, len(hidden)), ou...]
    pallas_call x1, Pallas kernels: 9.02 us -> 8.48 us  [merge(): pl.pallas_call(functools.partial(merge_all, lay, [e[:2] for e in entries]...]
  transfers between devices with their start and end apart: 13 -> 16, of which waited for: 5 -> 3; matrix products, arithmetic and copies ran while one was open for 0% -> 0% of each run, Pallas kernels for 32% -> 31%
where the time goes in v6:
time: 43.8 us; the launch traced here: 43.9 us
  Pallas kernels  23.4 us (53%)
  starting transfers between devices  12.4 us (28%)
  waiting for transfers between devices  7.16 us (16%)
  between operations  0.97 us (2%)
    pallas_call x3, Pallas kernels, cache_attention(): pl.pallas_call(functools.partial(attend_cache, pairs, ready, sizes, scale...  9.11 us
    pallas_call x1, Pallas kernels, merge(): pl.pallas_call(functools.partial(merge_all, lay, [e[:2] for e in entries]...  8.48 us
    ppermute x6, waiting for transfers between devices, shards(): send(came[d], perm=back if d < 0 and step + 1 == last_step else ring[d])  7.13 us
    ppermute x6, starting transfers between devices, shards(): send(came[d], perm=back if d < 0 and step + 1 == last_step else ring[d])  5.88 us
    pallas_call x2, Pallas kernels, project(): pl.pallas_call(functools.partial(project_old, part, lay, len(hidden)), ou...  3.72 us
    ppermute x2, starting transfers between devices, shards(): sent = {d: send(shard, perm=ring[d]) for d in ring}  3.53 us
    ppermute x1, starting transfers between devices, shards(): send(tokens, perm=lay.feature_step(i))  1.49 us
    pallas_call x1, Pallas kernels, begin(): pl.pallas_call(begin_all, out_shape=(pltpu.VMEM((count * tiles + 1, rank,...  1.19 us
  transfers between devices with their start and end apart: 16, of which 3 were waited for; matrix products, arithmetic and copies ran while one was open for 0% of the time, Pallas kernels for 31%

profile of v6, /device:TPU:0, one launch (start us, length us, event | category | flops | bytes accessed | tf_op | source)
XLA Modules:
  0.0 43.9 jit_solution(17799812091462689124)
XLA Ops:
  0.6 1.2 %begin.1 = (bf16[9,64,128]{2,1,0:T(8,128)(2,1)S(1)}, s32[8]{0:T(128)S(4)}, s32[8]{0:T(128)S(4)}, bf16[4,8,32,128]{3,2,1,0:T(8,128)(2,1)S(1)}) custom-call(bf16[2,64,512]{2,1,0:T(8,128)(2,1)} %bitcast.12, bf16[2,64,64]{2,1,0:T(8,128)(2,1)} %up.1, s32[8]{0:T(128)} %len_hbm.1, bf16[4,8,32,128]{3,2,1,0:T(8,128)(2,1)} %q_hbm.1), custom_call_target="tpu_custom_call" | custom-call | flops 1000 | bytes 1000 | tf_op jit(solution)/shard_map/begin/pallas_call | solution.py:147
  1.8 3.1 %collective-permute-start = (bf16[9,64,128]{2,1,0:T(8,128)(2,1)S(1)}, bf16[9,64,128]{2,1,0:T(8,128)(2,1)S(1)}, u32[]{:S(2)}, u32[]{:S(2)}) collective-permute-start(bf16[9,64,128]{2,1,0:T(8,128)(2,1)S(1)} %get-tuple-element.52.refs_6_.refs_0_.refs_1_), channel_id=1, source_target_pairs={{0,8},{1,9},{2,0},{3,1},{4,12},{5,13},{6,4},{7,5},{8,16},{9,17},{1... | collective-permute-start | bytes 442376 | tf_op jit(solution)/shard_map/ppermute | solution.py:614
  4.9 1.5 %collective-permute-start.3 = (bf16[32,4096]{1,0:T(8,128)(2,1)}, bf16[32,4096]{1,0:T(8,128)(2,1)S(1)}, u32[]{:S(2)}, u32[]{:S(2)}) collective-permute-start(bf16[32,4096]{1,0:T(8,128)(2,1)} %bitcast.4), channel_id=1, source_target_pairs={{1,0},{0,1},{3,2},{2,3},{5,4},{4,5},{7,6},{6,7},{9,8},{8,9},{11,10... | collective-permute-start | bytes 786440 | tf_op jit(solution)/shard_map/ppermute | solution.py:615
  6.4 0.4 %collective-permute-start.1 = (bf16[9,64,128]{2,1,0:T(8,128)(2,1)S(1)}, bf16[9,64,128]{2,1,0:T(8,128)(2,1)S(1)}, u32[]{:S(2)}, u32[]{:S(2)}) collective-permute-start(bf16[9,64,128]{2,1,0:T(8,128)(2,1)S(1)} %get-tuple-element.52.refs_6_.refs_0_.refs_1_), channel_id=1, source_target_pairs={{0,2},{1,3},{2,10},{3,11},{4,6},{5,7},{6,14},{7,15},{8,0},{9,1},{1... | collective-permute-start | bytes 442376 | tf_op jit(solution)/shard_map/ppermute | solution.py:614
  6.9 3.9 %cache_attention.3 = (bf16[8,3072,128]{2,1,0:T(8,128)(2,1)S(1)}, bf16[8,3072,128]{2,1,0:T(8,128)(2,1)S(1)}, bf16[2,8192,512]{2,1,0:T(8,128)(2,1)S(1)}, f32[2,128,128]{2,1,0:T(8,128)S(1)}, f32[2,128,128]{2,1,0:T(8,128)S(1)}) custom-call(s32[8]{0:T(128)S(4)} %get-tuple-element.49.refs_0_, s32[8]{0:T(128)S(4)} %get-tuple-element.50.refs_1_.refs_21_, ...), custom_call_target="tpu_custom_call" | custom-call | flops 1000 | bytes 1000 | tf_op jit(solution)/shard_map/cache_attention/pallas_call | solution.py:278
  10.8 0.0 collective-permute-done.refs_1_.refs_2_
  10.8 0.1 collective-permute-start.2
  10.9 1.6 %collective-permute-start.4 = (bf16[9,64,128]{2,1,0:T(8,128)(2,1)S(1)}, bf16[9,64,128]{2,1,0:T(8,128)(2,1)S(1)}, u32[]{:S(2)}, u32[]{:S(2)}) collective-permute-start(bf16[9,64,128]{2,1,0:T(8,128)(2,1)S(1)} %collective-permute-done.refs_1_.refs_2_), channel_id=1, source_target_pairs={{0,8},{1,9},{2,0},{3,1},{4,12},{5,13},{6,4},{7,5},{8,16},{9,17},{1... | collective-permute-start | bytes 442376 | tf_op jit(solution)/shard_map/ppermute | solution.py:628
  12.5 2.8 %cache_attention.4 = (bf16[8,3072,128]{2,1,0:T(8,128)(2,1)S(1)}, bf16[8,3072,128]{2,1,0:T(8,128)(2,1)S(1)}, bf16[2,8192,512]{2,1,0:T(8,128)(2,1)S(1)}, f32[2,128,128]{2,1,0:T(8,128)S(1)}, f32[2,128,128]{2,1,0:T(8,128)S(1)}) custom-call(s32[8]{0:T(128)S(4)} %get-tuple-element.49.refs_0_, ...), custom_call_target="tpu_custom_call", output_to_operand_aliasing={{0}: (6, {}), {1}: (7, {}), {2}: (8, {})} | custom-call | flops 1000 | bytes 1000 | tf_op jit(solution)/shard_map/cache_attention/pallas_call | solution.py:278
  15.3 0.0 collective-permute-done.1.refs_2_.refs_3_
  15.3 0.0 collective-permute-done.3.refs_3_
  15.3 0.0 collective-permute-done.2.refs_3_.refs_4_
  15.3 0.1 collective-permute-start.5
  15.4 0.4 collective-permute-start.6
  15.8 0.0 copy-start
  15.8 2.4 %cache_attention.5 = (bf16[8,3072,128]{2,1,0:T(8,128)(2,1)S(1)}, bf16[8,3072,128]{2,1,0:T(8,128)(2,1)S(1)}, bf16[2,8192,512]{2,1,0:T(8,128)(2,1)S(1)}, f32[4,128,128]{2,1,0:T(8,128)S(1)}, f32[4,128,128]{2,1,0:T(8,128)S(1)}) custom-call(s32[8]{0:T(128)S(4)} %get-tuple-element.49.refs_0_, ...), custom_call_target="tpu_custom_call", output_to_operand_aliasing={{0}: (6, {}), {1}: (7, {}), {2}: (8, {})} | custom-call | flops 1000 | bytes 1000 | tf_op jit(solution)/shard_map/cache_attention/pallas_call | solution.py:278
  18.2 0.0 collective-permute-done.4.refs_4_.refs_5_
  18.2 0.0 collective-permute-done.5.refs_5_.refs_6_
  18.3 0.1 collective-permute-start.7
  18.4 0.4 collective-permute-start.10
  18.8 1.8 %collective-permute-start.8 = (bf16[9,64,128]{2,1,0:T(8,128)(2,1)S(1)}, bf16[9,64,128]{2,1,0:T(8,128)(2,1)S(1)}, u32[]{:S(2)}, u32[]{:S(2)}) collective-permute-start(bf16[9,64,128]{2,1,0:T(8,128)(2,1)S(1)} %collective-permute-done.4.refs_4_.refs_5_), channel_id=1, source_target_pairs={{0,8},{1,9},{2,0},{3,1},{4,12},{5,13},{6,4},{7,5},{8,16},{9,17},{1... | collective-permute-start | bytes 442376 | tf_op jit(solution)/shard_map/ppermute | solution.py:628
  20.7 0.0 copy-done
  20.7 2.2 %project.2 = (bf16[2,8192,512]{2,1,0:T(8,128)(2,1)S(1)}, f32[32,512]{1,0:T(8,128)S(1)}, bf16[2,32,4096]{2,1,0:T(8,128)(2,1)S(1)}) custom-call(bf16[2,8192,512]{2,1,0:T(8,128)(2,1)S(1)} %get-tuple-element.64.refs_0_, bf16[2,8192,512]{2,1,0:T(8,128)(2,1)} %refs_1_.1, bf16[32,4096]{1,0:T(8,128)(2,1)S(1)} %bitcast.5, ...), custom_call_target="tpu_custom_call", output_to_operand_aliasing={{0}: (0, {})} | custom-call | flops 1000 | bytes 1000 | tf_op jit(solution)/shard_map/project/pallas_call | solution.py:338
  22.9 0.0 collective-permute-done.6.refs_6_.refs_7_
  22.9 0.0 collective-permute-done.7.refs_7_.refs_8_
  22.9 0.1 collective-permute-start.9
  23.0 0.2 collective-permute-start.11
  23.2 1.5 %project.3 = (bf16[2,8192,512]{2,1,0:T(8,128)(2,1)S(1)}, f32[32,512]{1,0:T(8,128)S(1)}) custom-call(bf16[2,8192,512]{2,1,0:T(8,128)(2,1)S(1)} %get-tuple-element.70.refs_0_, bf16[2,32,4096]{2,1,0:T(8,128)(2,1)S(1)} %get-tuple-element.71.refs_1_.refs_11_.refs_2_.refs_17_, ...), custom_call_target="tpu_custom_call", output_to_operand_aliasing={{0}: (0, {})} | custom-call | flops 1000 | bytes 1000 | tf_op jit(solution)/shard_map/project/pallas_call | solution.py:338
  24.7 0.0 collective-permute-done.10.refs_10_.refs_11_
  24.8 0.0 collective-permute-done.8.refs_8_.refs_9_
  24.8 0.0 collective-permute-done.9.refs_9_.refs_10_
  24.8 0.3 collective-permute-start.12
  25.1 1.7 %collective-permute-start.13 = (bf16[9,64,128]{2,1,0:T(8,128)(2,1)S(1)}, bf16[9,64,128]{2,1,0:T(8,128)(2,1)S(1)}, u32[]{:S(2)}, u32[]{:S(2)}) collective-permute-start(bf16[9,64,128]{2,1,0:T(8,128)(2,1)S(1)} %collective-permute-done.8.refs_8_.refs_9_), channel_id=1, source_target_pairs={{0,8},{1,9},{2,0},{3,1},{4,12},{5,13},{6,4},{7,5},{8,16},{9,17},{1... | collective-permute-start | bytes 442376 | tf_op jit(solution)/shard_map/ppermute | solution.py:628
  26.8 0.5 %project_low.3.refs_3_.refs_4_ = f32[2,32,64]{2,1,0:T(8,128)S(1)} custom-call(bf16[9,64,128]{2,1,0:T(8,128)(2,1)S(1)} %get-tuple-element.52.refs_6_.refs_0_.refs_1_, bf16[9,64,128]{2,1,0:T(8,128)(2,1)S(1)} %collective-permute-done.refs_1_.refs_2_, bf16[9,64,128]{2,1,0:T(8,128)(2,1)S(1)} %collective-permute-done.1.refs_2_.refs_3_, ...), custom_call_target="tpu_custom_call" | custom-call | flops 1000 | bytes 1000 | tf_op jit(solution)/shard_map/project_low/pallas_call | solution.py:410
  27.3 1.9 %collective-permute-done.11.refs_0_.refs_12_ = bf16[9,64,128]{2,1,0:T(8,128)(2,1)S(1)} collective-permute-done((bf16[9,64,128]{2,1,0:T(8,128)(2,1)S(1)}, bf16[9,64,128]{2,1,0:T(8,128)(2,1)S(1)}, u32[]{:S(2)}, u32[]{:S(2)}) %collective-permute-start.11) | collective-permute-done | bytes 147488 | tf_op jit(solution)/shard_map/ppermute | solution.py:628
  29.2 0.0 collective-permute-done.12.refs_1_.refs_13_
  29.2 0.0 collective-permute-start.14
  29.2 0.4 collective-permute-start.15
  29.6 0.2 project_low.4.refs_2_
  29.8 1.3 %collective-permute-done.13.refs_0_.refs_14_ = bf16[9,64,128]{2,1,0:T(8,128)(2,1)S(1)} collective-permute-done((bf16[9,64,128]{2,1,0:T(8,128)(2,1)S(1)}, bf16[9,64,128]{2,1,0:T(8,128)(2,1)S(1)}, u32[]{:S(2)}, u32[]{:S(2)}) %collective-permute-start.13) | collective-permute-done | bytes 147488 | tf_op jit(solution)/shard_map/ppermute | solution.py:628
  31.1 0.2 project_low.5.refs_18_
  31.3 3.9 %collective-permute-done.14.refs_16_ = bf16[9,64,128]{2,1,0:T(8,128)(2,1)S(1)} collective-permute-done((bf16[9,64,128]{2,1,0:T(8,128)(2,1)S(1)}, bf16[9,64,128]{2,1,0:T(8,128)(2,1)S(1)}, u32[]{:S(2)}, u32[]{:S(2)}) %collective-permute-start.14) | collective-permute-done | bytes 147488 | tf_op jit(solution)/shard_map/ppermute | solution.py:628
  35.2 0.0 collective-permute-done.15.refs_15_
  35.2 8.5 %merge.1 = (bf16[2,8192,512]{2,1,0:T(8,128)(2,1)}, bf16[4,8,32,128]{3,2,1,0:T(8,128)(2,1)}) custom-call(bf16[2,8192,512]{2,1,0:T(8,128)(2,1)S(1)} %get-tuple-element.75.refs_0_, bf16[9,64,128]{2,1,0:T(8,128)(2,1)S(1)} %get-tuple-element.52.refs_6_.refs_0_.refs_1_, bf16[9,64,128]{2,1,0:T(8,128)(2,1)S(1)} %collective-permute-done.refs_1_.refs_2_, ...), custom_call_target="tpu_custom_call" | custom-call | flops 1000 | bytes 1000 | tf_op jit(solution)/shard_map/merge/pallas_call | solution.py:541
Async XLA Ops:
  1.8 9.0 %collective-permute-start = (bf16[9,64,128]{2,1,0:T(8,128)(2,1)S(1)}, bf16[9,64,128]{2,1,0:T(8,128)(2,1)S(1)}, u32[]{:S(2)}, u32[]{:S(2)}) collective-permute-start(bf16[9,64,128]{2,1,0:T(8,128)(2,1)S(1)} %get-tuple-element.52.refs_6_.refs_0_.refs_1_), channel_id=1, source_target_pairs={{0,8},{1,9},{2,0},{3,1},{4,12},{5,13},{6,4},{7,5},{8,16},{9,17},{1... | collective-permute-start | bytes 442376 | tf_op jit(solution)/shard_map/ppermute | solution.py:614
  4.9 10.4 %collective-permute-start.3 = (bf16[32,4096]{1,0:T(8,128)(2,1)}, bf16[32,4096]{1,0:T(8,128)(2,1)S(1)}, u32[]{:S(2)}, u32[]{:S(2)}) collective-permute-start(bf16[32,4096]{1,0:T(8,128)(2,1)} %bitcast.4), channel_id=1, source_target_pairs={{1,0},{0,1},{3,2},{2,3},{5,4},{4,5},{7,6},{6,7},{9,8},{8,9},{11,10... | collective-permute-start | bytes 786440 | tf_op jit(solution)/shard_map/ppermute | solution.py:615
  6.4 8.9 %collective-permute-start.1 = (bf16[9,64,128]{2,1,0:T(8,128)(2,1)S(1)}, bf16[9,64,128]{2,1,0:T(8,128)(2,1)S(1)}, u32[]{:S(2)}, u32[]{:S(2)}) collective-permute-start(bf16[9,64,128]{2,1,0:T(8,128)(2,1)S(1)} %get-tuple-element.52.refs_6_.refs_0_.refs_1_), channel_id=1, source_target_pairs={{0,2},{1,3},{2,10},{3,11},{4,6},{5,7},{6,14},{7,15},{8,0},{9,1},{1... | collective-permute-start | bytes 442376 | tf_op jit(solution)/shard_map/ppermute | solution.py:614
  10.8 4.5 %collective-permute-start.2 = (bf16[9,64,128]{2,1,0:T(8,128)(2,1)S(1)}, bf16[9,64,128]{2,1,0:T(8,128)(2,1)S(1)}, u32[]{:S(2)}, u32[]{:S(2)}) collective-permute-start(bf16[9,64,128]{2,1,0:T(8,128)(2,1)S(1)} %collective-permute-done.refs_1_.refs_2_), channel_id=1, source_target_pairs={{0,4},{1,5},{2,6},{3,7},{4,0},{5,1},{6,2},{7,3},{8,12},{9,13},{10,... | collective-permute-start | bytes 442376 | tf_op jit(solution)/shard_map/ppermute | solution.py:629
  10.9 7.4 %collective-permute-start.4 = (bf16[9,64,128]{2,1,0:T(8,128)(2,1)S(1)}, bf16[9,64,128]{2,1,0:T(8,128)(2,1)S(1)}, u32[]{:S(2)}, u32[]{:S(2)}) collective-permute-start(bf16[9,64,128]{2,1,0:T(8,128)(2,1)S(1)} %collective-permute-done.refs_1_.refs_2_), channel_id=1, source_target_pairs={{0,8},{1,9},{2,0},{3,1},{4,12},{5,13},{6,4},{7,5},{8,16},{9,17},{1... | collective-permute-start | bytes 442376 | tf_op jit(solution)/shard_map/ppermute | solution.py:628
  15.3 2.9 %collective-permute-start.5 = (bf16[9,64,128]{2,1,0:T(8,128)(2,1)S(1)}, bf16[9,64,128]{2,1,0:T(8,128)(2,1)S(1)}, u32[]{:S(2)}, u32[]{:S(2)}) collective-permute-start(bf16[9,64,128]{2,1,0:T(8,128)(2,1)S(1)} %collective-permute-done.1.refs_2_.refs_3_), channel_id=1, source_target_pairs={{0,4},{1,5},{2,6},{3,7},{4,0},{5,1},{6,2},{7,3},{8,12},{9,13},{10,... | collective-permute-start | bytes 442376 | tf_op jit(solution)/shard_map/ppermute | solution.py:629
  15.4 7.5 %collective-permute-start.6 = (bf16[9,64,128]{2,1,0:T(8,128)(2,1)S(1)}, bf16[9,64,128]{2,1,0:T(8,128)(2,1)S(1)}, u32[]{:S(2)}, u32[]{:S(2)}) collective-permute-start(bf16[9,64,128]{2,1,0:T(8,128)(2,1)S(1)} %collective-permute-done.1.refs_2_.refs_3_), channel_id=1, source_target_pairs={{0,2},{1,3},{2,10},{3,11},{4,6},{5,7},{6,14},{7,15},{8,0},{9,1},{1... | collective-permute-start | bytes 442376 | tf_op jit(solution)/shard_map/ppermute | solution.py:628
  15.8 4.8 %copy-start = (bf16[4,8,4096]{2,1,0:T(8,128)(2,1)S(1)}, bf16[4,8,4096]{2,1,0:T(8,128)(2,1)}, u32[]{:S(2)}) copy-start(bf16[4,8,4096]{2,1,0:T(8,128)(2,1)} %param.8) | copy-start | bytes 786436
  18.3 4.6 %collective-permute-start.7 = (bf16[9,64,128]{2,1,0:T(8,128)(2,1)S(1)}, bf16[9,64,128]{2,1,0:T(8,128)(2,1)S(1)}, u32[]{:S(2)}, u32[]{:S(2)}) collective-permute-start(bf16[9,64,128]{2,1,0:T(8,128)(2,1)S(1)} %collective-permute-done.4.refs_4_.refs_5_), channel_id=1, source_target_pairs={{0,4},{1,5},{2,6},{3,7},{4,0},{5,1},{6,2},{7,3},{8,12},{9,13},{10,... | collective-permute-start | bytes 442376 | tf_op jit(solution)/shard_map/ppermute | solution.py:629
  18.4 6.4 %collective-permute-start.10 = (bf16[9,64,128]{2,1,0:T(8,128)(2,1)S(1)}, bf16[9,64,128]{2,1,0:T(8,128)(2,1)S(1)}, u32[]{:S(2)}, u32[]{:S(2)}) collective-permute-start(bf16[9,64,128]{2,1,0:T(8,128)(2,1)S(1)} %get-tuple-element.52.refs_6_.refs_0_.refs_1_), channel_id=1, source_target_pairs={{0,4},{1,5},{2,6},{3,7},{4,0},{5,1},{6,2},{7,3},{8,12},{9,13},{10,... | collective-permute-start | bytes 442376 | tf_op jit(solution)/shard_map/ppermute | solution.py:638
  18.8 5.9 %collective-permute-start.8 = (bf16[9,64,128]{2,1,0:T(8,128)(2,1)S(1)}, bf16[9,64,128]{2,1,0:T(8,128)(2,1)S(1)}, u32[]{:S(2)}, u32[]{:S(2)}) collective-permute-start(bf16[9,64,128]{2,1,0:T(8,128)(2,1)S(1)} %collective-permute-done.4.refs_4_.refs_5_), channel_id=1, source_target_pairs={{0,8},{1,9},{2,0},{3,1},{4,12},{5,13},{6,4},{7,5},{8,16},{9,17},{1... | collective-permute-start | bytes 442376 | tf_op jit(solution)/shard_map/ppermute | solution.py:628
  22.9 1.9 %collective-permute-start.9 = (bf16[9,64,128]{2,1,0:T(8,128)(2,1)S(1)}, bf16[9,64,128]{2,1,0:T(8,128)(2,1)S(1)}, u32[]{:S(2)}, u32[]{:S(2)}) collective-permute-start(bf16[9,64,128]{2,1,0:T(8,128)(2,1)S(1)} %collective-permute-done.6.refs_6_.refs_7_), channel_id=1, source_target_pairs={{0,4},{1,5},{2,6},{3,7},{4,0},{5,1},{6,2},{7,3},{8,12},{9,13},{10,... | collective-permute-start | bytes 442376 | tf_op jit(solution)/shard_map/ppermute | solution.py:629
  23.0 6.2 %collective-permute-start.11 = (bf16[9,64,128]{2,1,0:T(8,128)(2,1)S(1)}, bf16[9,64,128]{2,1,0:T(8,128)(2,1)S(1)}, u32[]{:S(2)}, u32[]{:S(2)}) collective-permute-start(bf16[9,64,128]{2,1,0:T(8,128)(2,1)S(1)} %collective-permute-done.6.refs_6_.refs_7_), channel_id=1, source_target_pairs={{0,2},{1,3},{2,10},{3,11},{4,6},{5,7},{6,14},{7,15},{8,0},{9,1},{1... | collective-permute-start | bytes 442376 | tf_op jit(solution)/shard_map/ppermute | solution.py:628
  24.8 4.5 %collective-permute-start.12 = (bf16[9,64,128]{2,1,0:T(8,128)(2,1)S(1)}, bf16[9,64,128]{2,1,0:T(8,128)(2,1)S(1)}, u32[]{:S(2)}, u32[]{:S(2)}) collective-permute-start(bf16[9,64,128]{2,1,0:T(8,128)(2,1)S(1)} %collective-permute-done.8.refs_8_.refs_9_), channel_id=1, source_target_pairs={{0,4},{1,5},{2,6},{3,7},{4,0},{5,1},{6,2},{7,3},{8,12},{9,13},{10,... | collective-permute-start | bytes 442376 | tf_op jit(solution)/shard_map/ppermute | solution.py:629
  25.1 6.0 %collective-permute-start.13 = (bf16[9,64,128]{2,1,0:T(8,128)(2,1)S(1)}, bf16[9,64,128]{2,1,0:T(8,128)(2,1)S(1)}, u32[]{:S(2)}, u32[]{:S(2)}) collective-permute-start(bf16[9,64,128]{2,1,0:T(8,128)(2,1)S(1)} %collective-permute-done.8.refs_8_.refs_9_), channel_id=1, source_target_pairs={{0,8},{1,9},{2,0},{3,1},{4,12},{5,13},{6,4},{7,5},{8,16},{9,17},{1... | collective-permute-start | bytes 442376 | tf_op jit(solution)/shard_map/ppermute | solution.py:628
  29.2 6.0 %collective-permute-start.14 = (bf16[9,64,128]{2,1,0:T(8,128)(2,1)S(1)}, bf16[9,64,128]{2,1,0:T(8,128)(2,1)S(1)}, u32[]{:S(2)}, u32[]{:S(2)}) collective-permute-start(bf16[9,64,128]{2,1,0:T(8,128)(2,1)S(1)} %collective-permute-done.11.refs_0_.refs_12_), channel_id=1, source_target_pairs={{0,6},{1,7},{2,14},{3,15},{4,2},{5,3},{6,10},{7,11},{8,4},{9,5},{1... | collective-permute-start | bytes 442376 | tf_op jit(solution)/shard_map/ppermute | solution.py:628
  29.2 6.0 %collective-permute-start.15 = (bf16[9,64,128]{2,1,0:T(8,128)(2,1)S(1)}, bf16[9,64,128]{2,1,0:T(8,128)(2,1)S(1)}, u32[]{:S(2)}, u32[]{:S(2)}) collective-permute-start(bf16[9,64,128]{2,1,0:T(8,128)(2,1)S(1)} %collective-permute-done.11.refs_0_.refs_12_), channel_id=1, source_target_pairs={{0,4},{1,5},{2,6},{3,7},{4,0},{5,1},{6,2},{7,3},{8,12},{9,13},{10,... | collective-permute-start | bytes 442376 | tf_op jit(solution)/shard_map/ppermute | solution.py:629

commit v7 on v6

--- a/solution.py
+++ b/solution.py
@@ -42,11 +42,29 @@
         g, z = divmod(position, self.depth)
         return (z if g % 2 == 0 else self.depth - 1 - z), g
 
-    def ring_step(self, step, flip=0):
+    def ring_step(self):
         pairs = []
         for z, core, g, t in self.devices():
-            to_z, to_g = self.at((self.place(z, g) + step) % self.ring)
-            pairs.append((self.flat(z, core, g, t), self.flat(to_z, core ^ flip, to_g, t)))
+            to_z, to_g = self.at((self.place(z, g) + (1 - 2 * core)) % self.ring)
+            pairs.append((self.flat(z, core, g, t), self.flat(to_z, core, to_g, t)))
+        return pairs
+
+    def plane_step(self):
+        return [
+            (
+                self.flat(t * self.block + z % self.block, c, g, z // self.block),
+                self.flat(z, c, g, t),
+            )
+            for z, c, g, t in self.devices()
+        ]
+
+    def near_step(self, turn, shift):
+        pairs = []
+        for z, c, g, t in self.devices():
+            source = z - z % self.block + (z % self.block + shift) % self.block
+            pairs.append(
+                (self.flat(source, c, (g + turn) % self.grp, t), self.flat(z, c, g, t))
+            )
         return pairs
 
     def core_swap(self):
@@ -115,13 +133,17 @@
     ]
 
 
-def begin_all(down, up, len_hbm, q_hbm, shard, lengths, order, q_ref, up_buf, sems, more):
-    lanes = shard.shape[2]
+def up_columns(up):
+    return jnp.concatenate([up[k] for k in range(up.shape[0])], axis=1)
+
+
+def begin_all(down, up, len_hbm, q_hbm, pair, up_pair, lengths, order, q_ref, up_buf, sems, more):
+    lanes = pair.shape[3]
     count, _, depth = down.shape
     tiles = depth // lanes
     copies = [
         pltpu.make_async_copy(
-            down.at[k, :, pl.ds(i * lanes, lanes)], shard.at[k * tiles + i], sems.at[k, i]
+            down.at[k, :, pl.ds(i * lanes, lanes)], pair.at[0, k * tiles + i], sems.at[k, i]
         )
         for k in range(count)
         for i in range(tiles)
@@ -129,40 +151,62 @@
     up_copy = pltpu.make_async_copy(up, up_buf, more.at[0])
     len_copy = pltpu.make_async_copy(len_hbm, lengths, more.at[1])
     q_copy = pltpu.make_async_copy(q_hbm, q_ref, more.at[2])
-    for copy in [up_copy, len_copy] + copies + [q_copy]:
+    for copy in [len_copy, up_copy] + copies + [q_copy]:
         copy.start()
-    up_copy.wait()
-    columns = jnp.concatenate([up_buf[k] for k in range(count)], axis=1)
-    shard[count * tiles, :, : columns.shape[1]] = columns
     len_copy.wait()
     sort_rows(lengths, order)
+    up_copy.wait()
+    up_pair[lax.rem(lax.axis_index("fsdp"), 2)] = up_columns(up_buf)
     for copy in copies + [q_copy]:
         copy.wait()
 
 
 def begin(down, up, lengths, queries):
     count, rank, depth = down.shape
-    tiles = depth // 128
     scalars = pltpu.SMEM(lengths.shape, jnp.int32)
     return pl.pallas_call(
         begin_all,
         out_shape=(
-            pltpu.VMEM((count * tiles + 1, rank, 128), down.dtype),
+            pltpu.VMEM((2, count * depth // 128, rank, 128), down.dtype),
+            pltpu.VMEM((2, rank, count * up.shape[2]), up.dtype),
             scalars,
             scalars,
             pltpu.VMEM(queries.shape, queries.dtype),
         ),
         in_specs=[HBM] * 4,
-        out_specs=(VMEM, SMEM, SMEM, VMEM),
+        out_specs=(VMEM, VMEM, SMEM, SMEM, VMEM),
         scratch_shapes=[
             pltpu.VMEM(up.shape, up.dtype),
-            pltpu.SemaphoreType.DMA((count, tiles)),
+            pltpu.SemaphoreType.DMA((count, depth // 128)),
             pltpu.SemaphoreType.DMA((3,)),
         ],
         compiler_params=pltpu.CompilerParams(vmem_limit_bytes=2 * MIB),
         cost_estimate=BRIEF,
         name="begin",
     )(pinned(down), pinned(up), pinned(lengths), pinned(queries))
+
+
+def pack_other(down, up, _, __, pair, up_pair):
+    lanes = pair.shape[3]
+    count, _, depth = down.shape
+    tiles = depth // lanes
+    for k in range(count):
+        for i in range(tiles):
+            pair[1, k * tiles + i] = down[k, :, i * lanes : (i + 1) * lanes]
+    up_pair[1 - lax.rem(lax.axis_index("fsdp"), 2)] = up_columns(up)
+
+
+def pack(down, up, pair, up_pair):
+    return pl.pallas_call(
+        pack_other,
+        out_shape=(like(pair), like(up_pair)),
+        in_specs=[VMEM] * 4,
+        out_specs=(VMEM, VMEM),
+        input_output_aliases={2: 0, 3: 1},
+        compiler_params=pltpu.CompilerParams(vmem_limit_bytes=2 * MIB),
+        cost_estimate=BRIEF,
+        name="pack_other",
+    )(down, up, pinned(pair, pltpu.VMEM), pinned(up_pair, pltpu.VMEM))
 
 
 def attend_cache(pairs, ready, sizes, scale, quarter, *refs):
@@ -291,83 +335,72 @@
     )(*operands)
 
 
-def project_old(part, lay, n_hidden, *refs):
-    refs = list(refs)
+def project_old(lay, n_hidden, *refs):
+    w_hbm, *hidden = refs[1 : 2 + n_hidden]
+    w_buf, out_ref, h_ref, sems = refs[-4:]
     tp = lax.axis_index("tp")
-    if part == 0:
-        sems = refs.pop()
-        w_hbm, *hidden = refs[1 : 2 + n_hidden]
-        w_buf, out_ref, h_ref = refs[-3:]
-        copies = quarter_copies(3, w_hbm, w_buf, sems)
-        for copy in copies:
-            copy.start()
-        for i, h in enumerate(hidden):
-            h_ref[lax.rem(tp + i, lay.tp)] = h[...]
-    else:
-        h_ref = refs[1]
-        w_buf, out_ref = refs[-2:]
+    copies = [quarter_copies(2 + i, w_hbm, w_buf, sems.at[i]) for i in range(2)]
+    for copy in copies[0] + copies[1]:
+        copy.start()
+    for i, h in enumerate(hidden):
+        h_ref[lax.rem(tp + i, lay.tp)] = h[...]
     features = h_ref.shape[2]
     chunk = min(features, 1024)
-    total = jnp.zeros(out_ref.shape, jnp.float32)
-    for t in range(lay.tp):
-        for low in range(0, features, chunk):
-            start = t * features + low
-            total += jnp.dot(
-                h_ref[t, :, low : low + chunk],
-                w_buf[part, start : start + chunk, :],
-                preferred_element_type=jnp.float32,
-            )
-    out_ref[...] = total
-    if part == 0:
-        for copy in copies:
-            copy.wait()
-
-
-def project(part, lay, w_buf, weights, hidden, after):
-    tokens, features = hidden[0].shape[-2:]
-    out_shape = [like(w_buf), pltpu.VMEM((tokens, weights.shape[2]), jnp.float32)]
-    scratch = []
-    if part == 0:
-        operands = [pinned(weights)] + hidden
-        specs = [HBM] + [VMEM] * len(hidden)
-        out_shape.append(pltpu.VMEM((lay.tp, tokens, features), jnp.bfloat16))
-        scratch = [pltpu.SemaphoreType.DMA((4,))]
-    else:
-        operands = [pinned(hidden[0], pltpu.VMEM)]
-        specs = [VMEM]
+    for k in range(2):
+        total = jnp.zeros(out_ref.shape[1:], jnp.float32)
+        for t in range(lay.tp):
+            if k == 1 and t % (lay.tp // 2) == 0:
+                for copy in copies[t // (lay.tp // 2)]:
+                    copy.wait()
+            for low in range(0, features, chunk):
+                start = t * features + low
+                total += jnp.dot(
+                    h_ref[t, :, low : low + chunk],
+                    w_buf[k, start : start + chunk, :],
+                    preferred_element_type=jnp.float32,
+                )
+        out_ref[k] = total
+
+
+def project(lay, w_buf, weights, hidden, after):
+    tokens, features = hidden[0].shape
     return pl.pallas_call(
-        functools.partial(project_old, part, lay, len(hidden)),
-        out_shape=out_shape,
-        in_specs=[VMEM] + specs + [ANY] * len(after),
-        out_specs=[VMEM] * len(out_shape),
+        functools.partial(project_old, lay, len(hidden)),
+        out_shape=(
+            like(w_buf),
+            pltpu.VMEM((2, tokens, weights.shape[2]), jnp.float32),
+            pltpu.VMEM((lay.tp, tokens, features), jnp.bfloat16),
+        ),
+        in_specs=[VMEM, HBM] + [VMEM] * len(hidden) + [ANY] * len(after),
+        out_specs=(VMEM, VMEM, VMEM),
         input_output_aliases={0: 0},
-        scratch_shapes=scratch,
-        compiler_params=pltpu.CompilerParams(vmem_limit_bytes=8 * MIB),
+        scratch_shapes=[pltpu.SemaphoreType.DMA((2, 4))],
+        compiler_params=pltpu.CompilerParams(vmem_limit_bytes=4 * MIB),
         cost_estimate=BRIEF,
         name="project",
-    )(pinned(w_buf, pltpu.VMEM), *operands, *after)
+    )(pinned(w_buf, pltpu.VMEM), pinned(weights), *hidden, *after)
 
 
 class Place:
     def __init__(self, lay):
-        fsdp, grp, self.tp = (lax.axis_index(a) for a in AXES)
-        z, self.core = fsdp // 2, lax.rem(fsdp, 2)
+        fsdp, self.grp, self.tp = (lax.axis_index(a) for a in AXES)
+        self.z, self.core = fsdp // 2, lax.rem(fsdp, 2)
         self.lay = lay
-        self.own = grp * lay.depth + jnp.where(lax.rem(grp, 2) == 0, z, lay.depth - 1 - z)
+        there = jnp.where(lax.rem(self.grp, 2) == 0, self.z, lay.depth - 1 - self.z)
+        self.own = self.grp * lay.depth + there
         self.per_lane = lay.fsdp * lay.grp // lay.tp
 
     def find(self, plan, downs):
         lay, found = self.lay, []
-        for (steps, flip), down in zip(plan, downs):
-            for i, step in enumerate(steps):
-                spot = lax.rem(self.own + (lay.ring + step), lay.ring)
-                g = spot // lay.depth
-                along = lax.rem(spot, lay.depth)
-                zz = jnp.where(lax.rem(g, 2) == 0, along, lay.depth - 1 - along)
-                core = 1 - self.core if flip else self.core
-                found.append(
-                    (down.at[i] if len(steps) > 1 else down, (zz * 2 + core) * lay.grp + g)
-                )
+        for (step, flip), down in zip(plan, downs):
+            towards = (1 - 2 * self.core if flip else 2 * self.core - 1) * step
+            spot = lax.rem(self.own + (lay.ring + towards), lay.ring)
+            g = spot // lay.depth
+            along = lax.rem(spot, lay.depth)
+            zz = jnp.where(lax.rem(g, 2) == 0, along, lay.depth - 1 - along)
+            for i in range(2):
+                core = lax.rem(self.core + (i + flip), 2)
+                found.append((down.at[i], (zz * 2 + core) * lay.grp + g))
         return found
 
     def add_low(self, total, k, shards, h_ref, depth):
@@ -383,42 +416,7 @@
         return total
 
 
-def low_part(lay, plan, depth, *refs):
-    downs, h_ref, out_ref = refs[: len(plan)], refs[len(plan)], refs[-1]
-    place = Place(lay)
-    shards = place.find(plan, downs)
-    for k in range(out_ref.shape[0]):
-        old = refs[len(plan) + 1][k]
-        out_ref[k] = place.add_low(old, k, shards, h_ref, depth)
-
-
-def low_start(lay, plan, depth, *refs):
-    downs, h_ref, out_ref = refs[: len(plan)], refs[len(plan)], refs[-1]
-    place = Place(lay)
-    shards = place.find(plan, downs)
-    for k in range(out_ref.shape[0]):
-        out_ref[k] = place.add_low(jnp.zeros(out_ref.shape[1:], jnp.float32), k, shards, h_ref, depth)
-
-
-def project_low(lay, entries, states, pairs, depth, old, after):
-    operands = [e[2] for e in entries] + [pinned(states, pltpu.VMEM)]
-    body = low_start
-    if old is not None:
-        body = low_part
-        operands.append(pinned(old, pltpu.VMEM))
-    rank = entries[0][2].shape[-2]
-    return pl.pallas_call(
-        functools.partial(body, lay, [e[:2] for e in entries], depth),
-        out_shape=pltpu.VMEM((pairs, states.shape[1], rank), jnp.float32),
-        in_specs=[VMEM] * len(operands) + [ANY] * len(after),
-        out_specs=VMEM,
-        compiler_params=pltpu.CompilerParams(vmem_limit_bytes=2 * MIB),
-        cost_estimate=BRIEF,
-        name="project_low",
-    )(*operands, *after)
-
-
-def merge_all(lay, plan, n_low, n_caches, scale, *refs):
+def merge_some(lay, plan, ups, n_caches, scale, *refs):
     refs = list(refs)
 
     def take(n):
@@ -426,32 +424,40 @@
         del refs[:n]
         return out
 
-    (weights,) = take(1)
+    first, last = ups is not None, n_caches > 0
     downs = take(len(plan))
-    h_buf, low_ref, *olds = take(4)
-    order, q_ref = take(2)
-    caches = [take(2) for _ in range(n_caches)]
-    m_hbm, out_ref, m_buf, u_parts, u_buf, sems = refs
-
+    (h_buf,) = take(1)
+    if first:
+        up_refs = take(len(ups))
+        weights = refs[1]
+        m_hbm, weights, u_buf, low_out, m_buf, sems, u_parts = refs[-7:]
+    else:
+        old, order, q_ref = take(3)
+        caches = [take(2) for _ in range(n_caches)]
+        u_buf, low_in = take(2)
+        m_hbm, weights, out_ref, m_buf, sems = refs[-5:]
     pairs, depth, width = m_buf.shape[1:]
     cut = min(width, 256)
     lanes = downs[0].shape[-1]
     tiles = depth // lanes
     place = Place(lay)
-    per_lane = place.per_lane
     shards = place.find(plan, downs)
 
-    columns = width // per_lane
-    for down, index in shards:
-
-        @pl.when(index // per_lane == place.tp)
-        def _():
-            u_parts[lax.rem(index, per_lane)] = down[pairs * tiles, :, : pairs * columns]
-
-    for k in range(pairs):
-        u_buf[k] = ADAPTER_SCALING * jnp.concatenate(
-            [u_parts[i, :, k * columns : (k + 1) * columns] for i in range(per_lane)], axis=1
-        )
+    if first:
+        columns = width // place.per_lane
+        for (turn, shift), up in zip(ups, up_refs):
+            zz = lax.rem(lax.rem(place.z, lay.block) + shift, lay.block)
+            g = lax.rem(place.grp + turn, lay.grp)
+            for c in range(2):
+                u_parts[(zz * 2 + c) * lay.grp + g] = up[c]
+        for k in range(pairs):
+            u_buf[k] = ADAPTER_SCALING * jnp.concatenate(
+                [
+                    u_parts[i, :, k * columns : (k + 1) * columns]
+                    for i in range(place.per_lane)
+                ],
+                axis=1,
+            )
 
     chunk = min(depth, 256)
     copies = []
@@ -478,19 +484,25 @@
             copy.start()
             copies.append(copy)
 
-    new = []
-    for k in range(pairs):
-        low = place.add_low(low_ref[k], k, shards[n_low:], h_buf, depth)
-        high = low.astype(jnp.bfloat16)
-        rest = (low - high.astype(jnp.float32)).astype(jnp.bfloat16)
-        new.append(
-            (
-                olds[k][...]
-                + jnp.dot(high, u_buf[k], preferred_element_type=jnp.float32)
-                + jnp.dot(rest, u_buf[k], preferred_element_type=jnp.float32)
-            ).astype(jnp.bfloat16)
-        )
-    add_new_tokens(q_ref, order, caches, new, out_ref, scale)
+    if first:
+        for k in range(pairs):
+            low_out[k] = place.add_low(
+                jnp.zeros(low_out.shape[1:], jnp.float32), k, shards, h_buf, depth
+            )
+    if last:
+        new = []
+        for k in range(pairs):
+            low = place.add_low(low_in[k], k, shards, h_buf, depth)
+            high = low.astype(jnp.bfloat16)
+            rest = (low - high.astype(jnp.float32)).astype(jnp.bfloat16)
+            new.append(
+                (
+                    old[k]
+                    + jnp.dot(high, u_buf[k], preferred_element_type=jnp.float32)
+                    + jnp.dot(rest, u_buf[k], preferred_element_type=jnp.float32)
+                ).astype(jnp.bfloat16)
+            )
+        add_new_tokens(q_ref, order, caches, new, out_ref, scale)
     for copy in copies:
         copy.wait()
 
@@ -527,42 +539,58 @@
         out_ref[:, row] = (o / divisor).reshape(steps, heads, size).astype(out_ref.dtype)
 
 
-def merge(lay, shape, entries, n_low, weights, states, low, olds, order, queries, caches):
+def merge(lay, shape, entries, states, w_buf, ups, state, final, after):
     pairs, total, width = shape
-    rank = entries[0][2].shape[-2]
+    tokens, rank = states.shape[1], entries[0][2].shape[-2]
     depth = total // (lay.fsdp * lay.grp)
     per_lane = lay.fsdp * lay.grp // lay.tp
-    n = sum(len(e[0]) for e in entries)
-    operands = [pinned(weights, pltpu.VMEM)] + [e[2] for e in entries]
-    operands += [states, low, *olds, pinned(order, pltpu.SMEM), pinned(queries, pltpu.VMEM)]
-    operands += caches
+    n = 2 * len(entries)
+    merged = pltpu.HBM(shape, jnp.bfloat16)
+    u_shape, low_shape = (pairs, rank, width), (pairs, tokens, rank)
+    operands = [e[2] for e in entries] + [pinned(states, pltpu.VMEM)]
+    scratch = [
+        pltpu.VMEM((n, pairs, depth, width), jnp.bfloat16),
+        pltpu.SemaphoreType.DMA((n, pairs)),
+    ]
     specs = [VMEM] * len(operands)
-    specs[-2 - len(caches)] = SMEM
+    if state is None:
+        operands += [x for _, _, x in ups] + [pinned(w_buf, pltpu.VMEM)]
+        specs += [VMEM] * (len(ups) + 1)
+        aliases = {len(operands) - 1: 1}
+        out_shape = [
+            merged,
+            like(w_buf),
+            pltpu.VMEM(u_shape, jnp.bfloat16),
+            pltpu.VMEM(low_shape, jnp.float32),
+        ]
+        out_specs = [HBM, VMEM, VMEM, VMEM]
+        scratch.append(pltpu.VMEM((per_lane, rank, pairs * width // per_lane), jnp.bfloat16))
+        n_caches, scale = 0, 0.0
+        plan_ups = [(turn, shift) for turn, shift, _ in ups]
+    else:
+        olds, order, queries, caches = final
+        m_prev, u_buf, low = state
+        operands += [olds, pinned(order, pltpu.SMEM), pinned(queries, pltpu.VMEM), *caches]
+        specs += [VMEM, SMEM, VMEM] + [VMEM] * len(caches)
+        operands += [pinned(u_buf, pltpu.VMEM), pinned(low, pltpu.VMEM)]
+        operands += [pinned(m_prev), pinned(w_buf, pltpu.VMEM)]
+        specs += [VMEM, VMEM, HBM, VMEM]
+        aliases = {len(operands) - 2: 0, len(operands) - 1: 1}
+        out_shape = [merged, like(w_buf), jax.ShapeDtypeStruct(queries.shape, jnp.bfloat16)]
+        out_specs = [HBM, VMEM, VMEM]
+        n_caches, scale = len(caches) // 2, LOG2E / math.sqrt(queries.shape[3])
+        plan_ups = None
     return pl.pallas_call(
-        functools.partial(
-            merge_all,
-            lay,
-            [e[:2] for e in entries],
-            sum(len(e[0]) for e in entries[:n_low]),
-            len(caches) // 2,
-            LOG2E / math.sqrt(queries.shape[3]),
-        ),
-        out_shape=(
-            pltpu.HBM(shape, jnp.bfloat16),
-            jax.ShapeDtypeStruct(queries.shape, jnp.bfloat16),
-        ),
-        in_specs=specs,
-        out_specs=(HBM, VMEM),
-        scratch_shapes=[
-            pltpu.VMEM((n, pairs, depth, width), jnp.bfloat16),
-            pltpu.VMEM((per_lane, rank, pairs * width // per_lane), jnp.bfloat16),
-            pltpu.VMEM((pairs, rank, width), jnp.bfloat16),
-            pltpu.SemaphoreType.DMA((n, pairs)),
-        ],
-        compiler_params=pltpu.CompilerParams(vmem_limit_bytes=24 * MIB),
+        functools.partial(merge_some, lay, [e[:2] for e in entries], plan_ups, n_caches, scale),
+        out_shape=out_shape,
+        in_specs=specs + [ANY] * len(after),
+        out_specs=out_specs,
+        input_output_aliases=aliases,
+        scratch_shapes=scratch,
+        compiler_params=pltpu.CompilerParams(vmem_limit_bytes=18 * MIB),
         cost_estimate=BRIEF,
         name="merge",
-    )(*operands)
+    )(*operands, *after)
 
 
 def shards(
@@ -585,16 +613,15 @@
     tokens = hidden_states.reshape(steps * rows, features)
     keys = cache_keys.reshape(rows, slots * kv, size)
     values = cache_values.reshape(rows, slots * kv, size)
-    swap, ring = lay.core_swap(), {d: lay.ring_step(d) for d in (1, -1)}
-    shard, *rows_args = begin(own, factor_up, cache_lengths, queries)
-    lengths, order, q = rows_args
+    swap, ring = lay.core_swap(), lay.ring_step()
     projections = projection_weight_matrices
     pair_count = rows // 2
-    depth = own.shape[2]
     last_step = lay.ring // 2
-    back = lay.ring_step(-1, 1)
-    caches, olds = [], []
-    buffers = []
+    buffers, caches = [], []
+
+    other, other_up = send(own, perm=swap), send(factor_up, perm=swap)
+    pair, up_pair, *rows_args = begin(own, factor_up, cache_lengths, queries)
+    pair, up_pair = pack(other, other_up, pair, up_pair)
 
     def attention(pairs, ready, quarter, after):
         nonlocal buffers
@@ -605,53 +632,48 @@
         caches.extend(out[3:])
         return out[3]
 
-    def project_one(part, arrays, after):
-        out = project(part, lay, buffers[2], projections, arrays, after)
-        buffers[2] = out[0]
-        olds.append(out[1])
-        return out[1], out[2:]
-
-    sent = {d: send(shard, perm=ring[d]) for d in ring}
+    came = send(pair, perm=ring)
+    up = send(up_pair, perm=lay.plane_step())
+    token = attention((0, 1), (0, 2), 0, [pair])
+    (came, up, tokens), token = after_all((came, up, tokens), token)
+    entries = [(0, 0, pair), (1, 0, came)]
+
+    sent, swapped = send(came, perm=ring), send(came, perm=swap)
+    up_y = [send(up, perm=lay.near_step(turn, 0)) for turn in range(1, lay.grp)]
+    up_z = [send(up, perm=lay.near_step(0, shift)) for shift in range(1, lay.block)]
     hidden = [tokens] + [send(tokens, perm=lay.feature_step(i)) for i in range(1, lay.tp)]
-    token = attention((0, 1), (0, 2), 0, [shard])
-    entries = [((0,), False, shard)]
-    came, swapped = {}, []
-    states = low = None
-    slot = n_low = 0
-    for step in range(1, last_step):
-        for d in ring:
-            slot += 1
-            held = [x for _, x in swapped] + (hidden if slot == 2 else [])
-            (came[d], held), token = after_all((sent[d], held), token)
-            entries.append(((-d * step,), False, came[d]))
-            entries += [(places, True, x) for (places, _), x in zip(swapped, held)]
-            sent[d] = send(came[d], perm=back if d < 0 and step + 1 == last_step else ring[d])
-            swapped = [((-d * step,), send(came[d], perm=swap))]
-            if slot == 1:
-                token = attention((1, 2), (2, pair_count), 1, [token])
-            elif slot == 2:
-                hidden = held[-lay.tp :]
-                token = attention((2, pair_count), (pair_count, pair_count), 2, [token])
-            elif slot == 3:
-                token, (states,) = project_one(0, hidden, [token])
-            elif slot == 4:
-                swapped.append(((0,), send(shard, perm=swap)))
-                token, _ = project_one(1, [states], [token])
-            elif slot == 5:
-                n_low = len(entries)
-                low = project_low(lay, entries, states, shape[0], depth, None, [token])
-                token = low
-    low = project_low(lay, entries[n_low:], states, shape[0], depth, low, [token])
-    forward, low = after_all(sent[1], low)
-    entries.append(((-last_step,), False, forward))
-    low = project_low(lay, entries[-1:], states, shape[0], depth, low, [])
-    n_low = len(entries)
-    (last, held), low = after_all((sent[-1], [x for _, x in swapped]), low)
-    entries += [(places, True, x) for (places, _), x in zip(swapped, held)]
-    entries.append(((last_step,), True, last))
-    return tuple(
-        merge(lay, shape, entries, n_low, buffers[2], states, low, olds, order, q, caches)
+    token = attention((1, pair_count), (2, pair_count), 1, [token])
+    (came, swapped, up_y, up_z), token = after_all((sent, swapped, up_y, up_z), token)
+    entries += [(1, 1, swapped), (2, 0, came)]
+    ups = [(0, 0, up)] + [(turn + 1, 0, x) for turn, x in enumerate(up_y)]
+    ups += [(0, shift + 1, x) for shift, x in enumerate(up_z)]
+
+    sent, swapped = send(came, perm=ring), send(came, perm=swap)
+    up_yz = [
+        (turn + 1, shift, send(x, perm=lay.near_step(0, shift)))
+        for turn, x in enumerate(up_y)
+        for shift in range(1, lay.block)
+    ]
+    w_buf, olds, states = project(lay, buffers[2], projections, hidden, [token])
+    (came, swapped, diagonal), token = after_all(
+        (sent, swapped, [x for _, _, x in up_yz]), olds
     )
+    entries += [(2, 1, swapped), (3, 0, came)]
+    ups += [(turn, shift, x) for (turn, shift, _), x in zip(up_yz, diagonal)]
+
+    for step in range(3, last_step - 1):
+        sent, swapped = send(came, perm=ring), send(came, perm=swap)
+        came, swapped = lax.optimization_barrier((sent, swapped))
+        entries += [(step, 1, swapped), (step + 1, 0, came)]
+    sent, swapped = send(came, perm=ring), send(came, perm=swap)
+    m, w_buf, *state = merge(lay, shape, entries, states, w_buf, ups, None, None, [token])
+    (came, swapped), low = after_all((sent, swapped), state[1])
+    entries = [(last_step - 1, 1, swapped), (last_step, 0, came)]
+    _, order, q = rows_args
+    m, _, attended = merge(
+        lay, shape, entries, states, w_buf, None, [m, state[0], low], (olds, order, q, caches), []
+    )
+    return m, attended
 
 
 def solution(mesh):

time: 43.8 us -> 40.8 us (0.932)
  waiting for transfers between devices: 7.16 us -> 2.27 us
  starting transfers between devices: 12.4 us -> 16.3 us
  Pallas kernels: 23.4 us -> 21.1 us
    ppermute x15 -> x13, waiting for transfers between devices: 7.15 us -> 0.55 us  [the longest x1 0.21 us: shards(): came = send(pair, perm=ring)]
    pallas_call x3 -> x2, Pallas kernels: 9.11 us -> 5.92 us  [cache_attention(): pl.pallas_call(functools.partial(attend_cache, pairs, ready, sizes, scale...]
    ppermute x15 -> x13, starting transfers between devices: 10.9 us -> 13.9 us  [the longest x1 4.41 us: shards(): send(up, perm=lay.near_step(0, shift))]
    ppermute x1, waiting for transfers between devices: 0.01 us -> 1.73 us  [shards(): send(tokens, perm=lay.feature_step(i))]
    pallas_call x7 -> x5, Pallas kernels: 14.3 us -> 15.2 us  [the longest x2 9.66 us: merge(): pl.pallas_call(functools.partial(merge_some, lay, [e[:2] for e in entries...]
    ppermute x1, starting transfers between devices: 1.49 us -> 2.39 us  [shards(): send(tokens, perm=lay.feature_step(i))]
  transfers between devices with their start and end apart: 16 -> 14, of which waited for: 3 -> 4; matrix products, arithmetic and copies ran while one was open for 0% -> 0% of each run, Pallas kernels for 31% -> 41%
where the time goes in v7:
time: 40.8 us; the launch traced here: 40.6 us
  Pallas kernels  21.1 us (52%)
  starting transfers between devices  16.3 us (40%)
  waiting for transfers between devices  2.27 us (6%)
  between operations  0.94 us (2%)
    pallas_call x2, Pallas kernels, merge(): pl.pallas_call(functools.partial(merge_some, lay, [e[:2] for e in entries...  9.66 us
    pallas_call x2, Pallas kernels, cache_attention(): pl.pallas_call(functools.partial(attend_cache, pairs, ready, sizes, scale...  5.92 us
    ppermute x1, starting transfers between devices, shards(): send(up, perm=lay.near_step(0, shift))  4.41 us
    pallas_call x1, Pallas kernels, project(): pl.pallas_call(functools.partial(project_old, lay, len(hidden)), out_shap...  4.29 us
    ppermute x6, starting transfers between devices, shards(): sent, swapped = (send(came, perm=ring), send(came, perm=swap))  4.01 us
    ppermute x1, starting transfers between devices, shards(): came = send(pair, perm=ring)  2.91 us
    ppermute x1, starting transfers between devices, shards(): send(tokens, perm=lay.feature_step(i))  2.39 us
    ppermute x1, waiting for transfers between devices, shards(): send(tokens, perm=lay.feature_step(i))  1.73 us
  transfers between devices with their start and end apart: 14, of which 4 were waited for; matrix products, arithmetic and copies ran while one was open for 0% of the time, Pallas kernels for 41%

profile of v7, /device:TPU:0, one launch (start us, length us, event | category | flops | bytes accessed | tf_op | source)
XLA Modules:
  0.0 40.6 jit_solution(6269330355278160352)
XLA Ops:
  0.6 0.0 copy-start
  0.6 0.5 %collective-permute-start = (bf16[2,64,512]{2,1,0:T(8,128)(2,1)}, bf16[2,64,512]{2,1,0:T(8,128)(2,1)S(1)}, u32[]{:S(2)}, u32[]{:S(2)}) collective-permute-start(bf16[2,64,512]{2,1,0:T(8,128)(2,1)} %bitcast.10), channel_id=1, source_target_pairs={{0,4},{1,5},{2,6},{3,7},{4,0},{5,1},{6,2},{7,3},{8,12},{9,13},{10,... | collective-permute-start | bytes 393224 | tf_op jit(solution)/shard_map/ppermute | solution.py:622
  1.2 0.1 collective-permute-start.1
  1.2 1.2 %begin.1 = (bf16[2,8,64,128]{3,2,1,0:T(8,128)(2,1)S(1)}, bf16[2,64,128]{2,1,0:T(8,128)(2,1)S(1)}, s32[8]{0:T(128)S(4)}, s32[8]{0:T(128)S(4)}, bf16[4,8,32,128]{3,2,1,0:T(8,128)(2,1)S(1)}) custom-call(bf16[2,64,512]{2,1,0:T(8,128)(2,1)} %bitcast.11, bf16[2,64,64]{2,1,0:T(8,128)(2,1)} %up.1, s32[8]{0:T(128)} %len_hbm.1, bf16[4,8,32,128]{3,2,1,0:T(8,128)(2,1)} %q_hbm.1), custom_call_target="tpu_custom_call" | custom-call | flops 1000 | bytes 1000 | tf_op jit(solution)/shard_map/begin/pallas_call | solution.py:167
  2.4 0.1 collective-permute-done.1.up
  2.6 0.0 collective-permute-done.down
  2.6 0.1 pack_other.1
  2.7 2.9 %collective-permute-start.2 = (bf16[2,8,64,128]{3,2,1,0:T(8,128)(2,1)S(1)}, bf16[2,8,64,128]{3,2,1,0:T(8,128)(2,1)S(1)}, u32[]{:S(2)}, u32[]{:S(2)}) collective-permute-start(bf16[2,8,64,128]{3,2,1,0:T(8,128)(2,1)S(1)} %get-tuple-element.44.refs_6_.refs_0_), channel_id=1, source_target_pairs={{0,8},{1,9},{2,0},{3,1},{4,6},{5,7},{6,14},{7,15},{8,16},{9,17},{1... | collective-permute-start | bytes 786440 | tf_op jit(solution)/shard_map/ppermute | solution.py:635
  5.6 0.7 %collective-permute-start.3 = (bf16[2,64,128]{2,1,0:T(8,128)(2,1)S(1)}, bf16[2,64,128]{2,1,0:T(8,128)(2,1)S(1)}, u32[]{:S(2)}, u32[]{:S(2)}) collective-permute-start(bf16[2,64,128]{2,1,0:T(8,128)(2,1)S(1)} %get-tuple-element.45), channel_id=1, source_target_pairs={{0,0},{16,1},{2,2},{18,3},{4,4},{20,5},{6,6},{22,7},{8,8},{24,9},{... | collective-permute-start | bytes 98312 | tf_op jit(solution)/shard_map/ppermute | solution.py:636
  6.2 3.4 %cache_attention.2 = (bf16[8,3072,128]{2,1,0:T(8,128)(2,1)S(1)}, bf16[8,3072,128]{2,1,0:T(8,128)(2,1)S(1)}, bf16[2,8192,512]{2,1,0:T(8,128)(2,1)S(1)}, f32[2,128,128]{2,1,0:T(8,128)S(1)}, f32[2,128,128]{2,1,0:T(8,128)S(1)}) custom-call(s32[8]{0:T(128)S(4)} %get-tuple-element.46.refs_0_, s32[8]{0:T(128)S(4)} %get-tuple-element.47.refs_1_.refs_4_, ...), custom_call_target="tpu_custom_call" | custom-call | flops 1000 | bytes 1000 | tf_op jit(solution)/shard_map/cache_attention/pallas_call | solution.py:322
  9.6 0.0 collective-permute-done.3.refs_7_
  9.6 0.2 collective-permute-done.2.refs_1_
  9.9 0.6 %collective-permute-start.5 = (bf16[2,8,64,128]{3,2,1,0:T(8,128)(2,1)S(1)}, bf16[2,8,64,128]{3,2,1,0:T(8,128)(2,1)S(1)}, u32[]{:S(2)}, u32[]{:S(2)}) collective-permute-start(bf16[2,8,64,128]{3,2,1,0:T(8,128)(2,1)S(1)} %collective-permute-done.2.refs_1_), channel_id=1, source_target_pairs={{0,4},{1,5},{2,6},{3,7},{4,0},{5,1},{6,2},{7,3},{8,12},{9,13},{10,... | collective-permute-start | bytes 786440 | tf_op jit(solution)/shard_map/ppermute | solution.py:641
  10.4 1.5 %collective-permute-start.4 = (bf16[2,8,64,128]{3,2,1,0:T(8,128)(2,1)S(1)}, bf16[2,8,64,128]{3,2,1,0:T(8,128)(2,1)S(1)}, u32[]{:S(2)}, u32[]{:S(2)}) collective-permute-start(bf16[2,8,64,128]{3,2,1,0:T(8,128)(2,1)S(1)} %collective-permute-done.2.refs_1_), channel_id=1, source_target_pairs={{0,8},{1,9},{2,0},{3,1},{4,6},{5,7},{6,14},{7,15},{8,16},{9,17},{1... | collective-permute-start | bytes 786440 | tf_op jit(solution)/shard_map/ppermute | solution.py:641
  11.9 4.4 %collective-permute-start.7 = (bf16[2,64,128]{2,1,0:T(8,128)(2,1)S(1)}, bf16[2,64,128]{2,1,0:T(8,128)(2,1)S(1)}, u32[]{:S(2)}, u32[]{:S(2)}) collective-permute-start(bf16[2,64,128]{2,1,0:T(8,128)(2,1)S(1)} %collective-permute-done.3.refs_7_), channel_id=1, source_target_pairs={{8,0},{9,1},{10,2},{11,3},{12,4},{13,5},{14,6},{15,7},{0,8},{1,9},... | collective-permute-start | bytes 98312 | tf_op jit(solution)/shard_map/ppermute | solution.py:643
  16.3 0.0 collective-permute-start.6
  16.4 0.0 copy-done
  16.4 2.4 %collective-permute-start.11 = (bf16[32,4096]{1,0:T(8,128)(2,1)S(1)}, bf16[32,4096]{1,0:T(8,128)(2,1)S(1)}, u32[]{:S(2)}, u32[]{:S(2)}) collective-permute-start(bf16[32,4096]{1,0:T(8,128)(2,1)S(1)} %bitcast.4), channel_id=1, source_target_pairs={{1,0},{0,1},{3,2},{2,3},{5,4},{4,5},{7,6},{6,7},{9,8},{8,9},{11,10... | collective-permute-start | bytes 786440 | tf_op jit(solution)/shard_map/ppermute | solution.py:644
  18.7 2.5 %cache_attention.3 = (bf16[8,3072,128]{2,1,0:T(8,128)(2,1)S(1)}, bf16[8,3072,128]{2,1,0:T(8,128)(2,1)S(1)}, bf16[2,8192,512]{2,1,0:T(8,128)(2,1)S(1)}, f32[6,128,128]{2,1,0:T(8,128)S(1)}, f32[6,128,128]{2,1,0:T(8,128)S(1)}) custom-call(s32[8]{0:T(128)S(4)} %get-tuple-element.46.refs_0_, ...), custom_call_target="tpu_custom_call", output_to_operand_aliasing={{0}: (6, {}), {1}: (7, {}), {2}: (8, {})} | custom-call | flops 1000 | bytes 1000 | tf_op jit(solution)/shard_map/cache_attention/pallas_call | solution.py:322
  21.3 0.0 collective-permute-done.7.refs_9_
  21.3 0.0 collective-permute-done.6.refs_8_
  21.3 0.0 collective-permute-done.5.refs_2_
  21.3 0.0 collective-permute-done.4.refs_3_
  21.3 0.1 collective-permute-start.9
  21.4 0.5 %collective-permute-start.8 = (bf16[2,8,64,128]{3,2,1,0:T(8,128)(2,1)S(1)}, bf16[2,8,64,128]{3,2,1,0:T(8,128)(2,1)S(1)}, u32[]{:S(2)}, u32[]{:S(2)}) collective-permute-start(bf16[2,8,64,128]{3,2,1,0:T(8,128)(2,1)S(1)} %collective-permute-done.4.refs_3_), channel_id=1, source_target_pairs={{0,8},{1,9},{2,0},{3,1},{4,6},{5,7},{6,14},{7,15},{8,16},{9,17},{1... | collective-permute-start | bytes 786440 | tf_op jit(solution)/shard_map/ppermute | solution.py:651
  21.9 1.3 %collective-permute-start.10 = (bf16[2,64,128]{2,1,0:T(8,128)(2,1)S(1)}, bf16[2,64,128]{2,1,0:T(8,128)(2,1)S(1)}, u32[]{:S(2)}, u32[]{:S(2)}) collective-permute-start(bf16[2,64,128]{2,1,0:T(8,128)(2,1)S(1)} %collective-permute-done.6.refs_8_), channel_id=1, source_target_pairs={{8,0},{9,1},{10,2},{11,3},{12,4},{13,5},{14,6},{15,7},{0,8},{1,9},... | collective-permute-start | bytes 98312 | tf_op jit(solution)/shard_map/ppermute | solution.py:653
  23.2 1.7 %collective-permute-done.11.refs_3_ = bf16[32,4096]{1,0:T(8,128)(2,1)S(1)} collective-permute-done((bf16[32,4096]{1,0:T(8,128)(2,1)S(1)}, bf16[32,4096]{1,0:T(8,128)(2,1)S(1)}, u32[]{:S(2)}, u32[]{:S(2)}) %collective-permute-start.11) | collective-permute-done | bytes 262176 | tf_op jit(solution)/shard_map/ppermute | solution.py:644
  24.9 4.3 %project.1 = (bf16[2,8192,512]{2,1,0:T(8,128)(2,1)S(1)}, f32[2,32,512]{2,1,0:T(8,128)S(1)}, bf16[2,32,4096]{2,1,0:T(8,128)(2,1)S(1)}) custom-call(bf16[2,8192,512]{2,1,0:T(8,128)(2,1)S(1)} %get-tuple-element.59.refs_0_, bf16[2,8192,512]{2,1,0:T(8,128)(2,1)} %refs_1_.1, bf16[32,4096]{1,0:T(8,128)(2,1)S(1)} %bitcast.5, ...), custom_call_target="tpu_custom_call", output_to_operand_aliasing={{0}: (0, {})} | custom-call | flops 1000 | bytes 1000 | tf_op jit(solution)/shard_map/project/pallas_call | solution.py:367
  29.2 0.0 collective-permute-done.10.refs_10_
  29.2 0.0 collective-permute-done.9.refs_4_
  29.2 0.0 collective-permute-done.8.refs_5_
  29.3 0.1 collective-permute-start.13
  29.3 1.3 %collective-permute-start.12 = (bf16[2,8,64,128]{3,2,1,0:T(8,128)(2,1)S(1)}, bf16[2,8,64,128]{3,2,1,0:T(8,128)(2,1)S(1)}, u32[]{:S(2)}, u32[]{:S(2)}) collective-permute-start(bf16[2,8,64,128]{3,2,1,0:T(8,128)(2,1)S(1)} %collective-permute-done.8.refs_5_), channel_id=1, source_target_pairs={{0,8},{1,9},{2,0},{3,1},{4,6},{5,7},{6,14},{7,15},{8,16},{9,17},{1... | collective-permute-start | bytes 786440 | tf_op jit(solution)/shard_map/ppermute | solution.py:668
  30.6 5.1 %merge.2 = (bf16[2,8192,512]{2,1,0:T(8,128)(2,1)}, bf16[2,8192,512]{2,1,0:T(8,128)(2,1)S(1)}, bf16[2,64,512]{2,1,0:T(8,128)(2,1)S(1)}, f32[2,32,64]{2,1,0:T(8,128)S(1)}) custom-call(bf16[2,8,64,128]{3,2,1,0:T(8,128)(2,1)S(1)} %get-tuple-element.44.refs_6_.refs_0_, ...), custom_call_target="tpu_custom_call", output_to_operand_aliasing={{1}: (11, {})} | custom-call | flops 1000 | bytes 1000 | tf_op jit(solution)/shard_map/merge/pallas_call | solution.py:583
  35.8 0.0 collective-permute-done.13.refs_0_
  35.8 0.2 collective-permute-done.12.refs_1_
  35.9 4.5 %merge.3 = (bf16[2,8192,512]{2,1,0:T(8,128)(2,1)}, bf16[2,8192,512]{2,1,0:T(8,128)(2,1)S(1)}, bf16[4,8,32,128]{3,2,1,0:T(8,128)(2,1)}) custom-call(bf16[2,8,64,128]{3,2,1,0:T(8,128)(2,1)S(1)} %collective-permute-done.13.refs_0_, bf16[2,8,64,128]{3,2,1,0:T(8,128)(2,1)S(1)} %collective-permute-done.12.refs_1_, ...), custom_call_target="tpu_custom_call", output_to_operand_aliasing={{0}: (12, {}), {1}: (13, {})} | custom-call | flops 1000 | bytes 1000 | tf_op jit(solution)/shard_map/merge/pallas_call | solution.py:583
Async XLA Ops:
  0.6 15.7 %copy-start = (bf16[4,8,4096]{2,1,0:T(8,128)(2,1)S(1)}, bf16[4,8,4096]{2,1,0:T(8,128)(2,1)}, u32[]{:S(2)}) copy-start(bf16[4,8,4096]{2,1,0:T(8,128)(2,1)} %param.8) | copy-start | bytes 786436
  0.6 1.9 %collective-permute-start = (bf16[2,64,512]{2,1,0:T(8,128)(2,1)}, bf16[2,64,512]{2,1,0:T(8,128)(2,1)S(1)}, u32[]{:S(2)}, u32[]{:S(2)}) collective-permute-start(bf16[2,64,512]{2,1,0:T(8,128)(2,1)} %bitcast.10), channel_id=1, source_target_pairs={{0,4},{1,5},{2,6},{3,7},{4,0},{5,1},{6,2},{7,3},{8,12},{9,13},{10,... | collective-permute-start | bytes 393224 | tf_op jit(solution)/shard_map/ppermute | solution.py:622
  1.2 1.4 %collective-permute-start.1 = (bf16[2,64,64]{2,1,0:T(8,128)(2,1)}, bf16[2,64,64]{2,1,0:T(8,128)(2,1)S(1)}, u32[]{:S(2)}, u32[]{:S(2)}) collective-permute-start(bf16[2,64,64]{2,1,0:T(8,128)(2,1)} %up.1), channel_id=1, source_target_pairs={{0,4},{1,5},{2,6},{3,7},{4,0},{5,1},{6,2},{7,3},{8,12},{9,13},{10,... | collective-permute-start | bytes 49160 | tf_op jit(solution)/shard_map/ppermute | solution.py:622
  2.7 7.2 %collective-permute-start.2 = (bf16[2,8,64,128]{3,2,1,0:T(8,128)(2,1)S(1)}, bf16[2,8,64,128]{3,2,1,0:T(8,128)(2,1)S(1)}, u32[]{:S(2)}, u32[]{:S(2)}) collective-permute-start(bf16[2,8,64,128]{3,2,1,0:T(8,128)(2,1)S(1)} %get-tuple-element.44.refs_6_.refs_0_), channel_id=1, source_target_pairs={{0,8},{1,9},{2,0},{3,1},{4,6},{5,7},{6,14},{7,15},{8,16},{9,17},{1... | collective-permute-start | bytes 786440 | tf_op jit(solution)/shard_map/ppermute | solution.py:635
  5.6 4.1 %collective-permute-start.3 = (bf16[2,64,128]{2,1,0:T(8,128)(2,1)S(1)}, bf16[2,64,128]{2,1,0:T(8,128)(2,1)S(1)}, u32[]{:S(2)}, u32[]{:S(2)}) collective-permute-start(bf16[2,64,128]{2,1,0:T(8,128)(2,1)S(1)} %get-tuple-element.45), channel_id=1, source_target_pairs={{0,0},{16,1},{2,2},{18,3},{4,4},{20,5},{6,6},{22,7},{8,8},{24,9},{... | collective-permute-start | bytes 98312 | tf_op jit(solution)/shard_map/ppermute | solution.py:636
  9.9 11.4 %collective-permute-start.5 = (bf16[2,8,64,128]{3,2,1,0:T(8,128)(2,1)S(1)}, bf16[2,8,64,128]{3,2,1,0:T(8,128)(2,1)S(1)}, u32[]{:S(2)}, u32[]{:S(2)}) collective-permute-start(bf16[2,8,64,128]{3,2,1,0:T(8,128)(2,1)S(1)} %collective-permute-done.2.refs_1_), channel_id=1, source_target_pairs={{0,4},{1,5},{2,6},{3,7},{4,0},{5,1},{6,2},{7,3},{8,12},{9,13},{10,... | collective-permute-start | bytes 786440 | tf_op jit(solution)/shard_map/ppermute | solution.py:641
  10.4 10.9 %collective-permute-start.4 = (bf16[2,8,64,128]{3,2,1,0:T(8,128)(2,1)S(1)}, bf16[2,8,64,128]{3,2,1,0:T(8,128)(2,1)S(1)}, u32[]{:S(2)}, u32[]{:S(2)}) collective-permute-start(bf16[2,8,64,128]{3,2,1,0:T(8,128)(2,1)S(1)} %collective-permute-done.2.refs_1_), channel_id=1, source_target_pairs={{0,8},{1,9},{2,0},{3,1},{4,6},{5,7},{6,14},{7,15},{8,16},{9,17},{1... | collective-permute-start | bytes 786440 | tf_op jit(solution)/shard_map/ppermute | solution.py:641
  11.9 9.3 %collective-permute-start.7 = (bf16[2,64,128]{2,1,0:T(8,128)(2,1)S(1)}, bf16[2,64,128]{2,1,0:T(8,128)(2,1)S(1)}, u32[]{:S(2)}, u32[]{:S(2)}) collective-permute-start(bf16[2,64,128]{2,1,0:T(8,128)(2,1)S(1)} %collective-permute-done.3.refs_7_), channel_id=1, source_target_pairs={{8,0},{9,1},{10,2},{11,3},{12,4},{13,5},{14,6},{15,7},{0,8},{1,9},... | collective-permute-start | bytes 98312 | tf_op jit(solution)/shard_map/ppermute | solution.py:643
  16.3 4.9 %collective-permute-start.6 = (bf16[2,64,128]{2,1,0:T(8,128)(2,1)S(1)}, bf16[2,64,128]{2,1,0:T(8,128)(2,1)S(1)}, u32[]{:S(2)}, u32[]{:S(2)}) collective-permute-start(bf16[2,64,128]{2,1,0:T(8,128)(2,1)S(1)} %collective-permute-done.3.refs_7_), channel_id=1, source_target_pairs={{2,0},{3,1},{0,2},{1,3},{6,4},{7,5},{4,6},{5,7},{10,8},{11,9},{8,1... | collective-permute-start | bytes 98312 | tf_op jit(solution)/shard_map/ppermute | solution.py:642
  16.4 8.6 %collective-permute-start.11 = (bf16[32,4096]{1,0:T(8,128)(2,1)S(1)}, bf16[32,4096]{1,0:T(8,128)(2,1)S(1)}, u32[]{:S(2)}, u32[]{:S(2)}) collective-permute-start(bf16[32,4096]{1,0:T(8,128)(2,1)S(1)} %bitcast.4), channel_id=1, source_target_pairs={{1,0},{0,1},{3,2},{2,3},{5,4},{4,5},{7,6},{6,7},{9,8},{8,9},{11,10... | collective-permute-start | bytes 786440 | tf_op jit(solution)/shard_map/ppermute | solution.py:644
  21.3 7.9 %collective-permute-start.9 = (bf16[2,8,64,128]{3,2,1,0:T(8,128)(2,1)S(1)}, bf16[2,8,64,128]{3,2,1,0:T(8,128)(2,1)S(1)}, u32[]{:S(2)}, u32[]{:S(2)}) collective-permute-start(bf16[2,8,64,128]{3,2,1,0:T(8,128)(2,1)S(1)} %collective-permute-done.4.refs_3_), channel_id=1, source_target_pairs={{0,4},{1,5},{2,6},{3,7},{4,0},{5,1},{6,2},{7,3},{8,12},{9,13},{10,... | collective-permute-start | bytes 786440 | tf_op jit(solution)/shard_map/ppermute | solution.py:651
  21.4 7.9 %collective-permute-start.8 = (bf16[2,8,64,128]{3,2,1,0:T(8,128)(2,1)S(1)}, bf16[2,8,64,128]{3,2,1,0:T(8,128)(2,1)S(1)}, u32[]{:S(2)}, u32[]{:S(2)}) collective-permute-start(bf16[2,8,64,128]{3,2,1,0:T(8,128)(2,1)S(1)} %collective-permute-done.4.refs_3_), channel_id=1, source_target_pairs={{0,8},{1,9},{2,0},{3,1},{4,6},{5,7},{6,14},{7,15},{8,16},{9,17},{1... | collective-permute-start | bytes 786440 | tf_op jit(solution)/shard_map/ppermute | solution.py:651
  21.9 7.3 %collective-permute-start.10 = (bf16[2,64,128]{2,1,0:T(8,128)(2,1)S(1)}, bf16[2,64,128]{2,1,0:T(8,128)(2,1)S(1)}, u32[]{:S(2)}, u32[]{:S(2)}) collective-permute-start(bf16[2,64,128]{2,1,0:T(8,128)(2,1)S(1)} %collective-permute-done.6.refs_8_), channel_id=1, source_target_pairs={{8,0},{9,1},{10,2},{11,3},{12,4},{13,5},{14,6},{15,7},{0,8},{1,9},... | collective-permute-start | bytes 98312 | tf_op jit(solution)/shard_map/ppermute | solution.py:653
  29.3 6.5 %collective-permute-start.13 = (bf16[2,8,64,128]{3,2,1,0:T(8,128)(2,1)S(1)}, bf16[2,8,64,128]{3,2,1,0:T(8,128)(2,1)S(1)}, u32[]{:S(2)}, u32[]{:S(2)}) collective-permute-start(bf16[2,8,64,128]{3,2,1,0:T(8,128)(2,1)S(1)} %collective-permute-done.8.refs_5_), channel_id=1, source_target_pairs={{0,4},{1,5},{2,6},{3,7},{4,0},{5,1},{6,2},{7,3},{8,12},{9,13},{10,... | collective-permute-start | bytes 786440 | tf_op jit(solution)/shard_map/ppermute | solution.py:668
  29.3 6.6 %collective-permute-start.12 = (bf16[2,8,64,128]{3,2,1,0:T(8,128)(2,1)S(1)}, bf16[2,8,64,128]{3,2,1,0:T(8,128)(2,1)S(1)}, u32[]{:S(2)}, u32[]{:S(2)}) collective-permute-start(bf16[2,8,64,128]{3,2,1,0:T(8,128)(2,1)S(1)} %collective-permute-done.8.refs_5_), channel_id=1, source_target_pairs={{0,8},{1,9},{2,0},{3,1},{4,6},{5,7},{6,14},{7,15},{8,16},{9,17},{1... | collective-permute-start | bytes 786440 | tf_op jit(solution)/shard_map/ppermute | solution.py:668

commit v8 on v7

--- a/solution.py
+++ b/solution.py
@@ -79,7 +79,7 @@
         ]
 
 
-BRIEF = pl.CostEstimate(flops=1000, bytes_accessed=1000, transcendentals=0)
+TYPICAL = pl.CostEstimate(flops=3 * 10**9, bytes_accessed=10**7, transcendentals=0)
 
 
 def over(x, n):
@@ -119,18 +119,6 @@
             act(slots)
 
         below = slots
-
-
-def quarter_copies(quarter, src, dst, sems):
-    k, half = divmod(quarter, 2)
-    rows = dst.shape[1] // (2 * sems.shape[0])
-    spans = [
-        pl.ds((half * sems.shape[0] + i) * rows, rows) for i in range(sems.shape[0])
-    ]
-    return [
-        pltpu.make_async_copy(src.at[k, span], dst.at[k, span], sems.at[i])
-        for i, span in enumerate(spans)
-    ]
 
 
 def up_columns(up):
@@ -181,7 +169,7 @@
             pltpu.SemaphoreType.DMA((3,)),
         ],
         compiler_params=pltpu.CompilerParams(vmem_limit_bytes=2 * MIB),
-        cost_estimate=BRIEF,
+        cost_estimate=TYPICAL,
         name="begin",
     )(pinned(down), pinned(up), pinned(lengths), pinned(queries))
 
@@ -204,15 +192,14 @@
         out_specs=(VMEM, VMEM),
         input_output_aliases={2: 0, 3: 1},
         compiler_params=pltpu.CompilerParams(vmem_limit_bytes=2 * MIB),
-        cost_estimate=BRIEF,
+        cost_estimate=TYPICAL,
         name="pack_other",
     )(down, up, pinned(pair, pltpu.VMEM), pinned(up_pair, pltpu.VMEM))
 
 
-def attend_cache(pairs, ready, sizes, scale, quarter, *refs):
-    lengths, order, q_ref, k_hbm, v_hbm, w_hbm = refs[:6]
-    sems, w_sems = refs[-2:]
-    k_buf, v_buf, w_buf, *outs = refs[-7:-2]
+def attend_cache(pairs, ready, sizes, scale, *refs):
+    lengths, order, q_ref, k_hbm, v_hbm = refs[:5]
+    k_buf, v_buf, *outs, sems = refs[-5:]
     done = pairs[0]
     o_ref, lse_ref = outs[:2]
     steps, _, heads, size = q_ref.shape
@@ -242,9 +229,6 @@
 
     for pair in range(*ready):
         by_length(lengths[order[2 * pair]], sizes, functools.partial(start, pair))
-    w_copies = quarter_copies(quarter, w_hbm, w_buf, w_sems)
-    for copy in w_copies:
-        copy.start()
 
     row_head = over(within(lax.broadcasted_iota(jnp.int32, (lanes, size), 0), heads), heads // kv)
     slot_head = within(lax.broadcasted_iota(jnp.int32, (lanes, size), 1), kv)
@@ -296,15 +280,13 @@
         pl.loop(*pairs)(attend)
     for pair in range(max(pairs[1], ready[0]), ready[1]):
         by_length(lengths[order[2 * pair]], sizes, functools.partial(finish, (0, 1), pair))
-    for copy in w_copies:
-        copy.wait()
 
 
 def like(x):
     return pltpu.VMEM(x.shape, x.dtype)
 
 
-def cache_attention(pairs, ready, rows_args, caches, weights, quarter, buffers, sizes, after):
+def cache_attention(pairs, ready, rows_args, caches, buffers, sizes, after):
     lengths, order, queries = rows_args
     keys, values = caches
     rows, steps, _, heads, size = (keys.shape[0], *queries.shape)
@@ -314,34 +296,30 @@
     piece = pltpu.VMEM((count, steps * heads, size), jnp.float32)
     operands = [pinned(x, pltpu.SMEM) for x in (lengths, order)]
     operands += [pinned(queries, pltpu.VMEM)]
-    operands += [pinned(x) for x in (keys, values, weights)]
+    operands += [pinned(keys), pinned(values)]
     aliases = {len(operands) + i: i for i in range(len(buffers))}
-    specs = [SMEM, SMEM, VMEM, HBM, HBM, HBM] + [VMEM] * len(buffers) + [ANY] * len(after)
+    specs = [SMEM, SMEM, VMEM, HBM, HBM] + [VMEM] * len(buffers) + [ANY] * len(after)
     operands += [pinned(b, pltpu.VMEM) for b in buffers] + after
-    out_shape = [pltpu.VMEM(x.shape, x.dtype) for x in (keys, values, weights)] + [piece] * 2
+    out_shape = [like(keys), like(values), piece, piece]
     return pl.pallas_call(
-        functools.partial(attend_cache, pairs, ready, sizes, scale, quarter),
+        functools.partial(attend_cache, pairs, ready, sizes, scale),
         out_shape=out_shape,
         in_specs=specs,
         out_specs=[VMEM] * len(out_shape),
         input_output_aliases=aliases,
         scratch_shapes=[
             pltpu.SemaphoreType.DMA((rows // 2, 2, 2)),
-            pltpu.SemaphoreType.DMA((4,)),
         ],
         compiler_params=pltpu.CompilerParams(vmem_limit_bytes=8 * MIB),
-        cost_estimate=BRIEF,
+        cost_estimate=TYPICAL,
         name="cache_attention",
     )(*operands)
 
 
 def project_old(lay, n_hidden, *refs):
-    w_hbm, *hidden = refs[1 : 2 + n_hidden]
-    w_buf, out_ref, h_ref, sems = refs[-4:]
+    w_buf, *hidden = refs[: 1 + n_hidden]
+    out_ref, h_ref = refs[-2:]
     tp = lax.axis_index("tp")
-    copies = [quarter_copies(2 + i, w_hbm, w_buf, sems.at[i]) for i in range(2)]
-    for copy in copies[0] + copies[1]:
-        copy.start()
     for i, h in enumerate(hidden):
         h_ref[lax.rem(tp + i, lay.tp)] = h[...]
     features = h_ref.shape[2]
@@ -349,9 +327,6 @@
     for k in range(2):
         total = jnp.zeros(out_ref.shape[1:], jnp.float32)
         for t in range(lay.tp):
-            if k == 1 and t % (lay.tp // 2) == 0:
-                for copy in copies[t // (lay.tp // 2)]:
-                    copy.wait()
             for low in range(0, features, chunk):
                 start = t * features + low
                 total += jnp.dot(
@@ -362,23 +337,20 @@
         out_ref[k] = total
 
 
-def project(lay, w_buf, weights, hidden, after):
+def project(lay, w_buf, hidden, after):
     tokens, features = hidden[0].shape
     return pl.pallas_call(
         functools.partial(project_old, lay, len(hidden)),
         out_shape=(
-            like(w_buf),
-            pltpu.VMEM((2, tokens, weights.shape[2]), jnp.float32),
+            pltpu.VMEM((2, tokens, w_buf.shape[2]), jnp.float32),
             pltpu.VMEM((lay.tp, tokens, features), jnp.bfloat16),
         ),
-        in_specs=[VMEM, HBM] + [VMEM] * len(hidden) + [ANY] * len(after),
-        out_specs=(VMEM, VMEM, VMEM),
-        input_output_aliases={0: 0},
-        scratch_shapes=[pltpu.SemaphoreType.DMA((2, 4))],
+        in_specs=[VMEM] * (1 + len(hidden)) + [ANY] * len(after),
+        out_specs=(VMEM, VMEM),
         compiler_params=pltpu.CompilerParams(vmem_limit_bytes=4 * MIB),
-        cost_estimate=BRIEF,
+        cost_estimate=TYPICAL,
         name="project",
-    )(pinned(w_buf, pltpu.VMEM), pinned(weights), *hidden, *after)
+    )(pinned(w_buf, pltpu.VMEM), *hidden, *after)
 
 
 class Place:
@@ -428,14 +400,14 @@
     downs = take(len(plan))
     (h_buf,) = take(1)
     if first:
-        up_refs = take(len(ups))
-        weights = refs[1]
-        m_hbm, weights, u_buf, low_out, m_buf, sems, u_parts = refs[-7:]
+        up_refs = refs[: len(ups)]
+        weights = refs[len(ups)]
+        m_hbm, u_buf, low_out, m_buf, sems, u_parts = refs[-6:]
     else:
         old, order, q_ref = take(3)
         caches = [take(2) for _ in range(n_caches)]
-        u_buf, low_in = take(2)
-        m_hbm, weights, out_ref, m_buf, sems = refs[-5:]
+        u_buf, low_in, _, weights = take(4)
+        m_hbm, out_hbm, m_buf, sems, out_buf, out_sem = refs[-6:]
     pairs, depth, width = m_buf.shape[1:]
     cut = min(width, 256)
     lanes = downs[0].shape[-1]
@@ -458,6 +430,23 @@
                 ],
                 axis=1,
             )
+
+    if last:
+        new = []
+        for k in range(pairs):
+            low = place.add_low(low_in[k], k, shards, h_buf, depth)
+            high = low.astype(jnp.bfloat16)
+            rest = (low - high.astype(jnp.float32)).astype(jnp.bfloat16)
+            new.append(
+                (
+                    old[k]
+                    + jnp.dot(high, u_buf[k], preferred_element_type=jnp.float32)
+                    + jnp.dot(rest, u_buf[k], preferred_element_type=jnp.float32)
+                ).astype(jnp.bfloat16)
+            )
+        add_new_tokens(q_ref, order, caches, new, out_buf, scale)
+        out_copy = pltpu.make_async_copy(out_buf, out_hbm, out_sem)
+        out_copy.start()
 
     chunk = min(depth, 256)
     copies = []
@@ -489,25 +478,11 @@
             low_out[k] = place.add_low(
                 jnp.zeros(low_out.shape[1:], jnp.float32), k, shards, h_buf, depth
             )
-    if last:
-        new = []
-        for k in range(pairs):
-            low = place.add_low(low_in[k], k, shards, h_buf, depth)
-            high = low.astype(jnp.bfloat16)
-            rest = (low - high.astype(jnp.float32)).astype(jnp.bfloat16)
-            new.append(
-                (
-                    old[k]
-                    + jnp.dot(high, u_buf[k], preferred_element_type=jnp.float32)
-                    + jnp.dot(rest, u_buf[k], preferred_element_type=jnp.float32)
-                ).astype(jnp.bfloat16)
-            )
-        add_new_tokens(q_ref, order, caches, new, out_ref, scale)
-    for copy in copies:
+    for copy in copies + ([out_copy] if last else []):
         copy.wait()
 
 
-def add_new_tokens(q_ref, order, caches, new, out_ref, scale):
+def add_new_tokens(q_ref, order, caches, new, out_buf, scale):
     steps, rows, heads, size = q_ref.shape
     kv = new[0].shape[1] // size
     new = [
@@ -520,23 +495,26 @@
     same_head = over(within(left, heads), heads // kv) == over(right, steps * rows)
     earlier = within(over(right, rows), steps) <= over(left, heads)
     right_row = jnp.where(same_head & earlier, within(right, rows), -1)
-    spots = [(o, lse, i) for o, lse in caches for i in range(o.shape[0])]
-    for spot, (o_ref, lse_ref, i) in enumerate(spots):
-        row = order[spot]
-        q = q_ref[:, row].reshape(lanes, size)
-        s = lax.dot_general(
-            q, new[0], (((1,), (1,)), ((), ())), preferred_element_type=jnp.float32
-        )
-        s = jnp.where(right_row == row, s * scale, -jnp.inf)
-        lse = lse_ref[i]
-        highest = jnp.maximum(jnp.max(s, axis=1, keepdims=True), lse)
-        p = jnp.exp2(s - highest[:, :n])
-        old = jnp.exp2(lse - highest)
-        divisor = jnp.sum(p, axis=1, keepdims=True) + old
-        o = old * o_ref[i] + jnp.dot(
-            p.astype(jnp.bfloat16), new[1], preferred_element_type=jnp.float32
-        )
-        out_ref[:, row] = (o / divisor).reshape(steps, heads, size).astype(out_ref.dtype)
+
+    def all_rows(pieces):
+        return jnp.concatenate(list(pieces), axis=0)
+
+    q = all_rows(q_ref[:, order[spot]].reshape(lanes, size) for spot in range(rows))
+    s = lax.dot_general(q, new[0], (((1,), (1,)), ((), ())), preferred_element_type=jnp.float32)
+    bias = all_rows(
+        jnp.where(right_row == order[spot], 0.0, -jnp.inf) for spot in range(rows)
+    )
+    s = s * scale + bias
+    lse = all_rows(ref[i] for _, ref in caches for i in range(ref.shape[0]))
+    highest = jnp.maximum(jnp.max(s, axis=1, keepdims=True), lse)
+    p = jnp.exp2(s - highest[:, :n])
+    old = jnp.exp2(lse - highest)
+    divisor = jnp.sum(p, axis=1, keepdims=True) + old
+    o = old * all_rows(ref[i] for ref, _ in caches for i in range(ref.shape[0]))
+    o = (o + jnp.dot(p.astype(jnp.bfloat16), new[1], preferred_element_type=jnp.float32)) / divisor
+    for spot in range(rows):
+        piece = o[spot * lanes : (spot + 1) * lanes].astype(out_buf.dtype)
+        out_buf[:, order[spot]] = piece.reshape(steps, heads, size)
 
 
 def merge(lay, shape, entries, states, w_buf, ups, state, final, after):
@@ -556,14 +534,13 @@
     if state is None:
         operands += [x for _, _, x in ups] + [pinned(w_buf, pltpu.VMEM)]
         specs += [VMEM] * (len(ups) + 1)
-        aliases = {len(operands) - 1: 1}
+        aliases = {}
         out_shape = [
             merged,
-            like(w_buf),
             pltpu.VMEM(u_shape, jnp.bfloat16),
             pltpu.VMEM(low_shape, jnp.float32),
         ]
-        out_specs = [HBM, VMEM, VMEM, VMEM]
+        out_specs = [HBM, VMEM, VMEM]
         scratch.append(pltpu.VMEM((per_lane, rank, pairs * width // per_lane), jnp.bfloat16))
         n_caches, scale = 0, 0.0
         plan_ups = [(turn, shift) for turn, shift, _ in ups]
@@ -575,9 +552,10 @@
         operands += [pinned(u_buf, pltpu.VMEM), pinned(low, pltpu.VMEM)]
         operands += [pinned(m_prev), pinned(w_buf, pltpu.VMEM)]
         specs += [VMEM, VMEM, HBM, VMEM]
-        aliases = {len(operands) - 2: 0, len(operands) - 1: 1}
-        out_shape = [merged, like(w_buf), jax.ShapeDtypeStruct(queries.shape, jnp.bfloat16)]
-        out_specs = [HBM, VMEM, VMEM]
+        aliases = {len(operands) - 2: 0}
+        out_shape = [merged, pltpu.HBM(queries.shape, jnp.bfloat16)]
+        out_specs = [HBM, HBM]
+        scratch += [pltpu.VMEM(queries.shape, jnp.bfloat16), pltpu.SemaphoreType.DMA]
         n_caches, scale = len(caches) // 2, LOG2E / math.sqrt(queries.shape[3])
         plan_ups = None
     return pl.pallas_call(
@@ -588,7 +566,7 @@
         input_output_aliases=aliases,
         scratch_shapes=scratch,
         compiler_params=pltpu.CompilerParams(vmem_limit_bytes=18 * MIB),
-        cost_estimate=BRIEF,
+        cost_estimate=TYPICAL,
         name="merge",
     )(*operands, *after)
 
@@ -614,7 +592,6 @@
     keys = cache_keys.reshape(rows, slots * kv, size)
     values = cache_values.reshape(rows, slots * kv, size)
     swap, ring = lay.core_swap(), lay.ring_step()
-    projections = projection_weight_matrices
     pair_count = rows // 2
     last_step = lay.ring // 2
     buffers, caches = [], []
@@ -623,18 +600,16 @@
     pair, up_pair, *rows_args = begin(own, factor_up, cache_lengths, queries)
     pair, up_pair = pack(other, other_up, pair, up_pair)
 
-    def attention(pairs, ready, quarter, after):
+    def attention(pairs, ready, after):
         nonlocal buffers
-        out = cache_attention(
-            pairs, ready, rows_args, (keys, values), projections, quarter, buffers, sizes, after
-        )
-        buffers = list(out[:3])
-        caches.extend(out[3:])
-        return out[3]
+        out = cache_attention(pairs, ready, rows_args, (keys, values), buffers, sizes, after)
+        buffers = list(out[:2])
+        caches.extend(out[2:])
+        return out[2]
 
     came = send(pair, perm=ring)
     up = send(up_pair, perm=lay.plane_step())
-    token = attention((0, 1), (0, 2), 0, [pair])
+    token = attention((0, 1), (0, 2), [pair])
     (came, up, tokens), token = after_all((came, up, tokens), token)
     entries = [(0, 0, pair), (1, 0, came)]
 
@@ -642,19 +617,20 @@
     up_y = [send(up, perm=lay.near_step(turn, 0)) for turn in range(1, lay.grp)]
     up_z = [send(up, perm=lay.near_step(0, shift)) for shift in range(1, lay.block)]
     hidden = [tokens] + [send(tokens, perm=lay.feature_step(i)) for i in range(1, lay.tp)]
-    token = attention((1, pair_count), (2, pair_count), 1, [token])
+    token = attention((1, pair_count), (2, pair_count), [token])
     (came, swapped, up_y, up_z), token = after_all((sent, swapped, up_y, up_z), token)
     entries += [(1, 1, swapped), (2, 0, came)]
     ups = [(0, 0, up)] + [(turn + 1, 0, x) for turn, x in enumerate(up_y)]
     ups += [(0, shift + 1, x) for shift, x in enumerate(up_z)]
 
-    sent, swapped = send(came, perm=ring), send(came, perm=swap)
     up_yz = [
         (turn + 1, shift, send(x, perm=lay.near_step(0, shift)))
         for turn, x in enumerate(up_y)
         for shift in range(1, lay.block)
     ]
-    w_buf, olds, states = project(lay, buffers[2], projections, hidden, [token])
+    sent, swapped = send(came, perm=ring), send(came, perm=swap)
+    w_buf = projection_weight_matrices
+    olds, states = project(lay, w_buf, hidden, [token])
     (came, swapped, diagonal), token = after_all(
         (sent, swapped, [x for _, _, x in up_yz]), olds
     )
@@ -666,11 +642,11 @@
         came, swapped = lax.optimization_barrier((sent, swapped))
         entries += [(step, 1, swapped), (step + 1, 0, came)]
     sent, swapped = send(came, perm=ring), send(came, perm=swap)
-    m, w_buf, *state = merge(lay, shape, entries, states, w_buf, ups, None, None, [token])
+    m, *state = merge(lay, shape, entries, states, w_buf, ups, None, None, [token])
     (came, swapped), low = after_all((sent, swapped), state[1])
     entries = [(last_step - 1, 1, swapped), (last_step, 0, came)]
     _, order, q = rows_args
-    m, _, attended = merge(
+    m, attended = merge(
         lay, shape, entries, states, w_buf, None, [m, state[0], low], (olds, order, q, caches), []
     )
     return m, attended

time: 40.8 us -> 40.4 us (level)
  Pallas kernels: 21.1 us -> 18.4 us
  starting transfers between devices: 16.3 us -> 17.7 us
  waiting for transfers between devices: 2.27 us -> 3.25 us
    ppermute x1, starting transfers between devices: 0.01 us -> 2.95 us  [shards(): up_y = [send(up, perm=lay.near_step(turn, 0)) for turn in range(1, lay.grp)]]
    ppermute x6, starting transfers between devices: 4.01 us -> 2.45 us  [shards(): sent, swapped = (send(came, perm=ring), send(came, perm=swap))]
    ppermute x6, waiting for transfers between devices: 0.18 us -> 1.7 us  [shards(): sent, swapped = (send(came, perm=ring), send(came, perm=swap))]
    pallas_call x1, Pallas kernels: 4.29 us -> 2.95 us  [project(): pl.pallas_call(functools.partial(project_old, lay, len(hidden)), out_shap...]
    ppermute x1, waiting for transfers between devices: 1.73 us -> 0.46 us  [shards(): send(tokens, perm=lay.feature_step(i))]
    pallas_call x2, Pallas kernels: 9.66 us -> 8.55 us  [merge(): pl.pallas_call(functools.partial(merge_some, lay, [e[:2] for e in entries...]
    ppermute x1, starting transfers between devices: 4.41 us -> 3.68 us  [shards(): send(up, perm=lay.near_step(0, shift))]
    ppermute x1, waiting for transfers between devices: 0.21 us -> 0.8 us  [shards(): came = send(pair, perm=ring)]
  transfers between devices with their start and end apart: 14 -> 14, of which waited for: 4 -> 5; matrix products, arithmetic and copies ran while one was open for 0% -> 0% of each run, Pallas kernels for 41% -> 37%
where the time goes in v8:
time: 40.4 us
  Pallas kernels  18.4 us (46%)
  starting transfers between devices  17.7 us (44%)
  waiting for transfers between devices  3.25 us (8%)
  between operations  0.93 us (2%)
    pallas_call x2, Pallas kernels, merge(): pl.pallas_call(functools.partial(merge_some, lay, [e[:2] for e in entries...  8.55 us
    pallas_call x2, Pallas kernels, cache_attention(): pl.pallas_call(functools.partial(attend_cache, pairs, ready, sizes, scale...  5.69 us
    ppermute x1, starting transfers between devices, shards(): send(up, perm=lay.near_step(0, shift))  3.68 us
    ppermute x1, starting transfers between devices, shards(): up_y = [send(up, perm=lay.near_step(turn, 0)) for turn in range(1, lay.grp)]  2.95 us
    pallas_call x1, Pallas kernels, project(): pl.pallas_call(functools.partial(project_old, lay, len(hidden)), out_shap...  2.95 us
    ppermute x1, starting transfers between devices, shards(): came = send(pair, perm=ring)  2.8 us
    ppermute x1, starting transfers between devices, shards(): send(tokens, perm=lay.feature_step(i))  2.7 us
    ppermute x6, starting transfers between devices, shards(): sent, swapped = (send(came, perm=ring), send(came, perm=swap))  2.45 us
  transfers between devices with their start and end apart: 14, of which 5 were waited for; matrix products, arithmetic and copies ran while one was open for 0% of the time, Pallas kernels for 37%

profile of v8, /device:TPU:0, one launch (start us, length us, event | category | flops | bytes accessed | tf_op | source)
XLA Modules:
  0.0 40.4 jit_solution(3026934611946032990)
XLA Ops:
  0.6 0.5 %collective-permute-start.1 = (bf16[2,64,64]{2,1,0:T(8,128)(2,1)}, bf16[2,64,64]{2,1,0:T(8,128)(2,1)S(1)}, u32[]{:S(2)}, u32[]{:S(2)}) collective-permute-start(bf16[2,64,64]{2,1,0:T(8,128)(2,1)} %up.1), channel_id=1, source_target_pairs={{0,4},{1,5},{2,6},{3,7},{4,0},{5,1},{6,2},{7,3},{8,12},{9,13},{10,... | collective-permute-start | bytes 49160 | tf_op jit(solution)/shard_map/ppermute | solution.py:599
  1.1 0.1 collective-permute-start
  1.2 1.2 %begin.1 = (bf16[2,8,64,128]{3,2,1,0:T(8,128)(2,1)S(1)}, bf16[2,64,128]{2,1,0:T(8,128)(2,1)S(1)}, s32[8]{0:T(128)S(4)}, s32[8]{0:T(128)S(4)}, bf16[4,8,32,128]{3,2,1,0:T(8,128)(2,1)S(1)}) custom-call(bf16[2,64,512]{2,1,0:T(8,128)(2,1)} %bitcast.13, bf16[2,64,64]{2,1,0:T(8,128)(2,1)} %up.1, s32[8]{0:T(128)} %len_hbm.1, bf16[4,8,32,128]{3,2,1,0:T(8,128)(2,1)} %q_hbm.1), custom_call_target="tpu_custom_call" | custom-call | flops 3000000000 | bytes 10000000 | tf_op jit(solution)/shard_map/begin/pallas_call | solution.py:155
  2.4 0.0 collective-permute-done.1.up
  2.4 0.3 collective-permute-done.down
  2.7 0.1 pack_other.1
  2.8 0.7 %collective-permute-start.3 = (bf16[2,64,128]{2,1,0:T(8,128)(2,1)S(1)}, bf16[2,64,128]{2,1,0:T(8,128)(2,1)S(1)}, u32[]{:S(2)}, u32[]{:S(2)}) collective-permute-start(bf16[2,64,128]{2,1,0:T(8,128)(2,1)S(1)} %get-tuple-element.39), channel_id=1, source_target_pairs={{0,0},{16,1},{2,2},{18,3},{4,4},{20,5},{6,6},{22,7},{8,8},{24,9},{... | collective-permute-start | bytes 98312 | tf_op jit(solution)/shard_map/ppermute | solution.py:611
  3.4 2.8 %collective-permute-start.2 = (bf16[2,8,64,128]{3,2,1,0:T(8,128)(2,1)S(1)}, bf16[2,8,64,128]{3,2,1,0:T(8,128)(2,1)S(1)}, u32[]{:S(2)}, u32[]{:S(2)}) collective-permute-start(bf16[2,8,64,128]{3,2,1,0:T(8,128)(2,1)S(1)} %get-tuple-element.38.refs_5_.refs_0_), channel_id=1, source_target_pairs={{0,8},{1,9},{2,0},{3,1},{4,6},{5,7},{6,14},{7,15},{8,16},{9,17},{1... | collective-permute-start | bytes 786440 | tf_op jit(solution)/shard_map/ppermute | solution.py:610
  6.2 0.0 copy-start
  6.2 0.0 slice-start
  6.2 0.0 slice-start.1
  6.2 3.5 %cache_attention.2 = (bf16[8,3072,128]{2,1,0:T(8,128)(2,1)S(1)}, bf16[8,3072,128]{2,1,0:T(8,128)(2,1)S(1)}, f32[2,128,128]{2,1,0:T(8,128)S(1)}, f32[2,128,128]{2,1,0:T(8,128)S(1)}) custom-call(s32[8]{0:T(128)S(4)} %get-tuple-element.40.refs_0_, s32[8]{0:T(128)S(4)} %get-tuple-element.41.refs_1_.refs_4_, ...), custom_call_target="tpu_custom_call" | custom-call | flops 3000000000 | bytes 10000000 | tf_op jit(solution)/shard_map/cache_attention/pallas_call | solution.py:304
  9.7 0.0 collective-permute-done.3.refs_7_
  9.7 0.8 %collective-permute-done.2.refs_1_ = bf16[2,8,64,128]{3,2,1,0:T(8,128)(2,1)S(1)} collective-permute-done((bf16[2,8,64,128]{3,2,1,0:T(8,128)(2,1)S(1)}, bf16[2,8,64,128]{3,2,1,0:T(8,128)(2,1)S(1)}, u32[]{:S(2)}, u32[]{:S(2)}) %collective-permute-start.2) | collective-permute-done | bytes 262176 | tf_op jit(solution)/shard_map/ppermute | solution.py:610
  10.5 3.7 %collective-permute-start.7 = (bf16[2,64,128]{2,1,0:T(8,128)(2,1)S(1)}, bf16[2,64,128]{2,1,0:T(8,128)(2,1)S(1)}, u32[]{:S(2)}, u32[]{:S(2)}) collective-permute-start(bf16[2,64,128]{2,1,0:T(8,128)(2,1)S(1)} %collective-permute-done.3.refs_7_), channel_id=1, source_target_pairs={{8,0},{9,1},{10,2},{11,3},{12,4},{13,5},{14,6},{15,7},{0,8},{1,9},... | collective-permute-start | bytes 98312 | tf_op jit(solution)/shard_map/ppermute | solution.py:618
  14.2 3.0 %collective-permute-start.6 = (bf16[2,64,128]{2,1,0:T(8,128)(2,1)S(1)}, bf16[2,64,128]{2,1,0:T(8,128)(2,1)S(1)}, u32[]{:S(2)}, u32[]{:S(2)}) collective-permute-start(bf16[2,64,128]{2,1,0:T(8,128)(2,1)S(1)} %collective-permute-done.3.refs_7_), channel_id=1, source_target_pairs={{2,0},{3,1},{0,2},{1,3},{6,4},{7,5},{4,6},{5,7},{10,8},{11,9},{8,1... | collective-permute-start | bytes 98312 | tf_op jit(solution)/shard_map/ppermute | solution.py:617
  17.2 0.0 collective-permute-start.5
  17.2 0.0 collective-permute-start.4
  17.2 0.0 copy-done
  17.2 2.7 %collective-permute-start.11 = (bf16[32,4096]{1,0:T(8,128)(2,1)S(1)}, bf16[32,4096]{1,0:T(8,128)(2,1)S(1)}, u32[]{:S(2)}, u32[]{:S(2)}) collective-permute-start(bf16[32,4096]{1,0:T(8,128)(2,1)S(1)} %bitcast.6), channel_id=1, source_target_pairs={{1,0},{0,1},{3,2},{2,3},{5,4},{4,5},{7,6},{6,7},{9,8},{8,9},{11,10... | collective-permute-start | bytes 786440 | tf_op jit(solution)/shard_map/ppermute | solution.py:619
  19.9 0.0 slice-start.2
  19.9 0.0 slice-start.3
  19.9 2.2 %cache_attention.3 = (bf16[8,3072,128]{2,1,0:T(8,128)(2,1)S(1)}, bf16[8,3072,128]{2,1,0:T(8,128)(2,1)S(1)}, f32[6,128,128]{2,1,0:T(8,128)S(1)}, f32[6,128,128]{2,1,0:T(8,128)S(1)}) custom-call(s32[8]{0:T(128)S(4)} %get-tuple-element.40.refs_0_, s32[8]{0:T(128)S(4)} %get-tuple-element.41.refs_1_.refs_4_, ...), custom_call_target="tpu_custom_call", output_to_operand_aliasing={{0}: (5, {}), {1}: (6, {})} | custom-call | flops 3000000000 | bytes 10000000 | tf_op jit(solution)/shard_map/cache_attention/pallas_call | solution.py:304
  22.1 0.0 collective-permute-done.7.refs_9_
  22.1 0.0 collective-permute-done.6.refs_8_
  22.1 0.0 collective-permute-done.5.refs_2_
  22.1 1.4 %collective-permute-done.4.refs_3_ = bf16[2,8,64,128]{3,2,1,0:T(8,128)(2,1)S(1)} collective-permute-done((bf16[2,8,64,128]{3,2,1,0:T(8,128)(2,1)S(1)}, bf16[2,8,64,128]{3,2,1,0:T(8,128)(2,1)S(1)}, u32[]{:S(2)}, u32[]{:S(2)}) %collective-permute-start.4) | collective-permute-done | bytes 262176 | tf_op jit(solution)/shard_map/ppermute | solution.py:616
  23.5 0.0 collective-permute-start.9
  23.5 0.7 %collective-permute-start.8 = (bf16[2,8,64,128]{3,2,1,0:T(8,128)(2,1)S(1)}, bf16[2,8,64,128]{3,2,1,0:T(8,128)(2,1)S(1)}, u32[]{:S(2)}, u32[]{:S(2)}) collective-permute-start(bf16[2,8,64,128]{3,2,1,0:T(8,128)(2,1)S(1)} %collective-permute-done.4.refs_3_), channel_id=1, source_target_pairs={{0,8},{1,9},{2,0},{3,1},{4,6},{5,7},{6,14},{7,15},{8,16},{9,17},{1... | collective-permute-start | bytes 786440 | tf_op jit(solution)/shard_map/ppermute | solution.py:631
  24.3 1.9 %collective-permute-start.10 = (bf16[2,64,128]{2,1,0:T(8,128)(2,1)S(1)}, bf16[2,64,128]{2,1,0:T(8,128)(2,1)S(1)}, u32[]{:S(2)}, u32[]{:S(2)}) collective-permute-start(bf16[2,64,128]{2,1,0:T(8,128)(2,1)S(1)} %collective-permute-done.6.refs_8_), channel_id=1, source_target_pairs={{8,0},{9,1},{10,2},{11,3},{12,4},{13,5},{14,6},{15,7},{0,8},{1,9},... | collective-permute-start | bytes 98312 | tf_op jit(solution)/shard_map/ppermute | solution.py:627
  26.2 0.5 %collective-permute-done.11.refs_2_ = bf16[32,4096]{1,0:T(8,128)(2,1)S(1)} collective-permute-done((bf16[32,4096]{1,0:T(8,128)(2,1)S(1)}, bf16[32,4096]{1,0:T(8,128)(2,1)S(1)}, u32[]{:S(2)}, u32[]{:S(2)}) %collective-permute-start.11) | collective-permute-done | bytes 262176 | tf_op jit(solution)/shard_map/ppermute | solution.py:619
  26.6 0.0 slice-done
  26.6 0.0 slice-done.1
  26.6 0.0 slice-done.2
  26.6 0.0 slice-done.3
  26.7 3.0 %project.1 = (f32[2,32,512]{2,1,0:T(8,128)S(1)}, bf16[2,32,4096]{2,1,0:T(8,128)(2,1)S(1)}) custom-call(bf16[2,8192,512]{2,1,0:T(8,128)(2,1)S(1)} %bitcast.5, bf16[32,4096]{1,0:T(8,128)(2,1)S(1)} %bitcast.7, bf16[32,4096]{1,0:T(8,128)(2,1)S(1)} %collective-permute-done.11.refs_2_, f32[6,128,128]{2,1,0:T(8,128)S(1)} %get-tuple-element.53.refs_3_.refs_8_), custom_call_target="tpu_custom_call" | custom-call | flops 3000000000 | bytes 10000000 | tf_op jit(solution)/shard_map/project/pallas_call | solution.py:342
  29.6 0.0 collective-permute-done.10.refs_10_
  29.6 0.0 collective-permute-done.9.refs_4_
  29.6 0.3 collective-permute-done.8.refs_5_
  29.9 0.1 collective-permute-start.13
  30.0 1.6 %collective-permute-start.12 = (bf16[2,8,64,128]{3,2,1,0:T(8,128)(2,1)S(1)}, bf16[2,8,64,128]{3,2,1,0:T(8,128)(2,1)S(1)}, u32[]{:S(2)}, u32[]{:S(2)}) collective-permute-start(bf16[2,8,64,128]{3,2,1,0:T(8,128)(2,1)S(1)} %collective-permute-done.8.refs_5_), channel_id=1, source_target_pairs={{0,8},{1,9},{2,0},{3,1},{4,6},{5,7},{6,14},{7,15},{8,16},{9,17},{1... | collective-permute-start | bytes 786440 | tf_op jit(solution)/shard_map/ppermute | solution.py:644
  31.6 5.1 %merge.2 = (bf16[2,8192,512]{2,1,0:T(8,128)(2,1)}, bf16[2,64,512]{2,1,0:T(8,128)(2,1)S(1)}, f32[2,32,64]{2,1,0:T(8,128)S(1)}) custom-call(bf16[2,8,64,128]{3,2,1,0:T(8,128)(2,1)S(1)} %get-tuple-element.38.refs_5_.refs_0_, bf16[2,8,64,128]{3,2,1,0:T(8,128)(2,1)S(1)} %collective-permute-done.2.refs_1_, ...), custom_call_target="tpu_custom_call" | custom-call | flops 3000000000 | bytes 10000000 | tf_op jit(solution)/shard_map/merge/pallas_call | solution.py:561
  36.8 0.0 collective-permute-done.13.refs_0_
  36.8 0.0 collective-permute-done.12.refs_1_
  36.8 3.4 %merge.3 = (bf16[2,8192,512]{2,1,0:T(8,128)(2,1)}, bf16[4,8,32,128]{3,2,1,0:T(8,128)(2,1)}) custom-call(bf16[2,8,64,128]{3,2,1,0:T(8,128)(2,1)S(1)} %collective-permute-done.13.refs_0_, bf16[2,8,64,128]{3,2,1,0:T(8,128)(2,1)S(1)} %collective-permute-done.12.refs_1_, ...), custom_call_target="tpu_custom_call", output_to_operand_aliasing={{0}: (12, {})} | custom-call | flops 3000000000 | bytes 10000000 | tf_op jit(solution)/shard_map/merge/pallas_call | solution.py:561
  (1 shorter events, 0.0 us)
Async XLA Ops:
  0.6 1.8 %collective-permute-start.1 = (bf16[2,64,64]{2,1,0:T(8,128)(2,1)}, bf16[2,64,64]{2,1,0:T(8,128)(2,1)S(1)}, u32[]{:S(2)}, u32[]{:S(2)}) collective-permute-start(bf16[2,64,64]{2,1,0:T(8,128)(2,1)} %up.1), channel_id=1, source_target_pairs={{0,4},{1,5},{2,6},{3,7},{4,0},{5,1},{6,2},{7,3},{8,12},{9,13},{10,... | collective-permute-start | bytes 49160 | tf_op jit(solution)/shard_map/ppermute | solution.py:599
  1.1 1.6 %collective-permute-start = (bf16[2,64,512]{2,1,0:T(8,128)(2,1)}, bf16[2,64,512]{2,1,0:T(8,128)(2,1)S(1)}, u32[]{:S(2)}, u32[]{:S(2)}) collective-permute-start(bf16[2,64,512]{2,1,0:T(8,128)(2,1)} %bitcast.12), channel_id=1, source_target_pairs={{0,4},{1,5},{2,6},{3,7},{4,0},{5,1},{6,2},{7,3},{8,12},{9,13},{10,... | collective-permute-start | bytes 393224 | tf_op jit(solution)/shard_map/ppermute | solution.py:599
  2.8 6.9 %collective-permute-start.3 = (bf16[2,64,128]{2,1,0:T(8,128)(2,1)S(1)}, bf16[2,64,128]{2,1,0:T(8,128)(2,1)S(1)}, u32[]{:S(2)}, u32[]{:S(2)}) collective-permute-start(bf16[2,64,128]{2,1,0:T(8,128)(2,1)S(1)} %get-tuple-element.39), channel_id=1, source_target_pairs={{0,0},{16,1},{2,2},{18,3},{4,4},{20,5},{6,6},{22,7},{8,8},{24,9},{... | collective-permute-start | bytes 98312 | tf_op jit(solution)/shard_map/ppermute | solution.py:611
  3.4 7.1 %collective-permute-start.2 = (bf16[2,8,64,128]{3,2,1,0:T(8,128)(2,1)S(1)}, bf16[2,8,64,128]{3,2,1,0:T(8,128)(2,1)S(1)}, u32[]{:S(2)}, u32[]{:S(2)}) collective-permute-start(bf16[2,8,64,128]{3,2,1,0:T(8,128)(2,1)S(1)} %get-tuple-element.38.refs_5_.refs_0_), channel_id=1, source_target_pairs={{0,8},{1,9},{2,0},{3,1},{4,6},{5,7},{6,14},{7,15},{8,16},{9,17},{1... | collective-permute-start | bytes 786440 | tf_op jit(solution)/shard_map/ppermute | solution.py:610
  6.2 10.9 %copy-start = (bf16[4,8,4096]{2,1,0:T(8,128)(2,1)S(1)}, bf16[4,8,4096]{2,1,0:T(8,128)(2,1)}, u32[]{:S(2)}) copy-start(bf16[4,8,4096]{2,1,0:T(8,128)(2,1)} %param.8) | copy-start | bytes 786436
  6.2 20.4 %slice-start = ((s8[16777216]{0:T(1024)(128)(4,1)}), s8[4194304]{0:T(1024)(128)(4,1)S(1)}, s32[]{:S(2)}) async-start(s8[16777216]{0:T(1024)(128)(4,1)} %bitcast.4), calls=%async_computation | async-start | bytes 8388608
  6.2 20.4 %slice-start.1 = ((s8[16777216]{0:T(1024)(128)(4,1)}), s8[4194304]{0:T(1024)(128)(4,1)S(1)}, s32[]{:S(2)}) async-start(s8[16777216]{0:T(1024)(128)(4,1)} %bitcast.4), calls=%async_computation.1 | async-start | bytes 8388608
  10.5 11.6 %collective-permute-start.7 = (bf16[2,64,128]{2,1,0:T(8,128)(2,1)S(1)}, bf16[2,64,128]{2,1,0:T(8,128)(2,1)S(1)}, u32[]{:S(2)}, u32[]{:S(2)}) collective-permute-start(bf16[2,64,128]{2,1,0:T(8,128)(2,1)S(1)} %collective-permute-done.3.refs_7_), channel_id=1, source_target_pairs={{8,0},{9,1},{10,2},{11,3},{12,4},{13,5},{14,6},{15,7},{0,8},{1,9},... | collective-permute-start | bytes 98312 | tf_op jit(solution)/shard_map/ppermute | solution.py:618
  14.2 7.9 %collective-permute-start.6 = (bf16[2,64,128]{2,1,0:T(8,128)(2,1)S(1)}, bf16[2,64,128]{2,1,0:T(8,128)(2,1)S(1)}, u32[]{:S(2)}, u32[]{:S(2)}) collective-permute-start(bf16[2,64,128]{2,1,0:T(8,128)(2,1)S(1)} %collective-permute-done.3.refs_7_), channel_id=1, source_target_pairs={{2,0},{3,1},{0,2},{1,3},{6,4},{7,5},{4,6},{5,7},{10,8},{11,9},{8,1... | collective-permute-start | bytes 98312 | tf_op jit(solution)/shard_map/ppermute | solution.py:617
  17.2 5.0 %collective-permute-start.5 = (bf16[2,8,64,128]{3,2,1,0:T(8,128)(2,1)S(1)}, bf16[2,8,64,128]{3,2,1,0:T(8,128)(2,1)S(1)}, u32[]{:S(2)}, u32[]{:S(2)}) collective-permute-start(bf16[2,8,64,128]{3,2,1,0:T(8,128)(2,1)S(1)} %collective-permute-done.2.refs_1_), channel_id=1, source_target_pairs={{0,4},{1,5},{2,6},{3,7},{4,0},{5,1},{6,2},{7,3},{8,12},{9,13},{10,... | collective-permute-start | bytes 786440 | tf_op jit(solution)/shard_map/ppermute | solution.py:616
  17.2 6.4 %collective-permute-start.4 = (bf16[2,8,64,128]{3,2,1,0:T(8,128)(2,1)S(1)}, bf16[2,8,64,128]{3,2,1,0:T(8,128)(2,1)S(1)}, u32[]{:S(2)}, u32[]{:S(2)}) collective-permute-start(bf16[2,8,64,128]{3,2,1,0:T(8,128)(2,1)S(1)} %collective-permute-done.2.refs_1_), channel_id=1, source_target_pairs={{0,8},{1,9},{2,0},{3,1},{4,6},{5,7},{6,14},{7,15},{8,16},{9,17},{1... | collective-permute-start | bytes 786440 | tf_op jit(solution)/shard_map/ppermute | solution.py:616
  17.2 9.5 %collective-permute-start.11 = (bf16[32,4096]{1,0:T(8,128)(2,1)S(1)}, bf16[32,4096]{1,0:T(8,128)(2,1)S(1)}, u32[]{:S(2)}, u32[]{:S(2)}) collective-permute-start(bf16[32,4096]{1,0:T(8,128)(2,1)S(1)} %bitcast.6), channel_id=1, source_target_pairs={{1,0},{0,1},{3,2},{2,3},{5,4},{4,5},{7,6},{6,7},{9,8},{8,9},{11,10... | collective-permute-start | bytes 786440 | tf_op jit(solution)/shard_map/ppermute | solution.py:619
  19.9 6.8 %slice-start.2 = ((s8[16777216]{0:T(1024)(128)(4,1)}), s8[4194304]{0:T(1024)(128)(4,1)S(1)}, s32[]{:S(2)}) async-start(s8[16777216]{0:T(1024)(128)(4,1)} %bitcast.4), calls=%async_computation.2 | async-start | bytes 8388608
  19.9 6.8 %slice-start.3 = ((s8[16777216]{0:T(1024)(128)(4,1)}), s8[4194304]{0:T(1024)(128)(4,1)S(1)}, s32[]{:S(2)}) async-start(s8[16777216]{0:T(1024)(128)(4,1)} %bitcast.4), calls=%async_computation.3 | async-start | bytes 8388608
  23.5 6.1 %collective-permute-start.9 = (bf16[2,8,64,128]{3,2,1,0:T(8,128)(2,1)S(1)}, bf16[2,8,64,128]{3,2,1,0:T(8,128)(2,1)S(1)}, u32[]{:S(2)}, u32[]{:S(2)}) collective-permute-start(bf16[2,8,64,128]{3,2,1,0:T(8,128)(2,1)S(1)} %collective-permute-done.4.refs_3_), channel_id=1, source_target_pairs={{0,4},{1,5},{2,6},{3,7},{4,0},{5,1},{6,2},{7,3},{8,12},{9,13},{10,... | collective-permute-start | bytes 786440 | tf_op jit(solution)/shard_map/ppermute | solution.py:631
  23.5 6.4 %collective-permute-start.8 = (bf16[2,8,64,128]{3,2,1,0:T(8,128)(2,1)S(1)}, bf16[2,8,64,128]{3,2,1,0:T(8,128)(2,1)S(1)}, u32[]{:S(2)}, u32[]{:S(2)}) collective-permute-start(bf16[2,8,64,128]{3,2,1,0:T(8,128)(2,1)S(1)} %collective-permute-done.4.refs_3_), channel_id=1, source_target_pairs={{0,8},{1,9},{2,0},{3,1},{4,6},{5,7},{6,14},{7,15},{8,16},{9,17},{1... | collective-permute-start | bytes 786440 | tf_op jit(solution)/shard_map/ppermute | solution.py:631
  24.3 5.3 %collective-permute-start.10 = (bf16[2,64,128]{2,1,0:T(8,128)(2,1)S(1)}, bf16[2,64,128]{2,1,0:T(8,128)(2,1)S(1)}, u32[]{:S(2)}, u32[]{:S(2)}) collective-permute-start(bf16[2,64,128]{2,1,0:T(8,128)(2,1)S(1)} %collective-permute-done.6.refs_8_), channel_id=1, source_target_pairs={{8,0},{9,1},{10,2},{11,3},{12,4},{13,5},{14,6},{15,7},{0,8},{1,9},... | collective-permute-start | bytes 98312 | tf_op jit(solution)/shard_map/ppermute | solution.py:627
  29.9 6.8 %collective-permute-start.13 = (bf16[2,8,64,128]{3,2,1,0:T(8,128)(2,1)S(1)}, bf16[2,8,64,128]{3,2,1,0:T(8,128)(2,1)S(1)}, u32[]{:S(2)}, u32[]{:S(2)}) collective-permute-start(bf16[2,8,64,128]{3,2,1,0:T(8,128)(2,1)S(1)} %collective-permute-done.8.refs_5_), channel_id=1, source_target_pairs={{0,4},{1,5},{2,6},{3,7},{4,0},{5,1},{6,2},{7,3},{8,12},{9,13},{10,... | collective-permute-start | bytes 786440 | tf_op jit(solution)/shard_map/ppermute | solution.py:644
  30.0 6.7 %collective-permute-start.12 = (bf16[2,8,64,128]{3,2,1,0:T(8,128)(2,1)S(1)}, bf16[2,8,64,128]{3,2,1,0:T(8,128)(2,1)S(1)}, u32[]{:S(2)}, u32[]{:S(2)}) collective-permute-start(bf16[2,8,64,128]{3,2,1,0:T(8,128)(2,1)S(1)} %collective-permute-done.8.refs_5_), channel_id=1, source_target_pairs={{0,8},{1,9},{2,0},{3,1},{4,6},{5,7},{6,14},{7,15},{8,16},{9,17},{1... | collective-permute-start | bytes 786440 | tf_op jit(solution)/shard_map/ppermute | solution.py:644

commit v9 on v8

--- a/solution.py
+++ b/solution.py
@@ -49,23 +49,8 @@
             pairs.append((self.flat(z, core, g, t), self.flat(to_z, core, to_g, t)))
         return pairs
 
-    def plane_step(self):
-        return [
-            (
-                self.flat(t * self.block + z % self.block, c, g, z // self.block),
-                self.flat(z, c, g, t),
-            )
-            for z, c, g, t in self.devices()
-        ]
-
-    def near_step(self, turn, shift):
-        pairs = []
-        for z, c, g, t in self.devices():
-            source = z - z % self.block + (z % self.block + shift) % self.block
-            pairs.append(
-                (self.flat(source, c, (g + turn) % self.grp, t), self.flat(z, c, g, t))
-            )
-        return pairs
+    def plane_swap(self):
+        return [(self.flat(z, c, g, t), self.flat(z, c, g, t ^ 1)) for z, c, g, t in self.devices()]
 
     def core_swap(self):
         return [
@@ -125,15 +110,20 @@
     return jnp.concatenate([up[k] for k in range(up.shape[0])], axis=1)
 
 
-def begin_all(down, up, len_hbm, q_hbm, pair, up_pair, lengths, order, q_ref, up_buf, sems, more):
+def plane_part():
+    return lax.rem(lax.axis_index("tp"), 2)
+
+
+def begin_all(down, up, len_hbm, q_hbm, pair, rest, lengths, order, q_ref, up_buf, sems, more):
     lanes = pair.shape[3]
-    count, _, depth = down.shape
+    depth = down.shape[2]
     tiles = depth // lanes
+    part = plane_part()
     copies = [
         pltpu.make_async_copy(
-            down.at[k, :, pl.ds(i * lanes, lanes)], pair.at[0, k * tiles + i], sems.at[k, i]
+            down.at[k, :, pl.ds(i * lanes, lanes)], array.at[0, i], sems.at[which, i]
         )
-        for k in range(count)
+        for which, (k, array) in enumerate(((part, pair), (1 - part, rest)))
         for i in range(tiles)
     ]
     up_copy = pltpu.make_async_copy(up, up_buf, more.at[0])
@@ -144,19 +134,21 @@
     len_copy.wait()
     sort_rows(lengths, order)
     up_copy.wait()
-    up_pair[lax.rem(lax.axis_index("fsdp"), 2)] = up_columns(up_buf)
+    columns = up_columns(up_buf)
+    pair[0, tiles, :, : columns.shape[1]] = columns
     for copy in copies + [q_copy]:
         copy.wait()
 
 
 def begin(down, up, lengths, queries):
     count, rank, depth = down.shape
+    tiles = depth // 128
     scalars = pltpu.SMEM(lengths.shape, jnp.int32)
     return pl.pallas_call(
         begin_all,
         out_shape=(
-            pltpu.VMEM((2, count * depth // 128, rank, 128), down.dtype),
-            pltpu.VMEM((2, rank, count * up.shape[2]), up.dtype),
+            pltpu.VMEM((2, tiles + 1, rank, 128), down.dtype),
+            pltpu.VMEM((2, tiles, rank, 128), down.dtype),
             scalars,
             scalars,
             pltpu.VMEM(queries.shape, queries.dtype),
@@ -165,7 +157,7 @@
         out_specs=(VMEM, VMEM, SMEM, SMEM, VMEM),
         scratch_shapes=[
             pltpu.VMEM(up.shape, up.dtype),
-            pltpu.SemaphoreType.DMA((count, depth // 128)),
+            pltpu.SemaphoreType.DMA((count, tiles)),
             pltpu.SemaphoreType.DMA((3,)),
         ],
         compiler_params=pltpu.CompilerParams(vmem_limit_bytes=2 * MIB),
@@ -174,27 +166,29 @@
     )(pinned(down), pinned(up), pinned(lengths), pinned(queries))
 
 
-def pack_other(down, up, _, __, pair, up_pair):
+def pack_other(down, up, _, __, pair, rest):
     lanes = pair.shape[3]
-    count, _, depth = down.shape
-    tiles = depth // lanes
-    for k in range(count):
-        for i in range(tiles):
-            pair[1, k * tiles + i] = down[k, :, i * lanes : (i + 1) * lanes]
-    up_pair[1 - lax.rem(lax.axis_index("fsdp"), 2)] = up_columns(up)
-
-
-def pack(down, up, pair, up_pair):
+    tiles = down.shape[2] // lanes
+    part = plane_part()
+    for i in range(tiles):
+        cols = slice(i * lanes, (i + 1) * lanes)
+        pair[1, i] = down[part, :, cols]
+        rest[1, i] = down[1 - part, :, cols]
+    columns = up_columns(up)
+    pair[1, tiles, :, : columns.shape[1]] = columns
+
+
+def pack(down, up, pair, rest):
     return pl.pallas_call(
         pack_other,
-        out_shape=(like(pair), like(up_pair)),
+        out_shape=(like(pair), like(rest)),
         in_specs=[VMEM] * 4,
         out_specs=(VMEM, VMEM),
         input_output_aliases={2: 0, 3: 1},
         compiler_params=pltpu.CompilerParams(vmem_limit_bytes=2 * MIB),
         cost_estimate=TYPICAL,
         name="pack_other",
-    )(down, up, pinned(pair, pltpu.VMEM), pinned(up_pair, pltpu.VMEM))
+    )(down, up, pinned(pair, pltpu.VMEM), pinned(rest, pltpu.VMEM))
 
 
 def attend_cache(pairs, ready, sizes, scale, *refs):
@@ -361,10 +355,11 @@
         there = jnp.where(lax.rem(self.grp, 2) == 0, self.z, lay.depth - 1 - self.z)
         self.own = self.grp * lay.depth + there
         self.per_lane = lay.fsdp * lay.grp // lay.tp
+        self.part = plane_part()
 
     def find(self, plan, downs):
         lay, found = self.lay, []
-        for (step, flip), down in zip(plan, downs):
+        for (step, flip, other), down in zip(plan, downs):
             towards = (1 - 2 * self.core if flip else 2 * self.core - 1) * step
             spot = lax.rem(self.own + (lay.ring + towards), lay.ring)
             g = spot // lay.depth
@@ -372,23 +367,26 @@
             zz = jnp.where(lax.rem(g, 2) == 0, along, lay.depth - 1 - along)
             for i in range(2):
                 core = lax.rem(self.core + (i + flip), 2)
-                found.append((down.at[i], (zz * 2 + core) * lay.grp + g))
+                index = (zz * 2 + core) * lay.grp + g
+                found.append((down.at[i], index, 1 - self.part if other else self.part))
         return found
 
-    def add_low(self, total, k, shards, h_ref, depth):
-        for down, index in shards:
-            tiles = depth // down.shape[-1]
+    def low(self, shards, h_ref, tiles):
+        total = None
+        for down, index, _ in shards:
+            depth = tiles * down.shape[-1]
             column = pl.multiple_of(lax.rem(index, self.per_lane) * depth, depth)
-            total += lax.dot_general(
+            term = lax.dot_general(
                 h_ref[index // self.per_lane, :, pl.ds(column, depth)],
-                jnp.concatenate([down[k * tiles + i] for i in range(tiles)], axis=1),
+                jnp.concatenate([down[i] for i in range(tiles)], axis=1),
                 (((1,), (1,)), ((), ())),
                 preferred_element_type=jnp.float32,
             )
+            total = term if total is None else total + term
         return total
 
 
-def merge_some(lay, plan, ups, n_caches, scale, *refs):
+def merge_some(lay, plan, n_caches, scale, *refs):
     refs = list(refs)
 
     def take(n):
@@ -396,47 +394,37 @@
         del refs[:n]
         return out
 
-    first, last = ups is not None, n_caches > 0
+    last = n_caches > 0
     downs = take(len(plan))
-    (h_buf,) = take(1)
-    if first:
-        up_refs = refs[: len(ups)]
-        weights = refs[len(ups)]
-        m_hbm, u_buf, low_out, m_buf, sems, u_parts = refs[-6:]
-    else:
+    h_buf, weights = take(2)
+    if last:
         old, order, q_ref = take(3)
         caches = [take(2) for _ in range(n_caches)]
-        u_buf, low_in, _, weights = take(4)
-        m_hbm, out_hbm, m_buf, sems, out_buf, out_sem = refs[-6:]
-    pairs, depth, width = m_buf.shape[1:]
+        u_buf, low_in, _ = take(3)
+        m_hbm, out_hbm, m_buf, sems, low, out_buf, out_sem = refs[-7:]
+    else:
+        m_hbm, u_buf, low, m_buf, sems, u_parts = refs[-6:]
+    depth, width = m_buf.shape[1:]
+    pairs = weights.shape[0]
     cut = min(width, 256)
     lanes = downs[0].shape[-1]
     tiles = depth // lanes
     place = Place(lay)
     shards = place.find(plan, downs)
-
-    if first:
-        columns = width // place.per_lane
-        for (turn, shift), up in zip(ups, up_refs):
-            zz = lax.rem(lax.rem(place.z, lay.block) + shift, lay.block)
-            g = lax.rem(place.grp + turn, lay.grp)
-            for c in range(2):
-                u_parts[(zz * 2 + c) * lay.grp + g] = up[c]
-        for k in range(pairs):
-            u_buf[k] = ADAPTER_SCALING * jnp.concatenate(
-                [
-                    u_parts[i, :, k * columns : (k + 1) * columns]
-                    for i in range(place.per_lane)
-                ],
-                axis=1,
-            )
+    groups = [
+        (place.part, [s for s, e in zip(shards, [e for e in plan for _ in range(2)]) if not e[2]]),
+        (1 - place.part, [s for s, e in zip(shards, [e for e in plan for _ in range(2)]) if e[2]]),
+    ]
 
     if last:
+        low[...] = low_in[...]
+        for part, group in groups:
+            if group:
+                low[part] += place.low(group, h_buf, tiles)
         new = []
         for k in range(pairs):
-            low = place.add_low(low_in[k], k, shards, h_buf, depth)
-            high = low.astype(jnp.bfloat16)
-            rest = (low - high.astype(jnp.float32)).astype(jnp.bfloat16)
+            high = low[k].astype(jnp.bfloat16)
+            rest = (low[k] - high.astype(jnp.float32)).astype(jnp.bfloat16)
             new.append(
                 (
                     old[k]
@@ -447,37 +435,48 @@
         add_new_tokens(q_ref, order, caches, new, out_buf, scale)
         out_copy = pltpu.make_async_copy(out_buf, out_hbm, out_sem)
         out_copy.start()
+    else:
+        columns = width // place.per_lane
+        for down, index, _ in groups[0][1]:
+
+            @pl.when(index // place.per_lane == place.tp)
+            def _():
+                u_parts[lax.rem(index, place.per_lane)] = down[tiles, :, : pairs * columns]
+
+        for k in range(pairs):
+            u_buf[k] = ADAPTER_SCALING * jnp.concatenate(
+                [
+                    u_parts[i, :, k * columns : (k + 1) * columns]
+                    for i in range(place.per_lane)
+                ],
+                axis=1,
+            )
 
     chunk = min(depth, 256)
     copies = []
-    for j, (down, index) in enumerate(shards):
+    for j, (down, index, k) in enumerate(shards):
         start = pl.multiple_of(index * depth, depth)
-        for k in range(pairs):
-            for begin in range(0, depth, chunk):
-                rows = slice(begin, begin + chunk)
-                tile = k * tiles + begin // lanes
-                d = jnp.concatenate([down[tile + i] for i in range(chunk // lanes)], axis=1)
-                for side in range(width // cut):
-                    cols = slice(side * cut, (side + 1) * cut)
-                    added = lax.dot_general(
-                        d,
-                        u_buf[k, :, cols],
-                        (((0,), (0,)), ((), ())),
-                        preferred_element_type=jnp.float32,
-                    )
-                    w = weights[k, pl.ds(start + begin, chunk), cols]
-                    m_buf[j, k, rows, cols] = (w.astype(jnp.float32) + added).astype(jnp.bfloat16)
-            copy = pltpu.make_async_copy(
-                m_buf.at[j, k], m_hbm.at[k, pl.ds(start, depth), :], sems.at[j, k]
-            )
-            copy.start()
-            copies.append(copy)
-
-    if first:
-        for k in range(pairs):
-            low_out[k] = place.add_low(
-                jnp.zeros(low_out.shape[1:], jnp.float32), k, shards, h_buf, depth
-            )
+        for begin in range(0, depth, chunk):
+            rows = slice(begin, begin + chunk)
+            tile = begin // lanes
+            d = jnp.concatenate([down[tile + i] for i in range(chunk // lanes)], axis=1)
+            for side in range(width // cut):
+                cols = slice(side * cut, (side + 1) * cut)
+                added = lax.dot_general(
+                    d,
+                    u_buf[k, :, cols],
+                    (((0,), (0,)), ((), ())),
+                    preferred_element_type=jnp.float32,
+                )
+                w = weights[k, pl.ds(start + begin, chunk), cols]
+                m_buf[j, rows, cols] = (w.astype(jnp.float32) + added).astype(jnp.bfloat16)
+        copy = pltpu.make_async_copy(m_buf.at[j], m_hbm.at[k, pl.ds(start, depth), :], sems.at[j])
+        copy.start()
+        copies.append(copy)
+
+    if not last:
+        for part, group in groups:
+            low[part] = place.low(group, h_buf, tiles)
     for copy in copies + ([out_copy] if last else []):
         copy.wait()
 
@@ -517,55 +516,51 @@
         out_buf[:, order[spot]] = piece.reshape(steps, heads, size)
 
 
-def merge(lay, shape, entries, states, w_buf, ups, state, final, after):
+def merge(lay, shape, entries, states, weights, state, final, after):
     pairs, total, width = shape
-    tokens, rank = states.shape[1], entries[0][2].shape[-2]
+    tokens, rank = states.shape[1], entries[0][3].shape[-2]
     depth = total // (lay.fsdp * lay.grp)
     per_lane = lay.fsdp * lay.grp // lay.tp
     n = 2 * len(entries)
     merged = pltpu.HBM(shape, jnp.bfloat16)
-    u_shape, low_shape = (pairs, rank, width), (pairs, tokens, rank)
-    operands = [e[2] for e in entries] + [pinned(states, pltpu.VMEM)]
-    scratch = [
-        pltpu.VMEM((n, pairs, depth, width), jnp.bfloat16),
-        pltpu.SemaphoreType.DMA((n, pairs)),
-    ]
+    low_shape = (pairs, tokens, rank)
+    operands = [e[3] for e in entries] + [pinned(states, pltpu.VMEM), pinned(weights, pltpu.VMEM)]
     specs = [VMEM] * len(operands)
+    scratch = [pltpu.VMEM((n, depth, width), jnp.bfloat16), pltpu.SemaphoreType.DMA((n,))]
+    aliases = {}
     if state is None:
-        operands += [x for _, _, x in ups] + [pinned(w_buf, pltpu.VMEM)]
-        specs += [VMEM] * (len(ups) + 1)
-        aliases = {}
         out_shape = [
             merged,
-            pltpu.VMEM(u_shape, jnp.bfloat16),
+            pltpu.VMEM((pairs, rank, width), jnp.bfloat16),
             pltpu.VMEM(low_shape, jnp.float32),
         ]
         out_specs = [HBM, VMEM, VMEM]
         scratch.append(pltpu.VMEM((per_lane, rank, pairs * width // per_lane), jnp.bfloat16))
         n_caches, scale = 0, 0.0
-        plan_ups = [(turn, shift) for turn, shift, _ in ups]
     else:
         olds, order, queries, caches = final
         m_prev, u_buf, low = state
         operands += [olds, pinned(order, pltpu.SMEM), pinned(queries, pltpu.VMEM), *caches]
         specs += [VMEM, SMEM, VMEM] + [VMEM] * len(caches)
-        operands += [pinned(u_buf, pltpu.VMEM), pinned(low, pltpu.VMEM)]
-        operands += [pinned(m_prev), pinned(w_buf, pltpu.VMEM)]
-        specs += [VMEM, VMEM, HBM, VMEM]
-        aliases = {len(operands) - 2: 0}
+        operands += [pinned(u_buf, pltpu.VMEM), pinned(low, pltpu.VMEM), pinned(m_prev)]
+        specs += [VMEM, VMEM, HBM]
+        aliases = {len(operands) - 1: 0}
         out_shape = [merged, pltpu.HBM(queries.shape, jnp.bfloat16)]
         out_specs = [HBM, HBM]
-        scratch += [pltpu.VMEM(queries.shape, jnp.bfloat16), pltpu.SemaphoreType.DMA]
+        scratch += [
+            pltpu.VMEM(low_shape, jnp.float32),
+            pltpu.VMEM(queries.shape, jnp.bfloat16),
+            pltpu.SemaphoreType.DMA,
+        ]
         n_caches, scale = len(caches) // 2, LOG2E / math.sqrt(queries.shape[3])
-        plan_ups = None
     return pl.pallas_call(
-        functools.partial(merge_some, lay, [e[:2] for e in entries], plan_ups, n_caches, scale),
+        functools.partial(merge_some, lay, [e[:3] for e in entries], n_caches, scale),
         out_shape=out_shape,
         in_specs=specs + [ANY] * len(after),
         out_specs=out_specs,
         input_output_aliases=aliases,
         scratch_shapes=scratch,
-        compiler_params=pltpu.CompilerParams(vmem_limit_bytes=18 * MIB),
+        compiler_params=pltpu.CompilerParams(vmem_limit_bytes=20 * MIB),
         cost_estimate=TYPICAL,
         name="merge",
     )(*operands, *after)
@@ -591,14 +586,14 @@
     tokens = hidden_states.reshape(steps * rows, features)
     keys = cache_keys.reshape(rows, slots * kv, size)
     values = cache_values.reshape(rows, slots * kv, size)
-    swap, ring = lay.core_swap(), lay.ring_step()
+    swap, ring, planes = lay.core_swap(), lay.ring_step(), lay.plane_swap()
     pair_count = rows // 2
     last_step = lay.ring // 2
     buffers, caches = [], []
 
     other, other_up = send(own, perm=swap), send(factor_up, perm=swap)
-    pair, up_pair, *rows_args = begin(own, factor_up, cache_lengths, queries)
-    pair, up_pair = pack(other, other_up, pair, up_pair)
+    pair, rest, *rows_args = begin(own, factor_up, cache_lengths, queries)
+    pair, rest = pack(other, other_up, pair, rest)
 
     def attention(pairs, ready, after):
         nonlocal buffers
@@ -607,49 +602,44 @@
         caches.extend(out[2:])
         return out[2]
 
-    came = send(pair, perm=ring)
-    up = send(up_pair, perm=lay.plane_step())
+    entries = [(0, 0, 0, pair), (0, 0, 1, rest)]
+    sent = send(pair, perm=ring)
+    hidden = [tokens] + [send(tokens, perm=lay.feature_step(i)) for i in range(1, lay.tp)]
     token = attention((0, 1), (0, 2), [pair])
-    (came, up, tokens), token = after_all((came, up, tokens), token)
-    entries = [(0, 0, pair), (1, 0, came)]
-
-    sent, swapped = send(came, perm=ring), send(came, perm=swap)
-    up_y = [send(up, perm=lay.near_step(turn, 0)) for turn in range(1, lay.grp)]
-    up_z = [send(up, perm=lay.near_step(0, shift)) for shift in range(1, lay.block)]
-    hidden = [tokens] + [send(tokens, perm=lay.feature_step(i)) for i in range(1, lay.tp)]
-    token = attention((1, pair_count), (2, pair_count), [token])
-    (came, swapped, up_y, up_z), token = after_all((sent, swapped, up_y, up_z), token)
-    entries += [(1, 1, swapped), (2, 0, came)]
-    ups = [(0, 0, up)] + [(turn + 1, 0, x) for turn, x in enumerate(up_y)]
-    ups += [(0, shift + 1, x) for shift, x in enumerate(up_z)]
-
-    up_yz = [
-        (turn + 1, shift, send(x, perm=lay.near_step(0, shift)))
-        for turn, x in enumerate(up_y)
-        for shift in range(1, lay.block)
-    ]
-    sent, swapped = send(came, perm=ring), send(came, perm=swap)
-    w_buf = projection_weight_matrices
-    olds, states = project(lay, w_buf, hidden, [token])
-    (came, swapped, diagonal), token = after_all(
-        (sent, swapped, [x for _, _, x in up_yz]), olds
+    came, token = after_all(sent, token)
+    crossed = []
+    for step in range(1, last_step):
+        entries.append((step, 0, 0, came))
+        crossed_on = [send(x, perm=swap) for x in crossed]
+        here = [send(came, perm=planes), send(came, perm=swap)]
+        sent = send(came, perm=ring)
+        waited = []
+        if step == 1:
+            waited = hidden
+            token = attention((1, pair_count), (2, pair_count), [token])
+        elif step == 2:
+            olds, states = project(lay, projection_weight_matrices, hidden, [token])
+            token = olds
+        (came, here, crossed_on, waited), token = after_all((sent, here, crossed_on, waited), token)
+        if step == 1:
+            hidden = waited
+        entries += [(step, 0, 1, here[0]), (step, 1, 0, here[1])]
+        entries += [(step - 1, 1, 1, x) for x in crossed_on]
+        crossed = here[:1]
+    entries.append((last_step, 0, 0, came))
+    late = [send(came, perm=planes), send(crossed[0], perm=swap)]
+    m, *state = merge(
+        lay, shape, entries, states, projection_weight_matrices, None, None, [token]
     )
-    entries += [(2, 1, swapped), (3, 0, came)]
-    ups += [(turn, shift, x) for (turn, shift, _), x in zip(up_yz, diagonal)]
-
-    for step in range(3, last_step - 1):
-        sent, swapped = send(came, perm=ring), send(came, perm=swap)
-        came, swapped = lax.optimization_barrier((sent, swapped))
-        entries += [(step, 1, swapped), (step + 1, 0, came)]
-    sent, swapped = send(came, perm=ring), send(came, perm=swap)
-    m, *state = merge(lay, shape, entries, states, w_buf, ups, None, None, [token])
-    (came, swapped), low = after_all((sent, swapped), state[1])
-    entries = [(last_step - 1, 1, swapped), (last_step, 0, came)]
+    late, state[1] = after_all(late, state[1])
+    entries = [(last_step, 0, 1, late[0]), (last_step - 1, 1, 1, late[1])]
     _, order, q = rows_args
-    m, attended = merge(
-        lay, shape, entries, states, w_buf, None, [m, state[0], low], (olds, order, q, caches), []
+    final = (olds, order, q, caches)
+    return tuple(
+        merge(
+            lay, shape, entries, states, projection_weight_matrices, [m, *state], final, []
+        )
     )
-    return m, attended
 
 
 def solution(mesh):

time: 40.4 us -> 41.4 us (1.025)
  starting transfers between devices: 17.7 us -> 13.6 us
  waiting for transfers between devices: 3.25 us -> 7.2 us
  Pallas kernels: 18.4 us -> 19.5 us
    ppermute x11 -> x14, waiting for transfers between devices: 2.51 us -> 7.19 us  [the longest x6 6.92 us: shards(): here = [send(came, perm=planes), send(came, perm=swap)]]
    ppermute x11 -> x14, starting transfers between devices: 14.4 us -> 10.1 us  [the longest x3 4.83 us: shards(): sent = send(came, perm=ring)]
    pallas_call x4, Pallas kernels: 9.81 us -> 10.4 us  [the longest x2 9.12 us: merge(): pl.pallas_call(functools.partial(merge_some, lay, [e[:3] for e in entries...]
    ppermute x1, waiting for transfers between devices: 0.46 us -> 0.01 us  [shards(): send(tokens, perm=lay.feature_step(i))]
    pallas_call x2, Pallas kernels: 5.69 us -> 6.11 us  [cache_attention(): pl.pallas_call(functools.partial(attend_cache, pairs, ready, sizes, scale...]
  transfers between devices with their start and end apart: 14 -> 17, of which waited for: 5 -> 4; matrix products, arithmetic and copies ran while one was open for 0% -> 0% of each run, Pallas kernels for 37% -> 41%
where the time goes in v9:
time: 41.4 us; the launch traced here: 41.2 us
  Pallas kernels  19.5 us (47%)
  starting transfers between devices  13.6 us (33%)
  waiting for transfers between devices  7.2 us (17%)
  between operations  0.93 us (2%)
    pallas_call x2, Pallas kernels, merge(): pl.pallas_call(functools.partial(merge_some, lay, [e[:3] for e in entries...  9.12 us
    ppermute x6, waiting for transfers between devices, shards(): here = [send(came, perm=planes), send(came, perm=swap)]  6.92 us
    pallas_call x2, Pallas kernels, cache_attention(): pl.pallas_call(functools.partial(attend_cache, pairs, ready, sizes, scale...  6.11 us
    ppermute x3, starting transfers between devices, shards(): sent = send(came, perm=ring)  4.83 us
    pallas_call x1, Pallas kernels, project(): pl.pallas_call(functools.partial(project_old, lay, len(hidden)), out_shap...  2.96 us
    ppermute x1, starting transfers between devices, shards(): send(tokens, perm=lay.feature_step(i))  2.92 us
    ppermute x6, starting transfers between devices, shards(): here = [send(came, perm=planes), send(came, perm=swap)]  2.4 us
    ppermute x1, starting transfers between devices, shards(): sent = send(pair, perm=ring)  1.6 us
  transfers between devices with their start and end apart: 17, of which 4 were waited for; matrix products, arithmetic and copies ran while one was open for 0% of the time, Pallas kernels for 41%

profile of v9, /device:TPU:0, one launch (start us, length us, event | category | flops | bytes accessed | tf_op | source)
XLA Modules:
  0.0 41.2 jit_solution(10074497342926743717)
XLA Ops:
  0.6 0.5 %collective-permute-start.1 = (bf16[2,64,64]{2,1,0:T(8,128)(2,1)}, bf16[2,64,64]{2,1,0:T(8,128)(2,1)S(1)}, u32[]{:S(2)}, u32[]{:S(2)}) collective-permute-start(bf16[2,64,64]{2,1,0:T(8,128)(2,1)} %up.1), channel_id=1, source_target_pairs={{0,4},{1,5},{2,6},{3,7},{4,0},{5,1},{6,2},{7,3},{8,12},{9,13},{10,... | collective-permute-start | bytes 49160 | tf_op jit(solution)/shard_map/ppermute | solution.py:594
  1.1 0.1 collective-permute-start
  1.2 2.9 %collective-permute-start.6 = (bf16[32,4096]{1,0:T(8,128)(2,1)}, bf16[32,4096]{1,0:T(8,128)(2,1)S(1)}, u32[]{:S(2)}, u32[]{:S(2)}) collective-permute-start(bf16[32,4096]{1,0:T(8,128)(2,1)} %bitcast.6), channel_id=1, source_target_pairs={{1,0},{0,1},{3,2},{2,3},{5,4},{4,5},{7,6},{6,7},{9,8},{8,9},{11,10... | collective-permute-start | bytes 786440 | tf_op jit(solution)/shard_map/ppermute | solution.py:607
  4.1 1.2 %begin.1 = (bf16[2,5,64,128]{3,2,1,0:T(8,128)(2,1)S(1)}, bf16[2,4,64,128]{3,2,1,0:T(8,128)(2,1)S(1)}, s32[8]{0:T(128)S(4)}, s32[8]{0:T(128)S(4)}, bf16[4,8,32,128]{3,2,1,0:T(8,128)(2,1)S(1)}) custom-call(bf16[2,64,512]{2,1,0:T(8,128)(2,1)} %bitcast.13, bf16[2,64,64]{2,1,0:T(8,128)(2,1)} %up.1, s32[8]{0:T(128)} %len_hbm.1, bf16[4,8,32,128]{3,2,1,0:T(8,128)(2,1)} %q_hbm.1), custom_call_target="tpu_custom_call" | custom-call | flops 3000000000 | bytes 10000000 | tf_op jit(solution)/shard_map/begin/pallas_call | solution.py:147
  5.3 0.0 collective-permute-done.1.up
  5.4 0.0 collective-permute-done.down
  5.4 0.1 pack_other.1
  5.4 1.6 %collective-permute-start.2 = (bf16[2,5,64,128]{3,2,1,0:T(8,128)(2,1)S(1)}, bf16[2,5,64,128]{3,2,1,0:T(8,128)(2,1)S(1)}, u32[]{:S(2)}, u32[]{:S(2)}) collective-permute-start(bf16[2,5,64,128]{3,2,1,0:T(8,128)(2,1)S(1)} %get-tuple-element.43.refs_5_.refs_0_), channel_id=1, source_target_pairs={{0,8},{1,9},{2,0},{3,1},{4,6},{5,7},{6,14},{7,15},{8,16},{9,17},{1... | collective-permute-start | bytes 491528 | tf_op jit(solution)/shard_map/ppermute | solution.py:606
  7.0 0.0 slice-start
  7.0 0.0 slice-start.1
  7.0 3.5 %cache_attention.2 = (bf16[8,3072,128]{2,1,0:T(8,128)(2,1)S(1)}, bf16[8,3072,128]{2,1,0:T(8,128)(2,1)S(1)}, f32[2,128,128]{2,1,0:T(8,128)S(1)}, f32[2,128,128]{2,1,0:T(8,128)S(1)}) custom-call(s32[8]{0:T(128)S(4)} %get-tuple-element.44.refs_0_, s32[8]{0:T(128)S(4)} %get-tuple-element.45.refs_1_.refs_5_, ...), custom_call_target="tpu_custom_call" | custom-call | flops 3000000000 | bytes 10000000 | tf_op jit(solution)/shard_map/cache_attention/pallas_call | solution.py:298
  10.5 0.3 collective-permute-done.2.refs_2_
  10.8 0.0 collective-permute-start.5
  10.8 0.4 %collective-permute-start.4 = (bf16[2,5,64,128]{3,2,1,0:T(8,128)(2,1)S(1)}, bf16[2,5,64,128]{3,2,1,0:T(8,128)(2,1)S(1)}, u32[]{:S(2)}, u32[]{:S(2)}) collective-permute-start(bf16[2,5,64,128]{3,2,1,0:T(8,128)(2,1)S(1)} %collective-permute-done.2.refs_2_), channel_id=1, source_target_pairs={{0,1},{1,0},{2,3},{3,2},{4,5},{5,4},{6,7},{7,6},{8,9},{9,8},{10,11... | collective-permute-start | bytes 491528 | tf_op jit(solution)/shard_map/ppermute | solution.py:614
  11.2 1.7 %collective-permute-start.3 = (bf16[2,5,64,128]{3,2,1,0:T(8,128)(2,1)S(1)}, bf16[2,5,64,128]{3,2,1,0:T(8,128)(2,1)S(1)}, u32[]{:S(2)}, u32[]{:S(2)}) collective-permute-start(bf16[2,5,64,128]{3,2,1,0:T(8,128)(2,1)S(1)} %collective-permute-done.2.refs_2_), channel_id=1, source_target_pairs={{0,8},{1,9},{2,0},{3,1},{4,6},{5,7},{6,14},{7,15},{8,16},{9,17},{1... | collective-permute-start | bytes 491528 | tf_op jit(solution)/shard_map/ppermute | solution.py:615
  12.9 2.6 %cache_attention.3 = (bf16[8,3072,128]{2,1,0:T(8,128)(2,1)S(1)}, bf16[8,3072,128]{2,1,0:T(8,128)(2,1)S(1)}, f32[6,128,128]{2,1,0:T(8,128)S(1)}, f32[6,128,128]{2,1,0:T(8,128)S(1)}) custom-call(s32[8]{0:T(128)S(4)} %get-tuple-element.44.refs_0_, s32[8]{0:T(128)S(4)} %get-tuple-element.45.refs_1_.refs_5_, ...), custom_call_target="tpu_custom_call", output_to_operand_aliasing={{0}: (5, {}), {1}: (6, {})} | custom-call | flops 3000000000 | bytes 10000000 | tf_op jit(solution)/shard_map/cache_attention/pallas_call | solution.py:298
  15.5 0.0 collective-permute-done.6.refs_2_
  15.6 0.0 collective-permute-done.5.refs_4_
  15.6 1.8 %collective-permute-done.4.refs_3_ = bf16[2,5,64,128]{3,2,1,0:T(8,128)(2,1)S(1)} collective-permute-done((bf16[2,5,64,128]{3,2,1,0:T(8,128)(2,1)S(1)}, bf16[2,5,64,128]{3,2,1,0:T(8,128)(2,1)S(1)}, u32[]{:S(2)}, u32[]{:S(2)}) %collective-permute-start.4) | collective-permute-done | bytes 163872 | tf_op jit(solution)/shard_map/ppermute | solution.py:614
  17.4 0.0 collective-permute-done.3.refs_5_
  17.4 0.0 collective-permute-start.9
  17.4 0.7 %collective-permute-start.8 = (bf16[2,5,64,128]{3,2,1,0:T(8,128)(2,1)S(1)}, bf16[2,5,64,128]{3,2,1,0:T(8,128)(2,1)S(1)}, u32[]{:S(2)}, u32[]{:S(2)}) collective-permute-start(bf16[2,5,64,128]{3,2,1,0:T(8,128)(2,1)S(1)} %collective-permute-done.3.refs_5_), channel_id=1, source_target_pairs={{0,1},{1,0},{2,3},{3,2},{4,5},{5,4},{6,7},{7,6},{8,9},{9,8},{10,11... | collective-permute-start | bytes 491528 | tf_op jit(solution)/shard_map/ppermute | solution.py:614
  18.1 1.6 %collective-permute-start.7 = (bf16[2,5,64,128]{3,2,1,0:T(8,128)(2,1)S(1)}, bf16[2,5,64,128]{3,2,1,0:T(8,128)(2,1)S(1)}, u32[]{:S(2)}, u32[]{:S(2)}) collective-permute-start(bf16[2,5,64,128]{3,2,1,0:T(8,128)(2,1)S(1)} %collective-permute-done.3.refs_5_), channel_id=1, source_target_pairs={{0,8},{1,9},{2,0},{3,1},{4,6},{5,7},{6,14},{7,15},{8,16},{9,17},{1... | collective-permute-start | bytes 491528 | tf_op jit(solution)/shard_map/ppermute | solution.py:615
  19.7 0.0 collective-permute-start.10
  19.7 0.0 slice-done
  19.7 0.0 slice-done.1
  19.7 0.0 slice-done.2
  19.7 0.0 slice-done.3
  19.7 0.0 copy-done
  19.8 3.0 %project.1 = (f32[2,32,512]{2,1,0:T(8,128)S(1)}, bf16[2,32,4096]{2,1,0:T(8,128)(2,1)S(1)}) custom-call(bf16[2,8192,512]{2,1,0:T(8,128)(2,1)S(1)} %bitcast.5, bf16[32,4096]{1,0:T(8,128)(2,1)S(1)} %bitcast.7, bf16[32,4096]{1,0:T(8,128)(2,1)S(1)} %collective-permute-done.6.refs_2_, f32[6,128,128]{2,1,0:T(8,128)S(1)} %get-tuple-element.57.refs_3_.refs_9_), custom_call_target="tpu_custom_call" | custom-call | flops 3000000000 | bytes 10000000 | tf_op jit(solution)/shard_map/project/pallas_call | solution.py:336
  22.7 0.0 collective-permute-done.10.refs_8_
  22.7 0.0 collective-permute-done.9.refs_7_
  22.7 1.3 %collective-permute-done.8.refs_6_ = bf16[2,5,64,128]{3,2,1,0:T(8,128)(2,1)S(1)} collective-permute-done((bf16[2,5,64,128]{3,2,1,0:T(8,128)(2,1)S(1)}, bf16[2,5,64,128]{3,2,1,0:T(8,128)(2,1)S(1)}, u32[]{:S(2)}, u32[]{:S(2)}) %collective-permute-start.8) | collective-permute-done | bytes 163872 | tf_op jit(solution)/shard_map/ppermute | solution.py:614
  24.0 0.0 collective-permute-done.7.refs_9_
  24.0 0.0 collective-permute-start.14
  24.0 0.5 %collective-permute-start.13 = (bf16[2,5,64,128]{3,2,1,0:T(8,128)(2,1)S(1)}, bf16[2,5,64,128]{3,2,1,0:T(8,128)(2,1)S(1)}, u32[]{:S(2)}, u32[]{:S(2)}) collective-permute-start(bf16[2,5,64,128]{3,2,1,0:T(8,128)(2,1)S(1)} %collective-permute-done.7.refs_9_), channel_id=1, source_target_pairs={{0,4},{1,5},{2,6},{3,7},{4,0},{5,1},{6,2},{7,3},{8,12},{9,13},{10,... | collective-permute-start | bytes 491528 | tf_op jit(solution)/shard_map/ppermute | solution.py:614
  24.5 0.7 %collective-permute-start.12 = (bf16[2,5,64,128]{3,2,1,0:T(8,128)(2,1)S(1)}, bf16[2,5,64,128]{3,2,1,0:T(8,128)(2,1)S(1)}, u32[]{:S(2)}, u32[]{:S(2)}) collective-permute-start(bf16[2,5,64,128]{3,2,1,0:T(8,128)(2,1)S(1)} %collective-permute-done.7.refs_9_), channel_id=1, source_target_pairs={{0,1},{1,0},{2,3},{3,2},{4,5},{5,4},{6,7},{7,6},{8,9},{9,8},{10,11... | collective-permute-start | bytes 491528 | tf_op jit(solution)/shard_map/ppermute | solution.py:614
  25.3 1.6 %collective-permute-start.11 = (bf16[2,5,64,128]{3,2,1,0:T(8,128)(2,1)S(1)}, bf16[2,5,64,128]{3,2,1,0:T(8,128)(2,1)S(1)}, u32[]{:S(2)}, u32[]{:S(2)}) collective-permute-start(bf16[2,5,64,128]{3,2,1,0:T(8,128)(2,1)S(1)} %collective-permute-done.7.refs_9_), channel_id=1, source_target_pairs={{0,8},{1,9},{2,0},{3,1},{4,6},{5,7},{6,14},{7,15},{8,16},{9,17},{1... | collective-permute-start | bytes 491528 | tf_op jit(solution)/shard_map/ppermute | solution.py:615
  26.8 0.0 collective-permute-done.14.refs_12_
  26.8 0.0 collective-permute-done.13.refs_11_
  26.9 3.8 %collective-permute-done.12.refs_10_ = bf16[2,5,64,128]{3,2,1,0:T(8,128)(2,1)S(1)} collective-permute-done((bf16[2,5,64,128]{3,2,1,0:T(8,128)(2,1)S(1)}, bf16[2,5,64,128]{3,2,1,0:T(8,128)(2,1)S(1)}, u32[]{:S(2)}, u32[]{:S(2)}) %collective-permute-start.12) | collective-permute-done | bytes 163872 | tf_op jit(solution)/shard_map/ppermute | solution.py:614
  30.6 0.0 collective-permute-done.11.refs_13_
  30.6 1.2 %collective-permute-start.15 = (bf16[2,5,64,128]{3,2,1,0:T(8,128)(2,1)S(1)}, bf16[2,5,64,128]{3,2,1,0:T(8,128)(2,1)S(1)}, u32[]{:S(2)}, u32[]{:S(2)}) collective-permute-start(bf16[2,5,64,128]{3,2,1,0:T(8,128)(2,1)S(1)} %collective-permute-done.11.refs_13_), channel_id=1, source_target_pairs={{0,1},{1,0},{2,3},{3,2},{4,5},{5,4},{6,7},{7,6},{8,9},{9,8},{10,11... | collective-permute-start | bytes 491528 | tf_op jit(solution)/shard_map/ppermute | solution.py:630
  31.9 0.0 collective-permute-start.16
  31.9 6.7 %merge.2 = (bf16[2,8192,512]{2,1,0:T(8,128)(2,1)}, bf16[2,64,512]{2,1,0:T(8,128)(2,1)S(1)}, f32[2,32,64]{2,1,0:T(8,128)S(1)}) custom-call(bf16[2,5,64,128]{3,2,1,0:T(8,128)(2,1)S(1)} %get-tuple-element.43.refs_5_.refs_0_, bf16[2,4,64,128]{3,2,1,0:T(8,128)(2,1)S(1)} %get-tuple-element.64.refs_1_, bf16[2,5,64,128]{3,2,1,0:T(8,128)(2,1)S(1)} %collective-permute-done.2.refs_2_, ...), custom_call_target="tpu_custom_call" | custom-call | flops 3000000000 | bytes 10000000 | tf_op jit(solution)/shard_map/merge/pallas_call | solution.py:556
  38.6 0.0 collective-permute-done.15.refs_0_
  38.6 0.0 collective-permute-done.16.refs_1_
  38.6 2.5 %merge.3 = (bf16[2,8192,512]{2,1,0:T(8,128)(2,1)}, bf16[4,8,32,128]{3,2,1,0:T(8,128)(2,1)}) custom-call(bf16[2,5,64,128]{3,2,1,0:T(8,128)(2,1)S(1)} %collective-permute-done.15.refs_0_, bf16[2,5,64,128]{3,2,1,0:T(8,128)(2,1)S(1)} %collective-permute-done.16.refs_1_, ...), custom_call_target="tpu_custom_call", output_to_operand_aliasing={{0}: (13, {})} | custom-call | flops 3000000000 | bytes 10000000 | tf_op jit(solution)/shard_map/merge/pallas_call | solution.py:556
  (4 shorter events, 0.0 us)
Async XLA Ops:
  0.6 4.7 %collective-permute-start.1 = (bf16[2,64,64]{2,1,0:T(8,128)(2,1)}, bf16[2,64,64]{2,1,0:T(8,128)(2,1)S(1)}, u32[]{:S(2)}, u32[]{:S(2)}) collective-permute-start(bf16[2,64,64]{2,1,0:T(8,128)(2,1)} %up.1), channel_id=1, source_target_pairs={{0,4},{1,5},{2,6},{3,7},{4,0},{5,1},{6,2},{7,3},{8,12},{9,13},{10,... | collective-permute-start | bytes 49160 | tf_op jit(solution)/shard_map/ppermute | solution.py:594
  1.1 4.2 %collective-permute-start = (bf16[2,64,512]{2,1,0:T(8,128)(2,1)}, bf16[2,64,512]{2,1,0:T(8,128)(2,1)S(1)}, u32[]{:S(2)}, u32[]{:S(2)}) collective-permute-start(bf16[2,64,512]{2,1,0:T(8,128)(2,1)} %bitcast.12), channel_id=1, source_target_pairs={{0,4},{1,5},{2,6},{3,7},{4,0},{5,1},{6,2},{7,3},{8,12},{9,13},{10,... | collective-permute-start | bytes 393224 | tf_op jit(solution)/shard_map/ppermute | solution.py:594
  1.2 14.3 %collective-permute-start.6 = (bf16[32,4096]{1,0:T(8,128)(2,1)}, bf16[32,4096]{1,0:T(8,128)(2,1)S(1)}, u32[]{:S(2)}, u32[]{:S(2)}) collective-permute-start(bf16[32,4096]{1,0:T(8,128)(2,1)} %bitcast.6), channel_id=1, source_target_pairs={{1,0},{0,1},{3,2},{2,3},{5,4},{4,5},{7,6},{6,7},{9,8},{8,9},{11,10... | collective-permute-start | bytes 786440 | tf_op jit(solution)/shard_map/ppermute | solution.py:607
  5.4 5.3 %collective-permute-start.2 = (bf16[2,5,64,128]{3,2,1,0:T(8,128)(2,1)S(1)}, bf16[2,5,64,128]{3,2,1,0:T(8,128)(2,1)S(1)}, u32[]{:S(2)}, u32[]{:S(2)}) collective-permute-start(bf16[2,5,64,128]{3,2,1,0:T(8,128)(2,1)S(1)} %get-tuple-element.43.refs_5_.refs_0_), channel_id=1, source_target_pairs={{0,8},{1,9},{2,0},{3,1},{4,6},{5,7},{6,14},{7,15},{8,16},{9,17},{1... | collective-permute-start | bytes 491528 | tf_op jit(solution)/shard_map/ppermute | solution.py:606
  7.0 12.7 %slice-start = ((s8[16777216]{0:T(1024)(128)(4,1)}), s8[4194304]{0:T(1024)(128)(4,1)S(1)}, s32[]{:S(2)}) async-start(s8[16777216]{0:T(1024)(128)(4,1)} %bitcast.4), calls=%async_computation | async-start | bytes 8388608
  7.0 12.7 %slice-start.1 = ((s8[16777216]{0:T(1024)(128)(4,1)}), s8[4194304]{0:T(1024)(128)(4,1)S(1)}, s32[]{:S(2)}) async-start(s8[16777216]{0:T(1024)(128)(4,1)} %bitcast.4), calls=%async_computation.1 | async-start | bytes 8388608
  10.8 4.8 %collective-permute-start.5 = (bf16[2,5,64,128]{3,2,1,0:T(8,128)(2,1)S(1)}, bf16[2,5,64,128]{3,2,1,0:T(8,128)(2,1)S(1)}, u32[]{:S(2)}, u32[]{:S(2)}) collective-permute-start(bf16[2,5,64,128]{3,2,1,0:T(8,128)(2,1)S(1)} %collective-permute-done.2.refs_2_), channel_id=1, source_target_pairs={{0,4},{1,5},{2,6},{3,7},{4,0},{5,1},{6,2},{7,3},{8,12},{9,13},{10,... | collective-permute-start | bytes 491528 | tf_op jit(solution)/shard_map/ppermute | solution.py:614
  10.8 6.6 %collective-permute-start.4 = (bf16[2,5,64,128]{3,2,1,0:T(8,128)(2,1)S(1)}, bf16[2,5,64,128]{3,2,1,0:T(8,128)(2,1)S(1)}, u32[]{:S(2)}, u32[]{:S(2)}) collective-permute-start(bf16[2,5,64,128]{3,2,1,0:T(8,128)(2,1)S(1)} %collective-permute-done.2.refs_2_), channel_id=1, source_target_pairs={{0,1},{1,0},{2,3},{3,2},{4,5},{5,4},{6,7},{7,6},{8,9},{9,8},{10,11... | collective-permute-start | bytes 491528 | tf_op jit(solution)/shard_map/ppermute | solution.py:614
  11.2 6.2 %collective-permute-start.3 = (bf16[2,5,64,128]{3,2,1,0:T(8,128)(2,1)S(1)}, bf16[2,5,64,128]{3,2,1,0:T(8,128)(2,1)S(1)}, u32[]{:S(2)}, u32[]{:S(2)}) collective-permute-start(bf16[2,5,64,128]{3,2,1,0:T(8,128)(2,1)S(1)} %collective-permute-done.2.refs_2_), channel_id=1, source_target_pairs={{0,8},{1,9},{2,0},{3,1},{4,6},{5,7},{6,14},{7,15},{8,16},{9,17},{1... | collective-permute-start | bytes 491528 | tf_op jit(solution)/shard_map/ppermute | solution.py:615
  12.9 6.8 %slice-start.2 = ((s8[16777216]{0:T(1024)(128)(4,1)}), s8[4194304]{0:T(1024)(128)(4,1)S(1)}, s32[]{:S(2)}) async-start(s8[16777216]{0:T(1024)(128)(4,1)} %bitcast.4), calls=%async_computation.2 | async-start | bytes 8388608
  12.9 6.8 %slice-start.3 = ((s8[16777216]{0:T(1024)(128)(4,1)}), s8[4194304]{0:T(1024)(128)(4,1)S(1)}, s32[]{:S(2)}) async-start(s8[16777216]{0:T(1024)(128)(4,1)} %bitcast.4), calls=%async_computation.3 | async-start | bytes 8388608
  12.9 6.8 %copy-start = (bf16[4,8,4096]{2,1,0:T(8,128)(2,1)S(1)}, bf16[4,8,4096]{2,1,0:T(8,128)(2,1)}, u32[]{:S(2)}) copy-start(bf16[4,8,4096]{2,1,0:T(8,128)(2,1)} %param.8) | copy-start | bytes 786436
  17.4 5.3 %collective-permute-start.9 = (bf16[2,5,64,128]{3,2,1,0:T(8,128)(2,1)S(1)}, bf16[2,5,64,128]{3,2,1,0:T(8,128)(2,1)S(1)}, u32[]{:S(2)}, u32[]{:S(2)}) collective-permute-start(bf16[2,5,64,128]{3,2,1,0:T(8,128)(2,1)S(1)} %collective-permute-done.3.refs_5_), channel_id=1, source_target_pairs={{0,4},{1,5},{2,6},{3,7},{4,0},{5,1},{6,2},{7,3},{8,12},{9,13},{10,... | collective-permute-start | bytes 491528 | tf_op jit(solution)/shard_map/ppermute | solution.py:614
  17.4 6.6 %collective-permute-start.8 = (bf16[2,5,64,128]{3,2,1,0:T(8,128)(2,1)S(1)}, bf16[2,5,64,128]{3,2,1,0:T(8,128)(2,1)S(1)}, u32[]{:S(2)}, u32[]{:S(2)}) collective-permute-start(bf16[2,5,64,128]{3,2,1,0:T(8,128)(2,1)S(1)} %collective-permute-done.3.refs_5_), channel_id=1, source_target_pairs={{0,1},{1,0},{2,3},{3,2},{4,5},{5,4},{6,7},{7,6},{8,9},{9,8},{10,11... | collective-permute-start | bytes 491528 | tf_op jit(solution)/shard_map/ppermute | solution.py:614
  18.1 5.9 %collective-permute-start.7 = (bf16[2,5,64,128]{3,2,1,0:T(8,128)(2,1)S(1)}, bf16[2,5,64,128]{3,2,1,0:T(8,128)(2,1)S(1)}, u32[]{:S(2)}, u32[]{:S(2)}) collective-permute-start(bf16[2,5,64,128]{3,2,1,0:T(8,128)(2,1)S(1)} %collective-permute-done.3.refs_5_), channel_id=1, source_target_pairs={{0,8},{1,9},{2,0},{3,1},{4,6},{5,7},{6,14},{7,15},{8,16},{9,17},{1... | collective-permute-start | bytes 491528 | tf_op jit(solution)/shard_map/ppermute | solution.py:615
  19.7 3.0 %collective-permute-start.10 = (bf16[2,5,64,128]{3,2,1,0:T(8,128)(2,1)S(1)}, bf16[2,5,64,128]{3,2,1,0:T(8,128)(2,1)S(1)}, u32[]{:S(2)}, u32[]{:S(2)}) collective-permute-start(bf16[2,5,64,128]{3,2,1,0:T(8,128)(2,1)S(1)} %collective-permute-done.4.refs_3_), channel_id=1, source_target_pairs={{0,4},{1,5},{2,6},{3,7},{4,0},{5,1},{6,2},{7,3},{8,12},{9,13},{10,... | collective-permute-start | bytes 491528 | tf_op jit(solution)/shard_map/ppermute | solution.py:613
  24.0 2.8 %collective-permute-start.14 = (bf16[2,5,64,128]{3,2,1,0:T(8,128)(2,1)S(1)}, bf16[2,5,64,128]{3,2,1,0:T(8,128)(2,1)S(1)}, u32[]{:S(2)}, u32[]{:S(2)}) collective-permute-start(bf16[2,5,64,128]{3,2,1,0:T(8,128)(2,1)S(1)} %collective-permute-done.8.refs_6_), channel_id=1, source_target_pairs={{0,4},{1,5},{2,6},{3,7},{4,0},{5,1},{6,2},{7,3},{8,12},{9,13},{10,... | collective-permute-start | bytes 491528 | tf_op jit(solution)/shard_map/ppermute | solution.py:613
  24.0 2.8 %collective-permute-start.13 = (bf16[2,5,64,128]{3,2,1,0:T(8,128)(2,1)S(1)}, bf16[2,5,64,128]{3,2,1,0:T(8,128)(2,1)S(1)}, u32[]{:S(2)}, u32[]{:S(2)}) collective-permute-start(bf16[2,5,64,128]{3,2,1,0:T(8,128)(2,1)S(1)} %collective-permute-done.7.refs_9_), channel_id=1, source_target_pairs={{0,4},{1,5},{2,6},{3,7},{4,0},{5,1},{6,2},{7,3},{8,12},{9,13},{10,... | collective-permute-start | bytes 491528 | tf_op jit(solution)/shard_map/ppermute | solution.py:614
  24.5 6.1 %collective-permute-start.12 = (bf16[2,5,64,128]{3,2,1,0:T(8,128)(2,1)S(1)}, bf16[2,5,64,128]{3,2,1,0:T(8,128)(2,1)S(1)}, u32[]{:S(2)}, u32[]{:S(2)}) collective-permute-start(bf16[2,5,64,128]{3,2,1,0:T(8,128)(2,1)S(1)} %collective-permute-done.7.refs_9_), channel_id=1, source_target_pairs={{0,1},{1,0},{2,3},{3,2},{4,5},{5,4},{6,7},{7,6},{8,9},{9,8},{10,11... | collective-permute-start | bytes 491528 | tf_op jit(solution)/shard_map/ppermute | solution.py:614
  25.3 5.4 %collective-permute-start.11 = (bf16[2,5,64,128]{3,2,1,0:T(8,128)(2,1)S(1)}, bf16[2,5,64,128]{3,2,1,0:T(8,128)(2,1)S(1)}, u32[]{:S(2)}, u32[]{:S(2)}) collective-permute-start(bf16[2,5,64,128]{3,2,1,0:T(8,128)(2,1)S(1)} %collective-permute-done.7.refs_9_), channel_id=1, source_target_pairs={{0,8},{1,9},{2,0},{3,1},{4,6},{5,7},{6,14},{7,15},{8,16},{9,17},{1... | collective-permute-start | bytes 491528 | tf_op jit(solution)/shard_map/ppermute | solution.py:615
  30.6 7.9 %collective-permute-start.15 = (bf16[2,5,64,128]{3,2,1,0:T(8,128)(2,1)S(1)}, bf16[2,5,64,128]{3,2,1,0:T(8,128)(2,1)S(1)}, u32[]{:S(2)}, u32[]{:S(2)}) collective-permute-start(bf16[2,5,64,128]{3,2,1,0:T(8,128)(2,1)S(1)} %collective-permute-done.11.refs_13_), channel_id=1, source_target_pairs={{0,1},{1,0},{2,3},{3,2},{4,5},{5,4},{6,7},{7,6},{8,9},{9,8},{10,11... | collective-permute-start | bytes 491528 | tf_op jit(solution)/shard_map/ppermute | solution.py:630
  31.9 6.7 %collective-permute-start.16 = (bf16[2,5,64,128]{3,2,1,0:T(8,128)(2,1)S(1)}, bf16[2,5,64,128]{3,2,1,0:T(8,128)(2,1)S(1)}, u32[]{:S(2)}, u32[]{:S(2)}) collective-permute-start(bf16[2,5,64,128]{3,2,1,0:T(8,128)(2,1)S(1)} %collective-permute-done.12.refs_10_), channel_id=1, source_target_pairs={{0,4},{1,5},{2,6},{3,7},{4,0},{5,1},{6,2},{7,3},{8,12},{9,13},{10,... | collective-permute-start | bytes 491528 | tf_op jit(solution)/shard_map/ppermute | solution.py:630
